TPU v7x, 32 devices: a whole 2x2x4 slice. The times are simulated.
32 devices in a mesh: gx: 4 (over x, core), gy: 8 (over z, y).
Axes of the slice: x: 2, y: 2, z: 4, core: 2. Of those that a mesh axis runs over, the one named last changes fastest.
Arguments:
- codes: int32 [32768, 1024], P(('gx', 'gy')), may hold values from 0 to 4095
- field_offsets: int32 [8, 1024], replicated, may hold values from 0 to 4095
- seg_mask: int32 [32768], P(('gx', 'gy')), may hold values from 0 to 1
- neg_mask: int32 [512, 512], P(('gx', 'gy')), may hold values from 0 to 1
- owners: int32 [256], replicated, may hold values from 0 to 255, each once
- w_hidden: float32 [256, 64, 64], P(('gx', 'gy')), may hold values from -0.1875 to 0.1875
- stat_left: float32 [256, 64, 64], P(('gx', 'gy')), as said below
- stat_right: float32 [256, 64, 64], P(('gx', 'gy')), as said below
- basis_left: float32 [256, 64, 64], P(('gx', 'gy')), as said below
- basis_right: float32 [256, 64, 64], P(('gx', 'gy')), as said below
- mom1_hidden: float32 [256, 64, 64], P(('gx', 'gy')), may hold values from -1.5258789e-05 to 1.5258789e-05
- mom2_hidden: float32 [256, 64, 64], P(('gx', 'gy')), may hold values from 5.0193387e-12 to 2.0077355e-11
- ema_hidden: float32 [256, 64, 64], P(('gx', 'gy')), may hold values from -0.1875 to 0.1875
- w_out: float32 [1024, 32], replicated, may hold values from -0.1875 to 0.1875
- mom1_out: float32 [1024, 32], replicated, may hold values from -3.0517578e-05 to 3.0517578e-05
- mom2_out: float32 [1024, 32], replicated, may hold values from 2.0077355e-11 to 8.030942e-11
- ema_out: float32 [1024, 32], replicated, may hold values from -0.1875 to 0.1875
- w_towers: float32 [2, 32, 32], replicated, may hold values from -0.5 to 0.5
- mom1_towers: float32 [2, 32, 32], replicated, may hold values from -7.6293945e-05 to 7.6293945e-05
- mom2_towers: float32 [2, 32, 32], replicated, may hold values from 1.2548346e-10 to 5.0193383e-10
- w_norm: float32 [2, 1024], replicated
- mom1_norm: float32 [2, 1024], replicated, may hold values from -0.00015258789 to 0.00015258789
- mom2_norm: float32 [2, 1024], replicated, may hold values from 5.0193383e-10 to 2.0077353e-09
Outputs:
- loss_sum: float32 [], replicated
- loss_count: float32 [], replicated
- grad_norm: float32 [], replicated
- w_hidden_new: float32 [256, 64, 64], P(('gx', 'gy'))
- w_hidden_low: bfloat16 [256, 64, 64], P(('gx', 'gy'))
- stat_left_new: float32 [256, 64, 64], P(('gx', 'gy'))
- stat_right_new: float32 [256, 64, 64], P(('gx', 'gy'))
- basis_left_new: float32 [256, 64, 64], P(('gx', 'gy'))
- basis_right_new: float32 [256, 64, 64], P(('gx', 'gy'))
- mom1_hidden_new: float32 [256, 64, 64], P(('gx', 'gy'))
- mom2_hidden_new: float32 [256, 64, 64], P(('gx', 'gy'))
- ema_hidden_new: float32 [256, 64, 64], P(('gx', 'gy'))
- w_out_new: float32 [1024, 32], replicated
- mom1_out_new: float32 [1024, 32], replicated
- mom2_out_new: float32 [1024, 32], replicated
- ema_out_new: float32 [1024, 32], replicated
- w_towers_new: float32 [2, 32, 32], replicated
- mom1_towers_new: float32 [2, 32, 32], replicated
- mom2_towers_new: float32 [2, 32, 32], replicated
- w_norm_new: float32 [2, 1024], replicated
- mom1_norm_new: float32 [2, 1024], replicated
- mom2_norm_new: float32 [2, 1024], replicated
Inputs may be any that keep to these rules, and one draw needn't show every extreme that they name: `stat_left`: symmetric positive definite. `stat_right`: symmetric positive definite. `basis_left`: orthogonal. `basis_right`: orthogonal.
All inputs are finite; a program needn't handle non-finite values.
Results may differ from a plain program's by a relative error of at most 0.0025.
The roundings to bfloat16 on the way count: a program that leaves them out, or rounds other values in their place, can miss the bound.
Values may be sent and summed in bfloat16 or wider, within the bound.
No kernel may reach another device: no remote copies, remote signals or barrier semaphores. Data moves between devices by JAX's collectives and lax.ppermute only.
A program may use at most 128 MiB of HBM per device.

v0:
```python
import math

import jax
import jax.numpy as jnp
from jax import lax
from jax.sharding import PartitionSpec as P

FIELDS = 4
BAG = 8
HASH_RANGE = 4096
STEP = 10


HIGH = lax.Precision.HIGHEST
BETA_ONE = 0.9
BETA_TWO = 0.95
EPSILON = 1e-08
RATE = 0.03
DECAY = 0.01
CLIP = 0.01
AVG_KEEP = 0.8
AVG_TAKE = 0.2


def mish(v):
    return v * jnp.tanh(jax.nn.softplus(v))


def to_blocks(full, side, bsize):
    return (
        full.reshape(side, bsize, side, bsize)
        .transpose(0, 2, 1, 3)
        .reshape(side * side, bsize, bsize)
    )


def from_blocks(blocks, side, bsize):
    return (
        blocks.reshape(side, side, bsize, bsize)
        .transpose(0, 2, 1, 3)
        .reshape(side * bsize, side * bsize)
    )


def hash_inputs(codes, field_offsets):
    width = codes.shape[1]
    salted = (
        codes.reshape(-1, 2 * FIELDS, BAG, width) + field_offsets[None, :, None, :]
    ) % HASH_RANGE
    scaled = salted.astype(jnp.float32) * (2.0 / (HASH_RANGE - 1)) - 1.0
    return scaled.reshape(-1, width).astype(jnp.bfloat16)


def contract_rows(left, right, precision=None, preferred_element_type=None):
    return lax.dot_general(
        left,
        right,
        (((0,), (0,)), ((), ())),
        precision=precision,
        preferred_element_type=preferred_element_type,
    )


def contract_cols(left, right, precision=None, preferred_element_type=None):
    return lax.dot_general(
        left,
        right,
        (((1,), (1,)), ((), ())),
        precision=precision,
        preferred_element_type=preferred_element_type,
    )


def orthonormal(stat, basis):
    power = jnp.dot(stat, basis, precision=HIGH)
    gram = jnp.dot(power.T, power, precision=HIGH)
    factor = jnp.linalg.cholesky(gram)
    return lax.linalg.triangular_solve(factor, power.T, left_side=True, lower=True).T


def soap(grad, weight, left, right, basis_l, basis_r, first, second):
    left_new = BETA_TWO * left + (1 - BETA_TWO) * jnp.dot(grad, grad.T, precision=HIGH)
    right_new = BETA_TWO * right + (1 - BETA_TWO) * jnp.dot(grad.T, grad, precision=HIGH)
    first_new = BETA_ONE * first + (1 - BETA_ONE) * grad
    turned = jnp.dot(jnp.dot(basis_l.T, grad, precision=HIGH), basis_r, precision=HIGH)
    second_new = BETA_TWO * second + (1 - BETA_TWO) * turned * turned
    moved = jnp.dot(jnp.dot(basis_l.T, first_new, precision=HIGH), basis_r, precision=HIGH) / (
        1 - BETA_ONE**STEP
    )
    ratio = moved / (jnp.sqrt(second_new / (1 - BETA_TWO**STEP)) + EPSILON)
    update = jnp.dot(jnp.dot(basis_l, ratio, precision=HIGH), basis_r.T, precision=HIGH)
    weight_new = weight - RATE * (update + DECAY * weight)
    return (
        weight_new,
        left_new,
        right_new,
        orthonormal(left_new, basis_l),
        orthonormal(right_new, basis_r),
        first_new,
        second_new,
    )


def adamw(grad, weight, first, second):
    first_new = BETA_ONE * first + (1 - BETA_ONE) * grad
    second_new = BETA_TWO * second + (1 - BETA_TWO) * grad * grad
    step = (
        first_new / (1 - BETA_ONE**STEP) / (jnp.sqrt(second_new / (1 - BETA_TWO**STEP)) + EPSILON)
    )
    return (weight - RATE * (step + DECAY * weight), first_new, second_new)


def on_device(
    codes,
    field_offsets,
    seg_mask,
    neg_mask,
    owners,
    w_hidden,
    stat_left,
    stat_right,
    basis_left,
    basis_right,
    mom1_hidden,
    mom2_hidden,
    ema_hidden,
    w_out,
    mom1_out,
    mom2_out,
    ema_out,
    w_towers,
    mom1_towers,
    mom2_towers,
    w_norm,
    mom1_norm,
    mom2_norm,
):
    local_blocks, bsize = (w_hidden.shape[0], w_hidden.shape[1])
    width, embed = (w_out.shape[0], w_out.shape[1])
    side = width // bsize
    gathered = lax.all_gather(w_hidden.astype(jnp.bfloat16), ("gx", "gy"), axis=0, tiled=True)
    w_first = from_blocks(gathered[jnp.argsort(owners)], side, bsize)
    inputs = hash_inputs(codes, field_offsets)
    live = seg_mask.astype(jnp.float32)[:, None]
    pre = jnp.dot(inputs, w_first, preferred_element_type=jnp.float32)
    neg_local = jnp.sum(neg_mask.astype(jnp.float32))
    sum_pre, live_total, neg_total = lax.psum(
        (jnp.sum(live * pre, axis=0), jnp.sum(live), neg_local), ("gx", "gy")
    )
    mean = sum_pre / live_total
    centered = pre - mean
    var = lax.psum(jnp.sum(live * centered * centered, axis=0), ("gx", "gy")) / live_total
    rstd = lax.rsqrt(var + 1e-05)
    normed = centered * rstd
    shifted = w_norm[0] * normed + w_norm[1]
    act_low = mish(shifted).astype(jnp.bfloat16)
    w_second = w_out.astype(jnp.bfloat16)
    emb = jnp.dot(act_low, w_second, preferred_element_type=jnp.float32)
    bags = (emb * live).reshape(-1, 2, FIELDS * BAG, embed).sum(axis=2)
    user = jnp.dot(bags[:, 0], w_towers[0], precision=HIGH)
    item = jnp.dot(bags[:, 1], w_towers[1], precision=HIGH)
    user_low = user.astype(jnp.bfloat16)
    all_items = lax.all_gather(item.astype(jnp.bfloat16), ("gx", "gy"), axis=0, tiled=True)
    root = math.sqrt(embed)
    logits = contract_cols(user_low, all_items, preferred_element_type=jnp.float32) / root
    rows = user.shape[0]
    total_rows = all_items.shape[0]
    first_row = lax.axis_index(("gx", "gy")) * rows
    own = lax.broadcasted_iota(jnp.int32, logits.shape, 1) == first_row + lax.broadcasted_iota(
        jnp.int32, logits.shape, 0
    )
    keep = own | (neg_mask == 1)
    top = jnp.max(jnp.where(keep, logits, -jnp.inf), axis=1, keepdims=True)
    weights = jnp.where(keep, jnp.exp(logits - top), 0.0)
    total = jnp.sum(weights, axis=1, keepdims=True)
    ce = top[:, 0] + jnp.log(total[:, 0]) - jnp.sum(jnp.where(own, logits, 0.0), axis=1)
    count = neg_total / total_rows
    dscores = (weights / total - own.astype(jnp.float32)) / count / root
    d_user = jnp.dot(dscores, all_items.astype(jnp.float32), precision=HIGH)
    d_item = lax.psum_scatter(
        contract_rows(dscores, user_low.astype(jnp.float32), precision=HIGH),
        ("gx", "gy"),
        scatter_dimension=0,
        tiled=True,
    )
    d_towers = jnp.stack(
        [
            jnp.dot(bags[:, 0].T, d_user, precision=HIGH),
            jnp.dot(bags[:, 1].T, d_item, precision=HIGH),
        ]
    )
    d_bags = jnp.stack(
        [
            jnp.dot(d_user, w_towers[0].T, precision=HIGH),
            jnp.dot(d_item, w_towers[1].T, precision=HIGH),
        ],
        axis=1,
    )
    spread = jnp.broadcast_to(d_bags[:, :, None, :], (rows, 2, FIELDS * BAG, embed)).reshape(
        -1, embed
    )
    d_emb = (spread * live).astype(jnp.bfloat16)
    d_second = contract_rows(act_low, d_emb, preferred_element_type=jnp.float32)
    d_act = contract_cols(d_emb, w_second, preferred_element_type=jnp.float32)
    unused, mish_back = jax.vjp(mish, shifted)
    d_shift = mish_back(d_act)[0]
    d_bias, d_gain, loss_sum = lax.psum(
        (jnp.sum(d_shift, axis=0), jnp.sum(d_shift * normed, axis=0), jnp.sum(ce)), ("gx", "gy")
    )
    d_pre = (
        live * w_norm[0] * rstd * (d_shift - d_bias / live_total - normed * d_gain / live_total)
    ).astype(jnp.bfloat16)
    d_first = contract_rows(inputs, d_pre, preferred_element_type=jnp.float32)
    d_norm = jnp.stack([d_gain, d_bias])
    slots = lax.axis_index(("gx", "gy")) * local_blocks + jnp.arange(local_blocks, dtype=jnp.int32)
    full_first, full_second, full_towers = lax.psum((d_first, d_second, d_towers), ("gx", "gy"))
    mine = to_blocks(full_first, side, bsize)[owners[slots]]
    squares = jnp.sum(full_first * full_first)
    squares = squares + jnp.sum(full_second * full_second) + jnp.sum(full_towers * full_towers)
    squares = squares + jnp.sum(d_norm * d_norm)
    grad_norm = jnp.sqrt(squares)
    factor = CLIP / jnp.maximum(grad_norm, CLIP)
    hidden = jax.vmap(soap)(
        mine * factor,
        w_hidden,
        stat_left,
        stat_right,
        basis_left,
        basis_right,
        mom1_hidden,
        mom2_hidden,
    )
    out_new = adamw(full_second * factor, w_out, mom1_out, mom2_out)
    towers_new = adamw(full_towers * factor, w_towers, mom1_towers, mom2_towers)
    norm_new = adamw(d_norm * factor, w_norm, mom1_norm, mom2_norm)
    return (
        loss_sum,
        count,
        grad_norm,
        hidden[0],
        hidden[0].astype(jnp.bfloat16),
        hidden[1],
        hidden[2],
        hidden[3],
        hidden[4],
        hidden[5],
        hidden[6],
        AVG_KEEP * ema_hidden + AVG_TAKE * hidden[0],
        out_new[0],
        out_new[1],
        out_new[2],
        AVG_KEEP * ema_out + AVG_TAKE * out_new[0],
        towers_new[0],
        towers_new[1],
        towers_new[2],
        norm_new[0],
        norm_new[1],
        norm_new[2],
    )


def solution(mesh):
    return jax.shard_map(
        on_device,
        mesh=mesh,
        in_specs=(
            P(("gx", "gy"), None),
            P(),
            P(("gx", "gy")),
            P(("gx", "gy"), None),
            P(),
            P(("gx", "gy"), None, None),
            P(("gx", "gy"), None, None),
            P(("gx", "gy"), None, None),
            P(("gx", "gy"), None, None),
            P(("gx", "gy"), None, None),
            P(("gx", "gy"), None, None),
            P(("gx", "gy"), None, None),
            P(("gx", "gy"), None, None),
            P(),
            P(),
            P(),
            P(),
            P(),
            P(),
            P(),
            P(),
            P(),
            P(),
        ),
        out_specs=(
            P(),
            P(),
            P(),
            P(("gx", "gy"), None, None),
            P(("gx", "gy"), None, None),
            P(("gx", "gy"), None, None),
            P(("gx", "gy"), None, None),
            P(("gx", "gy"), None, None),
            P(("gx", "gy"), None, None),
            P(("gx", "gy"), None, None),
            P(("gx", "gy"), None, None),
            P(("gx", "gy"), None, None),
            P(),
            P(),
            P(),
            P(),
            P(),
            P(),
            P(),
            P(),
            P(),
            P(),
        ),
        check_vma=False,
    )
```

profile of v0, /device:TPU:0, one launch (start us, length us, event | category | flops | bytes accessed | tf_op | source)
XLA Modules:
  0.0 833.4 jit_solution(11986226741456545240)
XLA Ops:
  7.3 1.7 convert_element_type.44
  9.7 4.3 fusion.4
  14.1 3.2 sort.17
  18.5 58.1 %all-gather.2.cloned.1.call-done = bf16[256,64,64]{2,1,0:T(8,128)(2,1)} async-done(((bf16[8,64,64]{2,1,0:T(8,128)(2,1)}), bf16[256,64,64]{2,1,0:T(8,128)(2,1)}) %all-gather.2.cloned.1.call-update) | async-done | bytes 2097168 | tf_op jit(solution)/shard_map/all_gather | solution.py:141
  76.6 5.2 gather_fusion
  81.8 7.6 copy.149
  89.4 6.5 reshape.116
  95.9 5.9 multiply_reduce_fusion.2
  101.8 39.3 %all-reduce.2 = (f32[1024]{0:T(1024)S(1)}, f32[]{:T(128)}) all-reduce(f32[1024]{0:T(1024)S(1)} %get-tuple-element.172, f32[]{:T(128)} %convert_reduce_fusion.1), channel_id=1, replica_groups=mesh['gx'=4,'gy'=8] {'gx','gy'}, use_global_device_ids=true, to_apply=%region_2.3 | all-reduce | flops 1025 | bytes 8200 | tf_op jit(solution)/shard_map/psum | solution.py:147
  141.8 2.8 fusion.5
  144.6 40.7 %all-reduce.1 = (f32[1024]{0:T(1024)S(1)}, f32[]{:T(128)}) all-reduce(f32[1024]{0:T(1024)S(1)} %fusion.5, f32[]{:T(128)} %convert_reduce_fusion), channel_id=1, replica_groups=mesh['gx'=4,'gy'=8] {'gx','gy'}, use_global_device_ids=true, to_apply=%region_6.7 | all-reduce | flops 1025 | bytes 8200 | tf_op jit(solution)/shard_map/psum | solution.py:152
  185.9 5.2 fusion.10
  193.8 66.5 %all_gather.7 = bf16[512,32]{1,0:T(8,128)(2,1)S(1)} all-gather(bf16[16,32]{1,0:T(8,128)(2,1)S(1)} %convolution_convert_fusion), channel_id=1, replica_groups=mesh['gx'=4,'gy'=8] {'gx','gy'}, dimensions={0}, use_global_device_ids=true | all-gather | bytes 33792 | tf_op jit(solution)/shard_map/all_gather | solution.py:163
  261.5 1.2 fusion.53
  263.9 129.8 %reduce-scatter.2.cloned.1.call-done = f32[16,32]{1,0:T(8,128)} async-done(((f32[512,32]{1,0:T(8,128)}), f32[16,32]{1,0:T(8,128)}) %reduce-scatter.2.cloned.1.call-update) | async-done | bytes 2064 | tf_op jit(solution)/shard_map/reduce_scatter | solution.py:180
  396.1 8.5 %fusion.55 = (f32[1024]{0:T(1024)S(1)}, f32[1024]{0:T(1024)S(1)}, f32[1024,1024]{1,0:T(8,128)}) fusion(f32[1024]{0:T(1024)S(1)} %add_rsqrt_fusion, f32[1024,1024]{1,0:T(8,128)} %get-tuple-element.173, f32[1024]{0:T(1024)S(1)} %broadcast_divide_fusion.1, f32[1024]{0:T(1024)S(1)} %bitcast.126, f32[1024]{0:T(1024)S(1)} %bitcast.123, ...), kind=kOutput, calls=%fused_computation.138 | convolution fusion | flops 94468096 | bytes 8679424 | tf_op jit(solution)/shard_map/dot_general | solution.py:65
  404.6 1.1 fusion.36
  406.0 37.5 %all-reduce = (f32[]{:T(128)}, f32[1024]{0:T(1024)S(1)}, f32[1024]{0:T(1024)S(1)}, f32[2,32,32]{2,1,0:T(8,128)S(1)}) all-reduce(f32[]{:T(128)} %subtract_reduce_fusion, f32[1024]{0:T(1024)S(1)} %get-tuple-element.137, f32[1024]{0:T(1024)S(1)} %get-tuple-element.136, ...), channel_id=1, replica_groups=mesh['gx'=4,'gy'=8] {'gx','gy'}, use_global_device_ids=true, to_apply=%region_12.13 | all-reduce | flops 4097 | bytes 32776 | tf_op jit(solution)/shard_map/psum | solution.py:207
  444.1 9.9 %fusion.11 = f32[1024,1024]{1,0:T(8,128)} fusion(bf16[1024,1024]{1,0:T(8,128)(2,1)} %copy-done.3, f32[1024,1024]{1,0:T(8,128)} %get-tuple-element.175, f32[1024,1024]{1,0:T(8,128)} %get-tuple-element.173, f32[]{:T(128)} %get-tuple-element.149, f32[1024]{0:T(1024)S(1)} %get-tuple-element.143, f32[1024]{0:T(1024)S(1)} %broadcast_divide_fusion, ...), kind=kOutput, calls=%fused_computation.32 | convolution fusion | flops 2157969408 | bytes 14704644 | tf_op jit(solution)/shard_map/dot_general | solution.py:55
  455.9 141.8 %all-reduce.6.cloned.1.call-done = (f32[1024,1024]{1,0:T(8,128)}, f32[1024,32]{0,1:T(8,128)}) async-done(((f32[1024,1024]{1,0:T(8,128)}, f32[1024,32]{0,1:T(8,128)}), (f32[1024,1024]{1,0:T(8,128)}, f32[1024,32]{0,1:T(8,128)})) %all-reduce.6.cloned.1.call-update) | async-done | bytes 4325392 | tf_op jit(solution)/shard_map/psum | solution.py:216
  597.7 3.9 multiply_reduce_fusion
  601.6 17.1 %reshape.119 = f32[16,64,16,64]{3,2,1,0:T(8,128)} reshape(f32[1024,1024]{1,0:T(8,128)} %get-tuple-element.150) | data formatting | bytes 8388608 | tf_op jit(solution)/shard_map/reshape | solution.py:31
  622.0 9.3 %copy.117 = f32[16,64,16,64]{3,1,2,0:T(8,128)} copy(f32[16,64,16,64]{3,2,1,0:T(8,128)} %reshape.119) | data formatting | bytes 8388608 | tf_op jit(solution)/shard_map/reshape | solution.py:31
  631.4 4.0 gather_fusion.2
  641.0 46.9 %custom-call.10 = f32[8,64,64]{2,1,0:T(8,128)S(1)} custom-call(f32[8,64,64]{2,1,0:T(8,128)S(1)} %fusion.20), custom_call_target="Cholesky" | custom-call | tf_op jit(solution)/shard_map/vmap(jit(cholesky))/cholesky | solution.py:77
  688.7 46.9 %custom-call.8 = f32[8,64,64]{2,1,0:T(8,128)S(1)} custom-call(f32[8,64,64]{2,1,0:T(8,128)S(1)} %fusion.23), custom_call_target="Cholesky" | custom-call | tf_op jit(solution)/shard_map/vmap(jit(cholesky))/cholesky | solution.py:77
  735.9 39.3 %custom-call.9 = f32[8,1,64,64]{2,3,1,0:T(8,128)S(1)} custom-call(f32[8,1,64,64]{3,2,1,0:T(8,128)S(1)} %get-tuple-element.169), custom_call_target="InvertDiagBlocksLowerTriangular" | custom-call | tf_op jit(solution)/shard_map/vmap()/triangular_solve/custom-call.0 | solution.py:78
  776.7 39.3 %custom-call.11 = f32[8,1,64,64]{2,3,1,0:T(8,128)S(1)} custom-call(f32[8,1,64,64]{3,2,1,0:T(8,128)S(1)} %get-tuple-element.168), custom_call_target="InvertDiagBlocksLowerTriangular" | custom-call | tf_op jit(solution)/shard_map/vmap()/triangular_solve/custom-call.0 | solution.py:78
  817.5 2.4 multiply_add_fusion.1
  819.9 1.4 multiply_subtract_fusion.1
  821.3 1.3 multiply_subtract_fusion.2
  822.6 1.8 multiply_add_fusion.3
  (119 shorter events, 22.9 us)
Async XLA Ops:
  7.2 629.4 %copy-start = (f32[8,64,64]{2,1,0:T(8,128)S(1)}, f32[8,64,64]{2,1,0:T(8,128)}, u32[]{:S(2)}) copy-start(f32[8,64,64]{2,1,0:T(8,128)} %param.35) | copy-start | bytes 393220
  7.2 10.0 %copy-start.22 = (s32[1024]{0:T(1024)S(1)}, s32[1024]{0:T(1024)}, u32[]{:S(2)}) copy-start(s32[1024]{0:T(1024)} %param.28) | copy-start | bytes 12292
  7.2 6.8 copy-start.1
  7.2 10.6 %copy-start.18 = (s32[16,512]{1,0:T(8,128)S(1)}, s32[16,512]{1,0:T(8,128)}, u32[]{:S(2)}) copy-start(s32[16,512]{1,0:T(8,128)} %param.29) | copy-start | bytes 98308
  7.2 11.2 %copy-start.20 = (f32[2,1024]{1,0:T(2,128)S(1)}, f32[2,1024]{1,0:T(2,128)}, u32[]{:S(2)}) copy-start(f32[2,1024]{1,0:T(2,128)} %param.46) | copy-start | bytes 24580
  7.2 69.3 %all-gather.2.cloned.1.call-start = ((), (), s32[]{:S(2)}) async-start(), calls=%async_computation.1 | async-start | bytes 4325376 | tf_op jit(solution)/shard_map/all_gather | solution.py:141
  9.0 384.8 %reduce-scatter.2.cloned.1.call-start = ((), (), s32[]{:S(2)}) async-start(), calls=%async_computation.2 | async-start | bytes 270336 | tf_op jit(solution)/shard_map/reduce_scatter | solution.py:180
  14.0 81.9 %copy-start.3 = (bf16[1024,1024]{1,0:T(8,128)(2,1)}, bf16[1024,1024]{1,0:T(8,128)(2,1)S(1)}, u32[]{:S(2)}) copy-start(bf16[1024,1024]{1,0:T(8,128)(2,1)S(1)} %fusion.4) | copy-start | bytes 6291460
  144.5 46.6 %copy-start.8 = (f32[1024,32]{0,1:T(8,128)S(1)}, f32[1024,32]{0,1:T(8,128)}, u32[]{:S(2)}) copy-start(f32[1024,32]{0,1:T(8,128)} %param.39) | copy-start | bytes 393220
  191.2 2.3 copy-start.10
  262.9 334.8 %all-reduce.6.cloned.1.call-start = ((), (), s32[]{:S(2)}) async-start(), calls=%async_computation.3 | async-start | bytes 8650752 | tf_op jit(solution)/shard_map/psum | solution.py:216
  396.1 9.7 %copy-start.21 = (f32[16,32]{1,0:T(8,128)S(1)}, f32[16,32]{1,0:T(8,128)}, u32[]{:S(2)}) copy-start(f32[16,32]{1,0:T(8,128)} %reduce-scatter.2.cloned.1.call-done) | copy-start | bytes 6148
  601.6 17.1 %copy-start.9 = (f32[1024,32]{0,1:T(8,128)S(1)}, f32[1024,32]{0,1:T(8,128)}, u32[]{:S(2)}) copy-start(f32[1024,32]{0,1:T(8,128)} %get-tuple-element.151) | copy-start | bytes 393220
  622.0 13.4 %copy-start.11 = (f32[8,64,64]{2,1,0:T(8,128)S(1)}, f32[8,64,64]{2,1,0:T(8,128)}, u32[]{:S(2)}) copy-start(f32[8,64,64]{2,1,0:T(8,128)} %param.36) | copy-start | bytes 393220
  622.0 13.4 %copy-start.2 = (f32[8,64,64]{2,1,0:T(8,128)S(1)}, f32[8,64,64]{2,1,0:T(8,128)}, u32[]{:S(2)}) copy-start(f32[8,64,64]{2,1,0:T(8,128)} %param.34) | copy-start | bytes 393220
  622.0 14.6 %copy-start.12 = (f32[8,64,64]{2,1,0:T(8,128)S(1)}, f32[8,64,64]{2,1,0:T(8,128)}, u32[]{:S(2)}) copy-start(f32[8,64,64]{2,1,0:T(8,128)} %param.37) | copy-start | bytes 393220
  631.3 6.8 copy-start.13
  631.3 7.4 copy-start.14
  635.4 5.3 copy-start.4
  637.1 0.7 copy-start.15
  638.7 137.2 %copy-start.5 = (f32[8,64,64]{2,1,0:T(8,128)}, f32[8,64,64]{2,1,0:T(8,128)S(1)}, u32[]{:S(2)}) copy-start(f32[8,64,64]{2,1,0:T(8,128)S(1)} %fusion.13) | copy-start | bytes 393220
  639.3 137.4 %copy-start.6 = (f32[8,64,64]{2,1,0:T(8,128)}, f32[8,64,64]{2,1,0:T(8,128)S(1)}, u32[]{:S(2)}) copy-start(f32[8,64,64]{2,1,0:T(8,128)S(1)} %fusion.12) | copy-start | bytes 393220
  640.1 177.4 %copy-start.7 = (f32[8,64,64]{2,1,0:T(8,128)S(1)}, f32[8,64,64]{2,1,0:T(8,128)}, u32[]{:S(2)}) copy-start(f32[8,64,64]{2,1,0:T(8,128)} %param.31) | copy-start | bytes 393220
  640.9 179.0 %copy-start.19 = (f32[2,32,32]{2,1,0:T(8,128)S(1)}, f32[2,32,32]{2,1,0:T(8,128)}, u32[]{:S(2)}) copy-start(f32[2,32,32]{2,1,0:T(8,128)} %param.44) | copy-start | bytes 24580
  640.9 180.4 %copy-start.23 = (f32[2,1024]{1,0:T(2,128)S(1)}, f32[2,1024]{1,0:T(2,128)}, u32[]{:S(2)}) copy-start(f32[2,1024]{1,0:T(2,128)} %param.47) | copy-start | bytes 24580
  641.0 181.7 %copy-start.16 = (f32[1024,32]{0,1:T(8,128)S(1)}, f32[1024,32]{0,1:T(8,128)}, u32[]{:S(2)}) copy-start(f32[1024,32]{0,1:T(8,128)} %param.42) | copy-start | bytes 393220
  641.0 181.7 %copy-start.17 = (f32[1024,32]{0,1:T(8,128)S(1)}, f32[1024,32]{0,1:T(8,128)}, u32[]{:S(2)}) copy-start(f32[1024,32]{0,1:T(8,128)} %param.40) | copy-start | bytes 393220
Sparse Core Ops, SparseCore 0:
  11.7 64.7 all-gather.1
  263.0 130.6 reduce-scatter.1
  454.1 143.5 all-reduce.5
where the time goes:
time: 843 us; the launch traced here: 833 us
  waiting for transfers between devices  330 us (39%)
  other arithmetic  206 us (24%)
  blocking collectives  184 us (22%)
  local copies, waits for them, and re-layouts  55.2 us (7%)
  matrix products  38.5 us (5%)
  between operations  20.2 us (2%)
    psum x1, waiting for transfers between devices, on_device(): lax.psum((d_first, d_second, d_towers), ('gx', 'gy'))  142 us
    reduce_scatter x1, waiting for transfers between devices, on_device(): lax.psum_scatter(contract_rows(dscores, user_low.astype(jnp.float32), pre...  130 us
    another operation x5, other arithmetic, orthonormal(): factor = jnp.linalg.cholesky(gram)  94 us
    another operation x4, other arithmetic, orthonormal(): lax.linalg.triangular_solve(factor, power.T, left_side=True, lower=True)  78.8 us
    all_gather x1, blocking collectives, on_device(): lax.all_gather(item.astype(jnp.bfloat16), ('gx', 'gy'), axis=0, tiled=True)  66.5 us
    all_gather x1, waiting for transfers between devices, on_device(): lax.all_gather(w_hidden.astype(jnp.bfloat16), ('gx', 'gy'), axis=0, tiled...  58.1 us
    psum x1, blocking collectives, on_device(): lax.psum(jnp.sum(live * centered * centered, axis=0), ('gx', 'gy'))  40.7 us
    psum x1, blocking collectives, on_device(): lax.psum((jnp.sum(live * pre, axis=0), jnp.sum(live), neg_local), ('gx',...  39.3 us
  transfers between devices with their start and end apart: 3, of which 3 were waited for; matrix products, arithmetic and copies ran while one was open for 1% of the time, Pallas kernels for 0%

commit v1 on v0

v1 whole, which is shorter than its diff:
```python
import functools
import math

import jax
import jax.numpy as jnp
from jax import lax
from jax.experimental import pallas as pl
from jax.experimental.pallas import tpu as pltpu
from jax.sharding import PartitionSpec as P

FIELDS = 4
BAG = 8
HASH_RANGE = 4096
STEP = 10
BETA_ONE = 0.9
BETA_TWO = 0.95
EPSILON = 1e-08
RATE = 0.03
DECAY = 0.01
CLIP = 0.01
AVG_KEEP = 0.8
AVG_TAKE = 0.2

F32 = jnp.float32
BF = jnp.bfloat16
HIGH = lax.Precision.HIGHEST
AXES = ("gx", "gy")
LANES = 128
SLOTS_BAG = FIELDS * BAG
PAIR = 16
MIB = 1 << 20


def dot(a, b, ca=1, cb=0, precision=None):
    return lax.dot_general(
        a, b, (((ca,), (cb,)), ((), ())), precision=precision, preferred_element_type=F32
    )


hdot = functools.partial(dot, precision=HIGH)


def spec(space=pltpu.VMEM):
    return pl.BlockSpec(memory_space=space)


def call(kernel, outs, args, smem=0, scratch=(), limit=32, name=None):
    specs = [spec(pltpu.SMEM)] * smem + [spec()] * (len(args) - smem)
    return pl.pallas_call(
        kernel,
        out_shape=[jax.ShapeDtypeStruct(s, t) for s, t in outs],
        in_specs=specs,
        out_specs=[spec() for _ in outs],
        scratch_shapes=list(scratch),
        compiler_params=pltpu.CompilerParams(vmem_limit_bytes=limit * MIB),
        name=name,
    )(*args)


def swap_halves(v):
    half = v.shape[1] // 2
    return jnp.concatenate([v[:, half:], v[:, :half]], axis=1)


class Plan:
    def __init__(self, gx, gy):
        self.gx, self.gy, self.n = gx, gy, gx * gy
        self.core = gy
        self.x = 2 * gy
        self.y = 1
        bits = []
        b = 2
        while b < gy:
            bits.append(b)
            b *= 2
        b = 4
        while b < gx:
            bits.append(b * gy)
            b *= 2
        self.bits = bits
        rest = [0]
        for b in bits:
            rest = rest + [m | b for m in rest]
        self.rest = rest

    def swap(self, a, mask):
        mx, my = mask // self.gy, mask % self.gy
        if my == 0:
            return lax.ppermute(a, "gx", [(i, i ^ mx) for i in range(self.gx)])
        if mx == 0:
            return lax.ppermute(a, "gy", [(i, i ^ my) for i in range(self.gy)])
        return lax.ppermute(a, AXES, [(i, i ^ mask) for i in range(self.n)])


def pack_kernel(me_ref, owners_ref, w_ref, neg_ref, seg_ref, out_ref, *, masked):
    local, bsize = w_ref.shape[0], w_ref.shape[1]
    half = bsize // 2
    for b in range(local):
        odd = owners_ref[me_ref[0] * local + b] % 2
        top, low = w_ref[b, :half, :], w_ref[b, half:, :]
        left = jnp.where(odd == 1, low, top)
        right = jnp.where(odd == 1, top, low)
        out_ref[b * half : (b + 1) * half, :] = jnp.concatenate([left, right], axis=1).astype(BF)
    at = local * half
    if masked:
        for c in range(neg_ref.shape[1] // LANES):
            part = neg_ref[:, c * LANES : (c + 1) * LANES].astype(F32)
            out_ref[at : at + PAIR, :] = part.astype(BF)
            at += PAIR
    used = jnp.sum(seg_ref[...].astype(F32), axis=0, keepdims=True)
    out_ref[at : at + PAIR, :] = jnp.broadcast_to(used, (PAIR, LANES)).astype(BF)


def gather_pieces(plan, payload, cut):
    stack = payload[None]
    if len(plan.rest) <= 4:
        stack = jnp.concatenate([stack] + [plan.swap(stack, m) for m in plan.rest[1:]], axis=0)
    else:
        for b in plan.bits:
            stack = jnp.concatenate([stack, plan.swap(stack, b)], axis=0)
    by_x = plan.swap(stack, plan.x)
    by_y = plan.swap(stack, plan.y)
    first = plan.swap(by_x[:, :cut], plan.y)
    second = plan.swap(by_y[:, cut:], plan.x)
    mine = [
        (stack, 0, 0),
        (by_x, plan.x, 0),
        (by_y, plan.y, 0),
        (first, plan.x | plan.y, 0),
        (second, plan.x | plan.y, cut),
    ]
    other = [(plan.swap(a, plan.core), m | plan.core, row) for a, m, row in mine]
    return mine + other


def hash_kernel(codes_ref, offsets_ref, x_ref, xt_ref):
    rows, width = codes_ref.shape
    groups = 2 * FIELDS
    salted = codes_ref[...].reshape(-1, groups, BAG, width) + offsets_ref[...][None, :, None, :]
    salted = (salted & (HASH_RANGE - 1)).reshape(rows, width)
    x = (salted.astype(F32) * (2.0 / (HASH_RANGE - 1)) - 1.0).astype(BF)
    x_ref[...] = x
    xt_ref[...] = x.T


def hash_inputs(codes, offsets):
    rows, width = codes.shape
    step = 128
    return pl.pallas_call(
        hash_kernel,
        grid=(rows // step,),
        in_specs=[
            pl.BlockSpec((step, width), lambda i: (i, 0)),
            pl.BlockSpec(offsets.shape, lambda i: (0, 0)),
        ],
        out_specs=[
            pl.BlockSpec((step, width), lambda i: (i, 0)),
            pl.BlockSpec((width, step), lambda i: (0, i)),
        ],
        out_shape=[
            jax.ShapeDtypeStruct((rows, width), BF),
            jax.ShapeDtypeStruct((width, rows), BF),
        ],
        compiler_params=pltpu.CompilerParams(vmem_limit_bytes=24 * MIB),
        cost_estimate=pl.CostEstimate(
            flops=10 * rows * width, bytes_accessed=8 * rows * width, transcendentals=0
        ),
        name="hash",
    )(codes, offsets)


def pre_kernel(*refs, holds, rest, local, masked, n, pieces):
    me_ref, owners_ref = refs[:2]
    piece_refs = refs[2 : 2 + pieces]
    x_ref, live_ref = refs[2 + pieces : 4 + pieces]
    pre_ref, stats_ref, count_ref, mask_ref, w_ref, row_ref = refs[4 + pieces :]
    width = x_ref.shape[1]
    bsize = LANES // 2
    half = bsize // 2
    side = width // bsize
    tiles = width // LANES
    me = me_ref[0]
    lane_half = lax.broadcasted_iota(jnp.int32, (half, LANES), 1) // bsize
    chunks = mask_ref.shape[1] // LANES if masked else 0
    for piece, (base, row0) in zip(piece_refs, holds):
        held = piece.shape[1]
        for k, m in enumerate(rest):
            d = me ^ (m | base)
            for b in range(local):
                at = b * half - row0
                if at < 0 or at + half > held:
                    continue
                q = owners_ref[d * local + b]
                r, c = q // side, q % side
                odd = c % 2
                tile = piece[k, at : at + half, :].astype(F32)
                rows = pl.multiple_of(r * bsize, bsize)
                cols = pl.multiple_of((c // 2) * LANES, LANES)
                keep = lane_half == odd
                pltpu.store(w_ref.at[pl.ds(rows, half), pl.ds(cols, LANES)], tile, mask=keep)
                pltpu.store(
                    w_ref.at[pl.ds(rows + half, half), pl.ds(cols, LANES)],
                    swap_halves(tile),
                    mask=keep,
                )
            for c in range(chunks):
                at = local * half + c * PAIR - row0
                if at < 0 or at + PAIR > held:
                    continue
                mask_ref[pl.ds(pl.multiple_of(d * PAIR, PAIR), PAIR), c * LANES : (c + 1) * LANES] = (
                    piece[k, at : at + PAIR, :]
                )
            at = local * half + chunks * PAIR - row0
            if 0 <= at and at + PAIR <= held:
                count_ref[pl.ds(d, 1), :] = piece[k, at : at + PAIR, :].astype(F32)[:1]
    live = live_ref[...]
    used = jnp.maximum(jnp.sum(live), 1.0)
    step = 2 * LANES
    for j in range(width // step):
        cols = slice(j * step, (j + 1) * step)
        pre_ref[:, cols] = dot(x_ref[...], w_ref[:, cols].astype(BF))
        total = jnp.sum(pre_ref[:, cols] * live, axis=0, keepdims=True)
        apart = pre_ref[:, cols] - total / used
        square = jnp.sum(apart * apart * live, axis=0, keepdims=True)
        for i in range(2):
            t = 2 * j + i
            row_ref[t : t + 1, :] = total[:, i * LANES : (i + 1) * LANES]
            row_ref[tiles + t : tiles + t + 1, :] = square[:, i * LANES : (i + 1) * LANES]
    for d in range(n):
        stats_ref[d * 2 * tiles : (d + 1) * 2 * tiles, :] = row_ref[...]


def act_kernel(
    stats_ref, count_ref, norm_ref, pre_ref, live_ref, w_out_ref,
    slope_ref, act_ref, one_ref, two_ref, coef_ref, bags_ref, pay_ref,
):
    n = count_ref.shape[0]
    rows, width = pre_ref.shape
    tiles = width // LANES
    counts = jnp.sum(count_ref[...], axis=1, keepdims=True)
    used = jnp.sum(counts)
    total = stats_ref[0:tiles, :]
    for d in range(1, n):
        total = total + stats_ref[2 * d * tiles : (2 * d + 1) * tiles, :]
    mean = total / used
    square = jnp.zeros_like(mean)
    for d in range(n):
        c = counts[d : d + 1, :]
        apart = stats_ref[2 * d * tiles : (2 * d + 1) * tiles, :] / jnp.maximum(c, 1.0) - mean
        square = square + (
            stats_ref[(2 * d + 1) * tiles : (2 * d + 2) * tiles, :] + c * apart * apart
        )
    rstd = lax.rsqrt(square / used + 1e-05)
    for j in range(tiles):
        coef_ref[0:1, j * LANES : (j + 1) * LANES] = mean[j : j + 1, :]
        coef_ref[1:2, j * LANES : (j + 1) * LANES] = rstd[j : j + 1, :]
    coef_ref[2:3, :] = jnp.full((1, width), used, F32)
    step = width // 2

    def bag(b, carry):
        at = pl.ds(pl.multiple_of(b * SLOTS_BAG, SLOTS_BAG), SLOTS_BAG)
        live = live_ref[at, :]
        for c in range(2):
            cols = slice(c * step, (c + 1) * step)
            xhat = (pre_ref[at, cols] - coef_ref[0:1, cols]) * coef_ref[1:2, cols]
            y = norm_ref[0:1, cols] * xhat + norm_ref[1:2, cols]
            capped = jnp.minimum(y, 20.0)
            e = jnp.exp(capped)
            top = e * (e + 2.0)
            below = top + 2.0
            guess = pl.reciprocal(below, approx=True)
            inv = guess * (2.0 - below * guess)
            gate = top * inv
            act = (y * gate).astype(BF).astype(F32)
            slope = gate + (4.0 * capped) * (e * inv) * ((1.0 + e) * inv)
            slope_ref[at, cols] = slope
            slope = slope * live
            act_ref[pl.ds(b, 1), cols] = jnp.sum(act * live, axis=0, keepdims=True)
            one_ref[pl.ds(b, 1), cols] = jnp.sum(slope, axis=0, keepdims=True)
            two_ref[pl.ds(b, 1), cols] = jnp.sum(slope * xhat, axis=0, keepdims=True)
        return carry

    lax.fori_loop(0, rows // SLOTS_BAG, bag, 0)
    second = w_out_ref[...].astype(BF).astype(F32)
    bags = hdot(act_ref[...], second)
    pairs = bags.shape[0] // 2
    split = jnp.concatenate([hdot(pick(pairs, 0), bags), hdot(pick(pairs, 1), bags)], axis=0)
    bags_ref[...] = split
    eighth = pairs // 2
    packed = jnp.concatenate([split[i * eighth : (i + 1) * eighth] for i in range(4)], axis=1)
    for d in range(n):
        pay_ref[d * eighth : (d + 1) * eighth, :] = packed


def pick(pairs, which):
    r = lax.broadcasted_iota(jnp.int32, (pairs, 2 * pairs), 0)
    c = lax.broadcasted_iota(jnp.int32, (pairs, 2 * pairs), 1)
    return (c == 2 * r + which).astype(F32)


def spread(pairs, which):
    r = lax.broadcasted_iota(jnp.int32, (2 * pairs, pairs), 0)
    c = lax.broadcasted_iota(jnp.int32, (2 * pairs, pairs), 1)
    return (r == 2 * c + which).astype(F32)


def three(v):
    a = v.astype(BF)
    v = v - a.astype(F32)
    b = v.astype(BF)
    v = v - b.astype(F32)
    return a, b, v.astype(BF)


def loss_kernel(
    me_ref, all_ref, mask_ref, towers_ref, w_out_ref, act_ref, one_ref, two_ref,
    dact_ref, pay_ref, d_towers_ref, scalar_ref,
    score_ref, user_ref, item_ref, second_ref, row_ref, *, n,
):
    me = me_ref[0]
    embed = towers_ref.shape[1]
    total_rows = mask_ref.shape[0]
    eighth = all_ref.shape[0] // n

    def full(i):
        a = all_ref[:, 2 * i * embed : (2 * i + 1) * embed].reshape(n, eighth, embed)
        b = all_ref[:, (2 * i + 1) * embed : (2 * i + 2) * embed].reshape(n, eighth, embed)
        return jnp.stack([a, b], axis=1).reshape(total_rows, embed)

    bags_user, bags_item = full(0), full(1)
    user = hdot(bags_user, towers_ref[0]).astype(BF)
    item = hdot(bags_item, towers_ref[1]).astype(BF)
    root = math.sqrt(embed)
    score_ref[...] = dot(user, item, 1, 1) / root
    negatives = jnp.sum(mask_ref[...].astype(F32))
    count = negatives / total_rows
    step = 32

    def rows(i, carry):
        at = pl.ds(pl.multiple_of(i * step, step), step)
        logits = score_ref[at, :]
        r = lax.broadcasted_iota(jnp.int32, logits.shape, 0) + i * step
        own = r == lax.broadcasted_iota(jnp.int32, logits.shape, 1)
        keep = own | (mask_ref[at, :].astype(F32) == 1.0)
        top = jnp.max(jnp.where(keep, logits, -jnp.inf), axis=1, keepdims=True)
        weights = jnp.where(keep, jnp.exp(logits - top), 0.0)
        total = jnp.sum(weights, axis=1, keepdims=True)
        hit = jnp.sum(jnp.where(own, logits, 0.0), axis=1, keepdims=True)
        score_ref[at, :] = (weights / total - own.astype(F32)) / count / root
        return carry + (top + jnp.log(total) - hit)

    ce = lax.fori_loop(0, total_rows // step, rows, jnp.zeros((step, 1), F32))
    scalar_ref[0:1, :] = jnp.full((1, LANES), jnp.sum(ce), F32)
    scalar_ref[1:2, :] = jnp.full((1, LANES), count, F32)
    parts = three(score_ref[...])
    d_user = sum(dot(p, item) for p in parts)
    d_item = sum(dot(user, p, 0, 0) for p in parts).T
    user_ref[...] = d_user
    item_ref[...] = d_item
    d_towers_ref[0] = hdot(bags_user, d_user, 0, 0)
    d_towers_ref[1] = hdot(bags_item, d_item, 0, 0)
    mine = pl.ds(pl.multiple_of(me * PAIR, PAIR), PAIR)
    back_user = hdot(user_ref[mine, :], towers_ref[0], 1, 1).astype(BF).astype(F32)
    back_item = hdot(item_ref[mine, :], towers_ref[1], 1, 1).astype(BF).astype(F32)
    d_emb = dot(spread(PAIR, 0), back_user) + dot(spread(PAIR, 1), back_item)
    d_act = dot(d_emb.astype(BF), w_out_ref[...].astype(BF), 1, 1)
    dact_ref[...] = d_act
    d_bias = jnp.sum(d_act * one_ref[...], axis=0, keepdims=True)
    d_gain = jnp.sum(d_act * two_ref[...], axis=0, keepdims=True)
    d_low = d_emb.T.astype(BF)
    second_ref[...] = sum(dot(d_low, p) for p in three(act_ref[...]))
    width = act_ref.shape[1]
    tiles = width // LANES
    for j in range(tiles):
        cols = slice(j * LANES, (j + 1) * LANES)
        row_ref[j : j + 1, :] = d_bias[:, cols]
        row_ref[tiles + j : tiles + j + 1, :] = d_gain[:, cols]
    chunk = embed * tiles // n
    for d in range(n):
        at = d * (2 * tiles + chunk)
        pay_ref[at : at + 2 * tiles, :] = row_ref[...]
        for i in range(chunk):
            e, j = (d * chunk + i) // tiles, (d * chunk + i) % tiles
            pay_ref[at + 2 * tiles + i : at + 2 * tiles + i + 1, :] = second_ref[
                e : e + 1, j * LANES : (j + 1) * LANES
            ]


def loss_spread(plan, bags, neg_mask, towers, w_out, act, one, two):
    embed = towers.shape[1]
    rows = neg_mask.shape[0]
    bags_user, bags_item = bags[:rows], bags[rows:]
    user = hdot(bags_user, towers[0]).astype(BF)
    item = hdot(bags_item, towers[1]).astype(BF)
    items = lax.all_gather(item, AXES, axis=0, tiled=True)
    root = math.sqrt(embed)
    logits = dot(user, items, 1, 1) / root
    at = lax.axis_index(AXES) * rows + lax.broadcasted_iota(jnp.int32, logits.shape, 0)
    own = lax.broadcasted_iota(jnp.int32, logits.shape, 1) == at
    keep = own | (neg_mask == 1)
    top = jnp.max(jnp.where(keep, logits, -jnp.inf), axis=1, keepdims=True)
    weights = jnp.where(keep, jnp.exp(logits - top), 0.0)
    total = jnp.sum(weights, axis=1, keepdims=True)
    ce = top + jnp.log(total) - jnp.sum(jnp.where(own, logits, 0.0), axis=1, keepdims=True)
    count = lax.psum(jnp.sum(neg_mask.astype(F32)), AXES) / items.shape[0]
    scores = (weights / total - own.astype(F32)) / count / root
    d_user = hdot(scores, items.astype(F32))
    d_item = lax.psum_scatter(
        hdot(scores, user.astype(F32), 0, 0), AXES, scatter_dimension=0, tiled=True
    )
    d_towers = jnp.stack([hdot(bags_user, d_user, 0, 0), hdot(bags_item, d_item, 0, 0)])
    back = jnp.stack([hdot(d_user, towers[0], 1, 1), hdot(d_item, towers[1], 1, 1)], axis=1)
    d_emb = back.reshape(2 * rows, embed).astype(BF)
    d_act = dot(d_emb, w_out.astype(BF), 1, 1)
    d_second = hdot(d_emb.astype(F32), act, 0, 0)
    sums = jnp.stack([jnp.sum(d_act * one, axis=0), jnp.sum(d_act * two, axis=0)])
    sums, d_second, d_towers, loss = lax.psum((sums, d_second, d_towers, jnp.sum(ce)), AXES)
    return d_act, sums.reshape(-1, LANES), d_second, d_towers, loss, count


def grad_kernel(
    me_ref, owners_ref, sums_ref, coef_ref, norm_ref, dact_ref, slope_ref, pre_ref, live_ref, xt_ref,
    keep_ref, send_ref, chunk_ref, d_norm_ref, d_pre_ref, g_ref, row_ref,
    *, parts, order, local,
):
    rows, width = pre_ref.shape
    tiles = width // LANES
    held = sums_ref.shape[0] // parts
    total = sums_ref[0:held, :]
    for d in range(1, parts):
        total = total + sums_ref[d * held : (d + 1) * held, :]
    d_norm_ref[0:tiles, :] = total[tiles : 2 * tiles]
    d_norm_ref[tiles : 2 * tiles, :] = total[:tiles]
    chunk_ref[...] = total[2 * tiles :] if held > 2 * tiles else jnp.zeros(chunk_ref.shape, F32)
    for j in range(tiles):
        cols = slice(j * LANES, (j + 1) * LANES)
        row_ref[0:1, cols] = total[j : j + 1]
        row_ref[1:2, cols] = total[tiles + j : tiles + j + 1]
    scale = norm_ref[0:1, :] * coef_ref[1:2, :]
    flat = scale * row_ref[0:1, :] / coef_ref[2:3, :]
    tilt = scale * row_ref[1:2, :] / coef_ref[2:3, :] * coef_ref[1:2, :]
    row_ref[2:3, :] = scale
    row_ref[3:4, :] = flat
    row_ref[4:5, :] = tilt
    step = width // 2

    def bag(b, carry):
        at = pl.ds(pl.multiple_of(b * SLOTS_BAG, SLOTS_BAG), SLOTS_BAG)
        live = live_ref[at, :]
        for c in range(2):
            cols = slice(c * step, (c + 1) * step)
            lead = dact_ref[pl.ds(b, 1), cols] * row_ref[2:3, cols]
            apart = (pre_ref[at, cols] - coef_ref[0:1, cols]) * row_ref[4:5, cols]
            d_pre = live * (slope_ref[at, cols] * lead - row_ref[3:4, cols] - apart)
            d_pre_ref[at, cols] = d_pre.astype(BF)
        return carry

    lax.fori_loop(0, rows // SLOTS_BAG, bag, 0)
    block = 2 * LANES
    for j in range(width // block):
        cols = slice(j * block, (j + 1) * block)
        g_ref[:, cols] = dot(xt_ref[...], d_pre_ref[:, cols])
    bsize = LANES // 2
    half = bsize // 2
    side = width // bsize
    lane_half = lax.broadcasted_iota(jnp.int32, (half, LANES), 1) // bsize
    me = me_ref[0]
    for out, masks in ((keep_ref, order[0]), (send_ref, order[1])):
        for i, m in enumerate(masks):
            for b in range(local):
                q = owners_ref[(me ^ m) * local + b]
                r, c = q // side, q % side
                at = pl.ds(pl.multiple_of(r * bsize, bsize), half)
                low = pl.ds(pl.multiple_of(r * bsize + half, half), half)
                cols = pl.ds(pl.multiple_of((c // 2) * LANES, LANES), LANES)
                packed = jnp.where(
                    lane_half == c % 2, g_ref[at, cols], swap_halves(g_ref[low, cols])
                )
                to = (i * local + b) * half
                out[to : to + half, :] = packed.astype(out.dtype)


def scatter_sum(plan, keep, send, rows):
    rest = len(plan.rest)
    shape = (2, 2, rest, rows, LANES)
    got = plan.swap(send, plan.core)
    mine = (keep + got.astype(F32)).reshape(shape)
    cut = rows // 2
    one, two = mine[..., :cut, :], mine[..., cut:, :]
    got_one = plan.swap(one[1].astype(BF), plan.x)
    got_two = plan.swap(two[:, 1].astype(BF), plan.y)
    one = one[0] + got_one.astype(F32)
    two = two[:, 0] + got_two.astype(F32)
    got_one = plan.swap(one[1].astype(BF), plan.y)
    got_two = plan.swap(two[1].astype(BF), plan.x)
    one = one[0] + got_one.astype(F32)
    two = two[0] + got_two.astype(F32)
    both = jnp.concatenate([one, two], axis=1)
    if rest <= 4:
        got = [plan.swap(both[k].astype(BF), m) for k, m in enumerate(plan.rest) if k]
        total = both[0]
        for g in got:
            total = total + g.astype(F32)
        return total
    for b in reversed(plan.bits):
        both = both.reshape(2, -1, rows, LANES)
        both = both[0] + plan.swap(both[1].astype(BF), b).astype(F32)
    return both.reshape(rows, LANES)


def norm_kernel(g_ref, chunk_ref, pay_ref, *, n):
    squares = jnp.sum(g_ref[...] * g_ref[...]) + jnp.sum(chunk_ref[...] * chunk_ref[...])
    rows = pay_ref.shape[0] // n
    chunk = chunk_ref.shape[0]
    for d in range(n):
        pay_ref[d * rows : d * rows + chunk, :] = chunk_ref[...]
        pay_ref[d * rows + chunk : (d + 1) * rows, :] = jnp.full((rows - chunk, LANES), squares, F32)


def adamw(grad, weight, first, second):
    first = BETA_ONE * first + (1 - BETA_ONE) * grad
    second = BETA_TWO * second + (1 - BETA_TWO) * grad * grad
    step = (
        first / (1 - BETA_ONE**STEP) / (jnp.sqrt(second / (1 - BETA_TWO**STEP)) + EPSILON)
    )
    return weight - RATE * (step + DECAY * weight), first, second


def eliminate(mat_ref):
    size = mat_ref.shape[1]
    group = 8
    for g in range(size // group):
        at = g * group
        for i in range(group):
            j = at + i
            row = mat_ref[:, j : j + 1, :]
            inv = lax.rsqrt(row[:, :, j : j + 1])
            row = row * inv
            head = mat_ref[:, at : at + group, :]
            index = lax.broadcasted_iota(jnp.int32, (1, group, 1), 1)
            down = head - (head[:, :, j : j + 1] * inv) * row
            mat_ref[:, at : at + group, :] = jnp.where(
                index > i, down, jnp.where(index == i, row, head)
            )
            if at + group < size:
                tail = mat_ref[:, at + group :, :]
                mat_ref[:, at + group :, :] = tail - (tail[:, :, j : j + 1] * inv) * row


def step_kernel(
    me_ref, owners_ref, got_ref, g_ref, d_norm_ref, d_towers_ref,
    w_ref, left_ref, right_ref, bl_ref, br_ref, first_ref, second_ref, ema_ref,
    wo_ref, mo_ref, vo_ref, eo_ref, wt_ref, mt_ref, vt_ref, wn_ref, mn_ref, vn_ref,
    gn_out, w_out, low_out, left_out, right_out, bl_out, br_out, first_out, second_out, ema_out,
    wo_out, mo_out, vo_out, eo_out, wt_out, mt_out, vt_out, wn_out, mn_out, vn_out,
    mat_ref, wide_ref, dn_ref, *, n,
):
    local, bsize = w_ref.shape[0], w_ref.shape[1]
    half = bsize // 2
    width, embed = wo_ref.shape
    tiles = width // LANES
    held = got_ref.shape[0] // n
    if n > 1:
        chunk = embed * tiles // n
        squares = 0.0
        for d in range(n):
            squares = squares + got_ref[d * held + chunk : d * held + chunk + 1, :]
            for i in range(chunk):
                e, j = (d * chunk + i) // tiles, (d * chunk + i) % tiles
                wide_ref[e : e + 1, j * LANES : (j + 1) * LANES] = got_ref[
                    d * held + i : d * held + i + 1, :
                ]
        squares = jnp.max(squares)
    else:
        squares = jnp.max(got_ref[0:1, :LANES])
        wide_ref[...] = got_ref[8 : 8 + embed, :]
    squares = squares + jnp.sum(d_towers_ref[...] * d_towers_ref[...])
    squares = squares + jnp.sum(d_norm_ref[...] * d_norm_ref[...])
    norm = jnp.sqrt(jnp.full((1, LANES), squares, F32))
    gn_out[...] = norm
    factor = (CLIP / jnp.maximum(norm, CLIP))[:, :1]
    for b in range(local):
        odd = owners_ref[me_ref[0] * local + b] % 2
        tile = g_ref[b * half : (b + 1) * half, :]
        tile = jnp.where(odd == 1, swap_halves(tile), tile)
        grad = jnp.concatenate([tile[:, :bsize], tile[:, bsize:]], axis=0) * factor
        bl, br = bl_ref[b], br_ref[b]
        left = BETA_TWO * left_ref[b] + (1 - BETA_TWO) * hdot(grad, grad, 1, 1)
        right = BETA_TWO * right_ref[b] + (1 - BETA_TWO) * hdot(grad, grad, 0, 0)
        left_out[b], right_out[b] = left, right
        first = BETA_ONE * first_ref[b] + (1 - BETA_ONE) * grad
        first_out[b] = first
        turned = hdot(hdot(bl, grad, 0, 0), br)
        second = BETA_TWO * second_ref[b] + (1 - BETA_TWO) * turned * turned
        second_out[b] = second
        moved = hdot(hdot(bl, first, 0, 0), br) / (1 - BETA_ONE**STEP)
        ratio = moved / (jnp.sqrt(second / (1 - BETA_TWO**STEP)) + EPSILON)
        update = hdot(hdot(bl, ratio), br, 1, 1)
        new = w_ref[b] - RATE * (update + DECAY * w_ref[b])
        w_out[b] = new
        low_out[b] = new.astype(BF)
        ema_out[b] = AVG_KEEP * ema_ref[b] + AVG_TAKE * new
        for i, (stat, basis) in enumerate(((left, bl), (right, br))):
            power = hdot(basis, stat, 0, 0)
            gram = hdot(power, power, 1, 1)
            mat_ref[2 * b + i] = jnp.concatenate([gram, power], axis=1)
    eliminate(mat_ref)
    for b in range(local):
        bl_out[b] = mat_ref[2 * b, :, bsize:].T
        br_out[b] = mat_ref[2 * b + 1, :, bsize:].T
    new, m, v = adamw(wide_ref[...].T * factor, wo_ref[...], mo_ref[...], vo_ref[...])
    wo_out[...], mo_out[...], vo_out[...] = new, m, v
    eo_out[...] = AVG_KEEP * eo_ref[...] + AVG_TAKE * new
    for t in range(2):
        wt_out[t], mt_out[t], vt_out[t] = adamw(
            d_towers_ref[t] * factor, wt_ref[t], mt_ref[t], vt_ref[t]
        )
        for j in range(tiles):
            dn_ref[t : t + 1, j * LANES : (j + 1) * LANES] = d_norm_ref[
                t * tiles + j : t * tiles + j + 1, :
            ]
    wn_out[...], mn_out[...], vn_out[...] = adamw(
        dn_ref[...] * factor, wn_ref[...], mn_ref[...], vn_ref[...]
    )


def exchange(payload):
    return lax.all_to_all(payload, AXES, 0, 0, tiled=True)


def on_device(
    plan,
    codes, field_offsets, seg_mask, neg_mask, owners,
    w_hidden, stat_left, stat_right, basis_left, basis_right, mom1_hidden, mom2_hidden, ema_hidden,
    w_out, mom1_out, mom2_out, ema_out,
    w_towers, mom1_towers, mom2_towers,
    w_norm, mom1_norm, mom2_norm,
):
    n = plan.n
    local, bsize = w_hidden.shape[0], w_hidden.shape[1]
    width, embed = w_out.shape
    slots = codes.shape[0]
    rows, total_rows = neg_mask.shape
    tiles = width // LANES
    half = bsize // 2
    bags = slots // SLOTS_BAG
    masked = total_rows <= 1024 and n <= embed
    me = lax.axis_index(AXES).astype(jnp.int32)[None]

    chunks = total_rows // LANES if masked else 0
    size = local * half + chunks * PAIR + PAIR
    (payload,) = call(
        functools.partial(pack_kernel, masked=masked),
        [((size, LANES), BF)],
        [me, owners, w_hidden, neg_mask, seg_mask.reshape(-1, LANES)],
        smem=2,
        name="pack",
    )
    cut = max(half, size // 2 // half * half)
    cut = min(cut, local * half)
    pieces = gather_pieces(plan, payload, cut)
    x, x_turned = hash_inputs(codes, field_offsets)
    live = seg_mask.astype(F32)[:, None]
    mask_shape = (total_rows, total_rows) if masked else (PAIR, LANES)
    pre, stats, counts, mask = call(
        functools.partial(
            pre_kernel,
            holds=[(m, row) for _, m, row in pieces],
            rest=plan.rest,
            local=local,
            masked=masked,
            n=n,
            pieces=len(pieces),
        ),
        [
            ((slots, width), F32),
            ((n * 2 * tiles, LANES), F32),
            ((n, LANES), F32),
            (mask_shape, BF),
        ],
        [me, owners] + [a for a, _, _ in pieces] + [x, live],
        smem=2,
        scratch=[pltpu.VMEM((width, width), F32), pltpu.VMEM((2 * tiles, LANES), F32)],
        limit=40,
        name="pre",
    )
    stats = exchange(stats)
    slope, act, one, two, coef, bag_sums, pay = call(
        act_kernel,
        [
            ((slots, width), F32),
            ((bags, width), F32),
            ((bags, width), F32),
            ((bags, width), F32),
            ((8, width), F32),
            ((bags, embed), F32),
            ((n * 8, LANES), F32),
        ],
        [stats, counts, w_norm, pre, live, w_out],
        limit=40,
        name="act",
    )
    if masked:
        chunk = embed * tiles // n
        everyone = exchange(pay)
        d_act, pay, d_towers, scalars = call(
            functools.partial(loss_kernel, n=n),
            [
                ((bags, width), F32),
                ((n * (2 * tiles + chunk), LANES), F32),
                ((2, embed, embed), F32),
                ((8, LANES), F32),
            ],
            [me, everyone, mask, w_towers, w_out, act, one, two],
            smem=1,
            scratch=[
                pltpu.VMEM((total_rows, total_rows), F32),
                pltpu.VMEM((total_rows, embed), F32),
                pltpu.VMEM((total_rows, embed), F32),
                pltpu.VMEM((embed, width), F32),
                pltpu.VMEM((2 * tiles, LANES), F32),
            ],
            name="loss",
        )
        sums, parts = exchange(pay), n
        loss_sum, count = scalars[0, 0], scalars[1, 0]
    else:
        d_act, sums, d_second, d_towers, loss_sum, count = loss_spread(
            plan, bag_sums, neg_mask, w_towers, w_out, act, one, two
        )
        parts = 1
        chunk = 8
    groups = [m for m in (0, plan.y, plan.x, plan.x | plan.y)]
    keep_order = [g | r for g in groups for r in plan.rest]
    order = (keep_order, [m | plan.core for m in keep_order])
    kept, sent, second_chunk, d_norm = call(
        functools.partial(grad_kernel, parts=parts, order=order, local=local),
        [
            ((n // 2 * local * half, LANES), F32),
            ((n // 2 * local * half, LANES), BF),
            ((chunk, LANES), F32),
            ((2 * tiles, LANES), F32),
        ],
        [me, owners, sums, coef, w_norm, d_act, slope, pre, live, x_turned],
        smem=2,
        scratch=[
            pltpu.VMEM((slots, width), BF),
            pltpu.VMEM((width, width), F32),
            pltpu.VMEM((8, width), F32),
        ],
        limit=48,
        name="grad",
    )
    grad = scatter_sum(plan, kept, sent, local * half)
    if masked:
        held = (chunk // 8 + 1) * 8
        (pay,) = call(
            functools.partial(norm_kernel, n=n),
            [((n * held, LANES), F32)],
            [grad, second_chunk],
            name="norm",
        )
        got = exchange(pay)
    else:
        squares = lax.psum(jnp.sum(grad * grad), AXES) + jnp.sum(d_second * d_second)
        got = jnp.concatenate([jnp.full((8, width), squares, F32), d_second], axis=0)
    blocks = (local, bsize, bsize)
    outs = [((1, LANES), F32), (blocks, F32), (blocks, BF)] + [(blocks, F32)] * 7
    outs += [((width, embed), F32)] * 4 + [((2, embed, embed), F32)] * 3 + [((2, width), F32)] * 3
    new = call(
        functools.partial(step_kernel, n=n if masked else 1),
        outs,
        [
            me, owners, got, grad, d_norm, d_towers,
            w_hidden, stat_left, stat_right, basis_left, basis_right,
            mom1_hidden, mom2_hidden, ema_hidden,
            w_out, mom1_out, mom2_out, ema_out,
            w_towers, mom1_towers, mom2_towers,
            w_norm, mom1_norm, mom2_norm,
        ],
        smem=2,
        scratch=[
            pltpu.VMEM((2 * local, bsize, 2 * bsize), F32),
            pltpu.VMEM((embed, width), F32),
            pltpu.VMEM((2, width), F32),
        ],
        name="step",
    )
    return (loss_sum, count, new[0][0, 0], *new[1:])


def solution(mesh):
    split = P(("gx", "gy"))
    plan = Plan(mesh.shape["gx"], mesh.shape["gy"])
    return jax.shard_map(
        functools.partial(on_device, plan),
        mesh=mesh,
        in_specs=(split, P(), split, split, P()) + (split,) * 8 + (P(),) * 10,
        out_specs=(P(),) * 3 + (split,) * 9 + (P(),) * 10,
        check_vma=False,
    )
```

time: 843 us -> 203 us (0.24)
  waiting for transfers between devices: 330 us -> 54.1 us
  other arithmetic: 206 us -> 0.46 us
  blocking collectives: 184 us -> 25.7 us
  Pallas kernels: 0 us -> 54.1 us
  matrix products: 38.5 us -> 0 us
  starting transfers between devices: 0.12 us -> 27 us
  between operations: 20.2 us -> 1.03 us
  local copies, waits for them, and re-layouts: 55.2 us -> 39.2 us
    another operation x11 -> x1, other arithmetic: 173 us -> 0.04 us  [the longest x5 94 us: orthonormal(): factor = jnp.linalg.cholesky(gram)]
    psum x1 -> x0, waiting for transfers between devices: 142 us -> none  [on_device(): lax.psum((d_first, d_second, d_towers), ('gx', 'gy'))]
    reduce_scatter x1 -> x0, waiting for transfers between devices: 130 us -> none  [on_device(): lax.psum_scatter(contract_rows(dscores, user_low.astype(jnp.float32), pre...]
    psum x3 -> x0, blocking collectives: 117 us -> none  [the longest x1 40.7 us: on_device(): lax.psum(jnp.sum(live * centered * centered, axis=0), ('gx', 'gy'))]
    all_gather x1 -> x0, blocking collectives: 66.5 us -> none  [on_device(): lax.all_gather(item.astype(jnp.bfloat16), ('gx', 'gy'), axis=0, tiled=True)]
    all_gather x1 -> x0, waiting for transfers between devices: 58.1 us -> none  [on_device(): lax.all_gather(w_hidden.astype(jnp.bfloat16), ('gx', 'gy'), axis=0, tiled...]
    pallas_call x0 -> x8, Pallas kernels: none -> 54.1 us  [the longest x7 52.3 us: call(): pl.pallas_call(kernel, out_shape=[jax.ShapeDtypeStruct(s, t) for s, t in...]
    reshape x6 -> x0, local copies, waits for them, and re-layouts: 41.6 us -> none  [the longest x2 26.4 us: to_blocks(): full.reshape(side, bsize, side, bsize).transpose(0, 2, 1, 3)]
  transfers between devices with their start and end apart: 3 -> 22, of which waited for: 3 -> 14; matrix products, arithmetic and copies ran while one was open for 1% -> 1% of each run, Pallas kernels for 0% -> 1%
where the time goes in v1:
time: 203 us; the launch traced here: 202 us
  Pallas kernels  54.1 us (27%)
  waiting for transfers between devices  54.1 us (27%)
  local copies, waits for them, and re-layouts  39.2 us (19%)
  starting transfers between devices  27 us (13%)
  blocking collectives  25.7 us (13%)
    pallas_call x7, Pallas kernels, call(): pl.pallas_call(kernel, out_shape=[jax.ShapeDtypeStruct(s, t) for s, t in...  52.3 us
    unnamed x92, local copies, waits for them, and re-layouts  38.3 us
    ppermute x10, waiting for transfers between devices, swap(): return lax.ppermute(a, 'gy', [(i, i ^ my) for i in range(self.gy)])  29 us
    all_to_all x2, blocking collectives, exchange(): return lax.all_to_all(payload, AXES, 0, 0, tiled=True)  25.7 us
    all_to_all x2, waiting for transfers between devices, exchange(): return lax.all_to_all(payload, AXES, 0, 0, tiled=True)  18.8 us
    ppermute x10, starting transfers between devices, swap(): return lax.ppermute(a, 'gy', [(i, i ^ my) for i in range(self.gy)])  15.5 us
    all_to_all x2, starting transfers between devices, exchange(): return lax.all_to_all(payload, AXES, 0, 0, tiled=True)  6.42 us
    ppermute x10, waiting for transfers between devices, swap(): return lax.ppermute(a, 'gx', [(i, i ^ mx) for i in range(self.gx)])  6.25 us
  transfers between devices with their start and end apart: 22, of which 14 were waited for; matrix products, arithmetic and copies ran while one was open for 1% of the time, Pallas kernels for 1%

profile of v1, /device:TPU:0, one launch (start us, length us, event | category | flops | bytes accessed | tf_op | source)
XLA Modules:
  0.0 201.6 jit_solution(12085823104692081806)
XLA Ops:
  4.4 5.1 %collective-permute-start.2 = (bf16[1,336,128]{2,1,0:T(8,128)(2,1)S(1)}, bf16[1,336,128]{2,1,0:T(8,128)(2,1)S(1)}, u32[]{:S(2)}, u32[]{:S(2)}) collective-permute-start(bf16[1,336,128]{2,1,0:T(8,128)(2,1)S(1)} %bitcast.60), channel_id=1, source_target_pairs={{0,6},{1,7},{2,4},{3,5},{4,2},{5,3},{6,0},{7,1},{8,14},{9,15},{10,... | collective-permute-start | bytes 258056 | tf_op jit(solution)/shard_map/ppermute | solution.py:91
  10.2 2.6 %collective-permute-done.2 = bf16[1,336,128]{2,1,0:T(8,128)(2,1)S(1)} collective-permute-done((bf16[1,336,128]{2,1,0:T(8,128)(2,1)S(1)}, bf16[1,336,128]{2,1,0:T(8,128)(2,1)S(1)}, u32[]{:S(2)}, u32[]{:S(2)}) %collective-permute-start.2) | collective-permute-done | bytes 86048 | tf_op jit(solution)/shard_map/ppermute | solution.py:91
  12.7 4.0 %collective-permute-done.1 = bf16[1,336,128]{2,1,0:T(8,128)(2,1)S(1)} collective-permute-done((bf16[1,336,128]{2,1,0:T(8,128)(2,1)S(1)}, bf16[1,336,128]{2,1,0:T(8,128)(2,1)S(1)}, u32[]{:S(2)}, u32[]{:S(2)}) %collective-permute-start.1) | collective-permute-done | bytes 86048 | tf_op jit(solution)/shard_map/ppermute | solution.py:91
  16.8 1.6 collective-permute-start.4
  19.9 6.2 %collective-permute-done.4.refs_4_ = bf16[4,336,128]{2,1,0:T(8,128)(2,1)S(1)} collective-permute-done((bf16[4,336,128]{2,1,0:T(8,128)(2,1)S(1)}, bf16[4,336,128]{2,1,0:T(8,128)(2,1)S(1)}, u32[]{:S(2)}, u32[]{:S(2)}) %collective-permute-start.4) | collective-permute-done | bytes 344096 | tf_op jit(solution)/shard_map/ppermute | solution.py:91
  26.0 1.7 collective-permute-start.6
  29.8 1.8 collective-permute-done.6.refs_6_
  31.6 3.3 %collective-permute-done.5.refs_5_ = bf16[4,160,128]{2,1,0:T(8,128)(2,1)S(1)} collective-permute-done((bf16[4,160,128]{2,1,0:T(8,128)(2,1)S(1)}, bf16[4,160,128]{2,1,0:T(8,128)(2,1)S(1)}, u32[]{:S(2)}, u32[]{:S(2)}) %collective-permute-start.5) | collective-permute-done | bytes 163872 | tf_op jit(solution)/shard_map/ppermute | solution.py:91
  35.2 2.2 %copy-done.2 = s32[1024,1024]{1,0:T(8,128)S(1)} copy-done((s32[1024,1024]{1,0:T(8,128)S(1)}, s32[1024,1024]{1,0:T(8,128)}, u32[]{:S(2)}) %copy-start.2) | copy-done | bytes 4194328
  37.4 1.8 hash.1
  44.6 8.5 %pre.1 = (f32[1024,1024]{1,0:T(8,128)S(1)}, f32[512,128]{1,0:T(8,128)}, f32[32,128]{1,0:T(8,128)S(1)}, bf16[512,512]{1,0:T(8,128)(2,1)S(1)}) custom-call(s32[1]{0:T(128)} %bitcast.me_ref.refs_0_, s32[256]{0:T(256)S(1)} %copy-done.34, bf16[4,336,128]{2,1,0:T(8,128)(2,1)S(1)} %pad_maximum_fusion.1.refs_2_, ...), custom_call_target="tpu_custom_call" | custom-call | tf_op jit(solution)/shard_map/pre/pallas_call | solution.py:49
  53.1 2.0 copy-done
  55.1 3.6 %all-to-all-start = ((f32[32,16,128]{2,1,0:T(8,128)}), f32[32,16,128]{2,1,0:T(8,128)S(1)}, u32[]{:S(2)}, u32[]{:S(2)}) async-start(f32[32,16,128]{2,1,0:T(8,128)} %bitcast.4), calls=%async_computation | async-start | bytes 524288 | tf_op jit(solution)/shard_map/all_to_all | solution.py:628
  59.8 9.5 %all-to-all-done = f32[32,16,128]{2,1,0:T(8,128)S(1)} async-done(((f32[32,16,128]{2,1,0:T(8,128)}), f32[32,16,128]{2,1,0:T(8,128)S(1)}, u32[]{:S(2)}, u32[]{:S(2)}) %all-to-all-start) | async-done | bytes 262176 | tf_op jit(solution)/shard_map/all_to_all | solution.py:628
  69.4 2.2 %copy-done.1 = f32[1024,1024]{1,0:T(8,128)S(1)} copy-done((f32[1024,1024]{1,0:T(8,128)S(1)}, f32[1024,1024]{1,0:T(8,128)}, u32[]{:S(2)}) %copy-start.1) | copy-done | bytes 4194328
  71.6 7.0 %act.1 = (f32[1024,1024]{1,0:T(8,128)S(1)}, f32[32,1024]{1,0:T(8,128)S(1)}, f32[32,1024]{1,0:T(8,128)S(1)}, f32[32,1024]{1,0:T(8,128)S(1)}, f32[8,1024]{1,0:T(8,...) custom-call(f32[512,128]{1,0:T(8,128)S(1)} %bitcast.57, f32[32,128]{1,0:T(8,128)S(1)} %get-tuple-element.64.count_ref, ...), custom_call_target="tpu_custom_call" | custom-call | tf_op jit(solution)/shard_map/act/pallas_call | solution.py:49
  78.5 2.0 %copy-done.3 = f32[1024,1024]{1,0:T(8,128)} copy-done((f32[1024,1024]{1,0:T(8,128)}, f32[1024,1024]{1,0:T(8,128)S(1)}, u32[]{:S(2)}) %copy-start.3) | copy-done | bytes 4194328
  80.6 9.9 %all_to_all.44 = f32[32,8,128]{2,1,0:T(8,128)S(1)} all-to-all(f32[32,8,128]{2,1,0:T(8,128)S(1)} %bitcast.64), channel_id=1, replica_groups=mesh['gx'=4,'gy'=8] {'gx','gy'}, dimensions={0} | all-to-all | bytes 262144 | tf_op jit(solution)/shard_map/all_to_all | solution.py:628
  90.5 6.1 %loss.1 = (f32[32,1024]{1,0:T(8,128)S(1)}, f32[768,128]{1,0:T(8,128)S(1)}, f32[2,32,32]{2,1,0:T(8,128)S(1)}, f32[8,128]{1,0:T(8,128)S(1)}) custom-call(s32[1]{0:T(128)} %bitcast.me_ref.refs_0_, f32[256,128]{1,0:T(8,128)S(1)} %bitcast.58, bf16[512,512]{1,0:T(8,128)(2,1)S(1)} %get-tuple-element.67.mask_ref, f32[2,32,32]{2,1,0:T(8,128)S(1)} %copy-done.23, ...), custom_call_target="tpu_custom_call" | custom-call | tf_op jit(solution)/shard_map/loss/pallas_call | solution.py:49
  96.5 15.8 %all_to_all.45 = f32[32,24,128]{2,1,0:T(8,128)S(1)} all-to-all(f32[32,24,128]{2,1,0:T(8,128)S(1)} %bitcast.59), channel_id=1, replica_groups=mesh['gx'=4,'gy'=8] {'gx','gy'}, dimensions={0} | all-to-all | bytes 786432 | tf_op jit(solution)/shard_map/all_to_all | solution.py:628
  112.4 12.7 %grad.1 = (f32[4096,128]{1,0:T(8,128)S(1)}, bf16[4096,128]{1,0:T(8,128)(2,1)S(1)}, f32[8,128]{1,0:T(8,128)S(1)}, f32[16,128]{1,0:T(8,128)S(1)}) custom-call(s32[1]{0:T(128)} %bitcast.me_ref.refs_0_, s32[256]{0:T(256)S(1)} %copy-done.34, f32[768,128]{1,0:T(8,128)S(1)} %bitcast.55, f32[8,1024]{1,0:T(8,128)S(1)} %get-tuple-element.73.coef_ref, ...), custom_call_target="tpu_custom_call" | custom-call | tf_op jit(solution)/shard_map/grad/pallas_call | solution.py:49
  125.1 2.6 %collective-permute-done.12 = bf16[4096,128]{1,0:T(8,128)(2,1)S(1)} collective-permute-done((bf16[4096,128]{1,0:T(8,128)(2,1)S(1)}, bf16[4096,128]{1,0:T(8,128)(2,1)S(1)}, u32[]{:S(2)}, u32[]{:S(2)}) %collective-permute-start.12) | collective-permute-done | bytes 1048608 | tf_op jit(solution)/shard_map/ppermute | solution.py:89
  129.6 6.9 %collective-permute-done.15 = bf16[2,4,128,128]{3,2,1,0:T(8,128)(2,1)S(1)} collective-permute-done((bf16[2,4,128,128]{3,2,1,0:T(8,128)(2,1)S(1)}, bf16[2,4,128,128]{3,2,1,0:T(8,128)(2,1)S(1)}, u32[]{:S(2)}, u32[]{:S(2)}) %collective-permute-start.15) | collective-permute-done | bytes 262176 | tf_op jit(solution)/shard_map/ppermute | solution.py:91
  139.3 3.0 %collective-permute-done.14 = bf16[4,128,128]{2,1,0:T(8,128)(2,1)S(1)} collective-permute-done((bf16[4,128,128]{2,1,0:T(8,128)(2,1)S(1)}, bf16[4,128,128]{2,1,0:T(8,128)(2,1)S(1)}, u32[]{:S(2)}, u32[]{:S(2)}) %collective-permute-start.14) | collective-permute-done | bytes 131104 | tf_op jit(solution)/shard_map/ppermute | solution.py:91
  146.0 2.1 %collective-permute-start.17 = (bf16[256,128]{1,0:T(8,128)(2,1)S(1)}, bf16[256,128]{1,0:T(8,128)(2,1)S(1)}, u32[]{:S(2)}, u32[]{:S(2)}) collective-permute-start(bf16[256,128]{1,0:T(8,128)(2,1)S(1)} %get-tuple-element.148), channel_id=1, source_target_pairs={{0,2},{1,3},{2,0},{3,1},{4,6},{5,7},{6,4},{7,5},{8,10},{9,11},{10,... | collective-permute-start | bytes 196616 | tf_op jit(solution)/shard_map/ppermute | solution.py:91
  148.1 1.8 collective-permute-done.19
  152.1 2.8 %all-to-all-start.3 = ((f32[32,16,128]{2,1,0:T(8,128)}), f32[32,16,128]{2,1,0:T(8,128)S(1)}, u32[]{:S(2)}, u32[]{:S(2)}) async-start(f32[32,16,128]{2,1,0:T(8,128)} %bitcast.25), calls=%async_computation.3 | async-start | bytes 524288 | tf_op jit(solution)/shard_map/all_to_all | solution.py:628
  156.1 9.3 %all-to-all-done.3 = f32[32,16,128]{2,1,0:T(8,128)S(1)} async-done(((f32[32,16,128]{2,1,0:T(8,128)}), f32[32,16,128]{2,1,0:T(8,128)S(1)}, u32[]{:S(2)}, u32[]{:S(2)}) %all-to-all-start.3) | async-done | bytes 262176 | tf_op jit(solution)/shard_map/all_to_all | solution.py:628
  176.2 16.5 %step.1 = (f32[1,128]{1,0:T(1,128)}, f32[8,64,64]{2,1,0:T(8,128)}, bf16[8,64,64]{2,1,0:T(8,128)(2,1)}, f32[8,64,64]{2,1,0:T(8,128)}, f32[8,64,64]{2,1,0:T(8,128)...) custom-call(s32[1]{0:T(128)} %bitcast.me_ref.refs_0_, ...), custom_call_target="tpu_custom_call" | custom-call | tf_op jit(solution)/shard_map/step/pallas_call | solution.py:49
  195.1 1.9 copy.66
  197.0 1.9 copy.67
  198.9 1.9 copy.68
  (131 shorter events, 40.4 us)
Async XLA Ops:
  3.7 31.4 %copy-start.26 = (s32[8,1024]{1,0:T(8,128)S(1)}, s32[8,1024]{1,0:T(8,128)}, u32[]{:S(2)}) copy-start(s32[8,1024]{1,0:T(8,128)} %offsets_ref.1) | copy-start | bytes 98308
  4.4 8.3 %collective-permute-start.2 = (bf16[1,336,128]{2,1,0:T(8,128)(2,1)S(1)}, bf16[1,336,128]{2,1,0:T(8,128)(2,1)S(1)}, u32[]{:S(2)}, u32[]{:S(2)}) collective-permute-start(bf16[1,336,128]{2,1,0:T(8,128)(2,1)S(1)} %bitcast.60), channel_id=1, source_target_pairs={{0,6},{1,7},{2,4},{3,5},{4,2},{5,3},{6,0},{7,1},{8,14},{9,15},{10,... | collective-permute-start | bytes 258056 | tf_op jit(solution)/shard_map/ppermute | solution.py:91
  9.5 7.2 %collective-permute-start.1 = (bf16[1,336,128]{2,1,0:T(8,128)(2,1)S(1)}, bf16[1,336,128]{2,1,0:T(8,128)(2,1)S(1)}, u32[]{:S(2)}, u32[]{:S(2)}) collective-permute-start(bf16[1,336,128]{2,1,0:T(8,128)(2,1)S(1)} %bitcast.61), channel_id=1, source_target_pairs={{0,4},{1,5},{2,6},{3,7},{4,0},{5,1},{6,2},{7,3},{8,12},{9,13},{10,... | collective-permute-start | bytes 258056 | tf_op jit(solution)/shard_map/ppermute | solution.py:91
  9.5 7.2 %collective-permute-start = (bf16[1,336,128]{2,1,0:T(8,128)(2,1)S(1)}, bf16[1,336,128]{2,1,0:T(8,128)(2,1)S(1)}, u32[]{:S(2)}, u32[]{:S(2)}) collective-permute-start(bf16[1,336,128]{2,1,0:T(8,128)(2,1)S(1)} %bitcast.62), channel_id=1, source_target_pairs={{0,2},{1,3},{2,0},{3,1},{4,6},{5,7},{6,4},{7,5},{8,10},{9,11},{10,... | collective-permute-start | bytes 258056 | tf_op jit(solution)/shard_map/ppermute | solution.py:91
  16.8 9.2 %collective-permute-start.4 = (bf16[4,336,128]{2,1,0:T(8,128)(2,1)S(1)}, bf16[4,336,128]{2,1,0:T(8,128)(2,1)S(1)}, u32[]{:S(2)}, u32[]{:S(2)}) collective-permute-start(bf16[4,336,128]{2,1,0:T(8,128)(2,1)S(1)} %pad_maximum_fusion.1.refs_2_), channel_id=1, source_target_pairs={{0,1},{1,0},{2,3},{3,2},{4,5},{5,4},{6,7},{7,6},{8,9},{9,8},{10,11... | collective-permute-start | bytes 1032200 | tf_op jit(solution)/shard_map/ppermute | solution.py:91
  18.4 9.3 %collective-permute-start.3 = (bf16[4,336,128]{2,1,0:T(8,128)(2,1)S(1)}, bf16[4,336,128]{2,1,0:T(8,128)(2,1)S(1)}, u32[]{:S(2)}, u32[]{:S(2)}) collective-permute-start(bf16[4,336,128]{2,1,0:T(8,128)(2,1)S(1)} %pad_maximum_fusion.1.refs_2_), channel_id=1, source_target_pairs={{0,16},{8,24},{16,0},{24,8},{1,17},{9,25},{17,1},{25,9},{2,18},{10... | collective-permute-start | bytes 1032200 | tf_op jit(solution)/shard_map/ppermute | solution.py:89
  26.0 5.6 %collective-permute-start.6 = (bf16[4,176,128]{2,1,0:T(8,128)(2,1)S(1)}, bf16[4,176,128]{2,1,0:T(8,128)(2,1)S(1)}, u32[]{:S(2)}, u32[]{:S(2)}) collective-permute-start(bf16[4,176,128]{2,1,0:T(8,128)(2,1)S(1)} %slice.82), channel_id=1, source_target_pairs={{0,16},{8,24},{16,0},{24,8},{1,17},{9,25},{17,1},{25,9},{2,18},{10... | collective-permute-start | bytes 540680 | tf_op jit(solution)/shard_map/ppermute | solution.py:89
  27.7 12.8 %collective-permute-start.7 = (bf16[4,336,128]{2,1,0:T(8,128)(2,1)S(1)}, bf16[4,336,128]{2,1,0:T(8,128)(2,1)S(1)}, u32[]{:S(2)}, u32[]{:S(2)}) collective-permute-start(bf16[4,336,128]{2,1,0:T(8,128)(2,1)S(1)} %pad_maximum_fusion.1.refs_2_), channel_id=1, source_target_pairs={{0,8},{8,0},{16,24},{24,16},{1,9},{9,1},{17,25},{25,17},{2,10},{10... | collective-permute-start | bytes 1032200 | tf_op jit(solution)/shard_map/ppermute | solution.py:89
  27.7 13.5 %collective-permute-start.8 = (bf16[4,336,128]{2,1,0:T(8,128)(2,1)S(1)}, bf16[4,336,128]{2,1,0:T(8,128)(2,1)S(1)}, u32[]{:S(2)}, u32[]{:S(2)}) collective-permute-start(bf16[4,336,128]{2,1,0:T(8,128)(2,1)S(1)} %collective-permute-done.3.refs_3_), channel_id=1, source_target_pairs={{0,8},{8,0},{16,24},{24,16},{1,9},{9,1},{17,25},{25,17},{2,10},{10... | collective-permute-start | bytes 1032200 | tf_op jit(solution)/shard_map/ppermute | solution.py:89
  28.2 13.0 %collective-permute-start.9 = (bf16[4,336,128]{2,1,0:T(8,128)(2,1)S(1)}, bf16[4,336,128]{2,1,0:T(8,128)(2,1)S(1)}, u32[]{:S(2)}, u32[]{:S(2)}) collective-permute-start(bf16[4,336,128]{2,1,0:T(8,128)(2,1)S(1)} %collective-permute-done.4.refs_4_), channel_id=1, source_target_pairs={{0,8},{8,0},{16,24},{24,16},{1,9},{9,1},{17,25},{25,17},{2,10},{10... | collective-permute-start | bytes 1032200 | tf_op jit(solution)/shard_map/ppermute | solution.py:89
  28.2 6.7 %collective-permute-start.5 = (bf16[4,160,128]{2,1,0:T(8,128)(2,1)S(1)}, bf16[4,160,128]{2,1,0:T(8,128)(2,1)S(1)}, u32[]{:S(2)}, u32[]{:S(2)}) collective-permute-start(bf16[4,160,128]{2,1,0:T(8,128)(2,1)S(1)} %slice.81), channel_id=1, source_target_pairs={{0,1},{1,0},{2,3},{3,2},{4,5},{5,4},{6,7},{7,6},{8,9},{9,8},{10,11... | collective-permute-start | bytes 491528 | tf_op jit(solution)/shard_map/ppermute | solution.py:91
  31.6 9.6 %collective-permute-start.11 = (bf16[4,176,128]{2,1,0:T(8,128)(2,1)S(1)}, bf16[4,176,128]{2,1,0:T(8,128)(2,1)S(1)}, u32[]{:S(2)}, u32[]{:S(2)}) collective-permute-start(bf16[4,176,128]{2,1,0:T(8,128)(2,1)S(1)} %collective-permute-done.6.refs_6_), channel_id=1, source_target_pairs={{0,8},{8,0},{16,24},{24,16},{1,9},{9,1},{17,25},{25,17},{2,10},{10... | collective-permute-start | bytes 540680 | tf_op jit(solution)/shard_map/ppermute | solution.py:89
  34.9 5.6 %collective-permute-start.10 = (bf16[4,160,128]{2,1,0:T(8,128)(2,1)S(1)}, bf16[4,160,128]{2,1,0:T(8,128)(2,1)S(1)}, u32[]{:S(2)}, u32[]{:S(2)}) collective-permute-start(bf16[4,160,128]{2,1,0:T(8,128)(2,1)S(1)} %collective-permute-done.5.refs_5_), channel_id=1, source_target_pairs={{0,8},{8,0},{16,24},{24,16},{1,9},{9,1},{17,25},{25,17},{2,10},{10... | collective-permute-start | bytes 491528 | tf_op jit(solution)/shard_map/ppermute | solution.py:89
  37.4 4.5 %copy-start.34 = (s32[256]{0:T(256)S(1)}, s32[256]{0:T(256)}, u32[]{:S(2)}) copy-start(s32[256]{0:T(256)} %owners_ref.5) | copy-start | bytes 3076
  44.6 24.8 %copy-start.25 = (f32[2,1024]{1,0:T(2,128)S(1)}, f32[2,1024]{1,0:T(2,128)}, u32[]{:S(2)}) copy-start(f32[2,1024]{1,0:T(2,128)} %wn_ref.1) | copy-start | bytes 24580
  55.1 14.3 %all-to-all-start = ((f32[32,16,128]{2,1,0:T(8,128)}), f32[32,16,128]{2,1,0:T(8,128)S(1)}, u32[]{:S(2)}, u32[]{:S(2)}) async-start(f32[32,16,128]{2,1,0:T(8,128)} %bitcast.4), calls=%async_computation | async-start | bytes 524288 | tf_op jit(solution)/shard_map/all_to_all | solution.py:628
  71.6 18.9 %copy-start.23 = (f32[2,32,32]{2,1,0:T(8,128)S(1)}, f32[2,32,32]{2,1,0:T(8,128)}, u32[]{:S(2)}) copy-start(f32[2,32,32]{2,1,0:T(8,128)} %wt_ref.1) | copy-start | bytes 24580
  96.5 15.8 %copy-start.29 = (f32[2,32,32]{2,1,0:T(8,128)}, f32[2,32,32]{2,1,0:T(8,128)S(1)}, u32[]{:S(2)}) copy-start(f32[2,32,32]{2,1,0:T(8,128)S(1)} %get-tuple-element.81.d_towers_ref) | copy-start | bytes 24580
  125.1 2.7 %collective-permute-start.12 = (bf16[4096,128]{1,0:T(8,128)(2,1)S(1)}, bf16[4096,128]{1,0:T(8,128)(2,1)S(1)}, u32[]{:S(2)}, u32[]{:S(2)}) collective-permute-start(bf16[4096,128]{1,0:T(8,128)(2,1)S(1)} %get-tuple-element.78), channel_id=1, source_target_pairs={{0,8},{8,0},{16,24},{24,16},{1,9},{9,1},{17,25},{25,17},{2,10},{10... | collective-permute-start | bytes 3145736 | tf_op jit(solution)/shard_map/ppermute | solution.py:89
  128.1 8.4 %collective-permute-start.15 = (bf16[2,4,128,128]{3,2,1,0:T(8,128)(2,1)S(1)}, bf16[2,4,128,128]{3,2,1,0:T(8,128)(2,1)S(1)}, u32[]{:S(2)}, u32[]{:S(2)}) collective-permute-start(bf16[2,4,128,128]{3,2,1,0:T(8,128)(2,1)S(1)} %slice_bitcast_fusion.3), channel_id=1, source_target_pairs={{0,1},{1,0},{2,3},{3,2},{4,5},{5,4},{6,7},{7,6},{8,9},{9,8},{10,11... | collective-permute-start | bytes 786440 | tf_op jit(solution)/shard_map/ppermute | solution.py:91
  129.0 8.1 %collective-permute-start.13 = (bf16[2,4,128,128]{3,2,1,0:T(8,128)(2,1)S(1)}, bf16[2,4,128,128]{3,2,1,0:T(8,128)(2,1)S(1)}, u32[]{:S(2)}, u32[]{:S(2)}) collective-permute-start(bf16[2,4,128,128]{3,2,1,0:T(8,128)(2,1)S(1)} %slice_bitcast_fusion.5), channel_id=1, source_target_pairs={{0,16},{8,24},{16,0},{24,8},{1,17},{9,25},{17,1},{25,9},{2,18},{10... | collective-permute-start | bytes 786440 | tf_op jit(solution)/shard_map/ppermute | solution.py:89
  137.2 5.0 %collective-permute-start.14 = (bf16[4,128,128]{2,1,0:T(8,128)(2,1)S(1)}, bf16[4,128,128]{2,1,0:T(8,128)(2,1)S(1)}, u32[]{:S(2)}, u32[]{:S(2)}) collective-permute-start(bf16[4,128,128]{2,1,0:T(8,128)(2,1)S(1)} %fusion.5), channel_id=1, source_target_pairs={{0,1},{1,0},{2,3},{3,2},{4,5},{5,4},{6,7},{7,6},{8,9},{9,8},{10,11... | collective-permute-start | bytes 393224 | tf_op jit(solution)/shard_map/ppermute | solution.py:91
  138.5 16.4 %copy-start.39 = (f32[1024,32]{0,1:T(8,128)S(1)}, f32[1024,32]{0,1:T(8,128)}, u32[]{:S(2)}) copy-start(f32[1024,32]{0,1:T(8,128)} %param.37) | copy-start | bytes 393220
  138.5 5.0 %collective-permute-start.16 = (bf16[4,128,128]{2,1,0:T(8,128)(2,1)S(1)}, bf16[4,128,128]{2,1,0:T(8,128)(2,1)S(1)}, u32[]{:S(2)}, u32[]{:S(2)}) collective-permute-start(bf16[4,128,128]{2,1,0:T(8,128)(2,1)S(1)} %fusion.6), channel_id=1, source_target_pairs={{0,16},{8,24},{16,0},{24,8},{1,17},{9,25},{17,1},{25,9},{2,18},{10... | collective-permute-start | bytes 393224 | tf_op jit(solution)/shard_map/ppermute | solution.py:89
  142.3 12.8 %copy-start.40 = (f32[1024,32]{0,1:T(8,128)S(1)}, f32[1024,32]{0,1:T(8,128)}, u32[]{:S(2)}) copy-start(f32[1024,32]{0,1:T(8,128)} %param.38) | copy-start | bytes 393220
  143.5 11.8 %copy-start.41 = (f32[1024,32]{0,1:T(8,128)S(1)}, f32[1024,32]{0,1:T(8,128)}, u32[]{:S(2)}) copy-start(f32[1024,32]{0,1:T(8,128)} %param.39) | copy-start | bytes 393220
  143.6 21.7 %copy-start.6 = (f32[8,64,64]{2,1,0:T(8,128)S(1)}, f32[8,64,64]{2,1,0:T(8,128)}, u32[]{:S(2)}) copy-start(f32[8,64,64]{2,1,0:T(8,128)} %w_ref.3) | copy-start | bytes 393220
  143.6 21.7 %copy-start.10 = (f32[8,64,64]{2,1,0:T(8,128)S(1)}, f32[8,64,64]{2,1,0:T(8,128)}, u32[]{:S(2)}) copy-start(f32[8,64,64]{2,1,0:T(8,128)} %left_ref.1) | copy-start | bytes 393220
  143.6 6.2 %collective-permute-start.19 = (bf16[256,128]{1,0:T(8,128)(2,1)S(1)}, bf16[256,128]{1,0:T(8,128)(2,1)S(1)}, u32[]{:S(2)}, u32[]{:S(2)}) collective-permute-start(bf16[256,128]{1,0:T(8,128)(2,1)S(1)} %get-tuple-element.149), channel_id=1, source_target_pairs={{0,6},{1,7},{2,4},{3,5},{4,2},{5,3},{6,0},{7,1},{8,14},{9,15},{10,... | collective-permute-start | bytes 196616 | tf_op jit(solution)/shard_map/ppermute | solution.py:91
  144.7 6.5 %collective-permute-start.18 = (bf16[256,128]{1,0:T(8,128)(2,1)S(1)}, bf16[256,128]{1,0:T(8,128)(2,1)S(1)}, u32[]{:S(2)}, u32[]{:S(2)}) collective-permute-start(bf16[256,128]{1,0:T(8,128)(2,1)S(1)} %get-tuple-element.150), channel_id=1, source_target_pairs={{0,4},{1,5},{2,6},{3,7},{4,0},{5,1},{6,2},{7,3},{8,12},{9,13},{10,... | collective-permute-start | bytes 196616 | tf_op jit(solution)/shard_map/ppermute | solution.py:91
  146.0 5.2 %collective-permute-start.17 = (bf16[256,128]{1,0:T(8,128)(2,1)S(1)}, bf16[256,128]{1,0:T(8,128)(2,1)S(1)}, u32[]{:S(2)}, u32[]{:S(2)}) collective-permute-start(bf16[256,128]{1,0:T(8,128)(2,1)S(1)} %get-tuple-element.148), channel_id=1, source_target_pairs={{0,2},{1,3},{2,0},{3,1},{4,6},{5,7},{6,4},{7,5},{8,10},{9,11},{10,... | collective-permute-start | bytes 196616 | tf_op jit(solution)/shard_map/ppermute | solution.py:91
  152.1 13.2 %all-to-all-start.3 = ((f32[32,16,128]{2,1,0:T(8,128)}), f32[32,16,128]{2,1,0:T(8,128)S(1)}, u32[]{:S(2)}, u32[]{:S(2)}) async-start(f32[32,16,128]{2,1,0:T(8,128)} %bitcast.25), calls=%async_computation.3 | async-start | bytes 524288 | tf_op jit(solution)/shard_map/all_to_all | solution.py:628
  (32 other events, 37.3 us)

commit v2 on v1

v2 whole, which is shorter than its diff:
```python
import functools
import math

import jax
import jax.numpy as jnp
from jax import lax
from jax.experimental import pallas as pl
from jax.experimental.pallas import tpu as pltpu
from jax.sharding import PartitionSpec as P

FIELDS = 4
BAG = 8
HASH_RANGE = 4096
STEP = 10
BETA_ONE = 0.9
BETA_TWO = 0.95
EPSILON = 1e-08
RATE = 0.03
DECAY = 0.01
CLIP = 0.01
AVG_KEEP = 0.8
AVG_TAKE = 0.2

F32 = jnp.float32
BF = jnp.bfloat16
HIGH = lax.Precision.HIGHEST
AXES = ("gx", "gy")
LANES = 128
SLOTS_BAG = FIELDS * BAG
PAIR = 16
MIB = 1 << 20


def dot(a, b, ca=1, cb=0, precision=None):
    return lax.dot_general(
        a, b, (((ca,), (cb,)), ((), ())), precision=precision, preferred_element_type=F32
    )


hdot = functools.partial(dot, precision=HIGH)


def spec(space=pltpu.VMEM):
    return pl.BlockSpec(memory_space=space)


def in_hbm(a):
    return pltpu.with_memory_space_constraint(a, pltpu.HBM)


def call(kernel, outs, args, smem=0, hbm=0, smem_outs=0, scratch=(), limit=16, name=None, cost=None):
    args = list(args)
    specs = [spec(pltpu.SMEM)] * smem + [spec()] * (len(args) - smem - hbm) + [spec(pltpu.HBM)] * hbm
    if hbm:
        args[-hbm:] = [in_hbm(a) for a in args[-hbm:]]
    spaces = [pltpu.VMEM] * (len(outs) - smem_outs) + [pltpu.SMEM] * smem_outs
    estimate = None
    if cost:
        estimate = pl.CostEstimate(flops=cost, bytes_accessed=cost // 100, transcendentals=0)
    return pl.pallas_call(
        kernel,
        out_shape=[jax.ShapeDtypeStruct(s, t) for s, t in outs],
        in_specs=specs,
        out_specs=[spec(space) for space in spaces],
        scratch_shapes=list(scratch),
        compiler_params=pltpu.CompilerParams(vmem_limit_bytes=limit * MIB),
        cost_estimate=estimate,
        name=name,
    )(*args)


def fetch(sources, targets, sems):
    copies = [pltpu.make_async_copy(a, b, sems.at[i]) for i, (a, b) in enumerate(zip(sources, targets))]
    for c in copies:
        c.start()
    for c in copies:
        c.wait()


def swap_halves(v):
    half = v.shape[1] // 2
    return jnp.concatenate([v[:, half:], v[:, :half]], axis=1)


def place(q, side):
    shift = side.bit_length() - 1
    return q >> shift, (q & (side - 1)) >> 1, q & 1


class Plan:
    def __init__(self, gx, gy):
        self.gx, self.gy, self.n = gx, gy, gx * gy
        self.core = gy
        self.x = 2 * gy
        self.y = 1
        bits = []
        b = 2
        while b < gy:
            bits.append(b)
            b *= 2
        b = 4
        while b < gx:
            bits.append(b * gy)
            b *= 2
        self.bits = bits
        rest = [0]
        for b in bits:
            rest = rest + [m | b for m in rest]
        self.rest = rest

    def swap(self, a, mask):
        mx, my = mask // self.gy, mask % self.gy
        if my == 0:
            return lax.ppermute(a, "gx", [(i, i ^ mx) for i in range(self.gx)])
        if mx == 0:
            return lax.ppermute(a, "gy", [(i, i ^ my) for i in range(self.gy)])
        return lax.ppermute(a, AXES, [(i, i ^ mask) for i in range(self.n)])


def pack_kernel(
    me_ref, owners_ref, w_hbm, neg_hbm, seg_hbm, out_ref, w_ref, neg_ref, seg_ref, sems, *, masked
):
    fetch((w_hbm, neg_hbm, seg_hbm), (w_ref, neg_ref, seg_ref), sems)
    local, bsize = w_ref.shape[0], w_ref.shape[1]
    half = bsize // 2
    for b in range(local):
        odd = owners_ref[me_ref[0] * local + b] % 2
        top, low = w_ref[b, :half, :], w_ref[b, half:, :]
        left = jnp.where(odd == 1, low, top)
        right = jnp.where(odd == 1, top, low)
        out_ref[b * half : (b + 1) * half, :] = jnp.concatenate([left, right], axis=1).astype(BF)
    at = local * half
    if masked:
        for c in range(neg_ref.shape[1] // LANES):
            part = neg_ref[:, c * LANES : (c + 1) * LANES].astype(F32)
            out_ref[at : at + PAIR, :] = part.astype(BF)
            at += PAIR
    used = jnp.sum(seg_ref[...].astype(F32), axis=0, keepdims=True)
    out_ref[at : at + PAIR, :] = jnp.broadcast_to(used, (PAIR, LANES)).astype(BF)


def gather_pieces(plan, payload, cut, zero, early, late):
    stack = payload[None]
    if len(plan.rest) <= 4:
        stack = jnp.concatenate([stack] + [plan.swap(stack, m) for m in plan.rest[1:]], axis=0)
    else:
        for b in plan.bits:
            stack = jnp.concatenate([stack, plan.swap(stack, b)], axis=0)
    stack, early = lax.optimization_barrier((stack, early))
    by_x = plan.swap(stack, plan.x)
    by_y = plan.swap(stack, plan.y)
    by_x, by_y, late = lax.optimization_barrier((by_x, by_y, late))
    first = plan.swap(by_x[:, :cut] + zero, plan.y)
    second = plan.swap(by_y[:, cut:] + zero, plan.x)
    mine = [
        (stack, 0, 0),
        (by_x, plan.x, 0),
        (by_y, plan.y, 0),
        (first, plan.x | plan.y, 0),
        (second, plan.x | plan.y, cut),
    ]
    other = [(plan.swap(a, plan.core), m | plan.core, row) for a, m, row in mine]
    return mine + other, early, late


def hash_kernel(codes_hbm, offsets_hbm, x_ref, xt_ref, codes_ref, offsets_ref, sems):
    rows, width = codes_ref.shape
    groups = 2 * FIELDS
    step = 128
    head = pltpu.make_async_copy(offsets_hbm, offsets_ref, sems.at[0])
    head.start()
    parts = []
    for i in range(rows // step):
        at = pl.ds(i * step, step)
        parts.append(pltpu.make_async_copy(codes_hbm.at[at], codes_ref.at[at], sems.at[1 + i]))
        parts[i].start()
    head.wait()
    for i, part in enumerate(parts):
        part.wait()
        at = slice(i * step, (i + 1) * step)
        salted = codes_ref[at, :].reshape(-1, groups, BAG, width) + offsets_ref[...][None, :, None, :]
        salted = (salted & (HASH_RANGE - 1)).reshape(step, width)
        x = (salted.astype(F32) * (2.0 / (HASH_RANGE - 1)) - 1.0).astype(BF)
        x_ref[at, :] = x
        xt_ref[:, at] = x.T


def hash_inputs(codes, offsets):
    rows, width = codes.shape
    return call(
        hash_kernel,
        [((rows, width), BF), ((width, rows), BF)],
        [codes, offsets],
        hbm=2,
        scratch=[
            pltpu.VMEM(codes.shape, jnp.int32),
            pltpu.VMEM(offsets.shape, jnp.int32),
            pltpu.SemaphoreType.DMA((1 + rows // 128,)),
        ],
        limit=12,
        name="hash",
        cost=20_000_000,
    )


def pre_kernel(*refs, holds, rest, local, masked, n, pieces):
    me_ref, owners_ref = refs[:2]
    piece_refs = refs[2 : 2 + pieces]
    x_ref, live_ref = refs[2 + pieces : 4 + pieces]
    pre_ref, stats_ref, count_ref, mask_ref, w_ref, row_ref = refs[4 + pieces :]
    width = x_ref.shape[1]
    bsize = LANES // 2
    half = bsize // 2
    side = width // bsize
    tiles = width // LANES
    me = me_ref[0]
    chunks = mask_ref.shape[1] // LANES if masked else 0
    for piece, (base, row0) in zip(piece_refs, holds):
        held = piece.shape[1]
        for k, m in enumerate(rest):
            d = me ^ (m | base)
            for b in range(local):
                at = b * half - row0
                if at < 0 or at + half > held:
                    continue
                r, c, odd = place(owners_ref[d * local + b], side)
                tile = piece[k, at : at + half, :]
                rows = pl.multiple_of(r * bsize, bsize)
                low = pl.multiple_of(r * bsize + half, half)
                cols = pl.ds(pl.multiple_of(c * LANES, LANES), LANES)
                w_ref[odd, pl.ds(rows, half), cols] = tile
                w_ref[odd, pl.ds(low, half), cols] = swap_halves(tile)
            for c in range(chunks):
                at = local * half + c * PAIR - row0
                if at < 0 or at + PAIR > held:
                    continue
                mask_ref[pl.ds(pl.multiple_of(d * PAIR, PAIR), PAIR), c * LANES : (c + 1) * LANES] = (
                    piece[k, at : at + PAIR, :]
                )
            at = local * half + chunks * PAIR - row0
            if 0 <= at and at + PAIR <= held:
                count_ref[pl.ds(d, 1), :] = piece[k, at : at + PAIR, :].astype(F32)[:1]
    live = live_ref[...]
    used = jnp.maximum(jnp.sum(live[:, :1]), 1.0)
    step = 2 * LANES
    left = lax.broadcasted_iota(jnp.int32, (width, step), 1) % LANES < bsize
    for j in range(width // step):
        cols = slice(j * step, (j + 1) * step)
        pre_ref[:, cols] = dot(x_ref[...], jnp.where(left, w_ref[0, :, cols], w_ref[1, :, cols]))
        for i in range(2):
            t = 2 * j + i
            tile = slice(t * LANES, (t + 1) * LANES)
            total = jnp.sum(pre_ref[:, tile] * live, axis=0, keepdims=True)
            apart = pre_ref[:, tile] - total / used
            row_ref[t : t + 1, :] = total
            row_ref[tiles + t : tiles + t + 1, :] = jnp.sum(
                apart * apart * live, axis=0, keepdims=True
            )
    for d in range(n):
        stats_ref[d * 2 * tiles : (d + 1) * 2 * tiles, :] = row_ref[...]


def act_kernel(
    stats_ref, count_ref, norm_ref, pre_ref, live_ref, pick_ref, w_out_ref,
    slope_ref, act_ref, one_ref, two_ref, coef_ref, bags_ref, pay_ref,
    low_ref, ones_ref, twos_ref,
):
    n = count_ref.shape[0]
    rows, width = pre_ref.shape
    tiles = width // LANES
    counts = jnp.sum(count_ref[...], axis=1, keepdims=True)
    used = jnp.sum(counts)
    total = stats_ref[0:tiles, :]
    for d in range(1, n):
        total = total + stats_ref[2 * d * tiles : (2 * d + 1) * tiles, :]
    mean = total / used
    square = jnp.zeros_like(mean)
    for d in range(n):
        c = counts[d : d + 1, :]
        apart = stats_ref[2 * d * tiles : (2 * d + 1) * tiles, :] / jnp.maximum(c, 1.0) - mean
        square = square + (
            stats_ref[(2 * d + 1) * tiles : (2 * d + 2) * tiles, :] + c * apart * apart
        )
    rstd = lax.rsqrt(square / used + 1e-05)
    for j in range(tiles):
        coef_ref[0:1, j * LANES : (j + 1) * LANES] = mean[j : j + 1, :]
        coef_ref[1:2, j * LANES : (j + 1) * LANES] = rstd[j : j + 1, :]
    coef_ref[2:3, :] = jnp.full((1, width), used, F32)
    coef_ref[3:4, :] = coef_ref[1:2, :] * norm_ref[0:1, :]
    bags = rows // SLOTS_BAG
    group = 8

    def fold(v):
        return (v[:group] + v[group : 2 * group]) + (v[2 * group : 3 * group] + v[3 * group :])

    def unfold(ref, j):
        total = ref[j, pl.ds(0, bags, stride=group), :]
        for i in range(1, group):
            total = total + ref[j, pl.ds(i, bags, stride=group), :]
        return total

    for j in range(tiles):
        cols = slice(j * LANES, (j + 1) * LANES)
        centre, scale, bias = coef_ref[0:1, cols], coef_ref[3:4, cols], norm_ref[1:2, cols]
        for b in range(bags):
            at = slice(b * SLOTS_BAG, (b + 1) * SLOTS_BAG)
            to = slice(b * group, (b + 1) * group)
            apart = pre_ref[at, cols] - centre
            y = scale * apart + bias
            capped = jnp.minimum(y, 20.0)
            e = jnp.exp(capped)
            top = e * (e + 2.0)
            below = top + 2.0
            guess = pl.reciprocal(below, approx=True)
            inv = guess * (2.0 - below * guess)
            gate = top * inv
            low_ref[at, :] = (y * gate).astype(BF)
            part = e * inv
            slope = gate + (4.0 * capped) * (part * (inv + part))
            slope_ref[at, cols] = slope
            slope = slope * live_ref[at, :]
            ones_ref[j, to, :] = fold(slope)
            twos_ref[j, to, :] = fold(slope * apart)
        act_ref[:, cols] = dot(pick_ref[...], low_ref[...])
        one_ref[:, cols] = unfold(ones_ref, j)
        two_ref[:, cols] = unfold(twos_ref, j) * coef_ref[1:2, cols]
    second = w_out_ref[...].astype(BF).astype(F32)
    bags = hdot(act_ref[...], second, 1, 1)
    pairs = bags.shape[0] // 2
    split = jnp.concatenate([hdot(pick(pairs, 0), bags), hdot(pick(pairs, 1), bags)], axis=0)
    bags_ref[...] = split
    eighth = pairs // 2
    packed = jnp.concatenate([split[i * eighth : (i + 1) * eighth] for i in range(4)], axis=1)
    for d in range(n):
        pay_ref[d * eighth : (d + 1) * eighth, :] = packed


def pick(pairs, which):
    r = lax.broadcasted_iota(jnp.int32, (pairs, 2 * pairs), 0)
    c = lax.broadcasted_iota(jnp.int32, (pairs, 2 * pairs), 1)
    return (c == 2 * r + which).astype(F32)


def spread(pairs, which):
    r = lax.broadcasted_iota(jnp.int32, (2 * pairs, pairs), 0)
    c = lax.broadcasted_iota(jnp.int32, (2 * pairs, pairs), 1)
    return (r == 2 * c + which).astype(F32)


def three(v):
    a = v.astype(BF)
    v = v - a.astype(F32)
    b = v.astype(BF)
    v = v - b.astype(F32)
    return a, b, v.astype(BF)


def loss_kernel(
    me_ref, all_ref, mask_ref, towers_ref, w_out_ref, act_ref, one_ref, two_ref,
    dact_ref, pay_ref, d_towers_ref, loss_ref, total_ref,
    score_ref, user_ref, item_ref, second_ref, row_ref, *, n,
):
    me = me_ref[0]
    embed = towers_ref.shape[1]
    total_rows = mask_ref.shape[0]
    eighth = all_ref.shape[0] // n

    def full(i):
        a = all_ref[:, 2 * i * embed : (2 * i + 1) * embed].reshape(n, eighth, embed)
        b = all_ref[:, (2 * i + 1) * embed : (2 * i + 2) * embed].reshape(n, eighth, embed)
        return jnp.stack([a, b], axis=1).reshape(total_rows, embed)

    bags_user, bags_item = full(0), full(1)
    user = hdot(bags_user, towers_ref[0]).astype(BF)
    item = hdot(bags_item, towers_ref[1]).astype(BF)
    root = math.sqrt(embed)
    score_ref[...] = dot(user, item, 1, 1) / root
    negatives = jnp.sum(mask_ref[...].astype(F32))
    count = negatives / total_rows
    step = 32

    def rows(i, carry):
        at = slice(i * step, (i + 1) * step)
        logits = score_ref[at, :]
        r = lax.broadcasted_iota(jnp.int32, logits.shape, 0) + i * step
        own = r == lax.broadcasted_iota(jnp.int32, logits.shape, 1)
        keep = own | (mask_ref[at, :].astype(F32) == 1.0)
        top = jnp.max(jnp.where(keep, logits, -jnp.inf), axis=1, keepdims=True)
        weights = jnp.where(keep, jnp.exp(logits - top), 0.0)
        total = jnp.sum(weights, axis=1, keepdims=True)
        hit = jnp.sum(jnp.where(own, logits, 0.0), axis=1, keepdims=True)
        score_ref[at, :] = (weights / total - own.astype(F32)) / count / root
        return carry + (top + jnp.log(total) - hit)

    ce = jnp.zeros((step, 1), F32)
    for i in range(total_rows // step):
        ce = rows(i, ce)
    loss_ref[0, 0] = jnp.sum(ce)
    total_ref[0, 0] = count
    parts = three(score_ref[...])
    d_user = sum(dot(p, item) for p in parts)
    d_item = sum(dot(user, p, 0, 0) for p in parts).T
    user_ref[...] = d_user
    item_ref[...] = d_item
    d_towers_ref[0] = hdot(bags_user, d_user, 0, 0)
    d_towers_ref[1] = hdot(bags_item, d_item, 0, 0)
    mine = pl.ds(pl.multiple_of(me * PAIR, PAIR), PAIR)
    back_user = hdot(user_ref[mine, :], towers_ref[0], 1, 1).astype(BF).astype(F32)
    back_item = hdot(item_ref[mine, :], towers_ref[1], 1, 1).astype(BF).astype(F32)
    d_emb = dot(spread(PAIR, 0), back_user) + dot(spread(PAIR, 1), back_item)
    d_act = dot(d_emb.astype(BF), w_out_ref[...].astype(BF))
    dact_ref[...] = d_act
    d_bias = jnp.sum(d_act * one_ref[...], axis=0, keepdims=True)
    d_gain = jnp.sum(d_act * two_ref[...], axis=0, keepdims=True)
    d_low = d_emb.T.astype(BF)
    second = sum(dot(d_low, p) for p in three(act_ref[...]))
    width = act_ref.shape[1]
    tiles = width // LANES
    for j in range(tiles):
        second_ref[pl.ds(j, embed, stride=tiles), :] = second[:, j * LANES : (j + 1) * LANES]
    for j in range(tiles):
        cols = slice(j * LANES, (j + 1) * LANES)
        row_ref[j : j + 1, :] = d_bias[:, cols]
        row_ref[tiles + j : tiles + j + 1, :] = d_gain[:, cols]
    sums = row_ref[...].astype(BF)
    chunk = embed * tiles // n
    for d in range(n):
        part = second_ref[d * chunk : (d + 1) * chunk, :]
        high = part.astype(BF)
        low = (part - high.astype(F32)).astype(BF)
        at = d * (2 * tiles + 2 * chunk)
        pay_ref[at : at + 2 * tiles, :] = sums
        pay_ref[at + 2 * tiles : at + 2 * tiles + 2 * chunk, :] = jnp.concatenate([high, low], axis=0)


def loss_spread(plan, bags, neg_mask, towers, w_out, act, one, two):
    embed = towers.shape[1]
    rows = neg_mask.shape[0]
    bags_user, bags_item = bags[:rows], bags[rows:]
    user = hdot(bags_user, towers[0]).astype(BF)
    item = hdot(bags_item, towers[1]).astype(BF)
    items = lax.all_gather(item, AXES, axis=0, tiled=True)
    root = math.sqrt(embed)
    logits = dot(user, items, 1, 1) / root
    at = lax.axis_index(AXES) * rows + lax.broadcasted_iota(jnp.int32, logits.shape, 0)
    own = lax.broadcasted_iota(jnp.int32, logits.shape, 1) == at
    keep = own | (neg_mask == 1)
    top = jnp.max(jnp.where(keep, logits, -jnp.inf), axis=1, keepdims=True)
    weights = jnp.where(keep, jnp.exp(logits - top), 0.0)
    total = jnp.sum(weights, axis=1, keepdims=True)
    ce = top + jnp.log(total) - jnp.sum(jnp.where(own, logits, 0.0), axis=1, keepdims=True)
    count = lax.psum(jnp.sum(neg_mask.astype(F32)), AXES) / items.shape[0]
    scores = (weights / total - own.astype(F32)) / count / root
    d_user = hdot(scores, items.astype(F32))
    d_item = lax.psum_scatter(
        hdot(scores, user.astype(F32), 0, 0), AXES, scatter_dimension=0, tiled=True
    )
    d_towers = jnp.stack([hdot(bags_user, d_user, 0, 0), hdot(bags_item, d_item, 0, 0)])
    back = jnp.stack([hdot(d_user, towers[0], 1, 1), hdot(d_item, towers[1], 1, 1)], axis=1)
    d_emb = back.reshape(2 * rows, embed).astype(BF)
    d_act = dot(d_emb, w_out.astype(BF))
    d_second = hdot(d_emb.astype(F32), act, 0, 0)
    sums = jnp.stack([jnp.sum(d_act * one, axis=0), jnp.sum(d_act * two, axis=0)])
    sums, d_second, d_towers, loss = lax.psum((sums, d_second, d_towers, jnp.sum(ce)), AXES)
    return d_act, sums.reshape(-1, LANES), d_second, d_towers, loss, count


def grad_kernel(
    me_ref, owners_ref, sums_ref, coef_ref, norm_ref, dact_ref, slope_ref, pre_ref, live_ref, xt_ref,
    keep_ref, send_ref, chunk_ref, d_norm_ref, d_pre_ref, g_ref, row_ref,
    *, parts, order, local,
):
    rows, width = pre_ref.shape
    tiles = width // LANES
    held = sums_ref.shape[0] // parts
    total = sums_ref[0:held, :].astype(F32)
    for d in range(1, parts):
        total = total + sums_ref[d * held : (d + 1) * held, :].astype(F32)
    d_norm_ref[0:tiles, :] = total[tiles : 2 * tiles]
    d_norm_ref[tiles : 2 * tiles, :] = total[:tiles]
    if held > 2 * tiles:
        chunk = chunk_ref.shape[0]
        chunk_ref[...] = total[2 * tiles : 2 * tiles + chunk] + total[2 * tiles + chunk :]
    else:
        chunk_ref[...] = jnp.zeros(chunk_ref.shape, F32)
    for j in range(tiles):
        cols = slice(j * LANES, (j + 1) * LANES)
        row_ref[0:1, cols] = total[j : j + 1]
        row_ref[1:2, cols] = total[tiles + j : tiles + j + 1]
    scale = norm_ref[0:1, :] * coef_ref[1:2, :]
    flat = scale * row_ref[0:1, :] / coef_ref[2:3, :]
    tilt = scale * row_ref[1:2, :] / coef_ref[2:3, :] * coef_ref[1:2, :]
    row_ref[2:3, :] = scale
    row_ref[3:4, :] = flat
    row_ref[4:5, :] = tilt
    block = 2 * LANES
    for j in range(width // block):
        for i in range(2):
            cols = slice(j * block + i * LANES, j * block + (i + 1) * LANES)
            for b in range(rows // SLOTS_BAG):
                at = slice(b * SLOTS_BAG, (b + 1) * SLOTS_BAG)
                lead = dact_ref[b : b + 1, cols] * row_ref[2:3, cols]
                apart = (pre_ref[at, cols] - coef_ref[0:1, cols]) * row_ref[4:5, cols]
                d_pre = slope_ref[at, cols] * lead - row_ref[3:4, cols] - apart
                d_pre_ref[at, cols] = (live_ref[at, :] * d_pre).astype(BF)
        cols = slice(j * block, (j + 1) * block)
        g_ref[:, cols] = dot(xt_ref[...], d_pre_ref[:, cols])
    bsize = LANES // 2
    half = bsize // 2
    side = width // bsize
    lane_half = lax.broadcasted_iota(jnp.int32, (half, LANES), 1) // bsize
    me = me_ref[0]
    for out, masks in ((send_ref, order[1]), (keep_ref, order[0])):
        for i, m in enumerate(masks):
            for b in range(local):
                r, c, odd = place(owners_ref[(me ^ m) * local + b], side)
                at = pl.ds(pl.multiple_of(r * bsize, bsize), half)
                low = pl.ds(pl.multiple_of(r * bsize + half, half), half)
                cols = pl.ds(pl.multiple_of(c * LANES, LANES), LANES)
                to = (i * local + b) * half
                out[to : to + half, :] = jnp.where(
                    lane_half == odd,
                    g_ref[at, cols].astype(out.dtype),
                    swap_halves(g_ref[low, cols].astype(out.dtype)),
                )


def scatter_sum(plan, keep, send, rows):
    rest = len(plan.rest)
    shape = (2, 2, rest, rows, LANES)
    got = plan.swap(send, plan.core)
    mine = (keep + got.astype(F32)).reshape(shape)
    cut = rows // 2
    one, two = mine[..., :cut, :], mine[..., cut:, :]
    got_one = plan.swap(one[1].astype(BF), plan.x)
    got_two = plan.swap(two[:, 1].astype(BF), plan.y)
    one = one[0] + got_one.astype(F32)
    two = two[:, 0] + got_two.astype(F32)
    got_one = plan.swap(one[1].astype(BF), plan.y)
    got_two = plan.swap(two[1].astype(BF), plan.x)
    one = one[0] + got_one.astype(F32)
    two = two[0] + got_two.astype(F32)
    if rest <= 4:
        both = jnp.concatenate([one[1:], two[1:]], axis=1).astype(BF)
        return one, two, [plan.swap(both[k], m) for k, m in enumerate(plan.rest[1:])]
    both = jnp.concatenate([one, two], axis=1)
    for b in reversed(plan.bits):
        both = both.reshape(2, -1, rows, LANES)
        both = both[0] + plan.swap(both[1].astype(BF), b).astype(F32)
    return both[:, :cut], both[:, cut:], []


def norm_kernel(*refs, n):
    one_ref, two_ref, chunk_ref = refs[:3]
    got = refs[3:-2]
    g_ref, pay_ref = refs[-2:]
    total = jnp.concatenate([one_ref[0], two_ref[0]], axis=0)
    for g in got:
        total = total + g[...].astype(F32)
    g_ref[...] = total
    chunk = chunk_ref[...]
    squares = jnp.sum(total * total, keepdims=True) + jnp.sum(chunk * chunk, keepdims=True)
    high = chunk.astype(BF)
    low = chunk - high.astype(F32)
    for i, v in enumerate(three(squares)):
        low = jnp.where(spare(chunk.shape, i), v.astype(F32), low)
    packed = jnp.concatenate([high, low.astype(BF)], axis=0)
    rows = packed.shape[0]
    for d in range(n):
        pay_ref[d * rows : (d + 1) * rows, :] = packed


def spare(shape, i):
    row = lax.broadcasted_iota(jnp.int32, shape, 0)
    lane = lax.broadcasted_iota(jnp.int32, shape, 1)
    return (row == shape[0] - 1) & (lane == LANES - 3 + i)


def adamw(grad, weight, first, second):
    first = BETA_ONE * first + (1 - BETA_ONE) * grad
    second = BETA_TWO * second + (1 - BETA_TWO) * grad * grad
    step = (
        first / (1 - BETA_ONE**STEP) / (jnp.sqrt(second / (1 - BETA_TWO**STEP)) + EPSILON)
    )
    return weight - RATE * (step + DECAY * weight), first, second


def panel_factor(panel, at):
    group = panel.shape[1]
    index = lax.broadcasted_iota(jnp.int32, (1, group, 1), 1)
    cols = [jnp.broadcast_to(panel[:, :, at + i : at + i + 1], panel.shape) for i in range(group)]
    for i in range(group):
        inv = lax.rsqrt(cols[i][:, i : i + 1, :])
        row = panel[:, i : i + 1, :] * inv
        f = cols[i] * inv
        panel = jnp.where(index > i, panel - f * row, jnp.where(index == i, row, panel))
        for j in range(i + 1, group):
            cols[j] = cols[j] - f * f[:, j : j + 1, :]
    return panel


def eliminate(mat_ref):
    count, size = mat_ref.shape[0], mat_ref.shape[1]
    group = 8
    for at in range(0, size, group):
        rest = at + group
        panel = panel_factor(mat_ref[:, at:rest, :], at)
        mat_ref[:, at:rest, :] = panel
        if rest == size:
            return
        a, b, c = (v.astype(F32) for v in three(panel))
        lhs = jnp.concatenate([a, a, b, b, a, c], axis=1)
        rhs = jnp.concatenate([a, b, a, b, c, a], axis=1).astype(BF)
        for m in range(count):
            turned = lhs[m].T[rest:size, :].astype(BF)
            mat_ref[m, rest:, :] = mat_ref[m, rest:, :] - dot(turned, rhs[m])


def pair(a, b):
    return jnp.concatenate([a, b], axis=1)


def prepare_kernel(
    w_hbm, left_hbm, right_hbm, bl_hbm, br_hbm, first_hbm, second_hbm, ema_hbm,
    moments_ref, stats_ref, bases_ref, weights_ref, turned_ref, powers_ref,
    w_ref, left_ref, right_ref, bl_ref, br_ref, first_ref, second_ref, ema_ref, sems,
):
    fetch(
        (w_hbm, left_hbm, right_hbm, bl_hbm, br_hbm, first_hbm, second_hbm, ema_hbm),
        (w_ref, left_ref, right_ref, bl_ref, br_ref, first_ref, second_ref, ema_ref),
        sems,
    )
    each = range(w_ref.shape[0])
    for b in each:
        moments_ref[b] = pair(first_ref[b], second_ref[b])
        stats_ref[b] = pair(left_ref[b], right_ref[b])
        bases_ref[b] = pair(bl_ref[b], br_ref[b])
        weights_ref[b] = pair(w_ref[b], ema_ref[b])
    half = [hdot(bl_ref[b], first_ref[b], 0, 0) for b in each]
    for b in each:
        turned_ref[b] = hdot(half[b], br_ref[b])
    lefts = [hdot(bl_ref[b], left_ref[b], 0, 0) for b in each]
    rights = [hdot(br_ref[b], right_ref[b], 0, 0) for b in each]
    for b in each:
        powers_ref[b] = pair(lefts[b], rights[b])


def turn_kernel(
    me_ref, owners_ref, g_ref, bases_ref,
    wo_hbm, mo_hbm, vo_hbm, eo_hbm, wt_hbm, mt_hbm, vt_hbm, wn_hbm, mn_hbm, vn_hbm,
    grad_ref, squares_ref, powers_ref, scale_ref,
    wide_ref, towers_ref, norms_ref, sems,
):
    local, bsize = bases_ref.shape[0], bases_ref.shape[1]
    sources = (wo_hbm, mo_hbm, vo_hbm, eo_hbm, wt_hbm, mt_hbm, vt_hbm, wn_hbm, mn_hbm, vn_hbm)
    targets = [wide_ref.at[i] for i in range(4)]
    targets += [towers_ref.at[i] for i in range(3)] + [norms_ref.at[i] for i in range(3)]
    copies = [pltpu.make_async_copy(a, b, sems.at[i]) for i, (a, b) in enumerate(zip(sources, targets))]
    for c in copies:
        c.start()
    largest = jnp.max(jnp.abs(g_ref[...]), keepdims=True)
    largest = jnp.where(largest > 0.0, largest, 1.0)
    scale_ref[...] = jnp.broadcast_to(largest, scale_ref.shape)
    half = bsize // 2
    each = range(local)
    grads = []
    for b in each:
        odd = owners_ref[me_ref[0] * local + b] % 2
        tile = g_ref[b * half : (b + 1) * half, :]
        tile = jnp.where(odd == 1, swap_halves(tile), tile)
        grads.append(jnp.concatenate([tile[:, :bsize], tile[:, bsize:]], axis=0) / largest)
    bl = [bases_ref[b, :, :bsize] for b in each]
    br = [bases_ref[b, :, bsize:] for b in each]
    by_left = [hdot(bl[b], grads[b], 0, 0) for b in each]
    by_right = [hdot(grads[b], br[b]) for b in each]
    outer = [hdot(grads[b], grads[b], 1, 1) for b in each]
    inner = [hdot(grads[b], grads[b], 0, 0) for b in each]
    for b in each:
        squares_ref[b] = pair(outer[b], inner[b])
    for b in each:
        grad_ref[b] = pair(grads[b], hdot(by_left[b], br[b]))
    lefts = [hdot(by_left[b], grads[b], 1, 1) for b in each]
    rights = [hdot(by_right[b], grads[b], 0, 0) for b in each]
    for b in each:
        powers_ref[b] = pair(lefts[b], rights[b])
    for c in copies:
        c.wait()


def step_kernel(
    got_ref, d_norm_ref, d_towers_ref,
    grad_ref, squares_ref, powers_ref, scale_ref,
    old_ref, towers_ref, norms_ref,
    moments_ref, stats_ref, bases_ref, weights_ref, turned_first_ref, powers_old_ref,
    w_out, low_out, left_out, right_out, bl_out, br_out, first_out, second_out, ema_out,
    wo_out, mo_out, vo_out, eo_out, wt_out, mt_out, vt_out, wn_out, mn_out, vn_out, gn_out,
    mat_ref, wide_ref, dn_ref, flat_ref, *, n,
):
    local, bsize = bases_ref.shape[0], bases_ref.shape[1]
    embed, width = old_ref.shape[1:]
    tiles = width // LANES
    held = got_ref.shape[0] // n
    if n > 1:
        chunk = held // 2
        used = functools.reduce(jnp.logical_or, [spare((chunk, LANES), i) for i in range(3)])
        squares = jnp.zeros((chunk, LANES), F32)
        for d in range(n):
            part = got_ref[d * held : (d + 1) * held, :].astype(F32)
            squares = squares + jnp.where(used, part[chunk:], 0.0)
            flat_ref[d * chunk : (d + 1) * chunk, :] = part[:chunk] + jnp.where(used, 0.0, part[chunk:])
        squares = jnp.sum(squares)
        for j in range(tiles):
            wide_ref[:, j * LANES : (j + 1) * LANES] = flat_ref[pl.ds(j, embed, stride=tiles), :]
    else:
        squares = jnp.max(got_ref[0:1, :LANES])
        wide_ref[...] = got_ref[8 : 8 + embed, :]
    squares = squares + jnp.sum(d_towers_ref[...] * d_towers_ref[...])
    squares = squares + jnp.sum(d_norm_ref[...] * d_norm_ref[...])
    norm = jnp.sqrt(jnp.full((1, LANES), squares, F32))
    gn_out[0, 0] = jnp.max(norm)
    factor = (CLIP / jnp.maximum(norm, CLIP))[:, :1]
    each = range(local)
    lead = factor * scale_ref[0:1, 0:1]
    twice = (1 - BETA_TWO) * lead * lead
    lefts, rights = [], []
    for b in each:
        powers = BETA_TWO * powers_old_ref[b] + twice * powers_ref[b]
        lefts.append(powers[:, :bsize])
        rights.append(powers[:, bsize:])
    for b in each:
        mat_ref[2 * b] = pair(hdot(lefts[b], lefts[b], 1, 1), lefts[b])
        mat_ref[2 * b + 1] = pair(hdot(rights[b], rights[b], 1, 1), rights[b])
    ratios = []
    for b in each:
        stats = BETA_TWO * stats_ref[b] + twice * squares_ref[b]
        left_out[b], right_out[b] = stats[:, :bsize], stats[:, bsize:]
        first_out[b] = BETA_ONE * moments_ref[b, :, :bsize] + (1 - BETA_ONE) * lead * grad_ref[b, :, :bsize]
        turned = grad_ref[b, :, bsize:]
        second = BETA_TWO * moments_ref[b, :, bsize:] + twice * turned * turned
        second_out[b] = second
        moved = BETA_ONE * turned_first_ref[b] + (1 - BETA_ONE) * lead * turned
        moved = moved / (1 - BETA_ONE**STEP)
        ratios.append(moved / (jnp.sqrt(second / (1 - BETA_TWO**STEP)) + EPSILON))
    half = [hdot(bases_ref[b, :, :bsize], ratios[b]) for b in each]
    updates = [hdot(half[b], bases_ref[b, :, bsize:], 1, 1) for b in each]
    for b in each:
        old = weights_ref[b, :, :bsize]
        new = old - RATE * (updates[b] + DECAY * old)
        w_out[b] = new
        low_out[b] = new.astype(BF)
        ema_out[b] = AVG_KEEP * weights_ref[b, :, bsize:] + AVG_TAKE * new
    new, m, v = adamw(wide_ref[...] * factor, old_ref[0], old_ref[1], old_ref[2])
    wo_out[...], mo_out[...], vo_out[...] = new, m, v
    eo_out[...] = AVG_KEEP * old_ref[3] + AVG_TAKE * new
    for t in range(2):
        wt_out[t], mt_out[t], vt_out[t] = adamw(
            d_towers_ref[t] * factor, towers_ref[0, t], towers_ref[1, t], towers_ref[2, t]
        )
        for j in range(tiles):
            dn_ref[t : t + 1, j * LANES : (j + 1) * LANES] = d_norm_ref[
                t * tiles + j : t * tiles + j + 1, :
            ]
    wn_out[...], mn_out[...], vn_out[...] = adamw(
        dn_ref[...] * factor, norms_ref[0], norms_ref[1], norms_ref[2]
    )
    eliminate(mat_ref)
    for b in each:
        bl_out[b] = mat_ref[2 * b, :, bsize:].T
        br_out[b] = mat_ref[2 * b + 1, :, bsize:].T


def exchange(payload):
    return lax.all_to_all(payload, AXES, 0, 0, tiled=True)


def on_device(
    plan,
    codes, field_offsets, seg_mask, neg_mask, owners,
    w_hidden, stat_left, stat_right, basis_left, basis_right, mom1_hidden, mom2_hidden, ema_hidden,
    w_out, mom1_out, mom2_out, ema_out,
    w_towers, mom1_towers, mom2_towers,
    w_norm, mom1_norm, mom2_norm,
):
    n = plan.n
    local, bsize = w_hidden.shape[0], w_hidden.shape[1]
    width, embed = w_out.shape
    slots = codes.shape[0]
    rows, total_rows = neg_mask.shape
    tiles = width // LANES
    half = bsize // 2
    bags = slots // SLOTS_BAG
    masked = total_rows <= 1024 and n <= embed
    me = lax.axis_index(AXES).astype(jnp.int32)[None]

    chunks = total_rows // LANES if masked else 0
    size = local * half + chunks * PAIR + PAIR
    (payload,) = call(
        functools.partial(pack_kernel, masked=masked),
        [((size, LANES), BF)],
        [me, in_hbm(owners), w_hidden, neg_mask, seg_mask.reshape(-1, LANES)],
        smem=2,
        hbm=3,
        scratch=[
            pltpu.VMEM(w_hidden.shape, F32),
            pltpu.VMEM(neg_mask.shape, jnp.int32),
            pltpu.VMEM((slots // LANES, LANES), jnp.int32),
            pltpu.SemaphoreType.DMA((3,)),
        ],
        name="pack",
    )
    cut = max(half, size // 2 // half * half)
    cut = min(cut, local * half)
    blocks = (local, bsize, bsize)
    twin = (local, bsize, 2 * bsize)
    state = [
        w_hidden, stat_left, stat_right, basis_left, basis_right, mom1_hidden, mom2_hidden, ema_hidden
    ]
    prepared = call(
        prepare_kernel,
        [(twin, F32)] * 4 + [(blocks, F32), (twin, F32)],
        state,
        hbm=len(state),
        scratch=[pltpu.VMEM(blocks, F32)] * len(state) + [pltpu.SemaphoreType.DMA((len(state),))],
        limit=12,
        name="prepare",
        cost=10_000_000,
    )
    turned_out, turned_mom1, turned_mom2, turned_ema = (
        a.T for a in (w_out, mom1_out, mom2_out, ema_out)
    )
    early = hash_inputs(codes, field_offsets)
    live = jnp.broadcast_to(seg_mask.astype(F32)[:, None], (slots, LANES))
    slot_bag = lax.broadcasted_iota(jnp.int32, (bags, slots), 1) // SLOTS_BAG
    in_bag = slot_bag == lax.broadcasted_iota(jnp.int32, (bags, slots), 0)
    chosen = jnp.where(in_bag, seg_mask.astype(F32)[None], 0.0).astype(BF)
    late = (*prepared, live, chosen)
    zero = (me[0] >> 16).astype(BF)
    pieces, (x, x_turned), (*prepared, live, chosen) = gather_pieces(
        plan, payload, cut, zero, early, late
    )
    mask_shape = (total_rows, total_rows) if masked else (PAIR, LANES)
    pre, stats, counts, mask = call(
        functools.partial(
            pre_kernel,
            holds=[(m, row) for _, m, row in pieces],
            rest=plan.rest,
            local=local,
            masked=masked,
            n=n,
            pieces=len(pieces),
        ),
        [
            ((slots, width), F32),
            ((n * 2 * tiles, LANES), F32),
            ((n, LANES), F32),
            (mask_shape, BF),
        ],
        [me, owners] + [a for a, _, _ in pieces] + [x, live],
        smem=2,
        scratch=[pltpu.VMEM((2, width, width), BF), pltpu.VMEM((2 * tiles, LANES), F32)],
        limit=16,
        name="pre",
    )
    stats = exchange(stats)
    slope, act, one, two, coef, bag_sums, pay = call(
        act_kernel,
        [
            ((slots, width), F32),
            ((bags, width), F32),
            ((bags, width), F32),
            ((bags, width), F32),
            ((8, width), F32),
            ((bags, embed), F32),
            ((n * 8, LANES), F32),
        ],
        [stats, counts, w_norm, pre, live, chosen, turned_out],
        scratch=[
            pltpu.VMEM((slots, LANES), BF),
            pltpu.VMEM((tiles, bags * 8, LANES), F32),
            pltpu.VMEM((tiles, bags * 8, LANES), F32),
        ],
        limit=12,
        name="act",
    )
    if masked:
        chunk = embed * tiles // n
        everyone = exchange(pay)
        d_act, pay, d_towers, loss_sum, count = call(
            functools.partial(loss_kernel, n=n),
            [
                ((bags, width), F32),
                ((n * (2 * tiles + 2 * chunk), LANES), BF),
                ((2, embed, embed), F32),
                ((1, 1), F32),
                ((1, 1), F32),
            ],
            [me, everyone, mask, w_towers, turned_out, act, one, two],
            smem=1,
            smem_outs=2,
            scratch=[
                pltpu.VMEM((total_rows, total_rows), F32),
                pltpu.VMEM((total_rows, embed), F32),
                pltpu.VMEM((total_rows, embed), F32),
                pltpu.VMEM((embed * tiles, LANES), F32),
                pltpu.VMEM((2 * tiles, LANES), F32),
            ],
            name="loss",
        )
        sums, parts = exchange(pay), n
        loss_sum, count = loss_sum[0, 0], count[0, 0]
    else:
        d_act, sums, d_second, d_towers, loss_sum, count = loss_spread(
            plan, bag_sums, neg_mask, w_towers, turned_out, act, one, two
        )
        parts = 1
        chunk = 8
    groups = [m for m in (0, plan.y, plan.x, plan.x | plan.y)]
    keep_order = [g | r for g in groups for r in plan.rest]
    order = (keep_order, [m | plan.core for m in keep_order])
    kept, sent, second_chunk, d_norm = call(
        functools.partial(grad_kernel, parts=parts, order=order, local=local),
        [
            ((n // 2 * local * half, LANES), F32),
            ((n // 2 * local * half, LANES), BF),
            ((chunk, LANES), F32),
            ((2 * tiles, LANES), F32),
        ],
        [me, owners, sums, coef, w_norm, d_act, slope, pre, live, x_turned],
        smem=2,
        scratch=[
            pltpu.VMEM((slots, width), BF),
            pltpu.VMEM((width, width), F32),
            pltpu.VMEM((8, width), F32),
        ],
        limit=20,
        name="grad",
    )
    one_sum, two_sum, others = scatter_sum(plan, kept, sent, local * half)
    copies = n if masked else 1
    grad, pay = call(
        functools.partial(norm_kernel, n=copies),
        [((local * half, LANES), F32), ((copies * 2 * chunk, LANES), BF)],
        [one_sum, two_sum, second_chunk, *others],
        name="norm",
    )
    if masked:
        got = exchange(pay)
    else:
        squares = lax.psum(jnp.sum(grad * grad), AXES) + jnp.sum(d_second * d_second)
        got = jnp.concatenate([jnp.full((8, width), squares, F32), d_second], axis=0)
    moments, stats, bases, weights, turned_first, powers_old = prepared
    plain = [
        turned_out, turned_mom1, turned_mom2, turned_ema,
        w_towers, mom1_towers, mom2_towers,
        w_norm, mom1_norm, mom2_norm,
    ]
    turned = call(
        turn_kernel,
        [(twin, F32)] * 3
        + [((8, LANES), F32), ((4, embed, width), F32), ((3, 2, embed, embed), F32), ((3, 2, width), F32)],
        [me, owners, grad, bases, *plain],
        smem=2,
        hbm=len(plain),
        scratch=[pltpu.SemaphoreType.DMA((len(plain),))],
        name="turn",
        cost=10_000_000,
    )
    outs = [(blocks, F32), (blocks, BF)] + [(blocks, F32)] * 7
    outs += [((embed, width), F32)] * 4 + [((2, embed, embed), F32)] * 3 + [((2, width), F32)] * 3
    new = call(
        functools.partial(step_kernel, n=n if masked else 1),
        outs + [((1, 1), F32)],
        [
            got, d_norm, d_towers, *turned,
            moments, stats, bases, weights, turned_first, powers_old,
        ],
        smem_outs=1,
        scratch=[
            pltpu.VMEM((2 * local, bsize, 2 * bsize), F32),
            pltpu.VMEM((embed, width), F32),
            pltpu.VMEM((2, width), F32),
            pltpu.VMEM((embed * tiles, LANES), F32),
        ],
        name="step",
    )
    return (loss_sum, count, new[-1][0, 0], *new[:9], *(a.T for a in new[9:13]), *new[13:-1])


def solution(mesh):
    split = P(("gx", "gy"))
    plan = Plan(mesh.shape["gx"], mesh.shape["gy"])
    return jax.shard_map(
        functools.partial(on_device, plan),
        mesh=mesh,
        in_specs=(split, P(), split, split, P()) + (split,) * 8 + (P(),) * 10,
        out_specs=(P(),) * 3 + (split,) * 9 + (P(),) * 10,
        check_vma=False,
    )
```

time: 203 us -> 137 us (0.67)
  local copies, waits for them, and re-layouts: 39.2 us -> 1.77 us
  waiting for transfers between devices: 54.1 us -> 35.2 us
  Pallas kernels: 54.1 us -> 39.2 us
  blocking collectives: 25.7 us -> 35.8 us
  starting transfers between devices: 27 us -> 23.3 us
    unnamed x92 -> x34, local copies, waits for them, and re-layouts: 38.3 us -> 1.43 us
    all_to_all x2 -> x1, waiting for transfers between devices: 18.8 us -> 4.22 us  [exchange(): return lax.all_to_all(payload, AXES, 0, 0, tiled=True)]
    pallas_call x7 -> x10, Pallas kernels: 52.3 us -> 39.2 us  [call(): pl.pallas_call(kernel, out_shape=[jax.ShapeDtypeStruct(s, t) for s, t in...]
    all_to_all x2 -> x3, blocking collectives: 25.7 us -> 35.8 us  [exchange(): return lax.all_to_all(payload, AXES, 0, 0, tiled=True)]
    ppermute x10, waiting for transfers between devices: 29 us -> 19.2 us  [swap(): return lax.ppermute(a, 'gy', [(i, i ^ my) for i in range(self.gy)])]
    ppermute x10, waiting for transfers between devices: 6.25 us -> 11.9 us  [swap(): return lax.ppermute(a, 'gx', [(i, i ^ mx) for i in range(self.gx)])]
    all_to_all x2 -> x1, starting transfers between devices: 6.42 us -> 3.87 us  [exchange(): return lax.all_to_all(payload, AXES, 0, 0, tiled=True)]
  transfers between devices with their start and end apart: 22 -> 21, of which waited for: 14 -> 14; matrix products, arithmetic and copies ran while one was open for 1% -> 0% of each run, Pallas kernels for 1% -> 6%
where the time goes in v2:
time: 137 us
  Pallas kernels  39.2 us (29%)
  blocking collectives  35.8 us (26%)
  waiting for transfers between devices  35.2 us (26%)
  starting transfers between devices  23.3 us (17%)
  local copies, waits for them, and re-layouts  1.77 us (1%)
    pallas_call x10, Pallas kernels, call(): pl.pallas_call(kernel, out_shape=[jax.ShapeDtypeStruct(s, t) for s, t in...  39.2 us
    all_to_all x3, blocking collectives, exchange(): return lax.all_to_all(payload, AXES, 0, 0, tiled=True)  35.8 us
    ppermute x10, waiting for transfers between devices, swap(): return lax.ppermute(a, 'gy', [(i, i ^ my) for i in range(self.gy)])  19.2 us
    ppermute x10, starting transfers between devices, swap(): return lax.ppermute(a, 'gy', [(i, i ^ my) for i in range(self.gy)])  14.5 us
    ppermute x10, waiting for transfers between devices, swap(): return lax.ppermute(a, 'gx', [(i, i ^ mx) for i in range(self.gx)])  11.9 us
    ppermute x10, starting transfers between devices, swap(): return lax.ppermute(a, 'gx', [(i, i ^ mx) for i in range(self.gx)])  4.91 us
    all_to_all x1, waiting for transfers between devices, exchange(): return lax.all_to_all(payload, AXES, 0, 0, tiled=True)  4.22 us
    all_to_all x1, starting transfers between devices, exchange(): return lax.all_to_all(payload, AXES, 0, 0, tiled=True)  3.87 us
  transfers between devices with their start and end apart: 21, of which 14 were waited for; matrix products, arithmetic and copies ran while one was open for 0% of the time, Pallas kernels for 6%

profile of v2, /device:TPU:0, one launch (start us, length us, event | category | flops | bytes accessed | tf_op | source)
XLA Modules:
  0.0 137.1 jit_solution(5866478122448273117)
XLA Ops:
  0.7 1.8 %pack.1 = bf16[336,128]{1,0:T(8,128)(2,1)S(1)} custom-call(s32[1]{0:T(128)} %bitcast.me_ref.refs_0_, s32[256]{0:T(256)} %owners_ref.5, f32[8,64,64]{2,1,0:T(8,128)} %w_hbm.3, s32[16,512]{1,0:T(8,128)} %neg_hbm.1, s32[8,128]{1,0:T(8,128)} %bitcast.73), custom_call_target="tpu_custom_call" | custom-call | tf_op jit(solution)/shard_map/pack/pallas_call | solution.py:60
  2.5 5.1 %collective-permute-start.2 = (bf16[1,336,128]{2,1,0:T(8,128)(2,1)S(1)}, bf16[1,336,128]{2,1,0:T(8,128)(2,1)S(1)}, u32[]{:S(2)}, u32[]{:S(2)}) collective-permute-start(bf16[1,336,128]{2,1,0:T(8,128)(2,1)S(1)} %bitcast.60), channel_id=1, source_target_pairs={{0,6},{1,7},{2,4},{3,5},{4,2},{5,3},{6,0},{7,1},{8,14},{9,15},{10,... | collective-permute-start | bytes 258056 | tf_op jit(solution)/shard_map/ppermute | solution.py:116
  8.2 2.6 %hash.1 = (bf16[1024,1024]{1,0:T(8,128)(2,1)S(1)}, bf16[1024,1024]{1,0:T(8,128)(2,1)S(1)}) custom-call(s32[1024,1024]{1,0:T(8,128)} %codes_hbm.1, s32[8,1024]{1,0:T(8,128)} %offsets_hbm.1), custom_call_target="tpu_custom_call" | custom-call | flops 20000000 | bytes 200000 | tf_op jit(solution)/shard_map/hash/pallas_call | solution.py:60
  10.8 1.3 copy-done
  12.2 2.6 %collective-permute-done.1 = bf16[1,336,128]{2,1,0:T(8,128)(2,1)S(1)} collective-permute-done((bf16[1,336,128]{2,1,0:T(8,128)(2,1)S(1)}, bf16[1,336,128]{2,1,0:T(8,128)(2,1)S(1)}, u32[]{:S(2)}, u32[]{:S(2)}) %collective-permute-start.1) | collective-permute-done | bytes 86048 | tf_op jit(solution)/shard_map/ppermute | solution.py:116
  14.8 1.6 %collective-permute-start.4 = (bf16[4,336,128]{2,1,0:T(8,128)(2,1)S(1)}, bf16[4,336,128]{2,1,0:T(8,128)(2,1)S(1)}, u32[]{:S(2)}, u32[]{:S(2)}) collective-permute-start(bf16[4,336,128]{2,1,0:T(8,128)(2,1)S(1)} %pad_maximum_fusion.refs_2_), channel_id=1, source_target_pairs={{0,1},{1,0},{2,3},{3,2},{4,5},{5,4},{6,7},{7,6},{8,9},{9,8},{10,11... | collective-permute-start | bytes 1032200 | tf_op jit(solution)/shard_map/ppermute | solution.py:116
  16.4 1.5 %collective-permute-start.3 = (bf16[4,336,128]{2,1,0:T(8,128)(2,1)S(1)}, bf16[4,336,128]{2,1,0:T(8,128)(2,1)S(1)}, u32[]{:S(2)}, u32[]{:S(2)}) collective-permute-start(bf16[4,336,128]{2,1,0:T(8,128)(2,1)S(1)} %pad_maximum_fusion.refs_2_), channel_id=1, source_target_pairs={{0,16},{8,24},{16,0},{24,8},{1,17},{9,25},{17,1},{25,9},{2,18},{10... | collective-permute-start | bytes 1032200 | tf_op jit(solution)/shard_map/ppermute | solution.py:114
  17.9 2.8 %prepare.1 = (f32[8,64,128]{2,1,0:T(8,128)S(1)}, f32[8,64,128]{2,1,0:T(8,128)S(1)}, f32[8,64,128]{2,1,0:T(8,128)S(1)}, f32[8,64,128]{2,1,0:T(8,128)S(1)}, f32[8,...) custom-call(f32[8,64,64]{2,1,0:T(8,128)} %w_hbm.3, f32[8,64,64]{2,1,0:T(8,128)} %left_hbm.1, f32[8,64,64]{2,1,0:T(8,128)} %right_hbm.1, ...), custom_call_target="tpu_custom_call" | custom-call | flops 10000000 | bytes 100000 | tf_op jit(solution)/shard_map/prepare/pallas_call | solution.py:60
  20.9 3.2 %collective-permute-done.4.refs_4_ = bf16[4,336,128]{2,1,0:T(8,128)(2,1)S(1)} collective-permute-done((bf16[4,336,128]{2,1,0:T(8,128)(2,1)S(1)}, bf16[4,336,128]{2,1,0:T(8,128)(2,1)S(1)}, u32[]{:S(2)}, u32[]{:S(2)}) %collective-permute-start.4) | collective-permute-done | bytes 344096 | tf_op jit(solution)/shard_map/ppermute | solution.py:116
  24.1 1.3 collective-permute-done.3.refs_3_
  25.7 1.6 %collective-permute-start.6 = (bf16[4,176,128]{2,1,0:T(8,128)(2,1)S(1)}, bf16[4,176,128]{2,1,0:T(8,128)(2,1)S(1)}, u32[]{:S(2)}, u32[]{:S(2)}) collective-permute-start(bf16[4,176,128]{2,1,0:T(8,128)(2,1)S(1)} %slice_add_fusion), channel_id=1, source_target_pairs={{0,16},{8,24},{16,0},{24,8},{1,17},{9,25},{17,1},{25,9},{2,18},{10... | collective-permute-start | bytes 540680 | tf_op jit(solution)/shard_map/ppermute | solution.py:114
  28.1 4.6 %collective-permute-done.6.refs_6_ = bf16[4,176,128]{2,1,0:T(8,128)(2,1)S(1)} collective-permute-done((bf16[4,176,128]{2,1,0:T(8,128)(2,1)S(1)}, bf16[4,176,128]{2,1,0:T(8,128)(2,1)S(1)}, u32[]{:S(2)}, u32[]{:S(2)}) %collective-permute-start.6) | collective-permute-done | bytes 180256 | tf_op jit(solution)/shard_map/ppermute | solution.py:114
  32.7 1.3 collective-permute-done.5.refs_5_
  34.0 1.4 %collective-permute-done.10.refs_10_ = bf16[4,160,128]{2,1,0:T(8,128)(2,1)S(1)} collective-permute-done((bf16[4,160,128]{2,1,0:T(8,128)(2,1)S(1)}, bf16[4,160,128]{2,1,0:T(8,128)(2,1)S(1)}, u32[]{:S(2)}, u32[]{:S(2)}) %collective-permute-start.10) | collective-permute-done | bytes 163872 | tf_op jit(solution)/shard_map/ppermute | solution.py:114
  35.5 5.7 %pre.1 = (f32[1024,1024]{1,0:T(8,128)S(1)}, f32[512,128]{1,0:T(8,128)S(1)}, f32[32,128]{1,0:T(8,128)S(1)}, bf16[512,512]{1,0:T(8,128)(2,1)S(1)}) custom-call(s32[1]{0:T(128)} %bitcast.me_ref.refs_0_, s32[256]{0:T(256)S(1)} %copy-done.15, bf16[4,336,128]{2,1,0:T(8,128)(2,1)S(1)} %pad_maximum_fusion.refs_2_, ...), custom_call_target="tpu_custom_call" | custom-call | tf_op jit(solution)/shard_map/pre/pallas_call | solution.py:60
  41.2 13.0 %all_to_all.44 = f32[32,16,128]{2,1,0:T(8,128)S(1)} all-to-all(f32[32,16,128]{2,1,0:T(8,128)S(1)} %bitcast.64), channel_id=1, replica_groups=mesh['gx'=4,'gy'=8] {'gx','gy'}, dimensions={0} | all-to-all | bytes 524288 | tf_op jit(solution)/shard_map/all_to_all | solution.py:773
  54.2 5.4 %act.1 = (f32[1024,1024]{1,0:T(8,128)S(1)}, f32[32,1024]{1,0:T(8,128)S(1)}, f32[32,1024]{1,0:T(8,128)S(1)}, f32[32,1024]{1,0:T(8,128)S(1)}, f32[8,1024]{1,0:T(8,...) custom-call(f32[512,128]{1,0:T(8,128)S(1)} %bitcast.56, f32[32,128]{1,0:T(8,128)S(1)} %get-tuple-element.105.count_ref, ...), custom_call_target="tpu_custom_call" | custom-call | tf_op jit(solution)/shard_map/act/pallas_call | solution.py:60
  59.6 9.9 %all_to_all.45 = f32[32,8,128]{2,1,0:T(8,128)S(1)} all-to-all(f32[32,8,128]{2,1,0:T(8,128)S(1)} %bitcast.66), channel_id=1, replica_groups=mesh['gx'=4,'gy'=8] {'gx','gy'}, dimensions={0} | all-to-all | bytes 262144 | tf_op jit(solution)/shard_map/all_to_all | solution.py:773
  69.5 3.8 %loss.1 = (f32[32,1024]{1,0:T(8,128)S(1)}, bf16[1024,128]{1,0:T(8,128)(2,1)S(1)}, f32[2,32,32]{2,1,0:T(8,128)S(1)}, f32[1,1]{1,0:T(1,128)}, f32[1,1]{1,0:T(1,128)}) custom-call(s32[1]{0:T(128)} %bitcast.me_ref.refs_0_, f32[256,128]{1,0:T(8,128)S(1)} %bitcast.59, bf16[512,512]{1,0:T(8,128)(2,1)S(1)} %get-tuple-element.109.mask_ref, ...), custom_call_target="tpu_custom_call" | custom-call | tf_op jit(solution)/shard_map/loss/pallas_call | solution.py:60
  73.4 12.9 %all_to_all.46 = bf16[32,32,128]{2,1,0:T(8,128)(2,1)S(1)} all-to-all(bf16[32,32,128]{2,1,0:T(8,128)(2,1)S(1)} %bitcast.65), channel_id=1, replica_groups=mesh['gx'=4,'gy'=8] {'gx','gy'}, dimensions={0} | all-to-all | bytes 524288 | tf_op jit(solution)/shard_map/all_to_all | solution.py:773
  86.3 5.2 %grad.1 = (f32[4096,128]{1,0:T(8,128)S(1)}, bf16[4096,128]{1,0:T(8,128)(2,1)S(1)}, f32[8,128]{1,0:T(8,128)S(1)}, f32[16,128]{1,0:T(8,128)S(1)}) custom-call(s32[1]{0:T(128)} %bitcast.me_ref.refs_0_, s32[256]{0:T(256)S(1)} %copy-done.15, bf16[1024,128]{1,0:T(8,128)(2,1)S(1)} %bitcast.57, f32[8,1024]{1,0:T(8,128)S(1)} %get-tuple-element.116.coef_ref, ...), custom_call_target="tpu_custom_call" | custom-call | tf_op jit(solution)/shard_map/grad/pallas_call | solution.py:60
  91.6 2.6 %collective-permute-done.12 = bf16[4096,128]{1,0:T(8,128)(2,1)S(1)} collective-permute-done((bf16[4096,128]{1,0:T(8,128)(2,1)S(1)}, bf16[4096,128]{1,0:T(8,128)(2,1)S(1)}, u32[]{:S(2)}, u32[]{:S(2)}) %collective-permute-start.12) | collective-permute-done | bytes 1048608 | tf_op jit(solution)/shard_map/ppermute | solution.py:114
  96.1 6.8 %collective-permute-done.15 = bf16[2,4,128,128]{3,2,1,0:T(8,128)(2,1)S(1)} collective-permute-done((bf16[2,4,128,128]{3,2,1,0:T(8,128)(2,1)S(1)}, bf16[2,4,128,128]{3,2,1,0:T(8,128)(2,1)S(1)}, u32[]{:S(2)}, u32[]{:S(2)}) %collective-permute-start.15) | collective-permute-done | bytes 262176 | tf_op jit(solution)/shard_map/ppermute | solution.py:116
  105.9 3.0 %collective-permute-done.14 = bf16[4,128,128]{2,1,0:T(8,128)(2,1)S(1)} collective-permute-done((bf16[4,128,128]{2,1,0:T(8,128)(2,1)S(1)}, bf16[4,128,128]{2,1,0:T(8,128)(2,1)S(1)}, u32[]{:S(2)}, u32[]{:S(2)}) %collective-permute-start.14) | collective-permute-done | bytes 131104 | tf_op jit(solution)/shard_map/ppermute | solution.py:116
  108.9 1.1 collective-permute-done.16
  110.1 1.2 collective-permute-start.19
  111.2 3.3 %collective-permute-start.18 = (bf16[256,128]{1,0:T(8,128)(2,1)S(1)}, bf16[256,128]{1,0:T(8,128)(2,1)S(1)}, u32[]{:S(2)}, u32[]{:S(2)}) collective-permute-start(bf16[256,128]{1,0:T(8,128)(2,1)S(1)} %get-tuple-element.164), channel_id=1, source_target_pairs={{0,4},{1,5},{2,6},{3,7},{4,0},{5,1},{6,2},{7,3},{8,12},{9,13},{10,... | collective-permute-start | bytes 196616 | tf_op jit(solution)/shard_map/ppermute | solution.py:116
  114.5 1.7 %collective-permute-done.19.refs_5_ = bf16[256,128]{1,0:T(8,128)(2,1)S(1)} collective-permute-done((bf16[256,128]{1,0:T(8,128)(2,1)S(1)}, bf16[256,128]{1,0:T(8,128)(2,1)S(1)}, u32[]{:S(2)}, u32[]{:S(2)}) %collective-permute-start.19) | collective-permute-done | bytes 65568 | tf_op jit(solution)/shard_map/ppermute | solution.py:116
  117.8 3.9 %all-to-all-start.3 = ((bf16[32,16,128]{2,1,0:T(8,128)(2,1)}), bf16[32,16,128]{2,1,0:T(8,128)(2,1)S(1)}, u32[]{:S(2)}, u32[]{:S(2)}) async-start(bf16[32,16,128]{2,1,0:T(8,128)(2,1)} %bitcast.24), calls=%async_computation.3 | async-start | bytes 262144 | tf_op jit(solution)/shard_map/all_to_all | solution.py:773
  121.7 3.3 %turn.1 = (f32[8,64,128]{2,1,0:T(8,128)S(1)}, f32[8,64,128]{2,1,0:T(8,128)S(1)}, f32[8,64,128]{2,1,0:T(8,128)S(1)}, f32[8,128]{1,0:T(8,128)S(1)}, f32[4,32,1024]...) custom-call(s32[1]{0:T(128)} %bitcast.me_ref.refs_0_, s32[256]{0:T(256)S(1)} %copy-done.15, ...), custom_call_target="tpu_custom_call" | custom-call | flops 10000000 | bytes 100000 | tf_op jit(solution)/shard_map/turn/pallas_call | solution.py:60
  124.9 4.2 %all-to-all-done.3 = bf16[32,16,128]{2,1,0:T(8,128)(2,1)S(1)} async-done(((bf16[32,16,128]{2,1,0:T(8,128)(2,1)}), bf16[32,16,128]{2,1,0:T(8,128)(2,1)S(1)}, u32[]{:S(2)}, u32[]{:S(2)}) %all-to-all-start.3) | async-done | bytes 131104 | tf_op jit(solution)/shard_map/all_to_all | solution.py:773
  129.2 7.7 %step.1 = (f32[8,64,64]{2,1,0:T(8,128)}, bf16[8,64,64]{2,1,0:T(8,128)(2,1)}, f32[8,64,64]{2,1,0:T(8,128)}, f32[8,64,64]{2,1,0:T(8,128)}, f32[8,64,64]{2,1,0:T(8,...) custom-call(bf16[512,128]{1,0:T(8,128)(2,1)S(1)} %bitcast.58, ...), custom_call_target="tpu_custom_call" | custom-call | tf_op jit(solution)/shard_map/step/pallas_call | solution.py:60
  (76 shorter events, 8.5 us)
Async XLA Ops:
  2.4 15.5 %copy-start.16 = (s32[1024]{0:T(1024)S(1)}, s32[1024]{0:T(1024)}, u32[]{:S(2)}) copy-start(s32[1024]{0:T(1024)} %param.25) | copy-start | bytes 12292
  2.5 9.7 %collective-permute-start.2 = (bf16[1,336,128]{2,1,0:T(8,128)(2,1)S(1)}, bf16[1,336,128]{2,1,0:T(8,128)(2,1)S(1)}, u32[]{:S(2)}, u32[]{:S(2)}) collective-permute-start(bf16[1,336,128]{2,1,0:T(8,128)(2,1)S(1)} %bitcast.60), channel_id=1, source_target_pairs={{0,6},{1,7},{2,4},{3,5},{4,2},{5,3},{6,0},{7,1},{8,14},{9,15},{10,... | collective-permute-start | bytes 258056 | tf_op jit(solution)/shard_map/ppermute | solution.py:116
  7.6 7.2 %collective-permute-start.1 = (bf16[1,336,128]{2,1,0:T(8,128)(2,1)S(1)}, bf16[1,336,128]{2,1,0:T(8,128)(2,1)S(1)}, u32[]{:S(2)}, u32[]{:S(2)}) collective-permute-start(bf16[1,336,128]{2,1,0:T(8,128)(2,1)S(1)} %bitcast.61), channel_id=1, source_target_pairs={{0,4},{1,5},{2,6},{3,7},{4,0},{5,1},{6,2},{7,3},{8,12},{9,13},{10,... | collective-permute-start | bytes 258056 | tf_op jit(solution)/shard_map/ppermute | solution.py:116
  7.6 7.2 %collective-permute-start = (bf16[1,336,128]{2,1,0:T(8,128)(2,1)S(1)}, bf16[1,336,128]{2,1,0:T(8,128)(2,1)S(1)}, u32[]{:S(2)}, u32[]{:S(2)}) collective-permute-start(bf16[1,336,128]{2,1,0:T(8,128)(2,1)S(1)} %bitcast.62), channel_id=1, source_target_pairs={{0,2},{1,3},{2,0},{3,1},{4,6},{5,7},{6,4},{7,5},{8,10},{9,11},{10,... | collective-permute-start | bytes 258056 | tf_op jit(solution)/shard_map/ppermute | solution.py:116
  12.2 23.3 %copy-start.15 = (s32[256]{0:T(256)S(1)}, s32[256]{0:T(256)}, u32[]{:S(2)}) copy-start(s32[256]{0:T(256)} %owners_ref.5) | copy-start | bytes 3076
  14.8 9.2 %collective-permute-start.4 = (bf16[4,336,128]{2,1,0:T(8,128)(2,1)S(1)}, bf16[4,336,128]{2,1,0:T(8,128)(2,1)S(1)}, u32[]{:S(2)}, u32[]{:S(2)}) collective-permute-start(bf16[4,336,128]{2,1,0:T(8,128)(2,1)S(1)} %pad_maximum_fusion.refs_2_), channel_id=1, source_target_pairs={{0,1},{1,0},{2,3},{3,2},{4,5},{5,4},{6,7},{7,6},{8,9},{9,8},{10,11... | collective-permute-start | bytes 1032200 | tf_op jit(solution)/shard_map/ppermute | solution.py:116
  16.4 9.0 %collective-permute-start.3 = (bf16[4,336,128]{2,1,0:T(8,128)(2,1)S(1)}, bf16[4,336,128]{2,1,0:T(8,128)(2,1)S(1)}, u32[]{:S(2)}, u32[]{:S(2)}) collective-permute-start(bf16[4,336,128]{2,1,0:T(8,128)(2,1)S(1)} %pad_maximum_fusion.refs_2_), channel_id=1, source_target_pairs={{0,16},{8,24},{16,0},{24,8},{1,17},{9,25},{17,1},{25,9},{2,18},{10... | collective-permute-start | bytes 1032200 | tf_op jit(solution)/shard_map/ppermute | solution.py:114
  20.9 13.2 %collective-permute-start.7 = (bf16[4,336,128]{2,1,0:T(8,128)(2,1)S(1)}, bf16[4,336,128]{2,1,0:T(8,128)(2,1)S(1)}, u32[]{:S(2)}, u32[]{:S(2)}) collective-permute-start(bf16[4,336,128]{2,1,0:T(8,128)(2,1)S(1)} %pad_maximum_fusion.refs_2_), channel_id=1, source_target_pairs={{0,8},{8,0},{16,24},{24,16},{1,9},{9,1},{17,25},{25,17},{2,10},{10... | collective-permute-start | bytes 1032200 | tf_op jit(solution)/shard_map/ppermute | solution.py:114
  25.6 9.8 %collective-permute-start.9 = (bf16[4,336,128]{2,1,0:T(8,128)(2,1)S(1)}, bf16[4,336,128]{2,1,0:T(8,128)(2,1)S(1)}, u32[]{:S(2)}, u32[]{:S(2)}) collective-permute-start(bf16[4,336,128]{2,1,0:T(8,128)(2,1)S(1)} %collective-permute-done.4.refs_4_), channel_id=1, source_target_pairs={{0,8},{8,0},{16,24},{24,16},{1,9},{9,1},{17,25},{25,17},{2,10},{10... | collective-permute-start | bytes 1032200 | tf_op jit(solution)/shard_map/ppermute | solution.py:114
  25.7 7.0 %collective-permute-start.6 = (bf16[4,176,128]{2,1,0:T(8,128)(2,1)S(1)}, bf16[4,176,128]{2,1,0:T(8,128)(2,1)S(1)}, u32[]{:S(2)}, u32[]{:S(2)}) collective-permute-start(bf16[4,176,128]{2,1,0:T(8,128)(2,1)S(1)} %slice_add_fusion), channel_id=1, source_target_pairs={{0,16},{8,24},{16,0},{24,8},{1,17},{9,25},{17,1},{25,9},{2,18},{10... | collective-permute-start | bytes 540680 | tf_op jit(solution)/shard_map/ppermute | solution.py:114
  27.3 8.1 %collective-permute-start.8 = (bf16[4,336,128]{2,1,0:T(8,128)(2,1)S(1)}, bf16[4,336,128]{2,1,0:T(8,128)(2,1)S(1)}, u32[]{:S(2)}, u32[]{:S(2)}) collective-permute-start(bf16[4,336,128]{2,1,0:T(8,128)(2,1)S(1)} %collective-permute-done.3.refs_3_), channel_id=1, source_target_pairs={{0,8},{8,0},{16,24},{24,16},{1,9},{9,1},{17,25},{25,17},{2,10},{10... | collective-permute-start | bytes 1032200 | tf_op jit(solution)/shard_map/ppermute | solution.py:114
  27.5 26.7 %copy-start.2 = (f32[1024,32]{0,1:T(8,128)S(1)}, f32[1024,32]{0,1:T(8,128)}, u32[]{:S(2)}) copy-start(f32[1024,32]{0,1:T(8,128)} %param.36) | copy-start | bytes 393220
  27.5 26.7 %copy-start.14 = (f32[2,1024]{1,0:T(2,128)S(1)}, f32[2,1024]{1,0:T(2,128)}, u32[]{:S(2)}) copy-start(f32[2,1024]{1,0:T(2,128)} %wn_hbm.1) | copy-start | bytes 24580
  27.5 6.5 %collective-permute-start.5 = (bf16[4,160,128]{2,1,0:T(8,128)(2,1)S(1)}, bf16[4,160,128]{2,1,0:T(8,128)(2,1)S(1)}, u32[]{:S(2)}, u32[]{:S(2)}) collective-permute-start(bf16[4,160,128]{2,1,0:T(8,128)(2,1)S(1)} %slice_add_fusion.1), channel_id=1, source_target_pairs={{0,1},{1,0},{2,3},{3,2},{4,5},{5,4},{6,7},{7,6},{8,9},{9,8},{10,11... | collective-permute-start | bytes 491528 | tf_op jit(solution)/shard_map/ppermute | solution.py:116
  32.7 2.7 %collective-permute-start.11 = (bf16[4,176,128]{2,1,0:T(8,128)(2,1)S(1)}, bf16[4,176,128]{2,1,0:T(8,128)(2,1)S(1)}, u32[]{:S(2)}, u32[]{:S(2)}) collective-permute-start(bf16[4,176,128]{2,1,0:T(8,128)(2,1)S(1)} %collective-permute-done.6.refs_6_), channel_id=1, source_target_pairs={{0,8},{8,0},{16,24},{24,16},{1,9},{9,1},{17,25},{25,17},{2,10},{10... | collective-permute-start | bytes 540680 | tf_op jit(solution)/shard_map/ppermute | solution.py:114
  34.0 1.4 %collective-permute-start.10 = (bf16[4,160,128]{2,1,0:T(8,128)(2,1)S(1)}, bf16[4,160,128]{2,1,0:T(8,128)(2,1)S(1)}, u32[]{:S(2)}, u32[]{:S(2)}) collective-permute-start(bf16[4,160,128]{2,1,0:T(8,128)(2,1)S(1)} %collective-permute-done.5.refs_5_), channel_id=1, source_target_pairs={{0,8},{8,0},{16,24},{24,16},{1,9},{9,1},{17,25},{25,17},{2,10},{10... | collective-permute-start | bytes 491528 | tf_op jit(solution)/shard_map/ppermute | solution.py:114
  54.2 15.3 %copy-start.13 = (f32[2,32,32]{2,1,0:T(8,128)S(1)}, f32[2,32,32]{2,1,0:T(8,128)}, u32[]{:S(2)}) copy-start(f32[2,32,32]{2,1,0:T(8,128)} %wt_hbm.1) | copy-start | bytes 24580
  54.2 32.1 %copy-start.1 = (bf16[1024,1024]{1,0:T(8,128)(2,1)S(1)}, bf16[1024,1024]{1,0:T(8,128)(2,1)}, u32[]{:S(2)}) copy-start(bf16[1024,1024]{1,0:T(8,128)(2,1)} %copy-done) | copy-start | bytes 6291460
  91.5 2.7 %collective-permute-start.12 = (bf16[4096,128]{1,0:T(8,128)(2,1)S(1)}, bf16[4096,128]{1,0:T(8,128)(2,1)S(1)}, u32[]{:S(2)}, u32[]{:S(2)}) collective-permute-start(bf16[4096,128]{1,0:T(8,128)(2,1)S(1)} %get-tuple-element.121), channel_id=1, source_target_pairs={{0,8},{8,0},{16,24},{24,16},{1,9},{9,1},{17,25},{25,17},{2,10},{10... | collective-permute-start | bytes 3145736 | tf_op jit(solution)/shard_map/ppermute | solution.py:114
  94.5 8.4 %collective-permute-start.15 = (bf16[2,4,128,128]{3,2,1,0:T(8,128)(2,1)S(1)}, bf16[2,4,128,128]{3,2,1,0:T(8,128)(2,1)S(1)}, u32[]{:S(2)}, u32[]{:S(2)}) collective-permute-start(bf16[2,4,128,128]{3,2,1,0:T(8,128)(2,1)S(1)} %slice_bitcast_fusion.3), channel_id=1, source_target_pairs={{0,1},{1,0},{2,3},{3,2},{4,5},{5,4},{6,7},{7,6},{8,9},{9,8},{10,11... | collective-permute-start | bytes 786440 | tf_op jit(solution)/shard_map/ppermute | solution.py:116
  95.6 8.1 %collective-permute-start.13 = (bf16[2,4,128,128]{3,2,1,0:T(8,128)(2,1)S(1)}, bf16[2,4,128,128]{3,2,1,0:T(8,128)(2,1)S(1)}, u32[]{:S(2)}, u32[]{:S(2)}) collective-permute-start(bf16[2,4,128,128]{3,2,1,0:T(8,128)(2,1)S(1)} %slice_bitcast_fusion.5), channel_id=1, source_target_pairs={{0,16},{8,24},{16,0},{24,8},{1,17},{9,25},{17,1},{25,9},{2,18},{10... | collective-permute-start | bytes 786440 | tf_op jit(solution)/shard_map/ppermute | solution.py:114
  103.8 5.0 %collective-permute-start.14 = (bf16[4,128,128]{2,1,0:T(8,128)(2,1)S(1)}, bf16[4,128,128]{2,1,0:T(8,128)(2,1)S(1)}, u32[]{:S(2)}, u32[]{:S(2)}) collective-permute-start(bf16[4,128,128]{2,1,0:T(8,128)(2,1)S(1)} %fusion.4), channel_id=1, source_target_pairs={{0,1},{1,0},{2,3},{3,2},{4,5},{5,4},{6,7},{7,6},{8,9},{9,8},{10,11... | collective-permute-start | bytes 393224 | tf_op jit(solution)/shard_map/ppermute | solution.py:116
  104.9 24.2 %copy-start.4 = (f32[8,64,128]{2,1,0:T(8,128)S(1)}, f32[8,64,128]{2,1,0:T(8,128)}, u32[]{:S(2)}) copy-start(f32[8,64,128]{2,1,0:T(8,128)} %copy-done.3) | copy-start | bytes 786436
  104.9 24.2 %copy-start.6 = (f32[8,64,128]{2,1,0:T(8,128)S(1)}, f32[8,64,128]{2,1,0:T(8,128)}, u32[]{:S(2)}) copy-start(f32[8,64,128]{2,1,0:T(8,128)} %copy-done.5) | copy-start | bytes 786436
  104.9 24.2 %copy-start.8 = (f32[8,64,128]{2,1,0:T(8,128)S(1)}, f32[8,64,128]{2,1,0:T(8,128)}, u32[]{:S(2)}) copy-start(f32[8,64,128]{2,1,0:T(8,128)} %copy-done.7) | copy-start | bytes 786436
  105.0 24.2 %copy-start.10 = (f32[8,64,64]{2,1,0:T(8,128)S(1)}, f32[8,64,64]{2,1,0:T(8,128)}, u32[]{:S(2)}) copy-start(f32[8,64,64]{2,1,0:T(8,128)} %copy-done.9) | copy-start | bytes 393220
  105.0 24.2 %copy-start.12 = (f32[8,64,128]{2,1,0:T(8,128)S(1)}, f32[8,64,128]{2,1,0:T(8,128)}, u32[]{:S(2)}) copy-start(f32[8,64,128]{2,1,0:T(8,128)} %copy-done.11) | copy-start | bytes 786436
  105.0 5.0 %collective-permute-start.16 = (bf16[4,128,128]{2,1,0:T(8,128)(2,1)S(1)}, bf16[4,128,128]{2,1,0:T(8,128)(2,1)S(1)}, u32[]{:S(2)}, u32[]{:S(2)}) collective-permute-start(bf16[4,128,128]{2,1,0:T(8,128)(2,1)S(1)} %fusion.5), channel_id=1, source_target_pairs={{0,16},{8,24},{16,0},{24,8},{1,17},{9,25},{17,1},{25,9},{2,18},{10... | collective-permute-start | bytes 393224 | tf_op jit(solution)/shard_map/ppermute | solution.py:114
  110.1 6.1 %collective-permute-start.19 = (bf16[256,128]{1,0:T(8,128)(2,1)S(1)}, bf16[256,128]{1,0:T(8,128)(2,1)S(1)}, u32[]{:S(2)}, u32[]{:S(2)}) collective-permute-start(bf16[256,128]{1,0:T(8,128)(2,1)S(1)} %get-tuple-element.162), channel_id=1, source_target_pairs={{0,6},{1,7},{2,4},{3,5},{4,2},{5,3},{6,0},{7,1},{8,14},{9,15},{10,... | collective-permute-start | bytes 196616 | tf_op jit(solution)/shard_map/ppermute | solution.py:116
  111.2 5.0 %collective-permute-start.17 = (bf16[256,128]{1,0:T(8,128)(2,1)S(1)}, bf16[256,128]{1,0:T(8,128)(2,1)S(1)}, u32[]{:S(2)}, u32[]{:S(2)}) collective-permute-start(bf16[256,128]{1,0:T(8,128)(2,1)S(1)} %get-tuple-element.163), channel_id=1, source_target_pairs={{0,2},{1,3},{2,0},{3,1},{4,6},{5,7},{6,4},{7,5},{8,10},{9,11},{10,... | collective-permute-start | bytes 196616 | tf_op jit(solution)/shard_map/ppermute | solution.py:116
  111.2 5.7 %collective-permute-start.18 = (bf16[256,128]{1,0:T(8,128)(2,1)S(1)}, bf16[256,128]{1,0:T(8,128)(2,1)S(1)}, u32[]{:S(2)}, u32[]{:S(2)}) collective-permute-start(bf16[256,128]{1,0:T(8,128)(2,1)S(1)} %get-tuple-element.164), channel_id=1, source_target_pairs={{0,4},{1,5},{2,6},{3,7},{4,0},{5,1},{6,2},{7,3},{8,12},{9,13},{10,... | collective-permute-start | bytes 196616 | tf_op jit(solution)/shard_map/ppermute | solution.py:116
  117.8 11.4 %all-to-all-start.3 = ((bf16[32,16,128]{2,1,0:T(8,128)(2,1)}), bf16[32,16,128]{2,1,0:T(8,128)(2,1)S(1)}, u32[]{:S(2)}, u32[]{:S(2)}) async-start(bf16[32,16,128]{2,1,0:T(8,128)(2,1)} %bitcast.24), calls=%async_computation.3 | async-start | bytes 262144 | tf_op jit(solution)/shard_map/all_to_all | solution.py:773
  (6 other events, 74.6 us)

commit v3 on v2

--- a/solution.py
+++ b/solution.py
@@ -48,7 +48,7 @@
     return pltpu.with_memory_space_constraint(a, pltpu.HBM)
 
 
-def call(kernel, outs, args, smem=0, hbm=0, smem_outs=0, scratch=(), limit=16, name=None, cost=None):
+def call(kernel, outs, args, smem=0, hbm=0, smem_outs=0, aliases=None, scratch=(), limit=16, name=None, cost=None):
     args = list(args)
     specs = [spec(pltpu.SMEM)] * smem + [spec()] * (len(args) - smem - hbm) + [spec(pltpu.HBM)] * hbm
     if hbm:
@@ -65,6 +65,7 @@
         scratch_shapes=list(scratch),
         compiler_params=pltpu.CompilerParams(vmem_limit_bytes=limit * MIB),
         cost_estimate=estimate,
+        input_output_aliases=aliases or {},
         name=name,
     )(*args)
 
@@ -203,33 +204,48 @@
     )
 
 
-def pre_kernel(*refs, holds, rest, local, masked, n, pieces):
-    me_ref, owners_ref = refs[:2]
-    piece_refs = refs[2 : 2 + pieces]
-    x_ref, live_ref = refs[2 + pieces : 4 + pieces]
-    pre_ref, stats_ref, count_ref, mask_ref, w_ref, row_ref = refs[4 + pieces :]
-    width = x_ref.shape[1]
+def assemble(w_ref, me, owners_ref, piece_refs, holds, local):
+    width = w_ref.shape[1]
     bsize = LANES // 2
     half = bsize // 2
     side = width // bsize
-    tiles = width // LANES
-    me = me_ref[0]
-    chunks = mask_ref.shape[1] // LANES if masked else 0
-    for piece, (base, row0) in zip(piece_refs, holds):
-        held = piece.shape[1]
-        for k, m in enumerate(rest):
-            d = me ^ (m | base)
+    for piece, (masks, row0) in zip(piece_refs, holds):
+        for k, m in enumerate(masks):
             for b in range(local):
                 at = b * half - row0
-                if at < 0 or at + half > held:
+                if at < 0 or at + half > piece.shape[1]:
                     continue
-                r, c, odd = place(owners_ref[d * local + b], side)
+                r, c, odd = place(owners_ref[(me ^ m) * local + b], side)
                 tile = piece[k, at : at + half, :]
                 rows = pl.multiple_of(r * bsize, bsize)
                 low = pl.multiple_of(r * bsize + half, half)
                 cols = pl.ds(pl.multiple_of(c * LANES, LANES), LANES)
                 w_ref[odd, pl.ds(rows, half), cols] = tile
                 w_ref[odd, pl.ds(low, half), cols] = swap_halves(tile)
+
+
+def assemble_kernel(me_ref, owners_ref, *refs, holds, local):
+    assemble(refs[-1], me_ref[0], owners_ref, refs[:-1], holds, local)
+
+
+def pre_kernel(*refs, holds, done, local, masked, core):
+    me_ref, owners_ref = refs[:2]
+    pieces = len(holds)
+    piece_refs = refs[3 : 3 + pieces]
+    x_ref, live_ref = refs[3 + pieces : 5 + pieces]
+    pre_ref, keep_ref, send_ref, count_ref, mask_ref, w_ref, row_ref = refs[5 + pieces :]
+    width = x_ref.shape[1]
+    bsize = LANES // 2
+    half = bsize // 2
+    tiles = width // LANES
+    me = me_ref[0]
+    chunks = mask_ref.shape[1] // LANES if masked else 0
+    rest = [i for i in range(pieces) if i not in done]
+    assemble(w_ref, me, owners_ref, [piece_refs[i] for i in rest], [holds[i] for i in rest], local)
+    for piece, (masks, row0) in zip(piece_refs, holds):
+        held = piece.shape[1]
+        for k, m in enumerate(masks):
+            d = me ^ m
             for c in range(chunks):
                 at = local * half + c * PAIR - row0
                 if at < 0 or at + PAIR > held:
@@ -256,31 +272,66 @@
             row_ref[tiles + t : tiles + t + 1, :] = jnp.sum(
                 apart * apart * live, axis=0, keepdims=True
             )
+    half = tiles // 2
+    parts = [
+        jnp.concatenate([row_ref[h * half : (h + 1) * half, :], row_ref[tiles + h * half : tiles + (h + 1) * half, :]])
+        for h in range(2)
+    ]
+    odd = (me // core) % 2
+    keep_ref[...] = jnp.where(odd == 1, parts[1], parts[0])
+    send_ref[...] = jnp.where(odd == 1, parts[0], parts[1])
+
+
+def combine(pairs):
+    used = sum(c for c, _, _ in pairs)
+    total = sum(t for _, t, _ in pairs)
+    mean = total / jnp.maximum(used, 1.0)
+    square = 0.0
+    for c, t, q in pairs:
+        apart = t / jnp.maximum(c, 1.0) - mean
+        square = square + (q + c * apart * apart)
+    return used, total, square
+
+
+def merge_kernel(me_ref, count_ref, keep_ref, got_ref, out_ref, *, core):
+    half = keep_ref.shape[0] // 2
+    n = count_ref.shape[0]
+    counts = [
+        jnp.sum(count_ref[pl.ds(d, 1), :], keepdims=True) for d in (me_ref[0], me_ref[0] ^ core)
+    ]
+    pairs = [(c, ref[:half, :], ref[half:, :]) for c, ref in zip(counts, (keep_ref, got_ref))]
+    _, total, square = combine(pairs)
+    packed = jnp.concatenate([total, square])
     for d in range(n):
-        stats_ref[d * 2 * tiles : (d + 1) * 2 * tiles, :] = row_ref[...]
+        out_ref[2 * half * d : 2 * half * (d + 1), :] = packed
 
 
 def act_kernel(
     stats_ref, count_ref, norm_ref, pre_ref, live_ref, pick_ref, w_out_ref,
     slope_ref, act_ref, one_ref, two_ref, coef_ref, bags_ref, pay_ref,
     low_ref, ones_ref, twos_ref,
+    *, core,
 ):
     n = count_ref.shape[0]
     rows, width = pre_ref.shape
     tiles = width // LANES
     counts = jnp.sum(count_ref[...], axis=1, keepdims=True)
-    used = jnp.sum(counts)
-    total = stats_ref[0:tiles, :]
-    for d in range(1, n):
-        total = total + stats_ref[2 * d * tiles : (2 * d + 1) * tiles, :]
-    mean = total / used
-    square = jnp.zeros_like(mean)
-    for d in range(n):
-        c = counts[d : d + 1, :]
-        apart = stats_ref[2 * d * tiles : (2 * d + 1) * tiles, :] / jnp.maximum(c, 1.0) - mean
-        square = square + (
-            stats_ref[(2 * d + 1) * tiles : (2 * d + 2) * tiles, :] + c * apart * apart
-        )
+    half = tiles // 2
+    used, total, square = [], [], []
+    for h in range(2):
+        pairs = [
+            (
+                counts[d : d + 1, :] + counts[d ^ core : (d ^ core) + 1, :],
+                stats_ref[d * tiles : d * tiles + half, :],
+                stats_ref[d * tiles + half : (d + 1) * tiles, :],
+            )
+            for d in range(n)
+            if (d // core) % 2 == h
+        ]
+        for held, v in zip((used, total, square), combine(pairs)):
+            held.append(v)
+    used = jnp.max(used[0])
+    mean, square = jnp.concatenate(total) / used, jnp.concatenate(square)
     rstd = lax.rsqrt(square / used + 1e-05)
     for j in range(tiles):
         coef_ref[0:1, j * LANES : (j + 1) * LANES] = mean[j : j + 1, :]
@@ -311,8 +362,7 @@
             e = jnp.exp(capped)
             top = e * (e + 2.0)
             below = top + 2.0
-            guess = pl.reciprocal(below, approx=True)
-            inv = guess * (2.0 - below * guess)
+            inv = 1.0 / below
             gate = top * inv
             low_ref[at, :] = (y * gate).astype(BF)
             part = e * inv
@@ -585,35 +635,41 @@
     return weight - RATE * (step + DECAY * weight), first, second
 
 
-def panel_factor(panel, at):
-    group = panel.shape[1]
-    index = lax.broadcasted_iota(jnp.int32, (1, group, 1), 1)
-    cols = [jnp.broadcast_to(panel[:, :, at + i : at + i + 1], panel.shape) for i in range(group)]
-    for i in range(group):
-        inv = lax.rsqrt(cols[i][:, i : i + 1, :])
-        row = panel[:, i : i + 1, :] * inv
-        f = cols[i] * inv
-        panel = jnp.where(index > i, panel - f * row, jnp.where(index == i, row, panel))
-        for j in range(i + 1, group):
-            cols[j] = cols[j] - f * f[:, j : j + 1, :]
-    return panel
-
-
-def eliminate(mat_ref):
-    count, size = mat_ref.shape[0], mat_ref.shape[1]
+def eliminate(gram_ref, power_ref):
+    count, size, lanes = gram_ref.shape
     group = 8
+    lane = lax.broadcasted_iota(jnp.int32, (count * group, lanes), 1)
+    left = lax.broadcasted_iota(jnp.int32, (1, lanes), 1) < size
     for at in range(0, size, group):
         rest = at + group
-        panel = panel_factor(mat_ref[:, at:rest, :], at)
-        mat_ref[:, at:rest, :] = panel
+        gram, power = gram_ref[:, at:rest, :], power_ref[:, at:rest, :]
+        flat = gram.reshape(count * group, lanes)
+        cols = [
+            jnp.take_along_axis(flat, (lane // size) * size + at + i, axis=1).reshape(gram.shape)
+            for i in range(group)
+        ]
+        for i in range(group):
+            inv = lax.rsqrt(cols[i][:, i : i + 1, :])
+            row, power_row = gram[:, i : i + 1, :] * inv, power[:, i : i + 1, :] * inv
+            gram_ref[:, at + i : at + i + 1, :] = row
+            power_ref[:, at + i : at + i + 1, :] = power_row
+            f = cols[i] * inv
+            gram, power = gram - f * row, power - f * power_row
+            for j in range(i + 1, group):
+                cols[j] = cols[j] - f * f[:, j : j + 1, :]
         if rest == size:
             return
-        a, b, c = (v.astype(F32) for v in three(panel))
-        lhs = jnp.concatenate([a, a, b, b, a, c], axis=1)
-        rhs = jnp.concatenate([a, b, a, b, c, a], axis=1).astype(BF)
+        a, b, c = (v.astype(F32) for v in three(gram_ref[:, at:rest, :]))
+        d, e, f = (v.astype(F32) for v in three(power_ref[:, at:rest, :]))
+        lhs = jnp.concatenate([a, a, b, b, a, c], axis=1).astype(BF)
+        rhs = jnp.concatenate([a, b, a, b, c, a], axis=1)
+        rhs = jnp.concatenate([rhs, jnp.concatenate([d, e, d, e, f, d], axis=1)], axis=2).astype(BF)
+        turned = [lhs[m].T for m in range(count)]
         for m in range(count):
-            turned = lhs[m].T[rest:size, :].astype(BF)
-            mat_ref[m, rest:, :] = mat_ref[m, rest:, :] - dot(turned, rhs[m])
+            one = dot(turned[m][rest:size], rhs[m])
+            two = dot(turned[m][size + rest :], rhs[m])
+            gram_ref[m, rest:, :] = gram_ref[m, rest:, :] - jnp.where(left, one[:, :lanes], two[:, :lanes])
+            power_ref[m, rest:, :] = power_ref[m, rest:, :] - jnp.where(left, one[:, lanes:], two[:, lanes:])
 
 
 def pair(a, b):
@@ -692,10 +748,13 @@
     grad_ref, squares_ref, powers_ref, scale_ref,
     old_ref, towers_ref, norms_ref,
     moments_ref, stats_ref, bases_ref, weights_ref, turned_first_ref, powers_old_ref,
-    w_out, low_out, left_out, right_out, bl_out, br_out, first_out, second_out, ema_out,
-    wo_out, mo_out, vo_out, eo_out, wt_out, mt_out, vt_out, wn_out, mn_out, vn_out, gn_out,
-    mat_ref, wide_ref, dn_ref, flat_ref, *, n,
+    *refs, n,
 ):
+    (
+        w_out, low_out, left_out, right_out, bl_out, br_out, first_out, second_out, ema_out,
+        wo_out, mo_out, vo_out, eo_out, wt_out, mt_out, vt_out, wn_out, mn_out, vn_out, gn_out,
+        gram_ref, power_ref, wide_ref, dn_ref, flat_ref,
+    ) = refs
     local, bsize = bases_ref.shape[0], bases_ref.shape[1]
     embed, width = old_ref.shape[1:]
     tiles = width // LANES
@@ -725,11 +784,11 @@
     lefts, rights = [], []
     for b in each:
         powers = BETA_TWO * powers_old_ref[b] + twice * powers_ref[b]
+        power_ref[b] = powers
         lefts.append(powers[:, :bsize])
         rights.append(powers[:, bsize:])
     for b in each:
-        mat_ref[2 * b] = pair(hdot(lefts[b], lefts[b], 1, 1), lefts[b])
-        mat_ref[2 * b + 1] = pair(hdot(rights[b], rights[b], 1, 1), rights[b])
+        gram_ref[b] = pair(hdot(lefts[b], lefts[b], 1, 1), hdot(rights[b], rights[b], 1, 1))
     ratios = []
     for b in each:
         stats = BETA_TWO * stats_ref[b] + twice * squares_ref[b]
@@ -763,10 +822,10 @@
     wn_out[...], mn_out[...], vn_out[...] = adamw(
         dn_ref[...] * factor, norms_ref[0], norms_ref[1], norms_ref[2]
     )
-    eliminate(mat_ref)
-    for b in each:
-        bl_out[b] = mat_ref[2 * b, :, bsize:].T
-        br_out[b] = mat_ref[2 * b + 1, :, bsize:].T
+    eliminate(gram_ref, power_ref)
+    for b in each:
+        turned = power_ref[b].T
+        bl_out[b], br_out[b] = turned[:bsize], turned[bsize:]
 
 
 def exchange(payload):
@@ -839,31 +898,48 @@
         plan, payload, cut, zero, early, late
     )
     mask_shape = (total_rows, total_rows) if masked else (PAIR, LANES)
-    pre, stats, counts, mask = call(
+    holds = [([m | base for m in plan.rest], row) for _, base, row in pieces]
+    arrays = [a for a, _, _ in pieces]
+    done = [0, 1, 2, 5, 6, 7]
+    (planes,) = call(
+        functools.partial(assemble_kernel, holds=[holds[i] for i in done], local=local),
+        [((2, width, width), BF)],
+        [me, owners] + [arrays[i] for i in done],
+        smem=2,
+        limit=8,
+        name="assemble",
+        cost=10_000_000,
+    )
+    pre, kept, sent, counts, mask, _ = call(
         functools.partial(
-            pre_kernel,
-            holds=[(m, row) for _, m, row in pieces],
-            rest=plan.rest,
-            local=local,
-            masked=masked,
-            n=n,
-            pieces=len(pieces),
+            pre_kernel, holds=holds, done=done, local=local, masked=masked, core=plan.core
         ),
         [
             ((slots, width), F32),
-            ((n * 2 * tiles, LANES), F32),
+            ((tiles, LANES), F32),
+            ((tiles, LANES), F32),
             ((n, LANES), F32),
             (mask_shape, BF),
+            ((2, width, width), BF),
         ],
-        [me, owners] + [a for a, _, _ in pieces] + [x, live],
+        [me, owners, planes] + arrays + [x, live],
         smem=2,
-        scratch=[pltpu.VMEM((2, width, width), BF), pltpu.VMEM((2 * tiles, LANES), F32)],
+        scratch=[pltpu.VMEM((2 * tiles, LANES), F32)],
+        aliases={2: 5},
         limit=16,
         name="pre",
     )
+    (stats,) = call(
+        functools.partial(merge_kernel, core=plan.core),
+        [((n * tiles, LANES), F32)],
+        [me, counts, kept, plan.swap(sent, plan.core)],
+        smem=1,
+        limit=4,
+        name="merge",
+    )
     stats = exchange(stats)
     slope, act, one, two, coef, bag_sums, pay = call(
-        act_kernel,
+        functools.partial(act_kernel, core=plan.core),
         [
             ((slots, width), F32),
             ((bags, width), F32),
@@ -976,7 +1052,8 @@
         ],
         smem_outs=1,
         scratch=[
-            pltpu.VMEM((2 * local, bsize, 2 * bsize), F32),
+            pltpu.VMEM(twin, F32),
+            pltpu.VMEM(twin, F32),
             pltpu.VMEM((embed, width), F32),
             pltpu.VMEM((2, width), F32),
             pltpu.VMEM((embed * tiles, LANES), F32),

time: 137 us -> 134 us (0.978)
  blocking collectives: 35.8 us -> 33 us
    all_to_all x3, blocking collectives: 35.8 us -> 33 us  [exchange(): return lax.all_to_all(payload, AXES, 0, 0, tiled=True)]
    pallas_call x10 -> x12, Pallas kernels: 39.2 us -> 38.3 us  [call(): pl.pallas_call(kernel, out_shape=[jax.ShapeDtypeStruct(s, t) for s, t in...]
    ppermute x10 -> x11, starting transfers between devices: 4.91 us -> 5.48 us  [swap(): return lax.ppermute(a, 'gx', [(i, i ^ mx) for i in range(self.gx)])]
    ppermute x10 -> x11, waiting for transfers between devices: 11.9 us -> 11.3 us  [swap(): return lax.ppermute(a, 'gx', [(i, i ^ mx) for i in range(self.gx)])]
  transfers between devices with their start and end apart: 21 -> 22, of which waited for: 14 -> 14; matrix products, arithmetic and copies ran while one was open for 0% -> 0% of each run, Pallas kernels for 6% -> 8%
where the time goes in v3:
time: 134 us; the launch traced here: 133 us
  Pallas kernels  38.3 us (29%)
  waiting for transfers between devices  34.7 us (26%)
  blocking collectives  33 us (25%)
  starting transfers between devices  23.9 us (18%)
  local copies, waits for them, and re-layouts  1.76 us (1%)
    pallas_call x12, Pallas kernels, call(): pl.pallas_call(kernel, out_shape=[jax.ShapeDtypeStruct(s, t) for s, t in...  38.3 us
    all_to_all x3, blocking collectives, exchange(): return lax.all_to_all(payload, AXES, 0, 0, tiled=True)  33 us
    ppermute x10, waiting for transfers between devices, swap(): return lax.ppermute(a, 'gy', [(i, i ^ my) for i in range(self.gy)])  19.1 us
    ppermute x10, starting transfers between devices, swap(): return lax.ppermute(a, 'gy', [(i, i ^ my) for i in range(self.gy)])  14.5 us
    ppermute x11, waiting for transfers between devices, swap(): return lax.ppermute(a, 'gx', [(i, i ^ mx) for i in range(self.gx)])  11.3 us
    ppermute x11, starting transfers between devices, swap(): return lax.ppermute(a, 'gx', [(i, i ^ mx) for i in range(self.gx)])  5.48 us
    all_to_all x1, waiting for transfers between devices, exchange(): return lax.all_to_all(payload, AXES, 0, 0, tiled=True)  4.22 us
    all_to_all x1, starting transfers between devices, exchange(): return lax.all_to_all(payload, AXES, 0, 0, tiled=True)  3.87 us
  transfers between devices with their start and end apart: 22, of which 14 were waited for; matrix products, arithmetic and copies ran while one was open for 0% of the time, Pallas kernels for 8%

profile of v3, /device:TPU:0, one launch (start us, length us, event | category | flops | bytes accessed | tf_op | source)
XLA Modules:
  0.0 133.4 jit_solution(12109061688178717201)
XLA Ops:
  0.7 1.8 %pack.1 = bf16[336,128]{1,0:T(8,128)(2,1)S(1)} custom-call(s32[1]{0:T(128)} %bitcast.me_ref.refs_0_, s32[256]{0:T(256)} %owners_ref.7, f32[8,64,64]{2,1,0:T(8,128)} %w_hbm.3, s32[16,512]{1,0:T(8,128)} %neg_hbm.1, s32[8,128]{1,0:T(8,128)} %bitcast.73), custom_call_target="tpu_custom_call" | custom-call | tf_op jit(solution)/shard_map/pack/pallas_call | solution.py:60
  2.5 5.1 %collective-permute-start.2 = (bf16[1,336,128]{2,1,0:T(8,128)(2,1)S(1)}, bf16[1,336,128]{2,1,0:T(8,128)(2,1)S(1)}, u32[]{:S(2)}, u32[]{:S(2)}) collective-permute-start(bf16[1,336,128]{2,1,0:T(8,128)(2,1)S(1)} %bitcast.61), channel_id=1, source_target_pairs={{0,6},{1,7},{2,4},{3,5},{4,2},{5,3},{6,0},{7,1},{8,14},{9,15},{10,... | collective-permute-start | bytes 258056 | tf_op jit(solution)/shard_map/ppermute | solution.py:117
  8.2 2.6 %hash.1 = (bf16[1024,1024]{1,0:T(8,128)(2,1)S(1)}, bf16[1024,1024]{1,0:T(8,128)(2,1)S(1)}) custom-call(s32[1024,1024]{1,0:T(8,128)} %codes_hbm.1, s32[8,1024]{1,0:T(8,128)} %offsets_hbm.1), custom_call_target="tpu_custom_call" | custom-call | flops 20000000 | bytes 200000 | tf_op jit(solution)/shard_map/hash/pallas_call | solution.py:60
  10.8 1.3 copy-done
  12.2 2.6 %collective-permute-done.1 = bf16[1,336,128]{2,1,0:T(8,128)(2,1)S(1)} collective-permute-done((bf16[1,336,128]{2,1,0:T(8,128)(2,1)S(1)}, bf16[1,336,128]{2,1,0:T(8,128)(2,1)S(1)}, u32[]{:S(2)}, u32[]{:S(2)}) %collective-permute-start.1) | collective-permute-done | bytes 86048 | tf_op jit(solution)/shard_map/ppermute | solution.py:117
  14.8 1.6 %collective-permute-start.4 = (bf16[4,336,128]{2,1,0:T(8,128)(2,1)S(1)}, bf16[4,336,128]{2,1,0:T(8,128)(2,1)S(1)}, u32[]{:S(2)}, u32[]{:S(2)}) collective-permute-start(bf16[4,336,128]{2,1,0:T(8,128)(2,1)S(1)} %pad_maximum_fusion.refs_0_.refs_3_), channel_id=1, source_target_pairs={{0,1},{1,0},{2,3},{3,2},{4,5},{5,4},{6,7},{7,6},{8,9},{9,8},{10,11... | collective-permute-start | bytes 1032200 | tf_op jit(solution)/shard_map/ppermute | solution.py:117
  16.4 1.5 %collective-permute-start.3 = (bf16[4,336,128]{2,1,0:T(8,128)(2,1)S(1)}, bf16[4,336,128]{2,1,0:T(8,128)(2,1)S(1)}, u32[]{:S(2)}, u32[]{:S(2)}) collective-permute-start(bf16[4,336,128]{2,1,0:T(8,128)(2,1)S(1)} %pad_maximum_fusion.refs_0_.refs_3_), channel_id=1, source_target_pairs={{0,16},{8,24},{16,0},{24,8},{1,17},{9,25},{17,1},{25,9},{2,18},{10... | collective-permute-start | bytes 1032200 | tf_op jit(solution)/shard_map/ppermute | solution.py:115
  17.9 2.8 %prepare.1 = (f32[8,64,128]{2,1,0:T(8,128)S(1)}, f32[8,64,128]{2,1,0:T(8,128)S(1)}, f32[8,64,128]{2,1,0:T(8,128)S(1)}, f32[8,64,128]{2,1,0:T(8,128)S(1)}, f32[8,...) custom-call(f32[8,64,64]{2,1,0:T(8,128)} %w_hbm.3, f32[8,64,64]{2,1,0:T(8,128)} %left_hbm.1, f32[8,64,64]{2,1,0:T(8,128)} %right_hbm.1, ...), custom_call_target="tpu_custom_call" | custom-call | flops 10000000 | bytes 100000 | tf_op jit(solution)/shard_map/prepare/pallas_call | solution.py:60
  20.9 3.2 %collective-permute-done.4.refs_2_.refs_5_ = bf16[4,336,128]{2,1,0:T(8,128)(2,1)S(1)} collective-permute-done((bf16[4,336,128]{2,1,0:T(8,128)(2,1)S(1)}, bf16[4,336,128]{2,1,0:T(8,128)(2,1)S(1)}, u32[]{:S(2)}, u32[]{:S(2)}) %collective-permute-start.4) | collective-permute-done | bytes 344096 | tf_op jit(solution)/shard_map/ppermute | solution.py:117
  24.1 1.3 %collective-permute-done.3.refs_1_.refs_4_ = bf16[4,336,128]{2,1,0:T(8,128)(2,1)S(1)} collective-permute-done((bf16[4,336,128]{2,1,0:T(8,128)(2,1)S(1)}, bf16[4,336,128]{2,1,0:T(8,128)(2,1)S(1)}, u32[]{:S(2)}, u32[]{:S(2)}) %collective-permute-start.3) | collective-permute-done | bytes 344096 | tf_op jit(solution)/shard_map/ppermute | solution.py:115
  25.7 1.6 %collective-permute-start.9 = (bf16[4,176,128]{2,1,0:T(8,128)(2,1)S(1)}, bf16[4,176,128]{2,1,0:T(8,128)(2,1)S(1)}, u32[]{:S(2)}, u32[]{:S(2)}) collective-permute-start(bf16[4,176,128]{2,1,0:T(8,128)(2,1)S(1)} %slice_add_fusion), channel_id=1, source_target_pairs={{0,16},{8,24},{16,0},{24,8},{1,17},{9,25},{17,1},{25,9},{2,18},{10... | collective-permute-start | bytes 540680 | tf_op jit(solution)/shard_map/ppermute | solution.py:115
  28.1 4.7 %collective-permute-done.9.refs_7_ = bf16[4,176,128]{2,1,0:T(8,128)(2,1)S(1)} collective-permute-done((bf16[4,176,128]{2,1,0:T(8,128)(2,1)S(1)}, bf16[4,176,128]{2,1,0:T(8,128)(2,1)S(1)}, u32[]{:S(2)}, u32[]{:S(2)}) %collective-permute-start.9) | collective-permute-done | bytes 180256 | tf_op jit(solution)/shard_map/ppermute | solution.py:115
  32.7 1.2 collective-permute-done.8.refs_6_
  34.0 1.7 %assemble.1.refs_2_ = bf16[2,1024,1024]{2,1,0:T(8,128)(2,1)S(1)} custom-call(s32[1]{0:T(128)} %bitcast.me_ref.refs_0_, s32[256]{0:T(256)S(1)} %copy-done.15, bf16[4,336,128]{2,1,0:T(8,128)(2,1)S(1)} %pad_maximum_fusion.refs_0_.refs_3_, bf16[4,336,128]{2,1,0:T(8,128)(2,1)S(1)} %collective-permute-done.3.refs_1_.refs_4_, ...), custom_call_target="tpu_custom_call" | custom-call | flops 10000000 | bytes 100000 | tf_op jit(solution)/shard_map/assemble/pallas_call | solution.py:60
  35.8 4.6 %pre.1 = (f32[1024,1024]{1,0:T(8,128)S(1)}, f32[8,128]{1,0:T(8,128)S(1)}, f32[8,128]{1,0:T(8,128)S(1)}, f32[32,128]{1,0:T(8,128)S(1)}, bf16[512,512]{1,0:T(8,128)(2,1)S(1)}, /*index=5*/bf16[2,1024,1024]{2,1,0:T(8,128)(2,1)S(1)}) custom-call(s32[1]{0:T(128)} %bitcast.me_ref.refs_0_, s32[256]{0:T(256)S(1)} %copy-done.15, ...), custom_call_target="tpu_custom_call", output_to_operand_aliasing={{5}: (2, {})} | custom-call | tf_op jit(solution)/shard_map/pre/pallas_call | solution.py:60
  42.0 10.1 %all_to_all.44 = f32[32,8,128]{2,1,0:T(8,128)S(1)} all-to-all(f32[32,8,128]{2,1,0:T(8,128)S(1)} %bitcast.60), channel_id=1, replica_groups=mesh['gx'=4,'gy'=8] {'gx','gy'}, dimensions={0} | all-to-all | bytes 262144 | tf_op jit(solution)/shard_map/all_to_all | solution.py:832
  52.1 4.9 %act.1 = (f32[1024,1024]{1,0:T(8,128)S(1)}, f32[32,1024]{1,0:T(8,128)S(1)}, f32[32,1024]{1,0:T(8,128)S(1)}, f32[32,1024]{1,0:T(8,128)S(1)}, f32[8,1024]{1,0:T(8,...) custom-call(f32[256,128]{1,0:T(8,128)S(1)} %bitcast.59, f32[32,128]{1,0:T(8,128)S(1)} %get-tuple-element.105.count_ref, ...), custom_call_target="tpu_custom_call" | custom-call | tf_op jit(solution)/shard_map/act/pallas_call | solution.py:60
  57.0 10.0 %all_to_all.45 = f32[32,8,128]{2,1,0:T(8,128)S(1)} all-to-all(f32[32,8,128]{2,1,0:T(8,128)S(1)} %bitcast.66), channel_id=1, replica_groups=mesh['gx'=4,'gy'=8] {'gx','gy'}, dimensions={0} | all-to-all | bytes 262144 | tf_op jit(solution)/shard_map/all_to_all | solution.py:832
  67.0 3.8 %loss.1 = (f32[32,1024]{1,0:T(8,128)S(1)}, bf16[1024,128]{1,0:T(8,128)(2,1)S(1)}, f32[2,32,32]{2,1,0:T(8,128)S(1)}, f32[1,1]{1,0:T(1,128)}, f32[1,1]{1,0:T(1,128)}) custom-call(s32[1]{0:T(128)} %bitcast.me_ref.refs_0_, f32[256,128]{1,0:T(8,128)S(1)} %bitcast.58, bf16[512,512]{1,0:T(8,128)(2,1)S(1)} %get-tuple-element.111.mask_ref, ...), custom_call_target="tpu_custom_call" | custom-call | tf_op jit(solution)/shard_map/loss/pallas_call | solution.py:60
  70.8 12.9 %all_to_all.46 = bf16[32,32,128]{2,1,0:T(8,128)(2,1)S(1)} all-to-all(bf16[32,32,128]{2,1,0:T(8,128)(2,1)S(1)} %bitcast.65), channel_id=1, replica_groups=mesh['gx'=4,'gy'=8] {'gx','gy'}, dimensions={0} | all-to-all | bytes 524288 | tf_op jit(solution)/shard_map/all_to_all | solution.py:832
  83.7 5.2 %grad.1 = (f32[4096,128]{1,0:T(8,128)S(1)}, bf16[4096,128]{1,0:T(8,128)(2,1)S(1)}, f32[8,128]{1,0:T(8,128)S(1)}, f32[16,128]{1,0:T(8,128)S(1)}) custom-call(s32[1]{0:T(128)} %bitcast.me_ref.refs_0_, s32[256]{0:T(256)S(1)} %copy-done.15, bf16[1024,128]{1,0:T(8,128)(2,1)S(1)} %bitcast.56, f32[8,1024]{1,0:T(8,128)S(1)} %get-tuple-element.118.coef_ref, ...), custom_call_target="tpu_custom_call" | custom-call | tf_op jit(solution)/shard_map/grad/pallas_call | solution.py:60
  89.0 2.6 %collective-permute-done.13 = bf16[4096,128]{1,0:T(8,128)(2,1)S(1)} collective-permute-done((bf16[4096,128]{1,0:T(8,128)(2,1)S(1)}, bf16[4096,128]{1,0:T(8,128)(2,1)S(1)}, u32[]{:S(2)}, u32[]{:S(2)}) %collective-permute-start.13) | collective-permute-done | bytes 1048608 | tf_op jit(solution)/shard_map/ppermute | solution.py:115
  93.6 6.8 %collective-permute-done.16 = bf16[2,4,128,128]{3,2,1,0:T(8,128)(2,1)S(1)} collective-permute-done((bf16[2,4,128,128]{3,2,1,0:T(8,128)(2,1)S(1)}, bf16[2,4,128,128]{3,2,1,0:T(8,128)(2,1)S(1)}, u32[]{:S(2)}, u32[]{:S(2)}) %collective-permute-start.16) | collective-permute-done | bytes 262176 | tf_op jit(solution)/shard_map/ppermute | solution.py:117
  103.3 3.0 %collective-permute-done.15 = bf16[4,128,128]{2,1,0:T(8,128)(2,1)S(1)} collective-permute-done((bf16[4,128,128]{2,1,0:T(8,128)(2,1)S(1)}, bf16[4,128,128]{2,1,0:T(8,128)(2,1)S(1)}, u32[]{:S(2)}, u32[]{:S(2)}) %collective-permute-start.15) | collective-permute-done | bytes 131104 | tf_op jit(solution)/shard_map/ppermute | solution.py:117
  106.3 1.1 collective-permute-done.17
  107.5 1.2 collective-permute-start.20
  108.7 3.3 %collective-permute-start.19 = (bf16[256,128]{1,0:T(8,128)(2,1)S(1)}, bf16[256,128]{1,0:T(8,128)(2,1)S(1)}, u32[]{:S(2)}, u32[]{:S(2)}) collective-permute-start(bf16[256,128]{1,0:T(8,128)(2,1)S(1)} %get-tuple-element.166), channel_id=1, source_target_pairs={{0,4},{1,5},{2,6},{3,7},{4,0},{5,1},{6,2},{7,3},{8,12},{9,13},{10,... | collective-permute-start | bytes 196616 | tf_op jit(solution)/shard_map/ppermute | solution.py:117
  112.0 1.7 %collective-permute-done.20.refs_5_ = bf16[256,128]{1,0:T(8,128)(2,1)S(1)} collective-permute-done((bf16[256,128]{1,0:T(8,128)(2,1)S(1)}, bf16[256,128]{1,0:T(8,128)(2,1)S(1)}, u32[]{:S(2)}, u32[]{:S(2)}) %collective-permute-start.20) | collective-permute-done | bytes 65568 | tf_op jit(solution)/shard_map/ppermute | solution.py:117
  115.2 3.9 %all-to-all-start.3 = ((bf16[32,16,128]{2,1,0:T(8,128)(2,1)}), bf16[32,16,128]{2,1,0:T(8,128)(2,1)S(1)}, u32[]{:S(2)}, u32[]{:S(2)}) async-start(bf16[32,16,128]{2,1,0:T(8,128)(2,1)} %bitcast.24), calls=%async_computation.3 | async-start | bytes 262144 | tf_op jit(solution)/shard_map/all_to_all | solution.py:832
  119.1 3.3 %turn.1 = (f32[8,64,128]{2,1,0:T(8,128)S(1)}, f32[8,64,128]{2,1,0:T(8,128)S(1)}, f32[8,64,128]{2,1,0:T(8,128)S(1)}, f32[8,128]{1,0:T(8,128)S(1)}, f32[4,32,1024]...) custom-call(s32[1]{0:T(128)} %bitcast.me_ref.refs_0_, s32[256]{0:T(256)S(1)} %copy-done.15, ...), custom_call_target="tpu_custom_call" | custom-call | flops 10000000 | bytes 100000 | tf_op jit(solution)/shard_map/turn/pallas_call | solution.py:60
  122.4 4.2 %all-to-all-done.3 = bf16[32,16,128]{2,1,0:T(8,128)(2,1)S(1)} async-done(((bf16[32,16,128]{2,1,0:T(8,128)(2,1)}), bf16[32,16,128]{2,1,0:T(8,128)(2,1)S(1)}, u32[]{:S(2)}, u32[]{:S(2)}) %all-to-all-start.3) | async-done | bytes 131104 | tf_op jit(solution)/shard_map/all_to_all | solution.py:832
  126.6 6.6 %step.1 = (f32[8,64,64]{2,1,0:T(8,128)}, bf16[8,64,64]{2,1,0:T(8,128)(2,1)}, f32[8,64,64]{2,1,0:T(8,128)}, f32[8,64,64]{2,1,0:T(8,128)}, f32[8,64,64]{2,1,0:T(8,...) custom-call(bf16[512,128]{1,0:T(8,128)(2,1)S(1)} %bitcast.57, ...), custom_call_target="tpu_custom_call" | custom-call | tf_op jit(solution)/shard_map/step/pallas_call | solution.py:60
  (80 shorter events, 10.0 us)
Async XLA Ops:
  2.4 15.5 %copy-start.16 = (s32[1024]{0:T(1024)S(1)}, s32[1024]{0:T(1024)}, u32[]{:S(2)}) copy-start(s32[1024]{0:T(1024)} %param.25) | copy-start | bytes 12292
  2.5 9.7 %collective-permute-start.2 = (bf16[1,336,128]{2,1,0:T(8,128)(2,1)S(1)}, bf16[1,336,128]{2,1,0:T(8,128)(2,1)S(1)}, u32[]{:S(2)}, u32[]{:S(2)}) collective-permute-start(bf16[1,336,128]{2,1,0:T(8,128)(2,1)S(1)} %bitcast.61), channel_id=1, source_target_pairs={{0,6},{1,7},{2,4},{3,5},{4,2},{5,3},{6,0},{7,1},{8,14},{9,15},{10,... | collective-permute-start | bytes 258056 | tf_op jit(solution)/shard_map/ppermute | solution.py:117
  7.6 7.2 %collective-permute-start.1 = (bf16[1,336,128]{2,1,0:T(8,128)(2,1)S(1)}, bf16[1,336,128]{2,1,0:T(8,128)(2,1)S(1)}, u32[]{:S(2)}, u32[]{:S(2)}) collective-permute-start(bf16[1,336,128]{2,1,0:T(8,128)(2,1)S(1)} %bitcast.62), channel_id=1, source_target_pairs={{0,4},{1,5},{2,6},{3,7},{4,0},{5,1},{6,2},{7,3},{8,12},{9,13},{10,... | collective-permute-start | bytes 258056 | tf_op jit(solution)/shard_map/ppermute | solution.py:117
  7.6 7.2 %collective-permute-start = (bf16[1,336,128]{2,1,0:T(8,128)(2,1)S(1)}, bf16[1,336,128]{2,1,0:T(8,128)(2,1)S(1)}, u32[]{:S(2)}, u32[]{:S(2)}) collective-permute-start(bf16[1,336,128]{2,1,0:T(8,128)(2,1)S(1)} %bitcast.63), channel_id=1, source_target_pairs={{0,2},{1,3},{2,0},{3,1},{4,6},{5,7},{6,4},{7,5},{8,10},{9,11},{10,... | collective-permute-start | bytes 258056 | tf_op jit(solution)/shard_map/ppermute | solution.py:117
  12.2 21.8 %copy-start.15 = (s32[256]{0:T(256)S(1)}, s32[256]{0:T(256)}, u32[]{:S(2)}) copy-start(s32[256]{0:T(256)} %owners_ref.7) | copy-start | bytes 3076
  14.8 9.2 %collective-permute-start.4 = (bf16[4,336,128]{2,1,0:T(8,128)(2,1)S(1)}, bf16[4,336,128]{2,1,0:T(8,128)(2,1)S(1)}, u32[]{:S(2)}, u32[]{:S(2)}) collective-permute-start(bf16[4,336,128]{2,1,0:T(8,128)(2,1)S(1)} %pad_maximum_fusion.refs_0_.refs_3_), channel_id=1, source_target_pairs={{0,1},{1,0},{2,3},{3,2},{4,5},{5,4},{6,7},{7,6},{8,9},{9,8},{10,11... | collective-permute-start | bytes 1032200 | tf_op jit(solution)/shard_map/ppermute | solution.py:117
  16.4 9.0 %collective-permute-start.3 = (bf16[4,336,128]{2,1,0:T(8,128)(2,1)S(1)}, bf16[4,336,128]{2,1,0:T(8,128)(2,1)S(1)}, u32[]{:S(2)}, u32[]{:S(2)}) collective-permute-start(bf16[4,336,128]{2,1,0:T(8,128)(2,1)S(1)} %pad_maximum_fusion.refs_0_.refs_3_), channel_id=1, source_target_pairs={{0,16},{8,24},{16,0},{24,8},{1,17},{9,25},{17,1},{25,9},{2,18},{10... | collective-permute-start | bytes 1032200 | tf_op jit(solution)/shard_map/ppermute | solution.py:115
  20.9 13.1 %collective-permute-start.5 = (bf16[4,336,128]{2,1,0:T(8,128)(2,1)S(1)}, bf16[4,336,128]{2,1,0:T(8,128)(2,1)S(1)}, u32[]{:S(2)}, u32[]{:S(2)}) collective-permute-start(bf16[4,336,128]{2,1,0:T(8,128)(2,1)S(1)} %pad_maximum_fusion.refs_0_.refs_3_), channel_id=1, source_target_pairs={{0,8},{8,0},{16,24},{24,16},{1,9},{9,1},{17,25},{25,17},{2,10},{10... | collective-permute-start | bytes 1032200 | tf_op jit(solution)/shard_map/ppermute | solution.py:115
  25.6 8.4 %collective-permute-start.7 = (bf16[4,336,128]{2,1,0:T(8,128)(2,1)S(1)}, bf16[4,336,128]{2,1,0:T(8,128)(2,1)S(1)}, u32[]{:S(2)}, u32[]{:S(2)}) collective-permute-start(bf16[4,336,128]{2,1,0:T(8,128)(2,1)S(1)} %collective-permute-done.4.refs_2_.refs_5_), channel_id=1, source_target_pairs={{0,8},{8,0},{16,24},{24,16},{1,9},{9,1},{17,25},{25,17},{2,10},{10... | collective-permute-start | bytes 1032200 | tf_op jit(solution)/shard_map/ppermute | solution.py:115
  25.7 7.0 %collective-permute-start.9 = (bf16[4,176,128]{2,1,0:T(8,128)(2,1)S(1)}, bf16[4,176,128]{2,1,0:T(8,128)(2,1)S(1)}, u32[]{:S(2)}, u32[]{:S(2)}) collective-permute-start(bf16[4,176,128]{2,1,0:T(8,128)(2,1)S(1)} %slice_add_fusion), channel_id=1, source_target_pairs={{0,16},{8,24},{16,0},{24,8},{1,17},{9,25},{17,1},{25,9},{2,18},{10... | collective-permute-start | bytes 540680 | tf_op jit(solution)/shard_map/ppermute | solution.py:115
  27.3 6.7 %collective-permute-start.6 = (bf16[4,336,128]{2,1,0:T(8,128)(2,1)S(1)}, bf16[4,336,128]{2,1,0:T(8,128)(2,1)S(1)}, u32[]{:S(2)}, u32[]{:S(2)}) collective-permute-start(bf16[4,336,128]{2,1,0:T(8,128)(2,1)S(1)} %collective-permute-done.3.refs_1_.refs_4_), channel_id=1, source_target_pairs={{0,8},{8,0},{16,24},{24,16},{1,9},{9,1},{17,25},{25,17},{2,10},{10... | collective-permute-start | bytes 1032200 | tf_op jit(solution)/shard_map/ppermute | solution.py:115
  27.5 6.5 %collective-permute-start.8 = (bf16[4,160,128]{2,1,0:T(8,128)(2,1)S(1)}, bf16[4,160,128]{2,1,0:T(8,128)(2,1)S(1)}, u32[]{:S(2)}, u32[]{:S(2)}) collective-permute-start(bf16[4,160,128]{2,1,0:T(8,128)(2,1)S(1)} %slice_add_fusion.1), channel_id=1, source_target_pairs={{0,1},{1,0},{2,3},{3,2},{4,5},{5,4},{6,7},{7,6},{8,9},{9,8},{10,11... | collective-permute-start | bytes 491528 | tf_op jit(solution)/shard_map/ppermute | solution.py:117
  32.7 3.1 %collective-permute-start.11 = (bf16[4,176,128]{2,1,0:T(8,128)(2,1)S(1)}, bf16[4,176,128]{2,1,0:T(8,128)(2,1)S(1)}, u32[]{:S(2)}, u32[]{:S(2)}) collective-permute-start(bf16[4,176,128]{2,1,0:T(8,128)(2,1)S(1)} %collective-permute-done.9.refs_7_), channel_id=1, source_target_pairs={{0,8},{8,0},{16,24},{24,16},{1,9},{9,1},{17,25},{25,17},{2,10},{10... | collective-permute-start | bytes 540680 | tf_op jit(solution)/shard_map/ppermute | solution.py:115
  34.0 1.8 %collective-permute-start.10 = (bf16[4,160,128]{2,1,0:T(8,128)(2,1)S(1)}, bf16[4,160,128]{2,1,0:T(8,128)(2,1)S(1)}, u32[]{:S(2)}, u32[]{:S(2)}) collective-permute-start(bf16[4,160,128]{2,1,0:T(8,128)(2,1)S(1)} %collective-permute-done.8.refs_6_), channel_id=1, source_target_pairs={{0,8},{8,0},{16,24},{24,16},{1,9},{9,1},{17,25},{25,17},{2,10},{10... | collective-permute-start | bytes 491528 | tf_op jit(solution)/shard_map/ppermute | solution.py:115
  35.8 16.3 %copy-start.2 = (f32[1024,32]{0,1:T(8,128)S(1)}, f32[1024,32]{0,1:T(8,128)}, u32[]{:S(2)}) copy-start(f32[1024,32]{0,1:T(8,128)} %param.36) | copy-start | bytes 393220
  35.8 16.3 %copy-start.14 = (f32[2,1024]{1,0:T(2,128)S(1)}, f32[2,1024]{1,0:T(2,128)}, u32[]{:S(2)}) copy-start(f32[2,1024]{1,0:T(2,128)} %wn_hbm.1) | copy-start | bytes 24580
  40.4 1.4 %collective-permute-start.12 = (f32[8,128]{1,0:T(8,128)S(1)}, f32[8,128]{1,0:T(8,128)S(1)}, u32[]{:S(2)}, u32[]{:S(2)}) collective-permute-start(f32[8,128]{1,0:T(8,128)S(1)} %get-tuple-element.107), channel_id=1, source_target_pairs={{0,8},{8,0},{16,24},{24,16},{1,9},{9,1},{17,25},{25,17},{2,10},{10... | collective-permute-start | bytes 12296 | tf_op jit(solution)/shard_map/ppermute | solution.py:115
  52.1 31.6 %copy-start.1 = (bf16[1024,1024]{1,0:T(8,128)(2,1)S(1)}, bf16[1024,1024]{1,0:T(8,128)(2,1)}, u32[]{:S(2)}) copy-start(bf16[1024,1024]{1,0:T(8,128)(2,1)} %copy-done) | copy-start | bytes 6291460
  88.9 2.7 %collective-permute-start.13 = (bf16[4096,128]{1,0:T(8,128)(2,1)S(1)}, bf16[4096,128]{1,0:T(8,128)(2,1)S(1)}, u32[]{:S(2)}, u32[]{:S(2)}) collective-permute-start(bf16[4096,128]{1,0:T(8,128)(2,1)S(1)} %get-tuple-element.123), channel_id=1, source_target_pairs={{0,8},{8,0},{16,24},{24,16},{1,9},{9,1},{17,25},{25,17},{2,10},{10... | collective-permute-start | bytes 3145736 | tf_op jit(solution)/shard_map/ppermute | solution.py:115
  91.9 8.4 %collective-permute-start.16 = (bf16[2,4,128,128]{3,2,1,0:T(8,128)(2,1)S(1)}, bf16[2,4,128,128]{3,2,1,0:T(8,128)(2,1)S(1)}, u32[]{:S(2)}, u32[]{:S(2)}) collective-permute-start(bf16[2,4,128,128]{3,2,1,0:T(8,128)(2,1)S(1)} %slice_bitcast_fusion.3), channel_id=1, source_target_pairs={{0,1},{1,0},{2,3},{3,2},{4,5},{5,4},{6,7},{7,6},{8,9},{9,8},{10,11... | collective-permute-start | bytes 786440 | tf_op jit(solution)/shard_map/ppermute | solution.py:117
  93.0 8.1 %collective-permute-start.14 = (bf16[2,4,128,128]{3,2,1,0:T(8,128)(2,1)S(1)}, bf16[2,4,128,128]{3,2,1,0:T(8,128)(2,1)S(1)}, u32[]{:S(2)}, u32[]{:S(2)}) collective-permute-start(bf16[2,4,128,128]{3,2,1,0:T(8,128)(2,1)S(1)} %slice_bitcast_fusion.5), channel_id=1, source_target_pairs={{0,16},{8,24},{16,0},{24,8},{1,17},{9,25},{17,1},{25,9},{2,18},{10... | collective-permute-start | bytes 786440 | tf_op jit(solution)/shard_map/ppermute | solution.py:115
  101.3 5.0 %collective-permute-start.15 = (bf16[4,128,128]{2,1,0:T(8,128)(2,1)S(1)}, bf16[4,128,128]{2,1,0:T(8,128)(2,1)S(1)}, u32[]{:S(2)}, u32[]{:S(2)}) collective-permute-start(bf16[4,128,128]{2,1,0:T(8,128)(2,1)S(1)} %fusion.4), channel_id=1, source_target_pairs={{0,1},{1,0},{2,3},{3,2},{4,5},{5,4},{6,7},{7,6},{8,9},{9,8},{10,11... | collective-permute-start | bytes 393224 | tf_op jit(solution)/shard_map/ppermute | solution.py:117
  102.4 24.2 %copy-start.4 = (f32[8,64,128]{2,1,0:T(8,128)S(1)}, f32[8,64,128]{2,1,0:T(8,128)}, u32[]{:S(2)}) copy-start(f32[8,64,128]{2,1,0:T(8,128)} %copy-done.3) | copy-start | bytes 786436
  102.4 24.2 %copy-start.6 = (f32[8,64,128]{2,1,0:T(8,128)S(1)}, f32[8,64,128]{2,1,0:T(8,128)}, u32[]{:S(2)}) copy-start(f32[8,64,128]{2,1,0:T(8,128)} %copy-done.5) | copy-start | bytes 786436
  102.4 24.2 %copy-start.8 = (f32[8,64,128]{2,1,0:T(8,128)S(1)}, f32[8,64,128]{2,1,0:T(8,128)}, u32[]{:S(2)}) copy-start(f32[8,64,128]{2,1,0:T(8,128)} %copy-done.7) | copy-start | bytes 786436
  102.4 24.2 %copy-start.10 = (f32[8,64,64]{2,1,0:T(8,128)S(1)}, f32[8,64,64]{2,1,0:T(8,128)}, u32[]{:S(2)}) copy-start(f32[8,64,64]{2,1,0:T(8,128)} %copy-done.9) | copy-start | bytes 393220
  102.4 24.2 %copy-start.12 = (f32[8,64,128]{2,1,0:T(8,128)S(1)}, f32[8,64,128]{2,1,0:T(8,128)}, u32[]{:S(2)}) copy-start(f32[8,64,128]{2,1,0:T(8,128)} %copy-done.11) | copy-start | bytes 786436
  102.4 5.0 %collective-permute-start.17 = (bf16[4,128,128]{2,1,0:T(8,128)(2,1)S(1)}, bf16[4,128,128]{2,1,0:T(8,128)(2,1)S(1)}, u32[]{:S(2)}, u32[]{:S(2)}) collective-permute-start(bf16[4,128,128]{2,1,0:T(8,128)(2,1)S(1)} %fusion.5), channel_id=1, source_target_pairs={{0,16},{8,24},{16,0},{24,8},{1,17},{9,25},{17,1},{25,9},{2,18},{10... | collective-permute-start | bytes 393224 | tf_op jit(solution)/shard_map/ppermute | solution.py:115
  107.5 6.1 %collective-permute-start.20 = (bf16[256,128]{1,0:T(8,128)(2,1)S(1)}, bf16[256,128]{1,0:T(8,128)(2,1)S(1)}, u32[]{:S(2)}, u32[]{:S(2)}) collective-permute-start(bf16[256,128]{1,0:T(8,128)(2,1)S(1)} %get-tuple-element.164), channel_id=1, source_target_pairs={{0,6},{1,7},{2,4},{3,5},{4,2},{5,3},{6,0},{7,1},{8,14},{9,15},{10,... | collective-permute-start | bytes 196616 | tf_op jit(solution)/shard_map/ppermute | solution.py:117
  108.7 5.0 %collective-permute-start.18 = (bf16[256,128]{1,0:T(8,128)(2,1)S(1)}, bf16[256,128]{1,0:T(8,128)(2,1)S(1)}, u32[]{:S(2)}, u32[]{:S(2)}) collective-permute-start(bf16[256,128]{1,0:T(8,128)(2,1)S(1)} %get-tuple-element.165), channel_id=1, source_target_pairs={{0,2},{1,3},{2,0},{3,1},{4,6},{5,7},{6,4},{7,5},{8,10},{9,11},{10,... | collective-permute-start | bytes 196616 | tf_op jit(solution)/shard_map/ppermute | solution.py:117
  108.7 5.7 %collective-permute-start.19 = (bf16[256,128]{1,0:T(8,128)(2,1)S(1)}, bf16[256,128]{1,0:T(8,128)(2,1)S(1)}, u32[]{:S(2)}, u32[]{:S(2)}) collective-permute-start(bf16[256,128]{1,0:T(8,128)(2,1)S(1)} %get-tuple-element.166), channel_id=1, source_target_pairs={{0,4},{1,5},{2,6},{3,7},{4,0},{5,1},{6,2},{7,3},{8,12},{9,13},{10,... | collective-permute-start | bytes 196616 | tf_op jit(solution)/shard_map/ppermute | solution.py:117
  115.2 11.4 %all-to-all-start.3 = ((bf16[32,16,128]{2,1,0:T(8,128)(2,1)}), bf16[32,16,128]{2,1,0:T(8,128)(2,1)S(1)}, u32[]{:S(2)}, u32[]{:S(2)}) async-start(bf16[32,16,128]{2,1,0:T(8,128)(2,1)} %bitcast.24), calls=%async_computation.3 | async-start | bytes 262144 | tf_op jit(solution)/shard_map/all_to_all | solution.py:832
  (7 other events, 91.0 us)

commit v4 on v3

--- a/solution.py
+++ b/solution.py
@@ -140,7 +140,7 @@
     out_ref[at : at + PAIR, :] = jnp.broadcast_to(used, (PAIR, LANES)).astype(BF)
 
 
-def gather_pieces(plan, payload, cut, zero, early, late):
+def gather_pieces(plan, payload, cut, zero, early, late, place_blocks):
     stack = payload[None]
     if len(plan.rest) <= 4:
         stack = jnp.concatenate([stack] + [plan.swap(stack, m) for m in plan.rest[1:]], axis=0)
@@ -153,15 +153,16 @@
     by_x, by_y, late = lax.optimization_barrier((by_x, by_y, late))
     first = plan.swap(by_x[:, :cut] + zero, plan.y)
     second = plan.swap(by_y[:, cut:] + zero, plan.x)
-    mine = [
-        (stack, 0, 0),
-        (by_x, plan.x, 0),
-        (by_y, plan.y, 0),
-        (first, plan.x | plan.y, 0),
-        (second, plan.x | plan.y, cut),
-    ]
-    other = [(plan.swap(a, plan.core), m | plan.core, row) for a, m, row in mine]
-    return mine + other, early, late
+    ready = [(stack, 0, 0), (by_x, plan.x, 0), (by_y, plan.y, 0)]
+    ready += swapped(plan, ready)
+    planes = place_blocks(ready)
+    first, second, planes = lax.optimization_barrier((first, second, planes))
+    last = [(first, plan.x | plan.y, 0), (second, plan.x | plan.y, cut)]
+    return ready + last + swapped(plan, last), len(ready), planes, early, late
+
+
+def swapped(plan, pieces):
+    return [(plan.swap(a, plan.core), m | plan.core, row) for a, m, row in pieces]
 
 
 def hash_kernel(codes_hbm, offsets_hbm, x_ref, xt_ref, codes_ref, offsets_ref, sems):
@@ -183,7 +184,10 @@
         salted = (salted & (HASH_RANGE - 1)).reshape(step, width)
         x = (salted.astype(F32) * (2.0 / (HASH_RANGE - 1)) - 1.0).astype(BF)
         x_ref[at, :] = x
-        xt_ref[:, at] = x.T
+        quarter = LANES // 4
+        turned = x.T.reshape(-1, 2, quarter, step)
+        for h in range(2):
+            xt_ref[h * width // 2 : (h + 1) * width // 2, at] = turned[:, h].reshape(-1, step)
 
 
 def hash_inputs(codes, offsets):
@@ -240,8 +244,7 @@
     tiles = width // LANES
     me = me_ref[0]
     chunks = mask_ref.shape[1] // LANES if masked else 0
-    rest = [i for i in range(pieces) if i not in done]
-    assemble(w_ref, me, owners_ref, [piece_refs[i] for i in rest], [holds[i] for i in rest], local)
+    assemble(w_ref, me, owners_ref, piece_refs[done:], holds[done:], local)
     for piece, (masks, row0) in zip(piece_refs, holds):
         held = piece.shape[1]
         for k, m in enumerate(masks):
@@ -515,9 +518,27 @@
     return d_act, sums.reshape(-1, LANES), d_second, d_towers, loss, count
 
 
+def block_halves(me, owners_ref, g_ref, outs, masks, local):
+    width = g_ref.shape[2]
+    bsize = LANES // 2
+    half, quarter = bsize // 2, bsize // 4
+    side = width // bsize
+    lane_half = lax.broadcasted_iota(jnp.int32, (quarter, LANES), 1) // bsize
+    for i, m in enumerate(masks):
+        for b in range(local):
+            r, c, odd = place(owners_ref[(me ^ m) * local + b], side)
+            base = pl.multiple_of(r * half, half)
+            cols = pl.ds(pl.multiple_of(c * LANES, LANES), LANES)
+            keep = lane_half == odd
+            to = (i * local + b) * quarter
+            for h, out in enumerate(outs):
+                tile = g_ref[h, pl.ds(base, half), cols].astype(out.dtype)
+                out[to : to + quarter, :] = jnp.where(keep, tile[:quarter], swap_halves(tile[quarter:]))
+
+
 def grad_kernel(
     me_ref, owners_ref, sums_ref, coef_ref, norm_ref, dact_ref, slope_ref, pre_ref, live_ref, xt_ref,
-    keep_ref, send_ref, chunk_ref, d_norm_ref, d_pre_ref, g_ref, row_ref,
+    top_ref, low_ref, chunk_ref, d_norm_ref, g_ref, d_pre_ref, row_ref,
     *, parts, order, local,
 ):
     rows, width = pre_ref.shape
@@ -554,34 +575,20 @@
                 d_pre = slope_ref[at, cols] * lead - row_ref[3:4, cols] - apart
                 d_pre_ref[at, cols] = (live_ref[at, :] * d_pre).astype(BF)
         cols = slice(j * block, (j + 1) * block)
-        g_ref[:, cols] = dot(xt_ref[...], d_pre_ref[:, cols])
-    bsize = LANES // 2
-    half = bsize // 2
-    side = width // bsize
-    lane_half = lax.broadcasted_iota(jnp.int32, (half, LANES), 1) // bsize
-    me = me_ref[0]
-    for out, masks in ((send_ref, order[1]), (keep_ref, order[0])):
-        for i, m in enumerate(masks):
-            for b in range(local):
-                r, c, odd = place(owners_ref[(me ^ m) * local + b], side)
-                at = pl.ds(pl.multiple_of(r * bsize, bsize), half)
-                low = pl.ds(pl.multiple_of(r * bsize + half, half), half)
-                cols = pl.ds(pl.multiple_of(c * LANES, LANES), LANES)
-                to = (i * local + b) * half
-                out[to : to + half, :] = jnp.where(
-                    lane_half == odd,
-                    g_ref[at, cols].astype(out.dtype),
-                    swap_halves(g_ref[low, cols].astype(out.dtype)),
-                )
-
-
-def scatter_sum(plan, keep, send, rows):
+        g_ref[:, :, cols] = dot(xt_ref[...], d_pre_ref[:, cols]).reshape(2, width // 2, block)
+    block_halves(me_ref[0], owners_ref, g_ref, (top_ref, low_ref), order, local)
+
+
+def keep_kernel(me_ref, owners_ref, g_ref, top_ref, low_ref, *, order, local):
+    block_halves(me_ref[0], owners_ref, g_ref, (top_ref, low_ref), order, local)
+
+
+def scatter_sum(plan, kept, sent, rows):
     rest = len(plan.rest)
     shape = (2, 2, rest, rows, LANES)
-    got = plan.swap(send, plan.core)
-    mine = (keep + got.astype(F32)).reshape(shape)
-    cut = rows // 2
-    one, two = mine[..., :cut, :], mine[..., cut:, :]
+    one, two = (
+        (k + plan.swap(s, plan.core).astype(F32)).reshape(shape) for k, s in zip(kept, sent)
+    )
     got_one = plan.swap(one[1].astype(BF), plan.x)
     got_two = plan.swap(two[:, 1].astype(BF), plan.y)
     one = one[0] + got_one.astype(F32)
@@ -595,9 +602,9 @@
         return one, two, [plan.swap(both[k], m) for k, m in enumerate(plan.rest[1:])]
     both = jnp.concatenate([one, two], axis=1)
     for b in reversed(plan.bits):
-        both = both.reshape(2, -1, rows, LANES)
+        both = both.reshape(2, -1, 2 * rows, LANES)
         both = both[0] + plan.swap(both[1].astype(BF), b).astype(F32)
-    return both[:, :cut], both[:, cut:], []
+    return both[:, :rows], both[:, rows:], []
 
 
 def norm_kernel(*refs, n):
@@ -722,9 +729,13 @@
     grads = []
     for b in each:
         odd = owners_ref[me_ref[0] * local + b] % 2
-        tile = g_ref[b * half : (b + 1) * half, :]
-        tile = jnp.where(odd == 1, swap_halves(tile), tile)
-        grads.append(jnp.concatenate([tile[:, :bsize], tile[:, bsize:]], axis=0) / largest)
+        quarters = []
+        for i in range(2):
+            at = (i * local + b) * half // 2
+            tile = g_ref[at : at + half // 2, :]
+            tile = jnp.where(odd == 1, swap_halves(tile), tile)
+            quarters += [tile[:, :bsize], tile[:, bsize:]]
+        grads.append(jnp.concatenate(quarters, axis=0) / largest)
     bl = [bases_ref[b, :, :bsize] for b in each]
     br = [bases_ref[b, :, bsize:] for b in each]
     by_left = [hdot(bl[b], grads[b], 0, 0) for b in each]
@@ -894,22 +905,28 @@
     chosen = jnp.where(in_bag, seg_mask.astype(F32)[None], 0.0).astype(BF)
     late = (*prepared, live, chosen)
     zero = (me[0] >> 16).astype(BF)
-    pieces, (x, x_turned), (*prepared, live, chosen) = gather_pieces(
-        plan, payload, cut, zero, early, late
+
+    def held_by(pieces):
+        return [([m | base for m in plan.rest], row) for _, base, row in pieces]
+
+    def place_blocks(pieces):
+        (planes,) = call(
+            functools.partial(assemble_kernel, holds=held_by(pieces), local=local),
+            [((2, width, width), BF)],
+            [me, owners] + [a for a, _, _ in pieces],
+            smem=2,
+            limit=8,
+            name="assemble",
+            cost=10_000_000,
+        )
+        return planes
+
+    pieces, done, planes, (x, x_turned), (*prepared, live, chosen) = gather_pieces(
+        plan, payload, cut, zero, early, late, place_blocks
     )
     mask_shape = (total_rows, total_rows) if masked else (PAIR, LANES)
-    holds = [([m | base for m in plan.rest], row) for _, base, row in pieces]
+    holds = held_by(pieces)
     arrays = [a for a, _, _ in pieces]
-    done = [0, 1, 2, 5, 6, 7]
-    (planes,) = call(
-        functools.partial(assemble_kernel, holds=[holds[i] for i in done], local=local),
-        [((2, width, width), BF)],
-        [me, owners] + [arrays[i] for i in done],
-        smem=2,
-        limit=8,
-        name="assemble",
-        cost=10_000_000,
-    )
     pre, kept, sent, counts, mask, _ = call(
         functools.partial(
             pre_kernel, holds=holds, done=done, local=local, masked=masked, core=plan.core
@@ -993,25 +1010,33 @@
     groups = [m for m in (0, plan.y, plan.x, plan.x | plan.y)]
     keep_order = [g | r for g in groups for r in plan.rest]
     order = (keep_order, [m | plan.core for m in keep_order])
-    kept, sent, second_chunk, d_norm = call(
-        functools.partial(grad_kernel, parts=parts, order=order, local=local),
+    packed = (n // 2 * local * half // 2, LANES)
+    packed = (n // 2 * local * half // 2, LANES)
+    *sent, second_chunk, d_norm, full = call(
+        functools.partial(grad_kernel, parts=parts, order=order[1], local=local),
         [
-            ((n // 2 * local * half, LANES), F32),
-            ((n // 2 * local * half, LANES), BF),
+            (packed, BF),
+            (packed, BF),
             ((chunk, LANES), F32),
             ((2 * tiles, LANES), F32),
+            ((2, width // 2, width), F32),
         ],
         [me, owners, sums, coef, w_norm, d_act, slope, pre, live, x_turned],
         smem=2,
-        scratch=[
-            pltpu.VMEM((slots, width), BF),
-            pltpu.VMEM((width, width), F32),
-            pltpu.VMEM((8, width), F32),
-        ],
-        limit=20,
+        scratch=[pltpu.VMEM((slots, width), BF), pltpu.VMEM((8, width), F32)],
+        limit=16,
         name="grad",
     )
-    one_sum, two_sum, others = scatter_sum(plan, kept, sent, local * half)
+    kept = call(
+        functools.partial(keep_kernel, order=order[0], local=local),
+        [(packed, F32), (packed, F32)],
+        [me, owners, full],
+        smem=2,
+        limit=8,
+        name="keep",
+        cost=100_000_000,
+    )
+    one_sum, two_sum, others = scatter_sum(plan, kept, sent, local * half // 2)
     copies = n if masked else 1
     grad, pay = call(
         functools.partial(norm_kernel, n=copies),

time: 134 us -> 131 us (0.978)
  waiting for transfers between devices: 34.7 us -> 30.6 us
    ppermute x10, waiting for transfers between devices: 19.1 us -> 14.8 us  [swap(): return lax.ppermute(a, 'gy', [(i, i ^ my) for i in range(self.gy)])]
    ppermute x11 -> x12, starting transfers between devices: 5.48 us -> 6.4 us  [swap(): return lax.ppermute(a, 'gx', [(i, i ^ mx) for i in range(self.gx)])]
    ppermute x11 -> x12, waiting for transfers between devices: 11.3 us -> 12.1 us  [swap(): return lax.ppermute(a, 'gx', [(i, i ^ mx) for i in range(self.gx)])]
    pallas_call x12 -> x13, Pallas kernels: 38.3 us -> 38.9 us  [call(): pl.pallas_call(kernel, out_shape=[jax.ShapeDtypeStruct(s, t) for s, t in...]
  transfers between devices with their start and end apart: 22 -> 23, of which waited for: 14 -> 14; matrix products, arithmetic and copies ran while one was open for 0% -> 1% of each run, Pallas kernels for 8% -> 9%
where the time goes in v4:
time: 131 us
  Pallas kernels  38.9 us (30%)
  blocking collectives  33 us (25%)
  waiting for transfers between devices  30.6 us (23%)
  starting transfers between devices  24.7 us (19%)
  local copies, waits for them, and re-layouts  1.79 us (1%)
  between operations  1.31 us (1%)
    pallas_call x13, Pallas kernels, call(): pl.pallas_call(kernel, out_shape=[jax.ShapeDtypeStruct(s, t) for s, t in...  38.9 us
    all_to_all x3, blocking collectives, exchange(): return lax.all_to_all(payload, AXES, 0, 0, tiled=True)  33 us
    ppermute x10, waiting for transfers between devices, swap(): return lax.ppermute(a, 'gy', [(i, i ^ my) for i in range(self.gy)])  14.8 us
    ppermute x10, starting transfers between devices, swap(): return lax.ppermute(a, 'gy', [(i, i ^ my) for i in range(self.gy)])  14.5 us
    ppermute x12, waiting for transfers between devices, swap(): return lax.ppermute(a, 'gx', [(i, i ^ mx) for i in range(self.gx)])  12.1 us
    ppermute x12, starting transfers between devices, swap(): return lax.ppermute(a, 'gx', [(i, i ^ mx) for i in range(self.gx)])  6.4 us
    all_to_all x1, starting transfers between devices, exchange(): return lax.all_to_all(payload, AXES, 0, 0, tiled=True)  3.81 us
    all_to_all x1, waiting for transfers between devices, exchange(): return lax.all_to_all(payload, AXES, 0, 0, tiled=True)  3.72 us
  transfers between devices with their start and end apart: 23, of which 14 were waited for; matrix products, arithmetic and copies ran while one was open for 1% of the time, Pallas kernels for 9%

profile of v4, /device:TPU:0, one launch (start us, length us, event | category | flops | bytes accessed | tf_op | source)
XLA Modules:
  0.0 130.7 jit_solution(4245819210721865498)
XLA Ops:
  0.7 1.8 %pack.1 = bf16[336,128]{1,0:T(8,128)(2,1)S(1)} custom-call(s32[1]{0:T(128)} %bitcast.me_ref.refs_0_, s32[256]{0:T(256)} %owners_ref.9, f32[8,64,64]{2,1,0:T(8,128)} %w_hbm.3, s32[16,512]{1,0:T(8,128)} %neg_hbm.1, s32[8,128]{1,0:T(8,128)} %bitcast.70), custom_call_target="tpu_custom_call" | custom-call | tf_op jit(solution)/shard_map/pack/pallas_call | solution.py:60
  2.5 5.1 %collective-permute-start.2 = (bf16[1,336,128]{2,1,0:T(8,128)(2,1)S(1)}, bf16[1,336,128]{2,1,0:T(8,128)(2,1)S(1)}, u32[]{:S(2)}, u32[]{:S(2)}) collective-permute-start(bf16[1,336,128]{2,1,0:T(8,128)(2,1)S(1)} %bitcast.57), channel_id=1, source_target_pairs={{0,6},{1,7},{2,4},{3,5},{4,2},{5,3},{6,0},{7,1},{8,14},{9,15},{10,... | collective-permute-start | bytes 258056 | tf_op jit(solution)/shard_map/ppermute | solution.py:117
  8.2 2.6 %hash.1 = (bf16[1024,1024]{1,0:T(8,128)(2,1)S(1)}, bf16[1024,1024]{1,0:T(8,128)(2,1)S(1)}) custom-call(s32[1024,1024]{1,0:T(8,128)} %codes_hbm.1, s32[8,1024]{1,0:T(8,128)} %offsets_hbm.1), custom_call_target="tpu_custom_call" | custom-call | flops 20000000 | bytes 200000 | tf_op jit(solution)/shard_map/hash/pallas_call | solution.py:60
  10.8 1.3 %copy-done = bf16[1024,1024]{1,0:T(8,128)(2,1)} copy-done((bf16[1024,1024]{1,0:T(8,128)(2,1)}, bf16[1024,1024]{1,0:T(8,128)(2,1)S(1)}, u32[]{:S(2)}) %copy-start) | copy-done | bytes 2097176
  12.2 2.6 %collective-permute-done.1 = bf16[1,336,128]{2,1,0:T(8,128)(2,1)S(1)} collective-permute-done((bf16[1,336,128]{2,1,0:T(8,128)(2,1)S(1)}, bf16[1,336,128]{2,1,0:T(8,128)(2,1)S(1)}, u32[]{:S(2)}, u32[]{:S(2)}) %collective-permute-start.1) | collective-permute-done | bytes 86048 | tf_op jit(solution)/shard_map/ppermute | solution.py:117
  14.8 1.6 %collective-permute-start.4 = (bf16[4,336,128]{2,1,0:T(8,128)(2,1)S(1)}, bf16[4,336,128]{2,1,0:T(8,128)(2,1)S(1)}, u32[]{:S(2)}, u32[]{:S(2)}) collective-permute-start(bf16[4,336,128]{2,1,0:T(8,128)(2,1)S(1)} %pad_maximum_fusion.refs_0_.refs_3_), channel_id=1, source_target_pairs={{0,1},{1,0},{2,3},{3,2},{4,5},{5,4},{6,7},{7,6},{8,9},{9,8},{10,11... | collective-permute-start | bytes 1032200 | tf_op jit(solution)/shard_map/ppermute | solution.py:117
  16.4 1.5 %collective-permute-start.3 = (bf16[4,336,128]{2,1,0:T(8,128)(2,1)S(1)}, bf16[4,336,128]{2,1,0:T(8,128)(2,1)S(1)}, u32[]{:S(2)}, u32[]{:S(2)}) collective-permute-start(bf16[4,336,128]{2,1,0:T(8,128)(2,1)S(1)} %pad_maximum_fusion.refs_0_.refs_3_), channel_id=1, source_target_pairs={{0,16},{8,24},{16,0},{24,8},{1,17},{9,25},{17,1},{25,9},{2,18},{10... | collective-permute-start | bytes 1032200 | tf_op jit(solution)/shard_map/ppermute | solution.py:115
  18.0 2.8 %prepare.1 = (f32[8,64,128]{2,1,0:T(8,128)S(1)}, f32[8,64,128]{2,1,0:T(8,128)S(1)}, f32[8,64,128]{2,1,0:T(8,128)S(1)}, f32[8,64,128]{2,1,0:T(8,128)S(1)}, f32[8,...) custom-call(f32[8,64,64]{2,1,0:T(8,128)} %w_hbm.3, f32[8,64,64]{2,1,0:T(8,128)} %left_hbm.1, f32[8,64,64]{2,1,0:T(8,128)} %right_hbm.1, ...), custom_call_target="tpu_custom_call" | custom-call | flops 10000000 | bytes 100000 | tf_op jit(solution)/shard_map/prepare/pallas_call | solution.py:60
  20.9 3.2 %collective-permute-done.4.refs_2_.refs_5_ = bf16[4,336,128]{2,1,0:T(8,128)(2,1)S(1)} collective-permute-done((bf16[4,336,128]{2,1,0:T(8,128)(2,1)S(1)}, bf16[4,336,128]{2,1,0:T(8,128)(2,1)S(1)}, u32[]{:S(2)}, u32[]{:S(2)}) %collective-permute-start.4) | collective-permute-done | bytes 344096 | tf_op jit(solution)/shard_map/ppermute | solution.py:117
  24.1 1.3 %collective-permute-done.3.refs_1_.refs_4_ = bf16[4,336,128]{2,1,0:T(8,128)(2,1)S(1)} collective-permute-done((bf16[4,336,128]{2,1,0:T(8,128)(2,1)S(1)}, bf16[4,336,128]{2,1,0:T(8,128)(2,1)S(1)}, u32[]{:S(2)}, u32[]{:S(2)}) %collective-permute-start.3) | collective-permute-done | bytes 344096 | tf_op jit(solution)/shard_map/ppermute | solution.py:115
  25.7 1.6 %collective-permute-start.6 = (bf16[4,176,128]{2,1,0:T(8,128)(2,1)S(1)}, bf16[4,176,128]{2,1,0:T(8,128)(2,1)S(1)}, u32[]{:S(2)}, u32[]{:S(2)}) collective-permute-start(bf16[4,176,128]{2,1,0:T(8,128)(2,1)S(1)} %slice_add_fusion), channel_id=1, source_target_pairs={{0,16},{8,24},{16,0},{24,8},{1,17},{9,25},{17,1},{25,9},{2,18},{10... | collective-permute-start | bytes 540680 | tf_op jit(solution)/shard_map/ppermute | solution.py:115
  29.0 1.7 %assemble.1.refs_2_ = bf16[2,1024,1024]{2,1,0:T(8,128)(2,1)S(1)} custom-call(s32[1]{0:T(128)} %bitcast.me_ref.refs_0_, s32[256]{0:T(256)S(1)} %copy-done.15, bf16[4,336,128]{2,1,0:T(8,128)(2,1)S(1)} %pad_maximum_fusion.refs_0_.refs_3_, bf16[4,336,128]{2,1,0:T(8,128)(2,1)S(1)} %collective-permute-done.3.refs_1_.refs_4_, ...), custom_call_target="tpu_custom_call" | custom-call | flops 10000000 | bytes 100000 | tf_op jit(solution)/shard_map/assemble/pallas_call | solution.py:60
  30.7 3.3 %collective-permute-done.5.refs_9_ = bf16[4,160,128]{2,1,0:T(8,128)(2,1)S(1)} collective-permute-done((bf16[4,160,128]{2,1,0:T(8,128)(2,1)S(1)}, bf16[4,160,128]{2,1,0:T(8,128)(2,1)S(1)}, u32[]{:S(2)}, u32[]{:S(2)}) %collective-permute-start.5) | collective-permute-done | bytes 163872 | tf_op jit(solution)/shard_map/ppermute | solution.py:117
  34.5 1.1 collective-permute-done.10.refs_11_
  35.7 4.6 %pre.1 = (f32[1024,1024]{1,0:T(8,128)S(1)}, f32[8,128]{1,0:T(8,128)S(1)}, f32[8,128]{1,0:T(8,128)S(1)}, f32[32,128]{1,0:T(8,128)S(1)}, bf16[512,512]{1,0:T(8,128)(2,1)S(1)}, /*index=5*/bf16[2,1024,1024]{2,1,0:T(8,128)(2,1)S(1)}) custom-call(s32[1]{0:T(128)} %bitcast.me_ref.refs_0_, s32[256]{0:T(256)S(1)} %copy-done.15, ...), custom_call_target="tpu_custom_call", output_to_operand_aliasing={{5}: (2, {})} | custom-call | tf_op jit(solution)/shard_map/pre/pallas_call | solution.py:60
  41.7 10.1 %all_to_all.44 = f32[32,8,128]{2,1,0:T(8,128)S(1)} all-to-all(f32[32,8,128]{2,1,0:T(8,128)S(1)} %bitcast.56), channel_id=1, replica_groups=mesh['gx'=4,'gy'=8] {'gx','gy'}, dimensions={0} | all-to-all | bytes 262144 | tf_op jit(solution)/shard_map/all_to_all | solution.py:843
  51.8 4.9 %act.1 = (f32[1024,1024]{1,0:T(8,128)S(1)}, f32[32,1024]{1,0:T(8,128)S(1)}, f32[32,1024]{1,0:T(8,128)S(1)}, f32[32,1024]{1,0:T(8,128)S(1)}, f32[8,1024]{1,0:T(8,...) custom-call(f32[256,128]{1,0:T(8,128)S(1)} %bitcast.55, f32[32,128]{1,0:T(8,128)S(1)} %get-tuple-element.114.count_ref, ...), custom_call_target="tpu_custom_call" | custom-call | tf_op jit(solution)/shard_map/act/pallas_call | solution.py:60
  56.7 10.0 %all_to_all.45 = f32[32,8,128]{2,1,0:T(8,128)S(1)} all-to-all(f32[32,8,128]{2,1,0:T(8,128)S(1)} %bitcast.62), channel_id=1, replica_groups=mesh['gx'=4,'gy'=8] {'gx','gy'}, dimensions={0} | all-to-all | bytes 262144 | tf_op jit(solution)/shard_map/all_to_all | solution.py:843
  66.7 3.8 %loss.1 = (f32[32,1024]{1,0:T(8,128)S(1)}, bf16[1024,128]{1,0:T(8,128)(2,1)S(1)}, f32[2,32,32]{2,1,0:T(8,128)S(1)}, f32[1,1]{1,0:T(1,128)}, f32[1,1]{1,0:T(1,128)}) custom-call(s32[1]{0:T(128)} %bitcast.me_ref.refs_0_, f32[256,128]{1,0:T(8,128)S(1)} %bitcast.54, bf16[512,512]{1,0:T(8,128)(2,1)S(1)} %get-tuple-element.120.mask_ref, ...), custom_call_target="tpu_custom_call" | custom-call | tf_op jit(solution)/shard_map/loss/pallas_call | solution.py:60
  70.5 12.9 %all_to_all.46 = bf16[32,32,128]{2,1,0:T(8,128)(2,1)S(1)} all-to-all(bf16[32,32,128]{2,1,0:T(8,128)(2,1)S(1)} %bitcast.61), channel_id=1, replica_groups=mesh['gx'=4,'gy'=8] {'gx','gy'}, dimensions={0} | all-to-all | bytes 524288 | tf_op jit(solution)/shard_map/all_to_all | solution.py:843
  83.4 4.2 %grad.1 = (bf16[2048,128]{1,0:T(8,128)(2,1)S(1)}, bf16[2048,128]{1,0:T(8,128)(2,1)S(1)}, f32[8,128]{1,0:T(8,128)S(1)}, f32[16,128]{1,0:T(8,128)S(1)}, f32[2,512,1024]{2,1,0:T(8,128)S(1)}) custom-call(s32[1]{0:T(128)} %bitcast.me_ref.refs_0_, s32[256]{0:T(256)S(1)} %copy-done.15, bf16[1024,128]{1,0:T(8,128)(2,1)S(1)} %bitcast.52, ...), custom_call_target="tpu_custom_call" | custom-call | tf_op jit(solution)/shard_map/grad/pallas_call | solution.py:60
  88.2 1.2 keep.1
  91.6 6.5 %collective-permute-done.14 = bf16[2,4,128,128]{3,2,1,0:T(8,128)(2,1)S(1)} collective-permute-done((bf16[2,4,128,128]{3,2,1,0:T(8,128)(2,1)S(1)}, bf16[2,4,128,128]{3,2,1,0:T(8,128)(2,1)S(1)}, u32[]{:S(2)}, u32[]{:S(2)}) %collective-permute-start.14) | collective-permute-done | bytes 262176 | tf_op jit(solution)/shard_map/ppermute | solution.py:115
  100.3 2.9 %collective-permute-done.15 = bf16[4,128,128]{2,1,0:T(8,128)(2,1)S(1)} collective-permute-done((bf16[4,128,128]{2,1,0:T(8,128)(2,1)S(1)}, bf16[4,128,128]{2,1,0:T(8,128)(2,1)S(1)}, u32[]{:S(2)}, u32[]{:S(2)}) %collective-permute-start.15) | collective-permute-done | bytes 131104 | tf_op jit(solution)/shard_map/ppermute | solution.py:117
  103.3 1.1 collective-permute-done.18
  104.5 1.5 %collective-permute-start.21 = (bf16[256,128]{1,0:T(8,128)(2,1)S(1)}, bf16[256,128]{1,0:T(8,128)(2,1)S(1)}, u32[]{:S(2)}, u32[]{:S(2)}) collective-permute-start(bf16[256,128]{1,0:T(8,128)(2,1)S(1)} %get-tuple-element.174), channel_id=1, source_target_pairs={{0,6},{1,7},{2,4},{3,5},{4,2},{5,3},{6,0},{7,1},{8,14},{9,15},{10,... | collective-permute-start | bytes 196616 | tf_op jit(solution)/shard_map/ppermute | solution.py:117
  106.0 2.9 %collective-permute-start.20 = (bf16[256,128]{1,0:T(8,128)(2,1)S(1)}, bf16[256,128]{1,0:T(8,128)(2,1)S(1)}, u32[]{:S(2)}, u32[]{:S(2)}) collective-permute-start(bf16[256,128]{1,0:T(8,128)(2,1)S(1)} %get-tuple-element.176), channel_id=1, source_target_pairs={{0,4},{1,5},{2,6},{3,7},{4,0},{5,1},{6,2},{7,3},{8,12},{9,13},{10,... | collective-permute-start | bytes 196616 | tf_op jit(solution)/shard_map/ppermute | solution.py:117
  108.9 1.8 %collective-permute-done.21.refs_5_ = bf16[256,128]{1,0:T(8,128)(2,1)S(1)} collective-permute-done((bf16[256,128]{1,0:T(8,128)(2,1)S(1)}, bf16[256,128]{1,0:T(8,128)(2,1)S(1)}, u32[]{:S(2)}, u32[]{:S(2)}) %collective-permute-start.21) | collective-permute-done | bytes 65568 | tf_op jit(solution)/shard_map/ppermute | solution.py:117
  112.5 3.8 %all-to-all-start.3 = ((bf16[32,16,128]{2,1,0:T(8,128)(2,1)}), bf16[32,16,128]{2,1,0:T(8,128)(2,1)S(1)}, u32[]{:S(2)}, u32[]{:S(2)}) async-start(bf16[32,16,128]{2,1,0:T(8,128)(2,1)} %bitcast.24), calls=%async_computation.3 | async-start | bytes 262144 | tf_op jit(solution)/shard_map/all_to_all | solution.py:843
  116.4 3.8 %turn.1 = (f32[8,64,128]{2,1,0:T(8,128)S(1)}, f32[8,64,128]{2,1,0:T(8,128)S(1)}, f32[8,64,128]{2,1,0:T(8,128)S(1)}, f32[8,128]{1,0:T(8,128)S(1)}, f32[4,32,1024]...) custom-call(s32[1]{0:T(128)} %bitcast.me_ref.refs_0_, s32[256]{0:T(256)S(1)} %copy-done.15, ...), custom_call_target="tpu_custom_call" | custom-call | flops 10000000 | bytes 100000 | tf_op jit(solution)/shard_map/turn/pallas_call | solution.py:60
  120.1 3.7 %all-to-all-done.3 = bf16[32,16,128]{2,1,0:T(8,128)(2,1)S(1)} async-done(((bf16[32,16,128]{2,1,0:T(8,128)(2,1)}), bf16[32,16,128]{2,1,0:T(8,128)(2,1)S(1)}, u32[]{:S(2)}, u32[]{:S(2)}) %all-to-all-start.3) | async-done | bytes 131104 | tf_op jit(solution)/shard_map/all_to_all | solution.py:843
  123.9 6.6 %step.1 = (f32[8,64,64]{2,1,0:T(8,128)}, bf16[8,64,64]{2,1,0:T(8,128)(2,1)}, f32[8,64,64]{2,1,0:T(8,128)}, f32[8,64,64]{2,1,0:T(8,128)}, f32[8,64,64]{2,1,0:T(8,...) custom-call(bf16[512,128]{1,0:T(8,128)(2,1)S(1)} %bitcast.53, ...), custom_call_target="tpu_custom_call" | custom-call | tf_op jit(solution)/shard_map/step/pallas_call | solution.py:60
  (86 shorter events, 11.6 us)
Async XLA Ops:
  2.5 26.5 %copy-start.15 = (s32[256]{0:T(256)S(1)}, s32[256]{0:T(256)}, u32[]{:S(2)}) copy-start(s32[256]{0:T(256)} %owners_ref.9) | copy-start | bytes 3076
  2.5 9.7 %collective-permute-start.2 = (bf16[1,336,128]{2,1,0:T(8,128)(2,1)S(1)}, bf16[1,336,128]{2,1,0:T(8,128)(2,1)S(1)}, u32[]{:S(2)}, u32[]{:S(2)}) collective-permute-start(bf16[1,336,128]{2,1,0:T(8,128)(2,1)S(1)} %bitcast.57), channel_id=1, source_target_pairs={{0,6},{1,7},{2,4},{3,5},{4,2},{5,3},{6,0},{7,1},{8,14},{9,15},{10,... | collective-permute-start | bytes 258056 | tf_op jit(solution)/shard_map/ppermute | solution.py:117
  7.6 7.2 %collective-permute-start.1 = (bf16[1,336,128]{2,1,0:T(8,128)(2,1)S(1)}, bf16[1,336,128]{2,1,0:T(8,128)(2,1)S(1)}, u32[]{:S(2)}, u32[]{:S(2)}) collective-permute-start(bf16[1,336,128]{2,1,0:T(8,128)(2,1)S(1)} %bitcast.58), channel_id=1, source_target_pairs={{0,4},{1,5},{2,6},{3,7},{4,0},{5,1},{6,2},{7,3},{8,12},{9,13},{10,... | collective-permute-start | bytes 258056 | tf_op jit(solution)/shard_map/ppermute | solution.py:117
  7.6 7.2 %collective-permute-start = (bf16[1,336,128]{2,1,0:T(8,128)(2,1)S(1)}, bf16[1,336,128]{2,1,0:T(8,128)(2,1)S(1)}, u32[]{:S(2)}, u32[]{:S(2)}) collective-permute-start(bf16[1,336,128]{2,1,0:T(8,128)(2,1)S(1)} %bitcast.59), channel_id=1, source_target_pairs={{0,2},{1,3},{2,0},{3,1},{4,6},{5,7},{6,4},{7,5},{8,10},{9,11},{10,... | collective-permute-start | bytes 258056 | tf_op jit(solution)/shard_map/ppermute | solution.py:117
  14.8 9.2 %collective-permute-start.4 = (bf16[4,336,128]{2,1,0:T(8,128)(2,1)S(1)}, bf16[4,336,128]{2,1,0:T(8,128)(2,1)S(1)}, u32[]{:S(2)}, u32[]{:S(2)}) collective-permute-start(bf16[4,336,128]{2,1,0:T(8,128)(2,1)S(1)} %pad_maximum_fusion.refs_0_.refs_3_), channel_id=1, source_target_pairs={{0,1},{1,0},{2,3},{3,2},{4,5},{5,4},{6,7},{7,6},{8,9},{9,8},{10,11... | collective-permute-start | bytes 1032200 | tf_op jit(solution)/shard_map/ppermute | solution.py:117
  16.4 9.0 %collective-permute-start.3 = (bf16[4,336,128]{2,1,0:T(8,128)(2,1)S(1)}, bf16[4,336,128]{2,1,0:T(8,128)(2,1)S(1)}, u32[]{:S(2)}, u32[]{:S(2)}) collective-permute-start(bf16[4,336,128]{2,1,0:T(8,128)(2,1)S(1)} %pad_maximum_fusion.refs_0_.refs_3_), channel_id=1, source_target_pairs={{0,16},{8,24},{16,0},{24,8},{1,17},{9,25},{17,1},{25,9},{2,18},{10... | collective-permute-start | bytes 1032200 | tf_op jit(solution)/shard_map/ppermute | solution.py:115
  20.9 7.2 %collective-permute-start.7 = (bf16[4,336,128]{2,1,0:T(8,128)(2,1)S(1)}, bf16[4,336,128]{2,1,0:T(8,128)(2,1)S(1)}, u32[]{:S(2)}, u32[]{:S(2)}) collective-permute-start(bf16[4,336,128]{2,1,0:T(8,128)(2,1)S(1)} %pad_maximum_fusion.refs_0_.refs_3_), channel_id=1, source_target_pairs={{0,8},{8,0},{16,24},{24,16},{1,9},{9,1},{17,25},{25,17},{2,10},{10... | collective-permute-start | bytes 1032200 | tf_op jit(solution)/shard_map/ppermute | solution.py:115
  25.6 3.3 %collective-permute-start.9 = (bf16[4,336,128]{2,1,0:T(8,128)(2,1)S(1)}, bf16[4,336,128]{2,1,0:T(8,128)(2,1)S(1)}, u32[]{:S(2)}, u32[]{:S(2)}) collective-permute-start(bf16[4,336,128]{2,1,0:T(8,128)(2,1)S(1)} %collective-permute-done.4.refs_2_.refs_5_), channel_id=1, source_target_pairs={{0,8},{8,0},{16,24},{24,16},{1,9},{9,1},{17,25},{25,17},{2,10},{10... | collective-permute-start | bytes 1032200 | tf_op jit(solution)/shard_map/ppermute | solution.py:115
  25.7 8.3 %collective-permute-start.6 = (bf16[4,176,128]{2,1,0:T(8,128)(2,1)S(1)}, bf16[4,176,128]{2,1,0:T(8,128)(2,1)S(1)}, u32[]{:S(2)}, u32[]{:S(2)}) collective-permute-start(bf16[4,176,128]{2,1,0:T(8,128)(2,1)S(1)} %slice_add_fusion), channel_id=1, source_target_pairs={{0,16},{8,24},{16,0},{24,8},{1,17},{9,25},{17,1},{25,9},{2,18},{10... | collective-permute-start | bytes 540680 | tf_op jit(solution)/shard_map/ppermute | solution.py:115
  27.3 1.7 %collective-permute-start.8 = (bf16[4,336,128]{2,1,0:T(8,128)(2,1)S(1)}, bf16[4,336,128]{2,1,0:T(8,128)(2,1)S(1)}, u32[]{:S(2)}, u32[]{:S(2)}) collective-permute-start(bf16[4,336,128]{2,1,0:T(8,128)(2,1)S(1)} %collective-permute-done.3.refs_1_.refs_4_), channel_id=1, source_target_pairs={{0,8},{8,0},{16,24},{24,16},{1,9},{9,1},{17,25},{25,17},{2,10},{10... | collective-permute-start | bytes 1032200 | tf_op jit(solution)/shard_map/ppermute | solution.py:115
  27.5 6.5 %collective-permute-start.5 = (bf16[4,160,128]{2,1,0:T(8,128)(2,1)S(1)}, bf16[4,160,128]{2,1,0:T(8,128)(2,1)S(1)}, u32[]{:S(2)}, u32[]{:S(2)}) collective-permute-start(bf16[4,160,128]{2,1,0:T(8,128)(2,1)S(1)} %slice_add_fusion.1), channel_id=1, source_target_pairs={{0,1},{1,0},{2,3},{3,2},{4,5},{5,4},{6,7},{7,6},{8,9},{9,8},{10,11... | collective-permute-start | bytes 491528 | tf_op jit(solution)/shard_map/ppermute | solution.py:117
  30.6 21.2 %copy-start.2 = (f32[1024,32]{0,1:T(8,128)S(1)}, f32[1024,32]{0,1:T(8,128)}, u32[]{:S(2)}) copy-start(f32[1024,32]{0,1:T(8,128)} %param.36) | copy-start | bytes 393220
  34.0 1.7 %collective-permute-start.11 = (bf16[4,176,128]{2,1,0:T(8,128)(2,1)S(1)}, bf16[4,176,128]{2,1,0:T(8,128)(2,1)S(1)}, u32[]{:S(2)}, u32[]{:S(2)}) collective-permute-start(bf16[4,176,128]{2,1,0:T(8,128)(2,1)S(1)} %collective-permute-done.6.refs_10_), channel_id=1, source_target_pairs={{0,8},{8,0},{16,24},{24,16},{1,9},{9,1},{17,25},{25,17},{2,10},{10... | collective-permute-start | bytes 540680 | tf_op jit(solution)/shard_map/ppermute | solution.py:115
  34.0 1.7 %collective-permute-start.10 = (bf16[4,160,128]{2,1,0:T(8,128)(2,1)S(1)}, bf16[4,160,128]{2,1,0:T(8,128)(2,1)S(1)}, u32[]{:S(2)}, u32[]{:S(2)}) collective-permute-start(bf16[4,160,128]{2,1,0:T(8,128)(2,1)S(1)} %collective-permute-done.5.refs_9_), channel_id=1, source_target_pairs={{0,8},{8,0},{16,24},{24,16},{1,9},{9,1},{17,25},{25,17},{2,10},{10... | collective-permute-start | bytes 491528 | tf_op jit(solution)/shard_map/ppermute | solution.py:115
  40.3 26.3 %copy-start.13 = (f32[2,32,32]{2,1,0:T(8,128)S(1)}, f32[2,32,32]{2,1,0:T(8,128)}, u32[]{:S(2)}) copy-start(f32[2,32,32]{2,1,0:T(8,128)} %wt_hbm.1) | copy-start | bytes 24580
  40.3 43.1 %copy-start.1 = (bf16[1024,1024]{1,0:T(8,128)(2,1)S(1)}, bf16[1024,1024]{1,0:T(8,128)(2,1)}, u32[]{:S(2)}) copy-start(bf16[1024,1024]{1,0:T(8,128)(2,1)} %copy-done) | copy-start | bytes 6291460
  40.3 1.2 collective-permute-start.12
  87.6 2.0 %collective-permute-start.13 = (bf16[2048,128]{1,0:T(8,128)(2,1)S(1)}, bf16[2048,128]{1,0:T(8,128)(2,1)S(1)}, u32[]{:S(2)}, u32[]{:S(2)}) collective-permute-start(bf16[2048,128]{1,0:T(8,128)(2,1)S(1)} %get-tuple-element.133), channel_id=1, source_target_pairs={{0,8},{8,0},{16,24},{24,16},{1,9},{9,1},{17,25},{25,17},{2,10},{10... | collective-permute-start | bytes 1572872 | tf_op jit(solution)/shard_map/ppermute | solution.py:115
  87.7 2.7 %collective-permute-start.16 = (bf16[2048,128]{1,0:T(8,128)(2,1)S(1)}, bf16[2048,128]{1,0:T(8,128)(2,1)S(1)}, u32[]{:S(2)}, u32[]{:S(2)}) collective-permute-start(bf16[2048,128]{1,0:T(8,128)(2,1)S(1)} %get-tuple-element.135), channel_id=1, source_target_pairs={{0,8},{8,0},{16,24},{24,16},{1,9},{9,1},{17,25},{25,17},{2,10},{10... | collective-permute-start | bytes 1572872 | tf_op jit(solution)/shard_map/ppermute | solution.py:115
  89.7 8.4 %collective-permute-start.14 = (bf16[2,4,128,128]{3,2,1,0:T(8,128)(2,1)S(1)}, bf16[2,4,128,128]{3,2,1,0:T(8,128)(2,1)S(1)}, u32[]{:S(2)}, u32[]{:S(2)}) collective-permute-start(bf16[2,4,128,128]{3,2,1,0:T(8,128)(2,1)S(1)} %bitcast.66), channel_id=1, source_target_pairs={{0,16},{8,24},{16,0},{24,8},{1,17},{9,25},{17,1},{25,9},{2,18},{10... | collective-permute-start | bytes 786440 | tf_op jit(solution)/shard_map/ppermute | solution.py:115
  90.4 33.4 %copy-start.4 = (f32[8,64,128]{2,1,0:T(8,128)S(1)}, f32[8,64,128]{2,1,0:T(8,128)}, u32[]{:S(2)}) copy-start(f32[8,64,128]{2,1,0:T(8,128)} %copy-done.3) | copy-start | bytes 786436
  90.4 33.4 %copy-start.6 = (f32[8,64,128]{2,1,0:T(8,128)S(1)}, f32[8,64,128]{2,1,0:T(8,128)}, u32[]{:S(2)}) copy-start(f32[8,64,128]{2,1,0:T(8,128)} %copy-done.5) | copy-start | bytes 786436
  90.4 33.4 %copy-start.8 = (f32[8,64,128]{2,1,0:T(8,128)S(1)}, f32[8,64,128]{2,1,0:T(8,128)}, u32[]{:S(2)}) copy-start(f32[8,64,128]{2,1,0:T(8,128)} %copy-done.7) | copy-start | bytes 786436
  90.5 33.4 %copy-start.10 = (f32[8,64,64]{2,1,0:T(8,128)S(1)}, f32[8,64,64]{2,1,0:T(8,128)}, u32[]{:S(2)}) copy-start(f32[8,64,64]{2,1,0:T(8,128)} %copy-done.9) | copy-start | bytes 393220
  90.5 33.4 %copy-start.12 = (f32[8,64,128]{2,1,0:T(8,128)S(1)}, f32[8,64,128]{2,1,0:T(8,128)}, u32[]{:S(2)}) copy-start(f32[8,64,128]{2,1,0:T(8,128)} %copy-done.11) | copy-start | bytes 786436
  90.6 8.7 %collective-permute-start.17 = (bf16[2,4,128,128]{3,2,1,0:T(8,128)(2,1)S(1)}, bf16[2,4,128,128]{3,2,1,0:T(8,128)(2,1)S(1)}, u32[]{:S(2)}, u32[]{:S(2)}) collective-permute-start(bf16[2,4,128,128]{3,2,1,0:T(8,128)(2,1)S(1)} %fusion.1), channel_id=1, source_target_pairs={{0,1},{1,0},{2,3},{3,2},{4,5},{5,4},{6,7},{7,6},{8,9},{9,8},{10,11... | collective-permute-start | bytes 786440 | tf_op jit(solution)/shard_map/ppermute | solution.py:117
  98.2 5.0 %collective-permute-start.15 = (bf16[4,128,128]{2,1,0:T(8,128)(2,1)S(1)}, bf16[4,128,128]{2,1,0:T(8,128)(2,1)S(1)}, u32[]{:S(2)}, u32[]{:S(2)}) collective-permute-start(bf16[4,128,128]{2,1,0:T(8,128)(2,1)S(1)} %fusion.4), channel_id=1, source_target_pairs={{0,1},{1,0},{2,3},{3,2},{4,5},{5,4},{6,7},{7,6},{8,9},{9,8},{10,11... | collective-permute-start | bytes 393224 | tf_op jit(solution)/shard_map/ppermute | solution.py:117
  99.3 5.0 %collective-permute-start.18 = (bf16[4,128,128]{2,1,0:T(8,128)(2,1)S(1)}, bf16[4,128,128]{2,1,0:T(8,128)(2,1)S(1)}, u32[]{:S(2)}, u32[]{:S(2)}) collective-permute-start(bf16[4,128,128]{2,1,0:T(8,128)(2,1)S(1)} %fusion.5), channel_id=1, source_target_pairs={{0,16},{8,24},{16,0},{24,8},{1,17},{9,25},{17,1},{25,9},{2,18},{10... | collective-permute-start | bytes 393224 | tf_op jit(solution)/shard_map/ppermute | solution.py:115
  104.5 6.2 %collective-permute-start.21 = (bf16[256,128]{1,0:T(8,128)(2,1)S(1)}, bf16[256,128]{1,0:T(8,128)(2,1)S(1)}, u32[]{:S(2)}, u32[]{:S(2)}) collective-permute-start(bf16[256,128]{1,0:T(8,128)(2,1)S(1)} %get-tuple-element.174), channel_id=1, source_target_pairs={{0,6},{1,7},{2,4},{3,5},{4,2},{5,3},{6,0},{7,1},{8,14},{9,15},{10,... | collective-permute-start | bytes 196616 | tf_op jit(solution)/shard_map/ppermute | solution.py:117
  106.0 5.7 %collective-permute-start.19 = (bf16[256,128]{1,0:T(8,128)(2,1)S(1)}, bf16[256,128]{1,0:T(8,128)(2,1)S(1)}, u32[]{:S(2)}, u32[]{:S(2)}) collective-permute-start(bf16[256,128]{1,0:T(8,128)(2,1)S(1)} %get-tuple-element.175), channel_id=1, source_target_pairs={{0,2},{1,3},{2,0},{3,1},{4,6},{5,7},{6,4},{7,5},{8,10},{9,11},{10,... | collective-permute-start | bytes 196616 | tf_op jit(solution)/shard_map/ppermute | solution.py:117
  106.0 5.7 %collective-permute-start.20 = (bf16[256,128]{1,0:T(8,128)(2,1)S(1)}, bf16[256,128]{1,0:T(8,128)(2,1)S(1)}, u32[]{:S(2)}, u32[]{:S(2)}) collective-permute-start(bf16[256,128]{1,0:T(8,128)(2,1)S(1)} %get-tuple-element.176), channel_id=1, source_target_pairs={{0,4},{1,5},{2,6},{3,7},{4,0},{5,1},{6,2},{7,3},{8,12},{9,13},{10,... | collective-permute-start | bytes 196616 | tf_op jit(solution)/shard_map/ppermute | solution.py:117
  112.5 11.3 %all-to-all-start.3 = ((bf16[32,16,128]{2,1,0:T(8,128)(2,1)}), bf16[32,16,128]{2,1,0:T(8,128)(2,1)S(1)}, u32[]{:S(2)}, u32[]{:S(2)}) async-start(bf16[32,16,128]{2,1,0:T(8,128)(2,1)} %bitcast.24), calls=%async_computation.3 | async-start | bytes 262144 | tf_op jit(solution)/shard_map/all_to_all | solution.py:843
  (8 other events, 114.1 us)

commit v5 on v4

--- a/solution.py
+++ b/solution.py
@@ -119,17 +119,14 @@
 
 
 def pack_kernel(
-    me_ref, owners_ref, w_hbm, neg_hbm, seg_hbm, out_ref, w_ref, neg_ref, seg_ref, sems, *, masked
+    w_hbm, neg_hbm, seg_hbm, out_ref, w_ref, neg_ref, seg_ref, sems, *, masked
 ):
     fetch((w_hbm, neg_hbm, seg_hbm), (w_ref, neg_ref, seg_ref), sems)
     local, bsize = w_ref.shape[0], w_ref.shape[1]
     half = bsize // 2
     for b in range(local):
-        odd = owners_ref[me_ref[0] * local + b] % 2
-        top, low = w_ref[b, :half, :], w_ref[b, half:, :]
-        left = jnp.where(odd == 1, low, top)
-        right = jnp.where(odd == 1, top, low)
-        out_ref[b * half : (b + 1) * half, :] = jnp.concatenate([left, right], axis=1).astype(BF)
+        both = jnp.concatenate([w_ref[b, :half, :], w_ref[b, half:, :]], axis=1)
+        out_ref[b * half : (b + 1) * half, :] = both.astype(BF)
     at = local * half
     if masked:
         for c in range(neg_ref.shape[1] // LANES):
@@ -224,8 +221,9 @@
                 rows = pl.multiple_of(r * bsize, bsize)
                 low = pl.multiple_of(r * bsize + half, half)
                 cols = pl.ds(pl.multiple_of(c * LANES, LANES), LANES)
-                w_ref[odd, pl.ds(rows, half), cols] = tile
-                w_ref[odd, pl.ds(low, half), cols] = swap_halves(tile)
+                other = swap_halves(tile)
+                w_ref[odd, pl.ds(rows, half), cols] = jnp.where(odd == 1, other, tile)
+                w_ref[odd, pl.ds(low, half), cols] = jnp.where(odd == 1, tile, other)
 
 
 def assemble_kernel(me_ref, owners_ref, *refs, holds, local):
@@ -410,8 +408,8 @@
 
 def loss_kernel(
     me_ref, all_ref, mask_ref, towers_ref, w_out_ref, act_ref, one_ref, two_ref,
-    dact_ref, pay_ref, d_towers_ref, loss_ref, total_ref,
-    score_ref, user_ref, item_ref, second_ref, row_ref, *, n,
+    dact_ref, keep_ref, send_ref, d_towers_ref, loss_ref, total_ref,
+    score_ref, user_ref, item_ref, halves_ref, *, n, core,
 ):
     me = me_ref[0]
     embed = towers_ref.shape[1]
@@ -469,21 +467,28 @@
     second = sum(dot(d_low, p) for p in three(act_ref[...]))
     width = act_ref.shape[1]
     tiles = width // LANES
-    for j in range(tiles):
-        second_ref[pl.ds(j, embed, stride=tiles), :] = second[:, j * LANES : (j + 1) * LANES]
+    half = tiles // 2
     for j in range(tiles):
         cols = slice(j * LANES, (j + 1) * LANES)
-        row_ref[j : j + 1, :] = d_bias[:, cols]
-        row_ref[tiles + j : tiles + j + 1, :] = d_gain[:, cols]
-    sums = row_ref[...].astype(BF)
-    chunk = embed * tiles // n
+        h, t = j // half, j % half
+        halves_ref[h, t : t + 1, :] = d_bias[:, cols]
+        halves_ref[h, half + t : half + t + 1, :] = d_gain[:, cols]
+        halves_ref[h, pl.ds(tiles + t, embed, stride=half), :] = second[:, cols]
+    odd = (me // core) % 2
+    keep_ref[...] = jnp.where(odd == 1, halves_ref[1], halves_ref[0])
+    send_ref[...] = jnp.where(odd == 1, halves_ref[0], halves_ref[1])
+
+
+def share_kernel(keep_ref, got_ref, pay_ref, *, n, tiles):
+    total = keep_ref[...] + got_ref[...]
+    sums, rows = total[:tiles].astype(BF), (total.shape[0] - tiles) // n
+    high = total[tiles:].astype(BF).astype(F32)
+    low = total[tiles:] - high
+    held = tiles + 2 * rows
     for d in range(n):
-        part = second_ref[d * chunk : (d + 1) * chunk, :]
-        high = part.astype(BF)
-        low = (part - high.astype(F32)).astype(BF)
-        at = d * (2 * tiles + 2 * chunk)
-        pay_ref[at : at + 2 * tiles, :] = sums
-        pay_ref[at + 2 * tiles : at + 2 * tiles + 2 * chunk, :] = jnp.concatenate([high, low], axis=0)
+        at = slice(d * rows, (d + 1) * rows)
+        part = jnp.concatenate([sums.astype(F32), high[at], low[at]], axis=0)
+        pay_ref[d * held : (d + 1) * held, :] = part.astype(BF)
 
 
 def loss_spread(plan, bags, neg_mask, towers, w_out, act, one, two):
@@ -539,21 +544,31 @@
 def grad_kernel(
     me_ref, owners_ref, sums_ref, coef_ref, norm_ref, dact_ref, slope_ref, pre_ref, live_ref, xt_ref,
     top_ref, low_ref, chunk_ref, d_norm_ref, g_ref, d_pre_ref, row_ref,
-    *, parts, order, local,
+    *, parts, order, local, core,
 ):
     rows, width = pre_ref.shape
     tiles = width // LANES
     held = sums_ref.shape[0] // parts
-    total = sums_ref[0:held, :].astype(F32)
-    for d in range(1, parts):
-        total = total + sums_ref[d * held : (d + 1) * held, :].astype(F32)
+    half = tiles // 2
+    if parts > 1:
+        sides = []
+        for h in range(2):
+            side = jnp.zeros((held, LANES), F32)
+            for d in range(parts):
+                if (d // core) % 2 == h:
+                    side = side + sums_ref[d * held : (d + 1) * held, :].astype(F32)
+            sides.append(side)
+        total = jnp.concatenate([s[i * half : (i + 1) * half] for i in range(2) for s in sides], axis=0)
+        share = (held - tiles) // 2
+        sides = [s[tiles : tiles + share] + s[tiles + share :] for s in sides]
+        chunk_ref[...] = jnp.concatenate(
+            [s[i * half : (i + 1) * half] for i in range(share // half) for s in sides], axis=0
+        )
+    else:
+        total = sums_ref[...]
+        chunk_ref[...] = jnp.zeros(chunk_ref.shape, F32)
     d_norm_ref[0:tiles, :] = total[tiles : 2 * tiles]
     d_norm_ref[tiles : 2 * tiles, :] = total[:tiles]
-    if held > 2 * tiles:
-        chunk = chunk_ref.shape[0]
-        chunk_ref[...] = total[2 * tiles : 2 * tiles + chunk] + total[2 * tiles + chunk :]
-    else:
-        chunk_ref[...] = jnp.zeros(chunk_ref.shape, F32)
     for j in range(tiles):
         cols = slice(j * LANES, (j + 1) * LANES)
         row_ref[0:1, cols] = total[j : j + 1]
@@ -867,8 +882,7 @@
     (payload,) = call(
         functools.partial(pack_kernel, masked=masked),
         [((size, LANES), BF)],
-        [me, in_hbm(owners), w_hidden, neg_mask, seg_mask.reshape(-1, LANES)],
-        smem=2,
+        [w_hidden, neg_mask, seg_mask.reshape(-1, LANES)],
         hbm=3,
         scratch=[
             pltpu.VMEM(w_hidden.shape, F32),
@@ -978,11 +992,13 @@
     if masked:
         chunk = embed * tiles // n
         everyone = exchange(pay)
-        d_act, pay, d_towers, loss_sum, count = call(
-            functools.partial(loss_kernel, n=n),
+        shared = (tiles + embed * tiles // 2, LANES)
+        d_act, kept, sent, d_towers, loss_sum, count = call(
+            functools.partial(loss_kernel, n=n, core=plan.core),
             [
                 ((bags, width), F32),
-                ((n * (2 * tiles + 2 * chunk), LANES), BF),
+                (shared, F32),
+                (shared, F32),
                 ((2, embed, embed), F32),
                 ((1, 1), F32),
                 ((1, 1), F32),
@@ -994,10 +1010,16 @@
                 pltpu.VMEM((total_rows, total_rows), F32),
                 pltpu.VMEM((total_rows, embed), F32),
                 pltpu.VMEM((total_rows, embed), F32),
-                pltpu.VMEM((embed * tiles, LANES), F32),
-                pltpu.VMEM((2 * tiles, LANES), F32),
+                pltpu.VMEM((2, *shared), F32),
             ],
             name="loss",
+        )
+        (pay,) = call(
+            functools.partial(share_kernel, n=n, tiles=tiles),
+            [((n * (tiles + chunk), LANES), BF)],
+            [kept, plan.swap(sent, plan.core)],
+            limit=4,
+            name="share",
         )
         sums, parts = exchange(pay), n
         loss_sum, count = loss_sum[0, 0], count[0, 0]
@@ -1013,7 +1035,7 @@
     packed = (n // 2 * local * half // 2, LANES)
     packed = (n // 2 * local * half // 2, LANES)
     *sent, second_chunk, d_norm, full = call(
-        functools.partial(grad_kernel, parts=parts, order=order[1], local=local),
+        functools.partial(grad_kernel, parts=parts, order=order[1], local=local, core=plan.core),
         [
             (packed, BF),
             (packed, BF),

time: 131 us -> 129 us (0.985)
  blocking collectives: 33 us -> 30.1 us
    all_to_all x3, blocking collectives: 33 us -> 30.1 us  [exchange(): return lax.all_to_all(payload, AXES, 0, 0, tiled=True)]
    ppermute x12 -> x13, waiting for transfers between devices: 12.1 us -> 13 us  [swap(): return lax.ppermute(a, 'gx', [(i, i ^ mx) for i in range(self.gx)])]
    pallas_call x13 -> x14, Pallas kernels: 38.9 us -> 38 us  [call(): pl.pallas_call(kernel, out_shape=[jax.ShapeDtypeStruct(s, t) for s, t in...]
    ppermute x12 -> x13, starting transfers between devices: 6.4 us -> 6.91 us  [swap(): return lax.ppermute(a, 'gx', [(i, i ^ mx) for i in range(self.gx)])]
  transfers between devices with their start and end apart: 23 -> 24, of which waited for: 14 -> 15; matrix products, arithmetic and copies ran while one was open for 1% -> 1% of each run, Pallas kernels for 9% -> 9%
where the time goes in v5:
time: 129 us; the launch traced here: 128 us
  Pallas kernels  38 us (29%)
  waiting for transfers between devices  31.4 us (24%)
  blocking collectives  30.1 us (23%)
  starting transfers between devices  25.4 us (20%)
  local copies, waits for them, and re-layouts  1.78 us (1%)
  between operations  1.3 us (1%)
    pallas_call x14, Pallas kernels, call(): pl.pallas_call(kernel, out_shape=[jax.ShapeDtypeStruct(s, t) for s, t in...  38 us
    all_to_all x3, blocking collectives, exchange(): return lax.all_to_all(payload, AXES, 0, 0, tiled=True)  30.1 us
    ppermute x10, waiting for transfers between devices, swap(): return lax.ppermute(a, 'gy', [(i, i ^ my) for i in range(self.gy)])  14.6 us
    ppermute x10, starting transfers between devices, swap(): return lax.ppermute(a, 'gy', [(i, i ^ my) for i in range(self.gy)])  14.6 us
    ppermute x13, waiting for transfers between devices, swap(): return lax.ppermute(a, 'gx', [(i, i ^ mx) for i in range(self.gx)])  13 us
    ppermute x13, starting transfers between devices, swap(): return lax.ppermute(a, 'gx', [(i, i ^ mx) for i in range(self.gx)])  6.91 us
    all_to_all x1, starting transfers between devices, exchange(): return lax.all_to_all(payload, AXES, 0, 0, tiled=True)  3.87 us
    all_to_all x1, waiting for transfers between devices, exchange(): return lax.all_to_all(payload, AXES, 0, 0, tiled=True)  3.72 us
  transfers between devices with their start and end apart: 24, of which 15 were waited for; matrix products, arithmetic and copies ran while one was open for 1% of the time, Pallas kernels for 9%

profile of v5, /device:TPU:0, one launch (start us, length us, event | category | flops | bytes accessed | tf_op | source)
XLA Modules:
  0.0 128.4 jit_solution(7691399536279844942)
XLA Ops:
  1.8 5.1 %collective-permute-start.2 = (bf16[1,336,128]{2,1,0:T(8,128)(2,1)S(1)}, bf16[1,336,128]{2,1,0:T(8,128)(2,1)S(1)}, u32[]{:S(2)}, u32[]{:S(2)}) collective-permute-start(bf16[1,336,128]{2,1,0:T(8,128)(2,1)S(1)} %bitcast.58), channel_id=1, source_target_pairs={{0,6},{1,7},{2,4},{3,5},{4,2},{5,3},{6,0},{7,1},{8,14},{9,15},{10,... | collective-permute-start | bytes 258056 | tf_op jit(solution)/shard_map/ppermute | solution.py:117
  7.5 2.6 %hash.1 = (bf16[1024,1024]{1,0:T(8,128)(2,1)S(1)}, bf16[1024,1024]{1,0:T(8,128)(2,1)S(1)}) custom-call(s32[1024,1024]{1,0:T(8,128)} %codes_hbm.1, s32[8,1024]{1,0:T(8,128)} %offsets_hbm.1), custom_call_target="tpu_custom_call" | custom-call | flops 20000000 | bytes 200000 | tf_op jit(solution)/shard_map/hash/pallas_call | solution.py:60
  10.1 1.3 %copy-done = bf16[1024,1024]{1,0:T(8,128)(2,1)} copy-done((bf16[1024,1024]{1,0:T(8,128)(2,1)}, bf16[1024,1024]{1,0:T(8,128)(2,1)S(1)}, u32[]{:S(2)}) %copy-start) | copy-done | bytes 2097176
  11.5 2.6 %collective-permute-done.1 = bf16[1,336,128]{2,1,0:T(8,128)(2,1)S(1)} collective-permute-done((bf16[1,336,128]{2,1,0:T(8,128)(2,1)S(1)}, bf16[1,336,128]{2,1,0:T(8,128)(2,1)S(1)}, u32[]{:S(2)}, u32[]{:S(2)}) %collective-permute-start.1) | collective-permute-done | bytes 86048 | tf_op jit(solution)/shard_map/ppermute | solution.py:117
  14.1 1.6 %collective-permute-start.4 = (bf16[4,336,128]{2,1,0:T(8,128)(2,1)S(1)}, bf16[4,336,128]{2,1,0:T(8,128)(2,1)S(1)}, u32[]{:S(2)}, u32[]{:S(2)}) collective-permute-start(bf16[4,336,128]{2,1,0:T(8,128)(2,1)S(1)} %pad_maximum_fusion.refs_0_.refs_3_), channel_id=1, source_target_pairs={{0,1},{1,0},{2,3},{3,2},{4,5},{5,4},{6,7},{7,6},{8,9},{9,8},{10,11... | collective-permute-start | bytes 1032200 | tf_op jit(solution)/shard_map/ppermute | solution.py:117
  15.7 1.5 %collective-permute-start.3 = (bf16[4,336,128]{2,1,0:T(8,128)(2,1)S(1)}, bf16[4,336,128]{2,1,0:T(8,128)(2,1)S(1)}, u32[]{:S(2)}, u32[]{:S(2)}) collective-permute-start(bf16[4,336,128]{2,1,0:T(8,128)(2,1)S(1)} %pad_maximum_fusion.refs_0_.refs_3_), channel_id=1, source_target_pairs={{0,16},{8,24},{16,0},{24,8},{1,17},{9,25},{17,1},{25,9},{2,18},{10... | collective-permute-start | bytes 1032200 | tf_op jit(solution)/shard_map/ppermute | solution.py:115
  17.3 2.8 %prepare.1 = (f32[8,64,128]{2,1,0:T(8,128)S(1)}, f32[8,64,128]{2,1,0:T(8,128)S(1)}, f32[8,64,128]{2,1,0:T(8,128)S(1)}, f32[8,64,128]{2,1,0:T(8,128)S(1)}, f32[8,...) custom-call(f32[8,64,64]{2,1,0:T(8,128)} %w_hbm.3, f32[8,64,64]{2,1,0:T(8,128)} %left_hbm.1, f32[8,64,64]{2,1,0:T(8,128)} %right_hbm.1, ...), custom_call_target="tpu_custom_call" | custom-call | flops 10000000 | bytes 100000 | tf_op jit(solution)/shard_map/prepare/pallas_call | solution.py:60
  20.2 3.1 %collective-permute-done.4.refs_2_.refs_5_ = bf16[4,336,128]{2,1,0:T(8,128)(2,1)S(1)} collective-permute-done((bf16[4,336,128]{2,1,0:T(8,128)(2,1)S(1)}, bf16[4,336,128]{2,1,0:T(8,128)(2,1)S(1)}, u32[]{:S(2)}, u32[]{:S(2)}) %collective-permute-start.4) | collective-permute-done | bytes 344096 | tf_op jit(solution)/shard_map/ppermute | solution.py:117
  23.4 1.3 %collective-permute-done.3.refs_1_.refs_4_ = bf16[4,336,128]{2,1,0:T(8,128)(2,1)S(1)} collective-permute-done((bf16[4,336,128]{2,1,0:T(8,128)(2,1)S(1)}, bf16[4,336,128]{2,1,0:T(8,128)(2,1)S(1)}, u32[]{:S(2)}, u32[]{:S(2)}) %collective-permute-start.3) | collective-permute-done | bytes 344096 | tf_op jit(solution)/shard_map/ppermute | solution.py:115
  25.0 1.6 %collective-permute-start.6 = (bf16[4,176,128]{2,1,0:T(8,128)(2,1)S(1)}, bf16[4,176,128]{2,1,0:T(8,128)(2,1)S(1)}, u32[]{:S(2)}, u32[]{:S(2)}) collective-permute-start(bf16[4,176,128]{2,1,0:T(8,128)(2,1)S(1)} %slice_add_fusion), channel_id=1, source_target_pairs={{0,16},{8,24},{16,0},{24,8},{1,17},{9,25},{17,1},{25,9},{2,18},{10... | collective-permute-start | bytes 540680 | tf_op jit(solution)/shard_map/ppermute | solution.py:115
  28.2 1.7 %assemble.1.refs_2_ = bf16[2,1024,1024]{2,1,0:T(8,128)(2,1)S(1)} custom-call(s32[1]{0:T(128)} %bitcast.me_ref.refs_0_, s32[256]{0:T(256)S(1)} %copy-done.15, bf16[4,336,128]{2,1,0:T(8,128)(2,1)S(1)} %pad_maximum_fusion.refs_0_.refs_3_, bf16[4,336,128]{2,1,0:T(8,128)(2,1)S(1)} %collective-permute-done.3.refs_1_.refs_4_, ...), custom_call_target="tpu_custom_call" | custom-call | flops 10000000 | bytes 100000 | tf_op jit(solution)/shard_map/assemble/pallas_call | solution.py:60
  30.0 3.3 %collective-permute-done.5.refs_9_ = bf16[4,160,128]{2,1,0:T(8,128)(2,1)S(1)} collective-permute-done((bf16[4,160,128]{2,1,0:T(8,128)(2,1)S(1)}, bf16[4,160,128]{2,1,0:T(8,128)(2,1)S(1)}, u32[]{:S(2)}, u32[]{:S(2)}) %collective-permute-start.5) | collective-permute-done | bytes 163872 | tf_op jit(solution)/shard_map/ppermute | solution.py:117
  35.0 4.5 %pre.1 = (f32[1024,1024]{1,0:T(8,128)S(1)}, f32[8,128]{1,0:T(8,128)S(1)}, f32[8,128]{1,0:T(8,128)S(1)}, f32[32,128]{1,0:T(8,128)S(1)}, bf16[512,512]{1,0:T(8,128)(2,1)S(1)}, /*index=5*/bf16[2,1024,1024]{2,1,0:T(8,128)(2,1)S(1)}) custom-call(s32[1]{0:T(128)} %bitcast.me_ref.refs_0_, s32[256]{0:T(256)S(1)} %copy-done.15, ...), custom_call_target="tpu_custom_call", output_to_operand_aliasing={{5}: (2, {})} | custom-call | tf_op jit(solution)/shard_map/pre/pallas_call | solution.py:60
  40.9 10.1 %all_to_all.44 = f32[32,8,128]{2,1,0:T(8,128)S(1)} all-to-all(f32[32,8,128]{2,1,0:T(8,128)S(1)} %bitcast.55), channel_id=1, replica_groups=mesh['gx'=4,'gy'=8] {'gx','gy'}, dimensions={0} | all-to-all | bytes 262144 | tf_op jit(solution)/shard_map/all_to_all | solution.py:858
  51.0 4.9 %act.1 = (f32[1024,1024]{1,0:T(8,128)S(1)}, f32[32,1024]{1,0:T(8,128)S(1)}, f32[32,1024]{1,0:T(8,128)S(1)}, f32[32,1024]{1,0:T(8,128)S(1)}, f32[8,1024]{1,0:T(8,...) custom-call(f32[256,128]{1,0:T(8,128)S(1)} %bitcast.54, f32[32,128]{1,0:T(8,128)S(1)} %get-tuple-element.115.count_ref, ...), custom_call_target="tpu_custom_call" | custom-call | tf_op jit(solution)/shard_map/act/pallas_call | solution.py:60
  55.8 10.0 %all_to_all.45 = f32[32,8,128]{2,1,0:T(8,128)S(1)} all-to-all(f32[32,8,128]{2,1,0:T(8,128)S(1)} %bitcast.62), channel_id=1, replica_groups=mesh['gx'=4,'gy'=8] {'gx','gy'}, dimensions={0} | all-to-all | bytes 262144 | tf_op jit(solution)/shard_map/all_to_all | solution.py:858
  65.8 3.8 %loss.1 = (f32[32,1024]{1,0:T(8,128)S(1)}, f32[136,128]{1,0:T(8,128)S(1)}, f32[136,128]{1,0:T(8,128)S(1)}, f32[2,32,32]{2,1,0:T(8,128)S(1)}, f32[1,1]{1,0:T(1,128)}, /*index=5*/f32[1,1]{1,0:T(1,128)}) custom-call(s32[1]{0:T(128)} %bitcast.me_ref.refs_0_, f32[256,128]{1,0:T(8,128)S(1)} %bitcast.53, bf16[512,512]{1,0:T(8,128)(2,1)S(1)} %get-tuple-element.121.mask_ref, ...), custom_call_target="tpu_custom_call" | custom-call | tf_op jit(solution)/shard_map/loss/pallas_call | solution.py:60
  69.8 1.2 collective-permute-done.13.got_ref
  71.0 10.0 %all_to_all.46 = bf16[32,16,128]{2,1,0:T(8,128)(2,1)S(1)} all-to-all(bf16[32,16,128]{2,1,0:T(8,128)(2,1)S(1)} %bitcast.56), channel_id=1, replica_groups=mesh['gx'=4,'gy'=8] {'gx','gy'}, dimensions={0} | all-to-all | bytes 262144 | tf_op jit(solution)/shard_map/all_to_all | solution.py:858
  81.0 4.1 %grad.1 = (bf16[2048,128]{1,0:T(8,128)(2,1)S(1)}, bf16[2048,128]{1,0:T(8,128)(2,1)S(1)}, f32[8,128]{1,0:T(8,128)S(1)}, f32[16,128]{1,0:T(8,128)S(1)}, f32[2,512,1024]{2,1,0:T(8,128)S(1)}) custom-call(s32[1]{0:T(128)} %bitcast.me_ref.refs_0_, s32[256]{0:T(256)S(1)} %copy-done.15, bf16[512,128]{1,0:T(8,128)(2,1)S(1)} %bitcast.57, ...), custom_call_target="tpu_custom_call" | custom-call | tf_op jit(solution)/shard_map/grad/pallas_call | solution.py:60
  85.7 1.2 keep.1
  89.6 6.1 %collective-permute-done.15 = bf16[2,4,128,128]{3,2,1,0:T(8,128)(2,1)S(1)} collective-permute-done((bf16[2,4,128,128]{3,2,1,0:T(8,128)(2,1)S(1)}, bf16[2,4,128,128]{3,2,1,0:T(8,128)(2,1)S(1)}, u32[]{:S(2)}, u32[]{:S(2)}) %collective-permute-start.15) | collective-permute-done | bytes 262176 | tf_op jit(solution)/shard_map/ppermute | solution.py:115
  95.7 1.3 %collective-permute-start.16 = (bf16[4,128,128]{2,1,0:T(8,128)(2,1)S(1)}, bf16[4,128,128]{2,1,0:T(8,128)(2,1)S(1)}, u32[]{:S(2)}, u32[]{:S(2)}) collective-permute-start(bf16[4,128,128]{2,1,0:T(8,128)(2,1)S(1)} %fusion.4), channel_id=1, source_target_pairs={{0,1},{1,0},{2,3},{3,2},{4,5},{5,4},{6,7},{7,6},{8,9},{9,8},{10,11... | collective-permute-start | bytes 393224 | tf_op jit(solution)/shard_map/ppermute | solution.py:117
  97.9 2.8 %collective-permute-done.16 = bf16[4,128,128]{2,1,0:T(8,128)(2,1)S(1)} collective-permute-done((bf16[4,128,128]{2,1,0:T(8,128)(2,1)S(1)}, bf16[4,128,128]{2,1,0:T(8,128)(2,1)S(1)}, u32[]{:S(2)}, u32[]{:S(2)}) %collective-permute-start.16) | collective-permute-done | bytes 131104 | tf_op jit(solution)/shard_map/ppermute | solution.py:117
  100.8 1.3 %collective-permute-done.19 = bf16[4,128,128]{2,1,0:T(8,128)(2,1)S(1)} collective-permute-done((bf16[4,128,128]{2,1,0:T(8,128)(2,1)S(1)}, bf16[4,128,128]{2,1,0:T(8,128)(2,1)S(1)}, u32[]{:S(2)}, u32[]{:S(2)}) %collective-permute-start.19) | collective-permute-done | bytes 131104 | tf_op jit(solution)/shard_map/ppermute | solution.py:115
  102.2 1.4 %collective-permute-start.22 = (bf16[256,128]{1,0:T(8,128)(2,1)S(1)}, bf16[256,128]{1,0:T(8,128)(2,1)S(1)}, u32[]{:S(2)}, u32[]{:S(2)}) collective-permute-start(bf16[256,128]{1,0:T(8,128)(2,1)S(1)} %get-tuple-element.176), channel_id=1, source_target_pairs={{0,6},{1,7},{2,4},{3,5},{4,2},{5,3},{6,0},{7,1},{8,14},{9,15},{10,... | collective-permute-start | bytes 196616 | tf_op jit(solution)/shard_map/ppermute | solution.py:117
  103.7 3.0 %collective-permute-start.21 = (bf16[256,128]{1,0:T(8,128)(2,1)S(1)}, bf16[256,128]{1,0:T(8,128)(2,1)S(1)}, u32[]{:S(2)}, u32[]{:S(2)}) collective-permute-start(bf16[256,128]{1,0:T(8,128)(2,1)S(1)} %get-tuple-element.178), channel_id=1, source_target_pairs={{0,4},{1,5},{2,6},{3,7},{4,0},{5,1},{6,2},{7,3},{8,12},{9,13},{10,... | collective-permute-start | bytes 196616 | tf_op jit(solution)/shard_map/ppermute | solution.py:117
  106.7 1.8 %collective-permute-done.22.refs_5_ = bf16[256,128]{1,0:T(8,128)(2,1)S(1)} collective-permute-done((bf16[256,128]{1,0:T(8,128)(2,1)S(1)}, bf16[256,128]{1,0:T(8,128)(2,1)S(1)}, u32[]{:S(2)}, u32[]{:S(2)}) %collective-permute-start.22) | collective-permute-done | bytes 65568 | tf_op jit(solution)/shard_map/ppermute | solution.py:117
  110.2 3.9 %all-to-all-start.3 = ((bf16[32,16,128]{2,1,0:T(8,128)(2,1)}), bf16[32,16,128]{2,1,0:T(8,128)(2,1)S(1)}, u32[]{:S(2)}, u32[]{:S(2)}) async-start(bf16[32,16,128]{2,1,0:T(8,128)(2,1)} %bitcast.24), calls=%async_computation.3 | async-start | bytes 262144 | tf_op jit(solution)/shard_map/all_to_all | solution.py:858
  114.1 3.8 %turn.1 = (f32[8,64,128]{2,1,0:T(8,128)S(1)}, f32[8,64,128]{2,1,0:T(8,128)S(1)}, f32[8,64,128]{2,1,0:T(8,128)S(1)}, f32[8,128]{1,0:T(8,128)S(1)}, f32[4,32,1024]...) custom-call(s32[1]{0:T(128)} %bitcast.me_ref.refs_0_, s32[256]{0:T(256)S(1)} %copy-done.15, ...), custom_call_target="tpu_custom_call" | custom-call | flops 10000000 | bytes 100000 | tf_op jit(solution)/shard_map/turn/pallas_call | solution.py:60
  117.9 3.7 %all-to-all-done.3 = bf16[32,16,128]{2,1,0:T(8,128)(2,1)S(1)} async-done(((bf16[32,16,128]{2,1,0:T(8,128)(2,1)}), bf16[32,16,128]{2,1,0:T(8,128)(2,1)S(1)}, u32[]{:S(2)}, u32[]{:S(2)}) %all-to-all-start.3) | async-done | bytes 131104 | tf_op jit(solution)/shard_map/all_to_all | solution.py:858
  121.6 6.6 %step.1 = (f32[8,64,64]{2,1,0:T(8,128)}, bf16[8,64,64]{2,1,0:T(8,128)(2,1)}, f32[8,64,64]{2,1,0:T(8,128)}, f32[8,64,64]{2,1,0:T(8,128)}, f32[8,64,64]{2,1,0:T(8,...) custom-call(bf16[512,128]{1,0:T(8,128)(2,1)S(1)} %bitcast.52, ...), custom_call_target="tpu_custom_call" | custom-call | tf_op jit(solution)/shard_map/step/pallas_call | solution.py:60
  (89 shorter events, 13.2 us)
Async XLA Ops:
  1.7 26.5 %copy-start.15 = (s32[256]{0:T(256)S(1)}, s32[256]{0:T(256)}, u32[]{:S(2)}) copy-start(s32[256]{0:T(256)} %owners_ref.7) | copy-start | bytes 3076
  1.8 9.7 %collective-permute-start.2 = (bf16[1,336,128]{2,1,0:T(8,128)(2,1)S(1)}, bf16[1,336,128]{2,1,0:T(8,128)(2,1)S(1)}, u32[]{:S(2)}, u32[]{:S(2)}) collective-permute-start(bf16[1,336,128]{2,1,0:T(8,128)(2,1)S(1)} %bitcast.58), channel_id=1, source_target_pairs={{0,6},{1,7},{2,4},{3,5},{4,2},{5,3},{6,0},{7,1},{8,14},{9,15},{10,... | collective-permute-start | bytes 258056 | tf_op jit(solution)/shard_map/ppermute | solution.py:117
  6.9 7.2 %collective-permute-start.1 = (bf16[1,336,128]{2,1,0:T(8,128)(2,1)S(1)}, bf16[1,336,128]{2,1,0:T(8,128)(2,1)S(1)}, u32[]{:S(2)}, u32[]{:S(2)}) collective-permute-start(bf16[1,336,128]{2,1,0:T(8,128)(2,1)S(1)} %bitcast.59), channel_id=1, source_target_pairs={{0,4},{1,5},{2,6},{3,7},{4,0},{5,1},{6,2},{7,3},{8,12},{9,13},{10,... | collective-permute-start | bytes 258056 | tf_op jit(solution)/shard_map/ppermute | solution.py:117
  6.9 7.2 %collective-permute-start = (bf16[1,336,128]{2,1,0:T(8,128)(2,1)S(1)}, bf16[1,336,128]{2,1,0:T(8,128)(2,1)S(1)}, u32[]{:S(2)}, u32[]{:S(2)}) collective-permute-start(bf16[1,336,128]{2,1,0:T(8,128)(2,1)S(1)} %bitcast.60), channel_id=1, source_target_pairs={{0,2},{1,3},{2,0},{3,1},{4,6},{5,7},{6,4},{7,5},{8,10},{9,11},{10,... | collective-permute-start | bytes 258056 | tf_op jit(solution)/shard_map/ppermute | solution.py:117
  14.1 9.2 %collective-permute-start.4 = (bf16[4,336,128]{2,1,0:T(8,128)(2,1)S(1)}, bf16[4,336,128]{2,1,0:T(8,128)(2,1)S(1)}, u32[]{:S(2)}, u32[]{:S(2)}) collective-permute-start(bf16[4,336,128]{2,1,0:T(8,128)(2,1)S(1)} %pad_maximum_fusion.refs_0_.refs_3_), channel_id=1, source_target_pairs={{0,1},{1,0},{2,3},{3,2},{4,5},{5,4},{6,7},{7,6},{8,9},{9,8},{10,11... | collective-permute-start | bytes 1032200 | tf_op jit(solution)/shard_map/ppermute | solution.py:117
  15.7 9.0 %collective-permute-start.3 = (bf16[4,336,128]{2,1,0:T(8,128)(2,1)S(1)}, bf16[4,336,128]{2,1,0:T(8,128)(2,1)S(1)}, u32[]{:S(2)}, u32[]{:S(2)}) collective-permute-start(bf16[4,336,128]{2,1,0:T(8,128)(2,1)S(1)} %pad_maximum_fusion.refs_0_.refs_3_), channel_id=1, source_target_pairs={{0,16},{8,24},{16,0},{24,8},{1,17},{9,25},{17,1},{25,9},{2,18},{10... | collective-permute-start | bytes 1032200 | tf_op jit(solution)/shard_map/ppermute | solution.py:115
  20.2 7.2 %collective-permute-start.7 = (bf16[4,336,128]{2,1,0:T(8,128)(2,1)S(1)}, bf16[4,336,128]{2,1,0:T(8,128)(2,1)S(1)}, u32[]{:S(2)}, u32[]{:S(2)}) collective-permute-start(bf16[4,336,128]{2,1,0:T(8,128)(2,1)S(1)} %pad_maximum_fusion.refs_0_.refs_3_), channel_id=1, source_target_pairs={{0,8},{8,0},{16,24},{24,16},{1,9},{9,1},{17,25},{25,17},{2,10},{10... | collective-permute-start | bytes 1032200 | tf_op jit(solution)/shard_map/ppermute | solution.py:115
  24.9 3.3 %collective-permute-start.9 = (bf16[4,336,128]{2,1,0:T(8,128)(2,1)S(1)}, bf16[4,336,128]{2,1,0:T(8,128)(2,1)S(1)}, u32[]{:S(2)}, u32[]{:S(2)}) collective-permute-start(bf16[4,336,128]{2,1,0:T(8,128)(2,1)S(1)} %collective-permute-done.4.refs_2_.refs_5_), channel_id=1, source_target_pairs={{0,8},{8,0},{16,24},{24,16},{1,9},{9,1},{17,25},{25,17},{2,10},{10... | collective-permute-start | bytes 1032200 | tf_op jit(solution)/shard_map/ppermute | solution.py:115
  25.0 8.3 %collective-permute-start.6 = (bf16[4,176,128]{2,1,0:T(8,128)(2,1)S(1)}, bf16[4,176,128]{2,1,0:T(8,128)(2,1)S(1)}, u32[]{:S(2)}, u32[]{:S(2)}) collective-permute-start(bf16[4,176,128]{2,1,0:T(8,128)(2,1)S(1)} %slice_add_fusion), channel_id=1, source_target_pairs={{0,16},{8,24},{16,0},{24,8},{1,17},{9,25},{17,1},{25,9},{2,18},{10... | collective-permute-start | bytes 540680 | tf_op jit(solution)/shard_map/ppermute | solution.py:115
  26.6 1.7 %collective-permute-start.8 = (bf16[4,336,128]{2,1,0:T(8,128)(2,1)S(1)}, bf16[4,336,128]{2,1,0:T(8,128)(2,1)S(1)}, u32[]{:S(2)}, u32[]{:S(2)}) collective-permute-start(bf16[4,336,128]{2,1,0:T(8,128)(2,1)S(1)} %collective-permute-done.3.refs_1_.refs_4_), channel_id=1, source_target_pairs={{0,8},{8,0},{16,24},{24,16},{1,9},{9,1},{17,25},{25,17},{2,10},{10... | collective-permute-start | bytes 1032200 | tf_op jit(solution)/shard_map/ppermute | solution.py:115
  26.8 6.5 %collective-permute-start.5 = (bf16[4,160,128]{2,1,0:T(8,128)(2,1)S(1)}, bf16[4,160,128]{2,1,0:T(8,128)(2,1)S(1)}, u32[]{:S(2)}, u32[]{:S(2)}) collective-permute-start(bf16[4,160,128]{2,1,0:T(8,128)(2,1)S(1)} %slice_add_fusion.1), channel_id=1, source_target_pairs={{0,1},{1,0},{2,3},{3,2},{4,5},{5,4},{6,7},{7,6},{8,9},{9,8},{10,11... | collective-permute-start | bytes 491528 | tf_op jit(solution)/shard_map/ppermute | solution.py:117
  33.3 1.7 %collective-permute-start.11 = (bf16[4,176,128]{2,1,0:T(8,128)(2,1)S(1)}, bf16[4,176,128]{2,1,0:T(8,128)(2,1)S(1)}, u32[]{:S(2)}, u32[]{:S(2)}) collective-permute-start(bf16[4,176,128]{2,1,0:T(8,128)(2,1)S(1)} %collective-permute-done.6.refs_10_), channel_id=1, source_target_pairs={{0,8},{8,0},{16,24},{24,16},{1,9},{9,1},{17,25},{25,17},{2,10},{10... | collective-permute-start | bytes 540680 | tf_op jit(solution)/shard_map/ppermute | solution.py:115
  33.3 1.7 %collective-permute-start.10 = (bf16[4,160,128]{2,1,0:T(8,128)(2,1)S(1)}, bf16[4,160,128]{2,1,0:T(8,128)(2,1)S(1)}, u32[]{:S(2)}, u32[]{:S(2)}) collective-permute-start(bf16[4,160,128]{2,1,0:T(8,128)(2,1)S(1)} %collective-permute-done.5.refs_9_), channel_id=1, source_target_pairs={{0,8},{8,0},{16,24},{24,16},{1,9},{9,1},{17,25},{25,17},{2,10},{10... | collective-permute-start | bytes 491528 | tf_op jit(solution)/shard_map/ppermute | solution.py:115
  39.5 26.3 %copy-start.13 = (f32[2,32,32]{2,1,0:T(8,128)S(1)}, f32[2,32,32]{2,1,0:T(8,128)}, u32[]{:S(2)}) copy-start(f32[2,32,32]{2,1,0:T(8,128)} %wt_hbm.1) | copy-start | bytes 24580
  39.5 41.5 %copy-start.1 = (bf16[1024,1024]{1,0:T(8,128)(2,1)S(1)}, bf16[1024,1024]{1,0:T(8,128)(2,1)}, u32[]{:S(2)}) copy-start(bf16[1024,1024]{1,0:T(8,128)(2,1)} %copy-done) | copy-start | bytes 6291460
  39.5 1.2 collective-permute-start.12
  69.6 1.3 %collective-permute-start.13 = (f32[136,128]{1,0:T(8,128)S(1)}, f32[136,128]{1,0:T(8,128)S(1)}, u32[]{:S(2)}, u32[]{:S(2)}) collective-permute-start(f32[136,128]{1,0:T(8,128)S(1)} %get-tuple-element.128), channel_id=1, source_target_pairs={{0,8},{8,0},{16,24},{24,16},{1,9},{9,1},{17,25},{25,17},{2,10},{10... | collective-permute-start | bytes 208904 | tf_op jit(solution)/shard_map/ppermute | solution.py:115
  85.1 2.0 %collective-permute-start.14 = (bf16[2048,128]{1,0:T(8,128)(2,1)S(1)}, bf16[2048,128]{1,0:T(8,128)(2,1)S(1)}, u32[]{:S(2)}, u32[]{:S(2)}) collective-permute-start(bf16[2048,128]{1,0:T(8,128)(2,1)S(1)} %get-tuple-element.135), channel_id=1, source_target_pairs={{0,8},{8,0},{16,24},{24,16},{1,9},{9,1},{17,25},{25,17},{2,10},{10... | collective-permute-start | bytes 1572872 | tf_op jit(solution)/shard_map/ppermute | solution.py:115
  85.3 3.0 %collective-permute-start.17 = (bf16[2048,128]{1,0:T(8,128)(2,1)S(1)}, bf16[2048,128]{1,0:T(8,128)(2,1)S(1)}, u32[]{:S(2)}, u32[]{:S(2)}) collective-permute-start(bf16[2048,128]{1,0:T(8,128)(2,1)S(1)} %get-tuple-element.137), channel_id=1, source_target_pairs={{0,8},{8,0},{16,24},{24,16},{1,9},{9,1},{17,25},{25,17},{2,10},{10... | collective-permute-start | bytes 1572872 | tf_op jit(solution)/shard_map/ppermute | solution.py:115
  87.2 8.4 %collective-permute-start.15 = (bf16[2,4,128,128]{3,2,1,0:T(8,128)(2,1)S(1)}, bf16[2,4,128,128]{3,2,1,0:T(8,128)(2,1)S(1)}, u32[]{:S(2)}, u32[]{:S(2)}) collective-permute-start(bf16[2,4,128,128]{3,2,1,0:T(8,128)(2,1)S(1)} %bitcast.66), channel_id=1, source_target_pairs={{0,16},{8,24},{16,0},{24,8},{1,17},{9,25},{17,1},{25,9},{2,18},{10... | collective-permute-start | bytes 786440 | tf_op jit(solution)/shard_map/ppermute | solution.py:115
  88.4 33.2 %copy-start.4 = (f32[8,64,128]{2,1,0:T(8,128)S(1)}, f32[8,64,128]{2,1,0:T(8,128)}, u32[]{:S(2)}) copy-start(f32[8,64,128]{2,1,0:T(8,128)} %copy-done.3) | copy-start | bytes 786436
  88.4 33.1 %copy-start.6 = (f32[8,64,128]{2,1,0:T(8,128)S(1)}, f32[8,64,128]{2,1,0:T(8,128)}, u32[]{:S(2)}) copy-start(f32[8,64,128]{2,1,0:T(8,128)} %copy-done.5) | copy-start | bytes 786436
  88.4 33.1 %copy-start.8 = (f32[8,64,128]{2,1,0:T(8,128)S(1)}, f32[8,64,128]{2,1,0:T(8,128)}, u32[]{:S(2)}) copy-start(f32[8,64,128]{2,1,0:T(8,128)} %copy-done.7) | copy-start | bytes 786436
  88.5 33.1 %copy-start.10 = (f32[8,64,64]{2,1,0:T(8,128)S(1)}, f32[8,64,64]{2,1,0:T(8,128)}, u32[]{:S(2)}) copy-start(f32[8,64,64]{2,1,0:T(8,128)} %copy-done.9) | copy-start | bytes 393220
  88.5 33.1 %copy-start.12 = (f32[8,64,128]{2,1,0:T(8,128)S(1)}, f32[8,64,128]{2,1,0:T(8,128)}, u32[]{:S(2)}) copy-start(f32[8,64,128]{2,1,0:T(8,128)} %copy-done.11) | copy-start | bytes 786436
  88.6 8.4 %collective-permute-start.18 = (bf16[2,4,128,128]{3,2,1,0:T(8,128)(2,1)S(1)}, bf16[2,4,128,128]{3,2,1,0:T(8,128)(2,1)S(1)}, u32[]{:S(2)}, u32[]{:S(2)}) collective-permute-start(bf16[2,4,128,128]{3,2,1,0:T(8,128)(2,1)S(1)} %fusion.1), channel_id=1, source_target_pairs={{0,1},{1,0},{2,3},{3,2},{4,5},{5,4},{6,7},{7,6},{8,9},{9,8},{10,11... | collective-permute-start | bytes 786440 | tf_op jit(solution)/shard_map/ppermute | solution.py:117
  95.7 5.0 %collective-permute-start.16 = (bf16[4,128,128]{2,1,0:T(8,128)(2,1)S(1)}, bf16[4,128,128]{2,1,0:T(8,128)(2,1)S(1)}, u32[]{:S(2)}, u32[]{:S(2)}) collective-permute-start(bf16[4,128,128]{2,1,0:T(8,128)(2,1)S(1)} %fusion.4), channel_id=1, source_target_pairs={{0,1},{1,0},{2,3},{3,2},{4,5},{5,4},{6,7},{7,6},{8,9},{9,8},{10,11... | collective-permute-start | bytes 393224 | tf_op jit(solution)/shard_map/ppermute | solution.py:117
  97.1 5.0 %collective-permute-start.19 = (bf16[4,128,128]{2,1,0:T(8,128)(2,1)S(1)}, bf16[4,128,128]{2,1,0:T(8,128)(2,1)S(1)}, u32[]{:S(2)}, u32[]{:S(2)}) collective-permute-start(bf16[4,128,128]{2,1,0:T(8,128)(2,1)S(1)} %fusion.5), channel_id=1, source_target_pairs={{0,16},{8,24},{16,0},{24,8},{1,17},{9,25},{17,1},{25,9},{2,18},{10... | collective-permute-start | bytes 393224 | tf_op jit(solution)/shard_map/ppermute | solution.py:115
  102.2 6.2 %collective-permute-start.22 = (bf16[256,128]{1,0:T(8,128)(2,1)S(1)}, bf16[256,128]{1,0:T(8,128)(2,1)S(1)}, u32[]{:S(2)}, u32[]{:S(2)}) collective-permute-start(bf16[256,128]{1,0:T(8,128)(2,1)S(1)} %get-tuple-element.176), channel_id=1, source_target_pairs={{0,6},{1,7},{2,4},{3,5},{4,2},{5,3},{6,0},{7,1},{8,14},{9,15},{10,... | collective-permute-start | bytes 196616 | tf_op jit(solution)/shard_map/ppermute | solution.py:117
  103.7 5.7 %collective-permute-start.20 = (bf16[256,128]{1,0:T(8,128)(2,1)S(1)}, bf16[256,128]{1,0:T(8,128)(2,1)S(1)}, u32[]{:S(2)}, u32[]{:S(2)}) collective-permute-start(bf16[256,128]{1,0:T(8,128)(2,1)S(1)} %get-tuple-element.177), channel_id=1, source_target_pairs={{0,2},{1,3},{2,0},{3,1},{4,6},{5,7},{6,4},{7,5},{8,10},{9,11},{10,... | collective-permute-start | bytes 196616 | tf_op jit(solution)/shard_map/ppermute | solution.py:117
  103.7 5.7 %collective-permute-start.21 = (bf16[256,128]{1,0:T(8,128)(2,1)S(1)}, bf16[256,128]{1,0:T(8,128)(2,1)S(1)}, u32[]{:S(2)}, u32[]{:S(2)}) collective-permute-start(bf16[256,128]{1,0:T(8,128)(2,1)S(1)} %get-tuple-element.178), channel_id=1, source_target_pairs={{0,4},{1,5},{2,6},{3,7},{4,0},{5,1},{6,2},{7,3},{8,12},{9,13},{10,... | collective-permute-start | bytes 196616 | tf_op jit(solution)/shard_map/ppermute | solution.py:117
  110.2 11.4 %all-to-all-start.3 = ((bf16[32,16,128]{2,1,0:T(8,128)(2,1)}), bf16[32,16,128]{2,1,0:T(8,128)(2,1)S(1)}, u32[]{:S(2)}, u32[]{:S(2)}) async-start(bf16[32,16,128]{2,1,0:T(8,128)(2,1)} %bitcast.24), calls=%async_computation.3 | async-start | bytes 262144 | tf_op jit(solution)/shard_map/all_to_all | solution.py:858
  (9 other events, 134.3 us)

commit v6 on v5

--- a/solution.py
+++ b/solution.py
@@ -475,8 +475,9 @@
         halves_ref[h, half + t : half + t + 1, :] = d_gain[:, cols]
         halves_ref[h, pl.ds(tiles + t, embed, stride=half), :] = second[:, cols]
     odd = (me // core) % 2
-    keep_ref[...] = jnp.where(odd == 1, halves_ref[1], halves_ref[0])
-    send_ref[...] = jnp.where(odd == 1, halves_ref[0], halves_ref[1])
+    one, two = (halves_ref[h, : keep_ref.shape[0], :] for h in range(2))
+    keep_ref[...] = jnp.where(odd == 1, two, one)
+    send_ref[...] = jnp.where(odd == 1, one, two)
 
 
 def share_kernel(keep_ref, got_ref, pay_ref, *, n, tiles):
@@ -983,8 +984,8 @@
         [stats, counts, w_norm, pre, live, chosen, turned_out],
         scratch=[
             pltpu.VMEM((slots, LANES), BF),
-            pltpu.VMEM((tiles, bags * 8, LANES), F32),
-            pltpu.VMEM((tiles, bags * 8, LANES), F32),
+            pltpu.VMEM((tiles, bags * 8 + 8, LANES), F32),
+            pltpu.VMEM((tiles, bags * 8 + 8, LANES), F32),
         ],
         limit=12,
         name="act",
@@ -1010,7 +1011,7 @@
                 pltpu.VMEM((total_rows, total_rows), F32),
                 pltpu.VMEM((total_rows, embed), F32),
                 pltpu.VMEM((total_rows, embed), F32),
-                pltpu.VMEM((2, *shared), F32),
+                pltpu.VMEM((2, shared[0] + 8, LANES), F32),
             ],
             name="loss",
         )
@@ -1103,7 +1104,7 @@
             pltpu.VMEM(twin, F32),
             pltpu.VMEM((embed, width), F32),
             pltpu.VMEM((2, width), F32),
-            pltpu.VMEM((embed * tiles, LANES), F32),
+            pltpu.VMEM((embed * tiles + tiles, LANES), F32),
         ],
         name="step",
     )

time: 129 us -> 129 us (level)
  no operation moved by 1% of the time
where the time goes in v6:
time: 129 us; the launch traced here: 128 us
  Pallas kernels  38 us (29%)
  waiting for transfers between devices  31.4 us (24%)
  blocking collectives  30.1 us (23%)
  starting transfers between devices  25.4 us (20%)
  local copies, waits for them, and re-layouts  1.78 us (1%)
  between operations  1.3 us (1%)
    pallas_call x14, Pallas kernels, call(): pl.pallas_call(kernel, out_shape=[jax.ShapeDtypeStruct(s, t) for s, t in...  38 us
    all_to_all x3, blocking collectives, exchange(): return lax.all_to_all(payload, AXES, 0, 0, tiled=True)  30.1 us
    ppermute x10, starting transfers between devices, swap(): return lax.ppermute(a, 'gy', [(i, i ^ my) for i in range(self.gy)])  14.6 us
    ppermute x10, waiting for transfers between devices, swap(): return lax.ppermute(a, 'gy', [(i, i ^ my) for i in range(self.gy)])  14.6 us
    ppermute x13, waiting for transfers between devices, swap(): return lax.ppermute(a, 'gx', [(i, i ^ mx) for i in range(self.gx)])  13 us
    ppermute x13, starting transfers between devices, swap(): return lax.ppermute(a, 'gx', [(i, i ^ mx) for i in range(self.gx)])  6.91 us
    all_to_all x1, starting transfers between devices, exchange(): return lax.all_to_all(payload, AXES, 0, 0, tiled=True)  3.87 us
    all_to_all x1, waiting for transfers between devices, exchange(): return lax.all_to_all(payload, AXES, 0, 0, tiled=True)  3.72 us
  transfers between devices with their start and end apart: 24, of which 15 were waited for; matrix products, arithmetic and copies ran while one was open for 1% of the time, Pallas kernels for 9%

profile of v6, /device:TPU:0, one launch (start us, length us, event | category | flops | bytes accessed | tf_op | source)
XLA Modules:
  0.0 128.4 jit_solution(14025959527244190519)
XLA Ops:
  1.8 5.1 %collective-permute-start.2 = (bf16[1,336,128]{2,1,0:T(8,128)(2,1)S(1)}, bf16[1,336,128]{2,1,0:T(8,128)(2,1)S(1)}, u32[]{:S(2)}, u32[]{:S(2)}) collective-permute-start(bf16[1,336,128]{2,1,0:T(8,128)(2,1)S(1)} %bitcast.58), channel_id=1, source_target_pairs={{0,6},{1,7},{2,4},{3,5},{4,2},{5,3},{6,0},{7,1},{8,14},{9,15},{10,... | collective-permute-start | bytes 258056 | tf_op jit(solution)/shard_map/ppermute | solution.py:117
  7.5 2.6 %hash.1 = (bf16[1024,1024]{1,0:T(8,128)(2,1)S(1)}, bf16[1024,1024]{1,0:T(8,128)(2,1)S(1)}) custom-call(s32[1024,1024]{1,0:T(8,128)} %codes_hbm.1, s32[8,1024]{1,0:T(8,128)} %offsets_hbm.1), custom_call_target="tpu_custom_call" | custom-call | flops 20000000 | bytes 200000 | tf_op jit(solution)/shard_map/hash/pallas_call | solution.py:60
  10.1 1.3 %copy-done = bf16[1024,1024]{1,0:T(8,128)(2,1)} copy-done((bf16[1024,1024]{1,0:T(8,128)(2,1)}, bf16[1024,1024]{1,0:T(8,128)(2,1)S(1)}, u32[]{:S(2)}) %copy-start) | copy-done | bytes 2097176
  11.5 2.6 %collective-permute-done.1 = bf16[1,336,128]{2,1,0:T(8,128)(2,1)S(1)} collective-permute-done((bf16[1,336,128]{2,1,0:T(8,128)(2,1)S(1)}, bf16[1,336,128]{2,1,0:T(8,128)(2,1)S(1)}, u32[]{:S(2)}, u32[]{:S(2)}) %collective-permute-start.1) | collective-permute-done | bytes 86048 | tf_op jit(solution)/shard_map/ppermute | solution.py:117
  14.1 1.6 %collective-permute-start.4 = (bf16[4,336,128]{2,1,0:T(8,128)(2,1)S(1)}, bf16[4,336,128]{2,1,0:T(8,128)(2,1)S(1)}, u32[]{:S(2)}, u32[]{:S(2)}) collective-permute-start(bf16[4,336,128]{2,1,0:T(8,128)(2,1)S(1)} %pad_maximum_fusion.refs_0_.refs_3_), channel_id=1, source_target_pairs={{0,1},{1,0},{2,3},{3,2},{4,5},{5,4},{6,7},{7,6},{8,9},{9,8},{10,11... | collective-permute-start | bytes 1032200 | tf_op jit(solution)/shard_map/ppermute | solution.py:117
  15.7 1.5 %collective-permute-start.3 = (bf16[4,336,128]{2,1,0:T(8,128)(2,1)S(1)}, bf16[4,336,128]{2,1,0:T(8,128)(2,1)S(1)}, u32[]{:S(2)}, u32[]{:S(2)}) collective-permute-start(bf16[4,336,128]{2,1,0:T(8,128)(2,1)S(1)} %pad_maximum_fusion.refs_0_.refs_3_), channel_id=1, source_target_pairs={{0,16},{8,24},{16,0},{24,8},{1,17},{9,25},{17,1},{25,9},{2,18},{10... | collective-permute-start | bytes 1032200 | tf_op jit(solution)/shard_map/ppermute | solution.py:115
  17.3 2.8 %prepare.1 = (f32[8,64,128]{2,1,0:T(8,128)S(1)}, f32[8,64,128]{2,1,0:T(8,128)S(1)}, f32[8,64,128]{2,1,0:T(8,128)S(1)}, f32[8,64,128]{2,1,0:T(8,128)S(1)}, f32[8,...) custom-call(f32[8,64,64]{2,1,0:T(8,128)} %w_hbm.3, f32[8,64,64]{2,1,0:T(8,128)} %left_hbm.1, f32[8,64,64]{2,1,0:T(8,128)} %right_hbm.1, ...), custom_call_target="tpu_custom_call" | custom-call | flops 10000000 | bytes 100000 | tf_op jit(solution)/shard_map/prepare/pallas_call | solution.py:60
  20.2 3.1 %collective-permute-done.4.refs_2_.refs_5_ = bf16[4,336,128]{2,1,0:T(8,128)(2,1)S(1)} collective-permute-done((bf16[4,336,128]{2,1,0:T(8,128)(2,1)S(1)}, bf16[4,336,128]{2,1,0:T(8,128)(2,1)S(1)}, u32[]{:S(2)}, u32[]{:S(2)}) %collective-permute-start.4) | collective-permute-done | bytes 344096 | tf_op jit(solution)/shard_map/ppermute | solution.py:117
  23.4 1.3 %collective-permute-done.3.refs_1_.refs_4_ = bf16[4,336,128]{2,1,0:T(8,128)(2,1)S(1)} collective-permute-done((bf16[4,336,128]{2,1,0:T(8,128)(2,1)S(1)}, bf16[4,336,128]{2,1,0:T(8,128)(2,1)S(1)}, u32[]{:S(2)}, u32[]{:S(2)}) %collective-permute-start.3) | collective-permute-done | bytes 344096 | tf_op jit(solution)/shard_map/ppermute | solution.py:115
  25.0 1.6 %collective-permute-start.6 = (bf16[4,176,128]{2,1,0:T(8,128)(2,1)S(1)}, bf16[4,176,128]{2,1,0:T(8,128)(2,1)S(1)}, u32[]{:S(2)}, u32[]{:S(2)}) collective-permute-start(bf16[4,176,128]{2,1,0:T(8,128)(2,1)S(1)} %slice_add_fusion), channel_id=1, source_target_pairs={{0,16},{8,24},{16,0},{24,8},{1,17},{9,25},{17,1},{25,9},{2,18},{10... | collective-permute-start | bytes 540680 | tf_op jit(solution)/shard_map/ppermute | solution.py:115
  28.2 1.7 %assemble.1.refs_2_ = bf16[2,1024,1024]{2,1,0:T(8,128)(2,1)S(1)} custom-call(s32[1]{0:T(128)} %bitcast.me_ref.refs_0_, s32[256]{0:T(256)S(1)} %copy-done.15, bf16[4,336,128]{2,1,0:T(8,128)(2,1)S(1)} %pad_maximum_fusion.refs_0_.refs_3_, bf16[4,336,128]{2,1,0:T(8,128)(2,1)S(1)} %collective-permute-done.3.refs_1_.refs_4_, ...), custom_call_target="tpu_custom_call" | custom-call | flops 10000000 | bytes 100000 | tf_op jit(solution)/shard_map/assemble/pallas_call | solution.py:60
  30.0 3.3 %collective-permute-done.5.refs_9_ = bf16[4,160,128]{2,1,0:T(8,128)(2,1)S(1)} collective-permute-done((bf16[4,160,128]{2,1,0:T(8,128)(2,1)S(1)}, bf16[4,160,128]{2,1,0:T(8,128)(2,1)S(1)}, u32[]{:S(2)}, u32[]{:S(2)}) %collective-permute-start.5) | collective-permute-done | bytes 163872 | tf_op jit(solution)/shard_map/ppermute | solution.py:117
  35.0 4.5 %pre.1 = (f32[1024,1024]{1,0:T(8,128)S(1)}, f32[8,128]{1,0:T(8,128)S(1)}, f32[8,128]{1,0:T(8,128)S(1)}, f32[32,128]{1,0:T(8,128)S(1)}, bf16[512,512]{1,0:T(8,128)(2,1)S(1)}, /*index=5*/bf16[2,1024,1024]{2,1,0:T(8,128)(2,1)S(1)}) custom-call(s32[1]{0:T(128)} %bitcast.me_ref.refs_0_, s32[256]{0:T(256)S(1)} %copy-done.15, ...), custom_call_target="tpu_custom_call", output_to_operand_aliasing={{5}: (2, {})} | custom-call | tf_op jit(solution)/shard_map/pre/pallas_call | solution.py:60
  40.9 10.1 %all_to_all.44 = f32[32,8,128]{2,1,0:T(8,128)S(1)} all-to-all(f32[32,8,128]{2,1,0:T(8,128)S(1)} %bitcast.55), channel_id=1, replica_groups=mesh['gx'=4,'gy'=8] {'gx','gy'}, dimensions={0} | all-to-all | bytes 262144 | tf_op jit(solution)/shard_map/all_to_all | solution.py:859
  51.0 4.9 %act.1 = (f32[1024,1024]{1,0:T(8,128)S(1)}, f32[32,1024]{1,0:T(8,128)S(1)}, f32[32,1024]{1,0:T(8,128)S(1)}, f32[32,1024]{1,0:T(8,128)S(1)}, f32[8,1024]{1,0:T(8,...) custom-call(f32[256,128]{1,0:T(8,128)S(1)} %bitcast.54, f32[32,128]{1,0:T(8,128)S(1)} %get-tuple-element.115.count_ref, ...), custom_call_target="tpu_custom_call" | custom-call | tf_op jit(solution)/shard_map/act/pallas_call | solution.py:60
  55.8 10.0 %all_to_all.45 = f32[32,8,128]{2,1,0:T(8,128)S(1)} all-to-all(f32[32,8,128]{2,1,0:T(8,128)S(1)} %bitcast.62), channel_id=1, replica_groups=mesh['gx'=4,'gy'=8] {'gx','gy'}, dimensions={0} | all-to-all | bytes 262144 | tf_op jit(solution)/shard_map/all_to_all | solution.py:859
  65.8 3.8 %loss.1 = (f32[32,1024]{1,0:T(8,128)S(1)}, f32[136,128]{1,0:T(8,128)S(1)}, f32[136,128]{1,0:T(8,128)S(1)}, f32[2,32,32]{2,1,0:T(8,128)S(1)}, f32[1,1]{1,0:T(1,128)}, /*index=5*/f32[1,1]{1,0:T(1,128)}) custom-call(s32[1]{0:T(128)} %bitcast.me_ref.refs_0_, f32[256,128]{1,0:T(8,128)S(1)} %bitcast.53, bf16[512,512]{1,0:T(8,128)(2,1)S(1)} %get-tuple-element.121.mask_ref, ...), custom_call_target="tpu_custom_call" | custom-call | tf_op jit(solution)/shard_map/loss/pallas_call | solution.py:60
  69.8 1.2 collective-permute-done.13.got_ref
  71.0 10.0 %all_to_all.46 = bf16[32,16,128]{2,1,0:T(8,128)(2,1)S(1)} all-to-all(bf16[32,16,128]{2,1,0:T(8,128)(2,1)S(1)} %bitcast.56), channel_id=1, replica_groups=mesh['gx'=4,'gy'=8] {'gx','gy'}, dimensions={0} | all-to-all | bytes 262144 | tf_op jit(solution)/shard_map/all_to_all | solution.py:859
  81.0 4.1 %grad.1 = (bf16[2048,128]{1,0:T(8,128)(2,1)S(1)}, bf16[2048,128]{1,0:T(8,128)(2,1)S(1)}, f32[8,128]{1,0:T(8,128)S(1)}, f32[16,128]{1,0:T(8,128)S(1)}, f32[2,512,1024]{2,1,0:T(8,128)S(1)}) custom-call(s32[1]{0:T(128)} %bitcast.me_ref.refs_0_, s32[256]{0:T(256)S(1)} %copy-done.15, bf16[512,128]{1,0:T(8,128)(2,1)S(1)} %bitcast.57, ...), custom_call_target="tpu_custom_call" | custom-call | tf_op jit(solution)/shard_map/grad/pallas_call | solution.py:60
  85.7 1.2 keep.1
  89.6 6.1 %collective-permute-done.15 = bf16[2,4,128,128]{3,2,1,0:T(8,128)(2,1)S(1)} collective-permute-done((bf16[2,4,128,128]{3,2,1,0:T(8,128)(2,1)S(1)}, bf16[2,4,128,128]{3,2,1,0:T(8,128)(2,1)S(1)}, u32[]{:S(2)}, u32[]{:S(2)}) %collective-permute-start.15) | collective-permute-done | bytes 262176 | tf_op jit(solution)/shard_map/ppermute | solution.py:115
  95.7 1.3 %collective-permute-start.16 = (bf16[4,128,128]{2,1,0:T(8,128)(2,1)S(1)}, bf16[4,128,128]{2,1,0:T(8,128)(2,1)S(1)}, u32[]{:S(2)}, u32[]{:S(2)}) collective-permute-start(bf16[4,128,128]{2,1,0:T(8,128)(2,1)S(1)} %fusion.4), channel_id=1, source_target_pairs={{0,1},{1,0},{2,3},{3,2},{4,5},{5,4},{6,7},{7,6},{8,9},{9,8},{10,11... | collective-permute-start | bytes 393224 | tf_op jit(solution)/shard_map/ppermute | solution.py:117
  97.9 2.8 %collective-permute-done.16 = bf16[4,128,128]{2,1,0:T(8,128)(2,1)S(1)} collective-permute-done((bf16[4,128,128]{2,1,0:T(8,128)(2,1)S(1)}, bf16[4,128,128]{2,1,0:T(8,128)(2,1)S(1)}, u32[]{:S(2)}, u32[]{:S(2)}) %collective-permute-start.16) | collective-permute-done | bytes 131104 | tf_op jit(solution)/shard_map/ppermute | solution.py:117
  100.8 1.3 %collective-permute-done.19 = bf16[4,128,128]{2,1,0:T(8,128)(2,1)S(1)} collective-permute-done((bf16[4,128,128]{2,1,0:T(8,128)(2,1)S(1)}, bf16[4,128,128]{2,1,0:T(8,128)(2,1)S(1)}, u32[]{:S(2)}, u32[]{:S(2)}) %collective-permute-start.19) | collective-permute-done | bytes 131104 | tf_op jit(solution)/shard_map/ppermute | solution.py:115
  102.2 1.4 %collective-permute-start.22 = (bf16[256,128]{1,0:T(8,128)(2,1)S(1)}, bf16[256,128]{1,0:T(8,128)(2,1)S(1)}, u32[]{:S(2)}, u32[]{:S(2)}) collective-permute-start(bf16[256,128]{1,0:T(8,128)(2,1)S(1)} %get-tuple-element.176), channel_id=1, source_target_pairs={{0,6},{1,7},{2,4},{3,5},{4,2},{5,3},{6,0},{7,1},{8,14},{9,15},{10,... | collective-permute-start | bytes 196616 | tf_op jit(solution)/shard_map/ppermute | solution.py:117
  103.7 3.0 %collective-permute-start.21 = (bf16[256,128]{1,0:T(8,128)(2,1)S(1)}, bf16[256,128]{1,0:T(8,128)(2,1)S(1)}, u32[]{:S(2)}, u32[]{:S(2)}) collective-permute-start(bf16[256,128]{1,0:T(8,128)(2,1)S(1)} %get-tuple-element.178), channel_id=1, source_target_pairs={{0,4},{1,5},{2,6},{3,7},{4,0},{5,1},{6,2},{7,3},{8,12},{9,13},{10,... | collective-permute-start | bytes 196616 | tf_op jit(solution)/shard_map/ppermute | solution.py:117
  106.7 1.8 %collective-permute-done.22.refs_5_ = bf16[256,128]{1,0:T(8,128)(2,1)S(1)} collective-permute-done((bf16[256,128]{1,0:T(8,128)(2,1)S(1)}, bf16[256,128]{1,0:T(8,128)(2,1)S(1)}, u32[]{:S(2)}, u32[]{:S(2)}) %collective-permute-start.22) | collective-permute-done | bytes 65568 | tf_op jit(solution)/shard_map/ppermute | solution.py:117
  110.2 3.9 %all-to-all-start.3 = ((bf16[32,16,128]{2,1,0:T(8,128)(2,1)}), bf16[32,16,128]{2,1,0:T(8,128)(2,1)S(1)}, u32[]{:S(2)}, u32[]{:S(2)}) async-start(bf16[32,16,128]{2,1,0:T(8,128)(2,1)} %bitcast.24), calls=%async_computation.3 | async-start | bytes 262144 | tf_op jit(solution)/shard_map/all_to_all | solution.py:859
  114.1 3.8 %turn.1 = (f32[8,64,128]{2,1,0:T(8,128)S(1)}, f32[8,64,128]{2,1,0:T(8,128)S(1)}, f32[8,64,128]{2,1,0:T(8,128)S(1)}, f32[8,128]{1,0:T(8,128)S(1)}, f32[4,32,1024]...) custom-call(s32[1]{0:T(128)} %bitcast.me_ref.refs_0_, s32[256]{0:T(256)S(1)} %copy-done.15, ...), custom_call_target="tpu_custom_call" | custom-call | flops 10000000 | bytes 100000 | tf_op jit(solution)/shard_map/turn/pallas_call | solution.py:60
  117.9 3.7 %all-to-all-done.3 = bf16[32,16,128]{2,1,0:T(8,128)(2,1)S(1)} async-done(((bf16[32,16,128]{2,1,0:T(8,128)(2,1)}), bf16[32,16,128]{2,1,0:T(8,128)(2,1)S(1)}, u32[]{:S(2)}, u32[]{:S(2)}) %all-to-all-start.3) | async-done | bytes 131104 | tf_op jit(solution)/shard_map/all_to_all | solution.py:859
  121.6 6.6 %step.1 = (f32[8,64,64]{2,1,0:T(8,128)}, bf16[8,64,64]{2,1,0:T(8,128)(2,1)}, f32[8,64,64]{2,1,0:T(8,128)}, f32[8,64,64]{2,1,0:T(8,128)}, f32[8,64,64]{2,1,0:T(8,...) custom-call(bf16[512,128]{1,0:T(8,128)(2,1)S(1)} %bitcast.52, ...), custom_call_target="tpu_custom_call" | custom-call | tf_op jit(solution)/shard_map/step/pallas_call | solution.py:60
  (89 shorter events, 13.2 us)
Async XLA Ops:
  1.7 26.5 %copy-start.15 = (s32[256]{0:T(256)S(1)}, s32[256]{0:T(256)}, u32[]{:S(2)}) copy-start(s32[256]{0:T(256)} %owners_ref.7) | copy-start | bytes 3076
  1.8 9.7 %collective-permute-start.2 = (bf16[1,336,128]{2,1,0:T(8,128)(2,1)S(1)}, bf16[1,336,128]{2,1,0:T(8,128)(2,1)S(1)}, u32[]{:S(2)}, u32[]{:S(2)}) collective-permute-start(bf16[1,336,128]{2,1,0:T(8,128)(2,1)S(1)} %bitcast.58), channel_id=1, source_target_pairs={{0,6},{1,7},{2,4},{3,5},{4,2},{5,3},{6,0},{7,1},{8,14},{9,15},{10,... | collective-permute-start | bytes 258056 | tf_op jit(solution)/shard_map/ppermute | solution.py:117
  6.9 7.2 %collective-permute-start.1 = (bf16[1,336,128]{2,1,0:T(8,128)(2,1)S(1)}, bf16[1,336,128]{2,1,0:T(8,128)(2,1)S(1)}, u32[]{:S(2)}, u32[]{:S(2)}) collective-permute-start(bf16[1,336,128]{2,1,0:T(8,128)(2,1)S(1)} %bitcast.59), channel_id=1, source_target_pairs={{0,4},{1,5},{2,6},{3,7},{4,0},{5,1},{6,2},{7,3},{8,12},{9,13},{10,... | collective-permute-start | bytes 258056 | tf_op jit(solution)/shard_map/ppermute | solution.py:117
  6.9 7.2 %collective-permute-start = (bf16[1,336,128]{2,1,0:T(8,128)(2,1)S(1)}, bf16[1,336,128]{2,1,0:T(8,128)(2,1)S(1)}, u32[]{:S(2)}, u32[]{:S(2)}) collective-permute-start(bf16[1,336,128]{2,1,0:T(8,128)(2,1)S(1)} %bitcast.60), channel_id=1, source_target_pairs={{0,2},{1,3},{2,0},{3,1},{4,6},{5,7},{6,4},{7,5},{8,10},{9,11},{10,... | collective-permute-start | bytes 258056 | tf_op jit(solution)/shard_map/ppermute | solution.py:117
  14.1 9.2 %collective-permute-start.4 = (bf16[4,336,128]{2,1,0:T(8,128)(2,1)S(1)}, bf16[4,336,128]{2,1,0:T(8,128)(2,1)S(1)}, u32[]{:S(2)}, u32[]{:S(2)}) collective-permute-start(bf16[4,336,128]{2,1,0:T(8,128)(2,1)S(1)} %pad_maximum_fusion.refs_0_.refs_3_), channel_id=1, source_target_pairs={{0,1},{1,0},{2,3},{3,2},{4,5},{5,4},{6,7},{7,6},{8,9},{9,8},{10,11... | collective-permute-start | bytes 1032200 | tf_op jit(solution)/shard_map/ppermute | solution.py:117
  15.7 9.0 %collective-permute-start.3 = (bf16[4,336,128]{2,1,0:T(8,128)(2,1)S(1)}, bf16[4,336,128]{2,1,0:T(8,128)(2,1)S(1)}, u32[]{:S(2)}, u32[]{:S(2)}) collective-permute-start(bf16[4,336,128]{2,1,0:T(8,128)(2,1)S(1)} %pad_maximum_fusion.refs_0_.refs_3_), channel_id=1, source_target_pairs={{0,16},{8,24},{16,0},{24,8},{1,17},{9,25},{17,1},{25,9},{2,18},{10... | collective-permute-start | bytes 1032200 | tf_op jit(solution)/shard_map/ppermute | solution.py:115
  20.2 7.2 %collective-permute-start.7 = (bf16[4,336,128]{2,1,0:T(8,128)(2,1)S(1)}, bf16[4,336,128]{2,1,0:T(8,128)(2,1)S(1)}, u32[]{:S(2)}, u32[]{:S(2)}) collective-permute-start(bf16[4,336,128]{2,1,0:T(8,128)(2,1)S(1)} %pad_maximum_fusion.refs_0_.refs_3_), channel_id=1, source_target_pairs={{0,8},{8,0},{16,24},{24,16},{1,9},{9,1},{17,25},{25,17},{2,10},{10... | collective-permute-start | bytes 1032200 | tf_op jit(solution)/shard_map/ppermute | solution.py:115
  24.9 3.3 %collective-permute-start.9 = (bf16[4,336,128]{2,1,0:T(8,128)(2,1)S(1)}, bf16[4,336,128]{2,1,0:T(8,128)(2,1)S(1)}, u32[]{:S(2)}, u32[]{:S(2)}) collective-permute-start(bf16[4,336,128]{2,1,0:T(8,128)(2,1)S(1)} %collective-permute-done.4.refs_2_.refs_5_), channel_id=1, source_target_pairs={{0,8},{8,0},{16,24},{24,16},{1,9},{9,1},{17,25},{25,17},{2,10},{10... | collective-permute-start | bytes 1032200 | tf_op jit(solution)/shard_map/ppermute | solution.py:115
  25.0 8.3 %collective-permute-start.6 = (bf16[4,176,128]{2,1,0:T(8,128)(2,1)S(1)}, bf16[4,176,128]{2,1,0:T(8,128)(2,1)S(1)}, u32[]{:S(2)}, u32[]{:S(2)}) collective-permute-start(bf16[4,176,128]{2,1,0:T(8,128)(2,1)S(1)} %slice_add_fusion), channel_id=1, source_target_pairs={{0,16},{8,24},{16,0},{24,8},{1,17},{9,25},{17,1},{25,9},{2,18},{10... | collective-permute-start | bytes 540680 | tf_op jit(solution)/shard_map/ppermute | solution.py:115
  26.6 1.7 %collective-permute-start.8 = (bf16[4,336,128]{2,1,0:T(8,128)(2,1)S(1)}, bf16[4,336,128]{2,1,0:T(8,128)(2,1)S(1)}, u32[]{:S(2)}, u32[]{:S(2)}) collective-permute-start(bf16[4,336,128]{2,1,0:T(8,128)(2,1)S(1)} %collective-permute-done.3.refs_1_.refs_4_), channel_id=1, source_target_pairs={{0,8},{8,0},{16,24},{24,16},{1,9},{9,1},{17,25},{25,17},{2,10},{10... | collective-permute-start | bytes 1032200 | tf_op jit(solution)/shard_map/ppermute | solution.py:115
  26.8 6.5 %collective-permute-start.5 = (bf16[4,160,128]{2,1,0:T(8,128)(2,1)S(1)}, bf16[4,160,128]{2,1,0:T(8,128)(2,1)S(1)}, u32[]{:S(2)}, u32[]{:S(2)}) collective-permute-start(bf16[4,160,128]{2,1,0:T(8,128)(2,1)S(1)} %slice_add_fusion.1), channel_id=1, source_target_pairs={{0,1},{1,0},{2,3},{3,2},{4,5},{5,4},{6,7},{7,6},{8,9},{9,8},{10,11... | collective-permute-start | bytes 491528 | tf_op jit(solution)/shard_map/ppermute | solution.py:117
  33.3 1.7 %collective-permute-start.11 = (bf16[4,176,128]{2,1,0:T(8,128)(2,1)S(1)}, bf16[4,176,128]{2,1,0:T(8,128)(2,1)S(1)}, u32[]{:S(2)}, u32[]{:S(2)}) collective-permute-start(bf16[4,176,128]{2,1,0:T(8,128)(2,1)S(1)} %collective-permute-done.6.refs_10_), channel_id=1, source_target_pairs={{0,8},{8,0},{16,24},{24,16},{1,9},{9,1},{17,25},{25,17},{2,10},{10... | collective-permute-start | bytes 540680 | tf_op jit(solution)/shard_map/ppermute | solution.py:115
  33.3 1.7 %collective-permute-start.10 = (bf16[4,160,128]{2,1,0:T(8,128)(2,1)S(1)}, bf16[4,160,128]{2,1,0:T(8,128)(2,1)S(1)}, u32[]{:S(2)}, u32[]{:S(2)}) collective-permute-start(bf16[4,160,128]{2,1,0:T(8,128)(2,1)S(1)} %collective-permute-done.5.refs_9_), channel_id=1, source_target_pairs={{0,8},{8,0},{16,24},{24,16},{1,9},{9,1},{17,25},{25,17},{2,10},{10... | collective-permute-start | bytes 491528 | tf_op jit(solution)/shard_map/ppermute | solution.py:115
  39.5 26.3 %copy-start.13 = (f32[2,32,32]{2,1,0:T(8,128)S(1)}, f32[2,32,32]{2,1,0:T(8,128)}, u32[]{:S(2)}) copy-start(f32[2,32,32]{2,1,0:T(8,128)} %wt_hbm.1) | copy-start | bytes 24580
  39.5 41.5 %copy-start.1 = (bf16[1024,1024]{1,0:T(8,128)(2,1)S(1)}, bf16[1024,1024]{1,0:T(8,128)(2,1)}, u32[]{:S(2)}) copy-start(bf16[1024,1024]{1,0:T(8,128)(2,1)} %copy-done) | copy-start | bytes 6291460
  39.5 1.2 collective-permute-start.12
  69.6 1.3 %collective-permute-start.13 = (f32[136,128]{1,0:T(8,128)S(1)}, f32[136,128]{1,0:T(8,128)S(1)}, u32[]{:S(2)}, u32[]{:S(2)}) collective-permute-start(f32[136,128]{1,0:T(8,128)S(1)} %get-tuple-element.128), channel_id=1, source_target_pairs={{0,8},{8,0},{16,24},{24,16},{1,9},{9,1},{17,25},{25,17},{2,10},{10... | collective-permute-start | bytes 208904 | tf_op jit(solution)/shard_map/ppermute | solution.py:115
  85.1 2.0 %collective-permute-start.14 = (bf16[2048,128]{1,0:T(8,128)(2,1)S(1)}, bf16[2048,128]{1,0:T(8,128)(2,1)S(1)}, u32[]{:S(2)}, u32[]{:S(2)}) collective-permute-start(bf16[2048,128]{1,0:T(8,128)(2,1)S(1)} %get-tuple-element.135), channel_id=1, source_target_pairs={{0,8},{8,0},{16,24},{24,16},{1,9},{9,1},{17,25},{25,17},{2,10},{10... | collective-permute-start | bytes 1572872 | tf_op jit(solution)/shard_map/ppermute | solution.py:115
  85.3 3.0 %collective-permute-start.17 = (bf16[2048,128]{1,0:T(8,128)(2,1)S(1)}, bf16[2048,128]{1,0:T(8,128)(2,1)S(1)}, u32[]{:S(2)}, u32[]{:S(2)}) collective-permute-start(bf16[2048,128]{1,0:T(8,128)(2,1)S(1)} %get-tuple-element.137), channel_id=1, source_target_pairs={{0,8},{8,0},{16,24},{24,16},{1,9},{9,1},{17,25},{25,17},{2,10},{10... | collective-permute-start | bytes 1572872 | tf_op jit(solution)/shard_map/ppermute | solution.py:115
  87.2 8.4 %collective-permute-start.15 = (bf16[2,4,128,128]{3,2,1,0:T(8,128)(2,1)S(1)}, bf16[2,4,128,128]{3,2,1,0:T(8,128)(2,1)S(1)}, u32[]{:S(2)}, u32[]{:S(2)}) collective-permute-start(bf16[2,4,128,128]{3,2,1,0:T(8,128)(2,1)S(1)} %bitcast.66), channel_id=1, source_target_pairs={{0,16},{8,24},{16,0},{24,8},{1,17},{9,25},{17,1},{25,9},{2,18},{10... | collective-permute-start | bytes 786440 | tf_op jit(solution)/shard_map/ppermute | solution.py:115
  88.4 33.2 %copy-start.4 = (f32[8,64,128]{2,1,0:T(8,128)S(1)}, f32[8,64,128]{2,1,0:T(8,128)}, u32[]{:S(2)}) copy-start(f32[8,64,128]{2,1,0:T(8,128)} %copy-done.3) | copy-start | bytes 786436
  88.4 33.1 %copy-start.6 = (f32[8,64,128]{2,1,0:T(8,128)S(1)}, f32[8,64,128]{2,1,0:T(8,128)}, u32[]{:S(2)}) copy-start(f32[8,64,128]{2,1,0:T(8,128)} %copy-done.5) | copy-start | bytes 786436
  88.4 33.1 %copy-start.8 = (f32[8,64,128]{2,1,0:T(8,128)S(1)}, f32[8,64,128]{2,1,0:T(8,128)}, u32[]{:S(2)}) copy-start(f32[8,64,128]{2,1,0:T(8,128)} %copy-done.7) | copy-start | bytes 786436
  88.5 33.1 %copy-start.10 = (f32[8,64,64]{2,1,0:T(8,128)S(1)}, f32[8,64,64]{2,1,0:T(8,128)}, u32[]{:S(2)}) copy-start(f32[8,64,64]{2,1,0:T(8,128)} %copy-done.9) | copy-start | bytes 393220
  88.5 33.1 %copy-start.12 = (f32[8,64,128]{2,1,0:T(8,128)S(1)}, f32[8,64,128]{2,1,0:T(8,128)}, u32[]{:S(2)}) copy-start(f32[8,64,128]{2,1,0:T(8,128)} %copy-done.11) | copy-start | bytes 786436
  88.6 8.4 %collective-permute-start.18 = (bf16[2,4,128,128]{3,2,1,0:T(8,128)(2,1)S(1)}, bf16[2,4,128,128]{3,2,1,0:T(8,128)(2,1)S(1)}, u32[]{:S(2)}, u32[]{:S(2)}) collective-permute-start(bf16[2,4,128,128]{3,2,1,0:T(8,128)(2,1)S(1)} %fusion.1), channel_id=1, source_target_pairs={{0,1},{1,0},{2,3},{3,2},{4,5},{5,4},{6,7},{7,6},{8,9},{9,8},{10,11... | collective-permute-start | bytes 786440 | tf_op jit(solution)/shard_map/ppermute | solution.py:117
  95.7 5.0 %collective-permute-start.16 = (bf16[4,128,128]{2,1,0:T(8,128)(2,1)S(1)}, bf16[4,128,128]{2,1,0:T(8,128)(2,1)S(1)}, u32[]{:S(2)}, u32[]{:S(2)}) collective-permute-start(bf16[4,128,128]{2,1,0:T(8,128)(2,1)S(1)} %fusion.4), channel_id=1, source_target_pairs={{0,1},{1,0},{2,3},{3,2},{4,5},{5,4},{6,7},{7,6},{8,9},{9,8},{10,11... | collective-permute-start | bytes 393224 | tf_op jit(solution)/shard_map/ppermute | solution.py:117
  97.1 5.0 %collective-permute-start.19 = (bf16[4,128,128]{2,1,0:T(8,128)(2,1)S(1)}, bf16[4,128,128]{2,1,0:T(8,128)(2,1)S(1)}, u32[]{:S(2)}, u32[]{:S(2)}) collective-permute-start(bf16[4,128,128]{2,1,0:T(8,128)(2,1)S(1)} %fusion.5), channel_id=1, source_target_pairs={{0,16},{8,24},{16,0},{24,8},{1,17},{9,25},{17,1},{25,9},{2,18},{10... | collective-permute-start | bytes 393224 | tf_op jit(solution)/shard_map/ppermute | solution.py:115
  102.2 6.2 %collective-permute-start.22 = (bf16[256,128]{1,0:T(8,128)(2,1)S(1)}, bf16[256,128]{1,0:T(8,128)(2,1)S(1)}, u32[]{:S(2)}, u32[]{:S(2)}) collective-permute-start(bf16[256,128]{1,0:T(8,128)(2,1)S(1)} %get-tuple-element.176), channel_id=1, source_target_pairs={{0,6},{1,7},{2,4},{3,5},{4,2},{5,3},{6,0},{7,1},{8,14},{9,15},{10,... | collective-permute-start | bytes 196616 | tf_op jit(solution)/shard_map/ppermute | solution.py:117
  103.6 5.7 %collective-permute-start.20 = (bf16[256,128]{1,0:T(8,128)(2,1)S(1)}, bf16[256,128]{1,0:T(8,128)(2,1)S(1)}, u32[]{:S(2)}, u32[]{:S(2)}) collective-permute-start(bf16[256,128]{1,0:T(8,128)(2,1)S(1)} %get-tuple-element.177), channel_id=1, source_target_pairs={{0,2},{1,3},{2,0},{3,1},{4,6},{5,7},{6,4},{7,5},{8,10},{9,11},{10,... | collective-permute-start | bytes 196616 | tf_op jit(solution)/shard_map/ppermute | solution.py:117
  103.7 5.7 %collective-permute-start.21 = (bf16[256,128]{1,0:T(8,128)(2,1)S(1)}, bf16[256,128]{1,0:T(8,128)(2,1)S(1)}, u32[]{:S(2)}, u32[]{:S(2)}) collective-permute-start(bf16[256,128]{1,0:T(8,128)(2,1)S(1)} %get-tuple-element.178), channel_id=1, source_target_pairs={{0,4},{1,5},{2,6},{3,7},{4,0},{5,1},{6,2},{7,3},{8,12},{9,13},{10,... | collective-permute-start | bytes 196616 | tf_op jit(solution)/shard_map/ppermute | solution.py:117
  110.2 11.4 %all-to-all-start.3 = ((bf16[32,16,128]{2,1,0:T(8,128)(2,1)}), bf16[32,16,128]{2,1,0:T(8,128)(2,1)S(1)}, u32[]{:S(2)}, u32[]{:S(2)}) async-start(bf16[32,16,128]{2,1,0:T(8,128)(2,1)} %bitcast.24), calls=%async_computation.3 | async-start | bytes 262144 | tf_op jit(solution)/shard_map/all_to_all | solution.py:859
  (9 other events, 134.3 us)

commit v7 on v6

--- a/solution.py
+++ b/solution.py
@@ -605,21 +605,21 @@
     one, two = (
         (k + plan.swap(s, plan.core).astype(F32)).reshape(shape) for k, s in zip(kept, sent)
     )
-    got_one = plan.swap(one[1].astype(BF), plan.x)
-    got_two = plan.swap(two[:, 1].astype(BF), plan.y)
+    got_one = plan.swap(one[1], plan.x)
+    got_two = plan.swap(two[:, 1], plan.y)
     one = one[0] + got_one.astype(F32)
     two = two[:, 0] + got_two.astype(F32)
-    got_one = plan.swap(one[1].astype(BF), plan.y)
-    got_two = plan.swap(two[1].astype(BF), plan.x)
+    got_one = plan.swap(one[1], plan.y)
+    got_two = plan.swap(two[1], plan.x)
     one = one[0] + got_one.astype(F32)
     two = two[0] + got_two.astype(F32)
     if rest <= 4:
-        both = jnp.concatenate([one[1:], two[1:]], axis=1).astype(BF)
+        both = jnp.concatenate([one[1:], two[1:]], axis=1)
         return one, two, [plan.swap(both[k], m) for k, m in enumerate(plan.rest[1:])]
     both = jnp.concatenate([one, two], axis=1)
     for b in reversed(plan.bits):
         both = both.reshape(2, -1, 2 * rows, LANES)
-        both = both[0] + plan.swap(both[1].astype(BF), b).astype(F32)
+        both = both[0] + plan.swap(both[1], b).astype(F32)
     return both[:, :rows], both[:, rows:], []
 
 
@@ -1038,8 +1038,8 @@
     *sent, second_chunk, d_norm, full = call(
         functools.partial(grad_kernel, parts=parts, order=order[1], local=local, core=plan.core),
         [
-            (packed, BF),
-            (packed, BF),
+            (packed, F32),
+            (packed, F32),
             ((chunk, LANES), F32),
             ((2 * tiles, LANES), F32),
             ((2, width // 2, width), F32),

time: 129 us -> 142 us (1.10)
  waiting for transfers between devices: 31.4 us -> 45.3 us
    ppermute x10, waiting for transfers between devices: 14.6 us -> 22.4 us  [swap(): return lax.ppermute(a, 'gy', [(i, i ^ my) for i in range(self.gy)])]
    ppermute x13, waiting for transfers between devices: 13 us -> 19.2 us  [swap(): return lax.ppermute(a, 'gx', [(i, i ^ mx) for i in range(self.gx)])]
  transfers between devices with their start and end apart: 24 -> 24, of which waited for: 15 -> 16; matrix products, arithmetic and copies ran while one was open for 1% -> 1% of each run, Pallas kernels for 9% -> 8%
where the time goes in v7:
time: 142 us
  waiting for transfers between devices  45.3 us (32%)
  Pallas kernels  38 us (27%)
  blocking collectives  30.1 us (21%)
  starting transfers between devices  25 us (18%)
  local copies, waits for them, and re-layouts  1.79 us (1%)
    pallas_call x14, Pallas kernels, call(): pl.pallas_call(kernel, out_shape=[jax.ShapeDtypeStruct(s, t) for s, t in...  38 us
    all_to_all x3, blocking collectives, exchange(): return lax.all_to_all(payload, AXES, 0, 0, tiled=True)  30.1 us
    ppermute x10, waiting for transfers between devices, swap(): return lax.ppermute(a, 'gy', [(i, i ^ my) for i in range(self.gy)])  22.4 us
    ppermute x13, waiting for transfers between devices, swap(): return lax.ppermute(a, 'gx', [(i, i ^ mx) for i in range(self.gx)])  19.2 us
    ppermute x10, starting transfers between devices, swap(): return lax.ppermute(a, 'gy', [(i, i ^ my) for i in range(self.gy)])  15 us
    ppermute x13, starting transfers between devices, swap(): return lax.ppermute(a, 'gx', [(i, i ^ mx) for i in range(self.gx)])  7.22 us
    all_to_all x1, waiting for transfers between devices, exchange(): return lax.all_to_all(payload, AXES, 0, 0, tiled=True)  3.72 us
  transfers between devices with their start and end apart: 24, of which 16 were waited for; matrix products, arithmetic and copies ran while one was open for 1% of the time, Pallas kernels for 8%

profile of v7, /device:TPU:0, one launch (start us, length us, event | category | flops | bytes accessed | tf_op | source)
XLA Modules:
  0.0 142.1 jit_solution(13189803559762810376)
XLA Ops:
  1.8 5.1 %collective-permute-start.2 = (bf16[1,336,128]{2,1,0:T(8,128)(2,1)S(1)}, bf16[1,336,128]{2,1,0:T(8,128)(2,1)S(1)}, u32[]{:S(2)}, u32[]{:S(2)}) collective-permute-start(bf16[1,336,128]{2,1,0:T(8,128)(2,1)S(1)} %bitcast.62), channel_id=1, source_target_pairs={{0,6},{1,7},{2,4},{3,5},{4,2},{5,3},{6,0},{7,1},{8,14},{9,15},{10,... | collective-permute-start | bytes 258056 | tf_op jit(solution)/shard_map/ppermute | solution.py:117
  7.5 2.6 %hash.1 = (bf16[1024,1024]{1,0:T(8,128)(2,1)S(1)}, bf16[1024,1024]{1,0:T(8,128)(2,1)S(1)}) custom-call(s32[1024,1024]{1,0:T(8,128)} %codes_hbm.1, s32[8,1024]{1,0:T(8,128)} %offsets_hbm.1), custom_call_target="tpu_custom_call" | custom-call | flops 20000000 | bytes 200000 | tf_op jit(solution)/shard_map/hash/pallas_call | solution.py:60
  10.1 1.3 copy-done
  11.5 2.6 %collective-permute-done.1 = bf16[1,336,128]{2,1,0:T(8,128)(2,1)S(1)} collective-permute-done((bf16[1,336,128]{2,1,0:T(8,128)(2,1)S(1)}, bf16[1,336,128]{2,1,0:T(8,128)(2,1)S(1)}, u32[]{:S(2)}, u32[]{:S(2)}) %collective-permute-start.1) | collective-permute-done | bytes 86048 | tf_op jit(solution)/shard_map/ppermute | solution.py:117
  14.1 1.6 %collective-permute-start.4 = (bf16[4,336,128]{2,1,0:T(8,128)(2,1)S(1)}, bf16[4,336,128]{2,1,0:T(8,128)(2,1)S(1)}, u32[]{:S(2)}, u32[]{:S(2)}) collective-permute-start(bf16[4,336,128]{2,1,0:T(8,128)(2,1)S(1)} %pad_maximum_fusion.refs_0_.refs_3_), channel_id=1, source_target_pairs={{0,1},{1,0},{2,3},{3,2},{4,5},{5,4},{6,7},{7,6},{8,9},{9,8},{10,11... | collective-permute-start | bytes 1032200 | tf_op jit(solution)/shard_map/ppermute | solution.py:117
  15.7 1.5 %collective-permute-start.3 = (bf16[4,336,128]{2,1,0:T(8,128)(2,1)S(1)}, bf16[4,336,128]{2,1,0:T(8,128)(2,1)S(1)}, u32[]{:S(2)}, u32[]{:S(2)}) collective-permute-start(bf16[4,336,128]{2,1,0:T(8,128)(2,1)S(1)} %pad_maximum_fusion.refs_0_.refs_3_), channel_id=1, source_target_pairs={{0,16},{8,24},{16,0},{24,8},{1,17},{9,25},{17,1},{25,9},{2,18},{10... | collective-permute-start | bytes 1032200 | tf_op jit(solution)/shard_map/ppermute | solution.py:115
  17.3 2.8 %prepare.1 = (f32[8,64,128]{2,1,0:T(8,128)S(1)}, f32[8,64,128]{2,1,0:T(8,128)S(1)}, f32[8,64,128]{2,1,0:T(8,128)S(1)}, f32[8,64,128]{2,1,0:T(8,128)S(1)}, f32[8,...) custom-call(f32[8,64,64]{2,1,0:T(8,128)} %w_hbm.3, f32[8,64,64]{2,1,0:T(8,128)} %left_hbm.1, f32[8,64,64]{2,1,0:T(8,128)} %right_hbm.1, ...), custom_call_target="tpu_custom_call" | custom-call | flops 10000000 | bytes 100000 | tf_op jit(solution)/shard_map/prepare/pallas_call | solution.py:60
  20.2 3.1 %collective-permute-done.4.refs_2_.refs_5_ = bf16[4,336,128]{2,1,0:T(8,128)(2,1)S(1)} collective-permute-done((bf16[4,336,128]{2,1,0:T(8,128)(2,1)S(1)}, bf16[4,336,128]{2,1,0:T(8,128)(2,1)S(1)}, u32[]{:S(2)}, u32[]{:S(2)}) %collective-permute-start.4) | collective-permute-done | bytes 344096 | tf_op jit(solution)/shard_map/ppermute | solution.py:117
  23.4 1.3 collective-permute-done.3.refs_1_.refs_4_
  25.0 1.6 %collective-permute-start.6 = (bf16[4,176,128]{2,1,0:T(8,128)(2,1)S(1)}, bf16[4,176,128]{2,1,0:T(8,128)(2,1)S(1)}, u32[]{:S(2)}, u32[]{:S(2)}) collective-permute-start(bf16[4,176,128]{2,1,0:T(8,128)(2,1)S(1)} %slice_add_fusion), channel_id=1, source_target_pairs={{0,16},{8,24},{16,0},{24,8},{1,17},{9,25},{17,1},{25,9},{2,18},{10... | collective-permute-start | bytes 540680 | tf_op jit(solution)/shard_map/ppermute | solution.py:115
  28.2 1.7 %assemble.1.refs_2_ = bf16[2,1024,1024]{2,1,0:T(8,128)(2,1)S(1)} custom-call(s32[1]{0:T(128)} %bitcast.me_ref.refs_0_, s32[256]{0:T(256)S(1)} %copy-done.15, bf16[4,336,128]{2,1,0:T(8,128)(2,1)S(1)} %pad_maximum_fusion.refs_0_.refs_3_, bf16[4,336,128]{2,1,0:T(8,128)(2,1)S(1)} %collective-permute-done.3.refs_1_.refs_4_, ...), custom_call_target="tpu_custom_call" | custom-call | flops 10000000 | bytes 100000 | tf_op jit(solution)/shard_map/assemble/pallas_call | solution.py:60
  30.0 3.3 %collective-permute-done.5.refs_9_ = bf16[4,160,128]{2,1,0:T(8,128)(2,1)S(1)} collective-permute-done((bf16[4,160,128]{2,1,0:T(8,128)(2,1)S(1)}, bf16[4,160,128]{2,1,0:T(8,128)(2,1)S(1)}, u32[]{:S(2)}, u32[]{:S(2)}) %collective-permute-start.5) | collective-permute-done | bytes 163872 | tf_op jit(solution)/shard_map/ppermute | solution.py:117
  35.0 4.5 %pre.1 = (f32[1024,1024]{1,0:T(8,128)S(1)}, f32[8,128]{1,0:T(8,128)S(1)}, f32[8,128]{1,0:T(8,128)S(1)}, f32[32,128]{1,0:T(8,128)S(1)}, bf16[512,512]{1,0:T(8,128)(2,1)S(1)}, /*index=5*/bf16[2,1024,1024]{2,1,0:T(8,128)(2,1)S(1)}) custom-call(s32[1]{0:T(128)} %bitcast.me_ref.refs_0_, s32[256]{0:T(256)S(1)} %copy-done.15, ...), custom_call_target="tpu_custom_call", output_to_operand_aliasing={{5}: (2, {})} | custom-call | tf_op jit(solution)/shard_map/pre/pallas_call | solution.py:60
  40.9 10.1 %all_to_all.44 = f32[32,8,128]{2,1,0:T(8,128)S(1)} all-to-all(f32[32,8,128]{2,1,0:T(8,128)S(1)} %bitcast.59), channel_id=1, replica_groups=mesh['gx'=4,'gy'=8] {'gx','gy'}, dimensions={0} | all-to-all | bytes 262144 | tf_op jit(solution)/shard_map/all_to_all | solution.py:859
  51.0 4.9 %act.1 = (f32[1024,1024]{1,0:T(8,128)S(1)}, f32[32,1024]{1,0:T(8,128)S(1)}, f32[32,1024]{1,0:T(8,128)S(1)}, f32[32,1024]{1,0:T(8,128)S(1)}, f32[8,1024]{1,0:T(8,...) custom-call(f32[256,128]{1,0:T(8,128)S(1)} %bitcast.58, f32[32,128]{1,0:T(8,128)S(1)} %get-tuple-element.115.count_ref, ...), custom_call_target="tpu_custom_call" | custom-call | tf_op jit(solution)/shard_map/act/pallas_call | solution.py:60
  55.8 10.0 %all_to_all.45 = f32[32,8,128]{2,1,0:T(8,128)S(1)} all-to-all(f32[32,8,128]{2,1,0:T(8,128)S(1)} %bitcast.66), channel_id=1, replica_groups=mesh['gx'=4,'gy'=8] {'gx','gy'}, dimensions={0} | all-to-all | bytes 262144 | tf_op jit(solution)/shard_map/all_to_all | solution.py:859
  65.8 3.8 %loss.1 = (f32[32,1024]{1,0:T(8,128)S(1)}, f32[136,128]{1,0:T(8,128)S(1)}, f32[136,128]{1,0:T(8,128)S(1)}, f32[2,32,32]{2,1,0:T(8,128)S(1)}, f32[1,1]{1,0:T(1,128)}, /*index=5*/f32[1,1]{1,0:T(1,128)}) custom-call(s32[1]{0:T(128)} %bitcast.me_ref.refs_0_, f32[256,128]{1,0:T(8,128)S(1)} %bitcast.57, bf16[512,512]{1,0:T(8,128)(2,1)S(1)} %get-tuple-element.121.mask_ref, ...), custom_call_target="tpu_custom_call" | custom-call | tf_op jit(solution)/shard_map/loss/pallas_call | solution.py:60
  71.0 10.0 %all_to_all.46 = bf16[32,16,128]{2,1,0:T(8,128)(2,1)S(1)} all-to-all(bf16[32,16,128]{2,1,0:T(8,128)(2,1)S(1)} %bitcast.60), channel_id=1, replica_groups=mesh['gx'=4,'gy'=8] {'gx','gy'}, dimensions={0} | all-to-all | bytes 262144 | tf_op jit(solution)/shard_map/all_to_all | solution.py:859
  81.0 4.1 %grad.1 = (f32[2048,128]{1,0:T(8,128)S(1)}, f32[2048,128]{1,0:T(8,128)S(1)}, f32[8,128]{1,0:T(8,128)S(1)}, f32[16,128]{1,0:T(8,128)S(1)}, f32[2,512,1024]{2,1,0:T(8,128)S(1)}) custom-call(s32[1]{0:T(128)} %bitcast.me_ref.refs_0_, s32[256]{0:T(256)S(1)} %copy-done.15, bf16[512,128]{1,0:T(8,128)(2,1)S(1)} %bitcast.61, ...), custom_call_target="tpu_custom_call" | custom-call | tf_op jit(solution)/shard_map/grad/pallas_call | solution.py:60
  89.5 1.3 collective-permute-start.18
  90.8 11.3 %collective-permute-done.15 = f32[2,4,128,128]{3,2,1,0:T(8,128)S(1)} collective-permute-done((f32[2,4,128,128]{3,2,1,0:T(8,128)S(1)}, f32[2,4,128,128]{3,2,1,0:T(8,128)S(1)}, u32[]{:S(2)}, u32[]{:S(2)}) %collective-permute-start.15) | collective-permute-done | bytes 524320 | tf_op jit(solution)/shard_map/ppermute | solution.py:115
  102.2 1.3 collective-permute-start.16
  104.7 5.1 %collective-permute-done.16 = f32[4,128,128]{2,1,0:T(8,128)S(1)} collective-permute-done((f32[4,128,128]{2,1,0:T(8,128)S(1)}, f32[4,128,128]{2,1,0:T(8,128)S(1)}, u32[]{:S(2)}, u32[]{:S(2)}) %collective-permute-start.16) | collective-permute-done | bytes 262176 | tf_op jit(solution)/shard_map/ppermute | solution.py:117
  109.9 1.3 collective-permute-done.19
  111.3 1.3 collective-permute-start.22
  113.3 2.5 %collective-permute-start.21 = (f32[256,128]{1,0:T(8,128)S(1)}, f32[256,128]{1,0:T(8,128)S(1)}, u32[]{:S(2)}, u32[]{:S(2)}) collective-permute-start(f32[256,128]{1,0:T(8,128)S(1)} %get-tuple-element.180), channel_id=1, source_target_pairs={{0,4},{1,5},{2,6},{3,7},{4,0},{5,1},{6,2},{7,3},{8,12},{9,13},{10,... | collective-permute-start | bytes 393224 | tf_op jit(solution)/shard_map/ppermute | solution.py:117
  115.8 3.9 %collective-permute-done.22.refs_5_ = f32[256,128]{1,0:T(8,128)S(1)} collective-permute-done((f32[256,128]{1,0:T(8,128)S(1)}, f32[256,128]{1,0:T(8,128)S(1)}, u32[]{:S(2)}, u32[]{:S(2)}) %collective-permute-start.22) | collective-permute-done | bytes 131104 | tf_op jit(solution)/shard_map/ppermute | solution.py:117
  119.7 4.3 %collective-permute-done.21.refs_4_ = f32[256,128]{1,0:T(8,128)S(1)} collective-permute-done((f32[256,128]{1,0:T(8,128)S(1)}, f32[256,128]{1,0:T(8,128)S(1)}, u32[]{:S(2)}, u32[]{:S(2)}) %collective-permute-start.21) | collective-permute-done | bytes 131104 | tf_op jit(solution)/shard_map/ppermute | solution.py:117
  124.9 2.8 %all-to-all-start.3 = ((bf16[32,16,128]{2,1,0:T(8,128)(2,1)}), bf16[32,16,128]{2,1,0:T(8,128)(2,1)S(1)}, u32[]{:S(2)}, u32[]{:S(2)}) async-start(bf16[32,16,128]{2,1,0:T(8,128)(2,1)} %bitcast.24), calls=%async_computation.3 | async-start | bytes 262144 | tf_op jit(solution)/shard_map/all_to_all | solution.py:859
  127.7 3.7 %turn.1 = (f32[8,64,128]{2,1,0:T(8,128)S(1)}, f32[8,64,128]{2,1,0:T(8,128)S(1)}, f32[8,64,128]{2,1,0:T(8,128)S(1)}, f32[8,128]{1,0:T(8,128)S(1)}, f32[4,32,1024]...) custom-call(s32[1]{0:T(128)} %bitcast.me_ref.refs_0_, s32[256]{0:T(256)S(1)} %copy-done.15, ...), custom_call_target="tpu_custom_call" | custom-call | flops 10000000 | bytes 100000 | tf_op jit(solution)/shard_map/turn/pallas_call | solution.py:60
  131.5 3.7 %all-to-all-done.3 = bf16[32,16,128]{2,1,0:T(8,128)(2,1)S(1)} async-done(((bf16[32,16,128]{2,1,0:T(8,128)(2,1)}), bf16[32,16,128]{2,1,0:T(8,128)(2,1)S(1)}, u32[]{:S(2)}, u32[]{:S(2)}) %all-to-all-start.3) | async-done | bytes 131104 | tf_op jit(solution)/shard_map/all_to_all | solution.py:859
  135.3 6.6 %step.1 = (f32[8,64,64]{2,1,0:T(8,128)}, bf16[8,64,64]{2,1,0:T(8,128)(2,1)}, f32[8,64,64]{2,1,0:T(8,128)}, f32[8,64,64]{2,1,0:T(8,128)}, f32[8,64,64]{2,1,0:T(8,...) custom-call(bf16[512,128]{1,0:T(8,128)(2,1)S(1)} %bitcast.56, ...), custom_call_target="tpu_custom_call" | custom-call | tf_op jit(solution)/shard_map/step/pallas_call | solution.py:60
  (88 shorter events, 15.6 us)
Async XLA Ops:
  1.7 26.5 %copy-start.15 = (s32[256]{0:T(256)S(1)}, s32[256]{0:T(256)}, u32[]{:S(2)}) copy-start(s32[256]{0:T(256)} %owners_ref.7) | copy-start | bytes 3076
  1.8 9.7 %collective-permute-start.2 = (bf16[1,336,128]{2,1,0:T(8,128)(2,1)S(1)}, bf16[1,336,128]{2,1,0:T(8,128)(2,1)S(1)}, u32[]{:S(2)}, u32[]{:S(2)}) collective-permute-start(bf16[1,336,128]{2,1,0:T(8,128)(2,1)S(1)} %bitcast.62), channel_id=1, source_target_pairs={{0,6},{1,7},{2,4},{3,5},{4,2},{5,3},{6,0},{7,1},{8,14},{9,15},{10,... | collective-permute-start | bytes 258056 | tf_op jit(solution)/shard_map/ppermute | solution.py:117
  6.9 7.2 %collective-permute-start.1 = (bf16[1,336,128]{2,1,0:T(8,128)(2,1)S(1)}, bf16[1,336,128]{2,1,0:T(8,128)(2,1)S(1)}, u32[]{:S(2)}, u32[]{:S(2)}) collective-permute-start(bf16[1,336,128]{2,1,0:T(8,128)(2,1)S(1)} %bitcast.63), channel_id=1, source_target_pairs={{0,4},{1,5},{2,6},{3,7},{4,0},{5,1},{6,2},{7,3},{8,12},{9,13},{10,... | collective-permute-start | bytes 258056 | tf_op jit(solution)/shard_map/ppermute | solution.py:117
  6.9 7.2 %collective-permute-start = (bf16[1,336,128]{2,1,0:T(8,128)(2,1)S(1)}, bf16[1,336,128]{2,1,0:T(8,128)(2,1)S(1)}, u32[]{:S(2)}, u32[]{:S(2)}) collective-permute-start(bf16[1,336,128]{2,1,0:T(8,128)(2,1)S(1)} %bitcast.64), channel_id=1, source_target_pairs={{0,2},{1,3},{2,0},{3,1},{4,6},{5,7},{6,4},{7,5},{8,10},{9,11},{10,... | collective-permute-start | bytes 258056 | tf_op jit(solution)/shard_map/ppermute | solution.py:117
  14.1 9.2 %collective-permute-start.4 = (bf16[4,336,128]{2,1,0:T(8,128)(2,1)S(1)}, bf16[4,336,128]{2,1,0:T(8,128)(2,1)S(1)}, u32[]{:S(2)}, u32[]{:S(2)}) collective-permute-start(bf16[4,336,128]{2,1,0:T(8,128)(2,1)S(1)} %pad_maximum_fusion.refs_0_.refs_3_), channel_id=1, source_target_pairs={{0,1},{1,0},{2,3},{3,2},{4,5},{5,4},{6,7},{7,6},{8,9},{9,8},{10,11... | collective-permute-start | bytes 1032200 | tf_op jit(solution)/shard_map/ppermute | solution.py:117
  15.7 9.0 %collective-permute-start.3 = (bf16[4,336,128]{2,1,0:T(8,128)(2,1)S(1)}, bf16[4,336,128]{2,1,0:T(8,128)(2,1)S(1)}, u32[]{:S(2)}, u32[]{:S(2)}) collective-permute-start(bf16[4,336,128]{2,1,0:T(8,128)(2,1)S(1)} %pad_maximum_fusion.refs_0_.refs_3_), channel_id=1, source_target_pairs={{0,16},{8,24},{16,0},{24,8},{1,17},{9,25},{17,1},{25,9},{2,18},{10... | collective-permute-start | bytes 1032200 | tf_op jit(solution)/shard_map/ppermute | solution.py:115
  20.2 7.2 %collective-permute-start.7 = (bf16[4,336,128]{2,1,0:T(8,128)(2,1)S(1)}, bf16[4,336,128]{2,1,0:T(8,128)(2,1)S(1)}, u32[]{:S(2)}, u32[]{:S(2)}) collective-permute-start(bf16[4,336,128]{2,1,0:T(8,128)(2,1)S(1)} %pad_maximum_fusion.refs_0_.refs_3_), channel_id=1, source_target_pairs={{0,8},{8,0},{16,24},{24,16},{1,9},{9,1},{17,25},{25,17},{2,10},{10... | collective-permute-start | bytes 1032200 | tf_op jit(solution)/shard_map/ppermute | solution.py:115
  24.9 3.3 %collective-permute-start.9 = (bf16[4,336,128]{2,1,0:T(8,128)(2,1)S(1)}, bf16[4,336,128]{2,1,0:T(8,128)(2,1)S(1)}, u32[]{:S(2)}, u32[]{:S(2)}) collective-permute-start(bf16[4,336,128]{2,1,0:T(8,128)(2,1)S(1)} %collective-permute-done.4.refs_2_.refs_5_), channel_id=1, source_target_pairs={{0,8},{8,0},{16,24},{24,16},{1,9},{9,1},{17,25},{25,17},{2,10},{10... | collective-permute-start | bytes 1032200 | tf_op jit(solution)/shard_map/ppermute | solution.py:115
  25.0 8.3 %collective-permute-start.6 = (bf16[4,176,128]{2,1,0:T(8,128)(2,1)S(1)}, bf16[4,176,128]{2,1,0:T(8,128)(2,1)S(1)}, u32[]{:S(2)}, u32[]{:S(2)}) collective-permute-start(bf16[4,176,128]{2,1,0:T(8,128)(2,1)S(1)} %slice_add_fusion), channel_id=1, source_target_pairs={{0,16},{8,24},{16,0},{24,8},{1,17},{9,25},{17,1},{25,9},{2,18},{10... | collective-permute-start | bytes 540680 | tf_op jit(solution)/shard_map/ppermute | solution.py:115
  26.6 1.7 %collective-permute-start.8 = (bf16[4,336,128]{2,1,0:T(8,128)(2,1)S(1)}, bf16[4,336,128]{2,1,0:T(8,128)(2,1)S(1)}, u32[]{:S(2)}, u32[]{:S(2)}) collective-permute-start(bf16[4,336,128]{2,1,0:T(8,128)(2,1)S(1)} %collective-permute-done.3.refs_1_.refs_4_), channel_id=1, source_target_pairs={{0,8},{8,0},{16,24},{24,16},{1,9},{9,1},{17,25},{25,17},{2,10},{10... | collective-permute-start | bytes 1032200 | tf_op jit(solution)/shard_map/ppermute | solution.py:115
  26.8 6.5 %collective-permute-start.5 = (bf16[4,160,128]{2,1,0:T(8,128)(2,1)S(1)}, bf16[4,160,128]{2,1,0:T(8,128)(2,1)S(1)}, u32[]{:S(2)}, u32[]{:S(2)}) collective-permute-start(bf16[4,160,128]{2,1,0:T(8,128)(2,1)S(1)} %slice_add_fusion.1), channel_id=1, source_target_pairs={{0,1},{1,0},{2,3},{3,2},{4,5},{5,4},{6,7},{7,6},{8,9},{9,8},{10,11... | collective-permute-start | bytes 491528 | tf_op jit(solution)/shard_map/ppermute | solution.py:117
  33.3 1.7 %collective-permute-start.11 = (bf16[4,176,128]{2,1,0:T(8,128)(2,1)S(1)}, bf16[4,176,128]{2,1,0:T(8,128)(2,1)S(1)}, u32[]{:S(2)}, u32[]{:S(2)}) collective-permute-start(bf16[4,176,128]{2,1,0:T(8,128)(2,1)S(1)} %collective-permute-done.6.refs_10_), channel_id=1, source_target_pairs={{0,8},{8,0},{16,24},{24,16},{1,9},{9,1},{17,25},{25,17},{2,10},{10... | collective-permute-start | bytes 540680 | tf_op jit(solution)/shard_map/ppermute | solution.py:115
  33.3 1.7 %collective-permute-start.10 = (bf16[4,160,128]{2,1,0:T(8,128)(2,1)S(1)}, bf16[4,160,128]{2,1,0:T(8,128)(2,1)S(1)}, u32[]{:S(2)}, u32[]{:S(2)}) collective-permute-start(bf16[4,160,128]{2,1,0:T(8,128)(2,1)S(1)} %collective-permute-done.5.refs_9_), channel_id=1, source_target_pairs={{0,8},{8,0},{16,24},{24,16},{1,9},{9,1},{17,25},{25,17},{2,10},{10... | collective-permute-start | bytes 491528 | tf_op jit(solution)/shard_map/ppermute | solution.py:115
  39.5 26.3 %copy-start.13 = (f32[2,32,32]{2,1,0:T(8,128)S(1)}, f32[2,32,32]{2,1,0:T(8,128)}, u32[]{:S(2)}) copy-start(f32[2,32,32]{2,1,0:T(8,128)} %wt_hbm.1) | copy-start | bytes 24580
  39.5 41.5 %copy-start.1 = (bf16[1024,1024]{1,0:T(8,128)(2,1)S(1)}, bf16[1024,1024]{1,0:T(8,128)(2,1)}, u32[]{:S(2)}) copy-start(bf16[1024,1024]{1,0:T(8,128)(2,1)} %copy-done) | copy-start | bytes 6291460
  39.5 1.2 collective-permute-start.12
  69.6 1.3 collective-permute-start.13
  85.1 2.7 %collective-permute-start.14 = (f32[2048,128]{1,0:T(8,128)S(1)}, f32[2048,128]{1,0:T(8,128)S(1)}, u32[]{:S(2)}, u32[]{:S(2)}) collective-permute-start(f32[2048,128]{1,0:T(8,128)S(1)} %get-tuple-element.135), channel_id=1, source_target_pairs={{0,8},{8,0},{16,24},{24,16},{1,9},{9,1},{17,25},{25,17},{2,10},{10... | collective-permute-start | bytes 3145736 | tf_op jit(solution)/shard_map/ppermute | solution.py:115
  85.3 4.0 %collective-permute-start.17 = (f32[2048,128]{1,0:T(8,128)S(1)}, f32[2048,128]{1,0:T(8,128)S(1)}, u32[]{:S(2)}, u32[]{:S(2)}) collective-permute-start(f32[2048,128]{1,0:T(8,128)S(1)} %get-tuple-element.137), channel_id=1, source_target_pairs={{0,8},{8,0},{16,24},{24,16},{1,9},{9,1},{17,25},{25,17},{2,10},{10... | collective-permute-start | bytes 3145736 | tf_op jit(solution)/shard_map/ppermute | solution.py:115
  88.0 14.0 %collective-permute-start.15 = (f32[2,4,128,128]{3,2,1,0:T(8,128)S(1)}, f32[2,4,128,128]{3,2,1,0:T(8,128)S(1)}, u32[]{:S(2)}, u32[]{:S(2)}) collective-permute-start(f32[2,4,128,128]{3,2,1,0:T(8,128)S(1)} %bitcast.70), channel_id=1, source_target_pairs={{0,16},{8,24},{16,0},{24,8},{1,17},{9,25},{17,1},{25,9},{2,18},{10... | collective-permute-start | bytes 1572872 | tf_op jit(solution)/shard_map/ppermute | solution.py:115
  89.5 14.0 %collective-permute-start.18 = (f32[2,4,128,128]{3,2,1,0:T(8,128)S(1)}, f32[2,4,128,128]{3,2,1,0:T(8,128)S(1)}, u32[]{:S(2)}, u32[]{:S(2)}) collective-permute-start(f32[2,4,128,128]{3,2,1,0:T(8,128)S(1)} %slice_bitcast_fusion), channel_id=1, source_target_pairs={{0,1},{1,0},{2,3},{3,2},{4,5},{5,4},{6,7},{7,6},{8,9},{9,8},{10,11... | collective-permute-start | bytes 1572872 | tf_op jit(solution)/shard_map/ppermute | solution.py:117
  102.1 33.1 %copy-start.4 = (f32[8,64,128]{2,1,0:T(8,128)S(1)}, f32[8,64,128]{2,1,0:T(8,128)}, u32[]{:S(2)}) copy-start(f32[8,64,128]{2,1,0:T(8,128)} %copy-done.3) | copy-start | bytes 786436
  102.1 33.1 %copy-start.6 = (f32[8,64,128]{2,1,0:T(8,128)S(1)}, f32[8,64,128]{2,1,0:T(8,128)}, u32[]{:S(2)}) copy-start(f32[8,64,128]{2,1,0:T(8,128)} %copy-done.5) | copy-start | bytes 786436
  102.1 33.1 %copy-start.8 = (f32[8,64,128]{2,1,0:T(8,128)S(1)}, f32[8,64,128]{2,1,0:T(8,128)}, u32[]{:S(2)}) copy-start(f32[8,64,128]{2,1,0:T(8,128)} %copy-done.7) | copy-start | bytes 786436
  102.2 33.1 %copy-start.10 = (f32[8,64,64]{2,1,0:T(8,128)S(1)}, f32[8,64,64]{2,1,0:T(8,128)}, u32[]{:S(2)}) copy-start(f32[8,64,64]{2,1,0:T(8,128)} %copy-done.9) | copy-start | bytes 393220
  102.2 33.1 %copy-start.12 = (f32[8,64,128]{2,1,0:T(8,128)S(1)}, f32[8,64,128]{2,1,0:T(8,128)}, u32[]{:S(2)}) copy-start(f32[8,64,128]{2,1,0:T(8,128)} %copy-done.11) | copy-start | bytes 786436
  102.2 7.6 %collective-permute-start.16 = (f32[4,128,128]{2,1,0:T(8,128)S(1)}, f32[4,128,128]{2,1,0:T(8,128)S(1)}, u32[]{:S(2)}, u32[]{:S(2)}) collective-permute-start(f32[4,128,128]{2,1,0:T(8,128)S(1)} %slice_bitcast_fusion.4), channel_id=1, source_target_pairs={{0,1},{1,0},{2,3},{3,2},{4,5},{5,4},{6,7},{7,6},{8,9},{9,8},{10,11... | collective-permute-start | bytes 786440 | tf_op jit(solution)/shard_map/ppermute | solution.py:117
  103.6 7.6 %collective-permute-start.19 = (f32[4,128,128]{2,1,0:T(8,128)S(1)}, f32[4,128,128]{2,1,0:T(8,128)S(1)}, u32[]{:S(2)}, u32[]{:S(2)}) collective-permute-start(f32[4,128,128]{2,1,0:T(8,128)S(1)} %slice_bitcast_fusion.2), channel_id=1, source_target_pairs={{0,16},{8,24},{16,0},{24,8},{1,17},{9,25},{17,1},{25,9},{2,18},{10... | collective-permute-start | bytes 786440 | tf_op jit(solution)/shard_map/ppermute | solution.py:115
  111.3 8.4 %collective-permute-start.22 = (f32[256,128]{1,0:T(8,128)S(1)}, f32[256,128]{1,0:T(8,128)S(1)}, u32[]{:S(2)}, u32[]{:S(2)}) collective-permute-start(f32[256,128]{1,0:T(8,128)S(1)} %get-tuple-element.178), channel_id=1, source_target_pairs={{0,6},{1,7},{2,4},{3,5},{4,2},{5,3},{6,0},{7,1},{8,14},{9,15},{10,... | collective-permute-start | bytes 393224 | tf_op jit(solution)/shard_map/ppermute | solution.py:117
  112.6 7.1 %collective-permute-start.20 = (f32[256,128]{1,0:T(8,128)S(1)}, f32[256,128]{1,0:T(8,128)S(1)}, u32[]{:S(2)}, u32[]{:S(2)}) collective-permute-start(f32[256,128]{1,0:T(8,128)S(1)} %get-tuple-element.179), channel_id=1, source_target_pairs={{0,2},{1,3},{2,0},{3,1},{4,6},{5,7},{6,4},{7,5},{8,10},{9,11},{10,... | collective-permute-start | bytes 393224 | tf_op jit(solution)/shard_map/ppermute | solution.py:117
  113.3 10.7 %collective-permute-start.21 = (f32[256,128]{1,0:T(8,128)S(1)}, f32[256,128]{1,0:T(8,128)S(1)}, u32[]{:S(2)}, u32[]{:S(2)}) collective-permute-start(f32[256,128]{1,0:T(8,128)S(1)} %get-tuple-element.180), channel_id=1, source_target_pairs={{0,4},{1,5},{2,6},{3,7},{4,0},{5,1},{6,2},{7,3},{8,12},{9,13},{10,... | collective-permute-start | bytes 393224 | tf_op jit(solution)/shard_map/ppermute | solution.py:117
  124.9 10.3 %all-to-all-start.3 = ((bf16[32,16,128]{2,1,0:T(8,128)(2,1)}), bf16[32,16,128]{2,1,0:T(8,128)(2,1)S(1)}, u32[]{:S(2)}, u32[]{:S(2)}) async-start(bf16[32,16,128]{2,1,0:T(8,128)(2,1)} %bitcast.24), calls=%async_computation.3 | async-start | bytes 262144 | tf_op jit(solution)/shard_map/all_to_all | solution.py:859
  (9 other events, 134.3 us)
